TPU v7x, 32 devices: a whole 2x2x4 slice. The times are simulated.
32 devices in a mesh: grp: 4 (over y, core), gx: 2 (over x), gy: 4 (over z).
Axes of the slice: x: 2, y: 2, z: 4, core: 2. Of those that a mesh axis runs over, the one named last changes fastest.
Arguments:
- terminal: float32 [4, 8, 64, 512], P(None, 'gx', 'gy', 'grp'), may hold values from -6 to 6
- diffusion: float32 [4], replicated, may hold values from 0.03 to 0.1
- velocity: float32 [8, 64, 512], P('gx', 'gy', 'grp'), may hold values from 0.02 to 0.3
- material: int32 [8, 64, 512], P('gx', 'gy', 'grp'), may hold values from 0 to 7
- rates: float32 [8, 8], replicated, may hold values from 0.005 to 0.04
- stoich: int32 [8, 4], replicated, may hold values from -1 to 1
- plan: int32 [8], replicated, may hold values from 0 to 15, as said below
- basis: bfloat16 [4, 8, 64, 512, 256], P('grp', 'gx', 'gy')
Outputs:
- coefficients: float32 [8, 256], replicated
- adjoint: float32 [4, 8, 64, 512], P(None, 'gx', 'gy', 'grp')
Inputs may be any that keep to these rules, and one draw needn't show every extreme that they name: `plan`: 8 different step numbers in increasing order.
All inputs are finite; a program needn't handle non-finite values.
Results may differ from a plain program's by a relative error of at most 0.0045.
Values sent between devices are 32-bit elements; how exact they have to be, the bound alone decides.
No kernel may reach another device: no remote copies, remote signals or barrier semaphores. Data moves between devices by JAX's collectives and lax.ppermute only.
A program may use at most 64 MiB of HBM per device.

v0:
```python
import jax
import jax.numpy as jnp
from jax import lax
from jax.sharding import PartitionSpec as P

STEPS = 16


def padded_2(value, sides, width):
    for axis, dim in sides:
        count, length = (lax.axis_size(axis), value.shape[dim])
        up = [(i, (i + 1) % count) for i in range(count - 1)]
        down = [(j, i) for i, j in up]
        last = lax.slice_in_dim(value, length - width, length, axis=dim)
        leading = lax.slice_in_dim(value, 0, width, axis=dim)
        before = lax.ppermute(last, axis, up)
        after = lax.ppermute(leading, axis, down)
        value = jnp.concatenate([before, value, after], axis=dim)
    return value


def reaction_table(rates, stoich):
    react_count, spec = stoich.shape
    owner = jnp.arange(react_count) % spec
    pick = (owner[:, None] == jnp.arange(spec)[None, :]).astype(jnp.float32)
    return jnp.einsum(
        "mr,ra,rs->mas", rates, pick, stoich.astype(jnp.float32), precision=lax.Precision.HIGHEST
    )


def advance(padded, diffusion, velocity, react):
    center = padded[:, 1:-1, 1:-1, 1:-1]
    ahead = padded[:, 2:, 1:-1, 1:-1]
    beside = ahead + padded[:, :-2, 1:-1, 1:-1]
    beside = beside + padded[:, 1:-1, 2:, 1:-1] + padded[:, 1:-1, :-2, 1:-1]
    beside = beside + padded[:, 1:-1, 1:-1, 2:] + padded[:, 1:-1, 1:-1, :-2]
    spec = center.shape[0]
    sources = []
    for first in range(spec):
        total = react[first * spec] * center[0]
        for second in range(1, spec):
            total = total + react[first * spec + second] * center[second]
        sources.append(total)
    source = jnp.stack(sources)
    return (
        center
        + diffusion[:, None, None, None] * (beside - 6.0 * center)
        + velocity[None] * (ahead - center)
        + source
    )


def body(terminal, diffusion, velocity, material, rates, stoich, plan, basis):
    spec, cells_x, cells_y, cells_z = terminal.shape
    kinds_count = rates.shape[0]
    table = reaction_table(rates, stoich).reshape(kinds_count, spec * spec)
    kinds = jnp.arange(kinds_count, dtype=jnp.int32)
    onehot = (material.reshape(1, -1) == kinds[:, None]).astype(jnp.float32)
    react = jnp.dot(table.T, onehot, precision=lax.Precision.HIGHEST).reshape(
        spec * spec, cells_x, cells_y, cells_z
    )
    snaps_start = jnp.zeros((plan.shape[0],) + terminal.shape, jnp.float32)

    def keep(snaps, lam, index):
        hit = (plan == index).reshape(-1, 1, 1, 1, 1)
        return jnp.where(hit, lam[None], snaps)

    inside = jnp.ones((1, cells_x, cells_y, cells_z), jnp.float32)
    coeffs = jnp.concatenate([velocity[None], inside, react], 0)
    rim = padded_2(coeffs, (("grp", 3), ("gx", 1), ("gy", 2)), 1)

    def pair_step(turn, carry):
        lam, snaps = carry
        padded = padded_2(lam, (("grp", 3), ("gx", 1), ("gy", 2)), 2)
        middle = advance(padded, diffusion, rim[0], rim[2:]) * rim[1][None]
        lam = advance(middle, diffusion, velocity, react)
        snaps = keep(snaps, middle[:, 1:-1, 1:-1, 1:-1], 2 * turn)
        snaps = keep(snaps, lam, 2 * turn + 1)
        return (lam, snaps)

    final, snaps = lax.fori_loop(0, STEPS // 2, pair_step, (terminal, snaps_start))
    moved = lax.all_to_all(snaps, "grp", split_axis=1, concat_axis=4, tiled=True)
    flat = moved.reshape(moved.shape[0], -1)
    local = basis.reshape(-1, basis.shape[-1])
    first = lax.psum(
        jnp.dot(flat.astype(jnp.bfloat16), local, preferred_element_type=jnp.float32),
        ("grp", "gx", "gy"),
    )
    proj = lax.dot_general(
        first.astype(jnp.bfloat16),
        local,
        (((1,), (1,)), ((), ())),
        preferred_element_type=jnp.float32,
    )
    rest = flat - proj
    second = lax.psum(
        jnp.dot(rest.astype(jnp.bfloat16), local, preferred_element_type=jnp.float32),
        ("grp", "gx", "gy"),
    )
    return (first + second, final)


def solution(mesh):
    in_specs = (
        P(None, "gx", "gy", "grp"),
        P(),
        P("gx", "gy", "grp"),
        P("gx", "gy", "grp"),
        P(),
        P(),
        P(),
        P("grp", "gx", "gy", None, None),
    )
    out_specs = (P(), P(None, "gx", "gy", "grp"))
    return jax.shard_map(body, mesh=mesh, in_specs=in_specs, out_specs=out_specs, check_vma=False)
```

profile of v0, /device:TPU:0, one launch (start us, length us, event | category | flops | bytes accessed | tf_op | source)
XLA Modules:
  0.0 414.8 jit_solution(11730460473265042817)
XLA Ops:
  4.4 2.4 collective-permute-start.6
  9.0 3.4 collective-permute-done.7
  13.5 3.4 collective-permute-start.8
  17.0 1.3 collective-permute-start.9
  18.3 6.4 %collective-permute-done.8 = f32[18,1,16,130]{3,0,2,1:T(8,128)S(1)} collective-permute-done((f32[18,1,16,130]{3,0,2,1:T(8,128)S(1)}, f32[18,1,16,130]{3,0,2,1:T(8,128)S(1)}, u32[]{:S(2)}, u32[]{:S(2)}) %collective-permute-start.8) | collective-permute-done | bytes 149792 | tf_op jit(solution)/shard_map/ppermute | solution.py:16
  24.7 4.7 %collective-permute-done.9 = f32[18,1,16,130]{3,0,2,1:T(8,128)S(1)} collective-permute-done((f32[18,1,16,130]{3,0,2,1:T(8,128)S(1)}, f32[18,1,16,130]{3,0,2,1:T(8,128)S(1)}, u32[]{:S(2)}, u32[]{:S(2)}) %collective-permute-start.9) | collective-permute-done | bytes 149792 | tf_op jit(solution)/shard_map/ppermute | solution.py:17
  30.3 3.5 collective-permute-start.10
  33.7 1.3 collective-permute-start.11
  36.0 2.0 collective-permute-done.10
  38.0 4.4 %collective-permute-done.11 = f32[18,6,1,130]{3,0,2,1:T(8,128)S(1)} collective-permute-done((f32[18,6,1,130]{3,0,2,1:T(8,128)S(1)}, f32[18,6,1,130]{3,0,2,1:T(8,128)S(1)}, u32[]{:S(2)}, u32[]{:S(2)}) %collective-permute-start.11) | collective-permute-done | bytes 56192 | tf_op jit(solution)/shard_map/ppermute | solution.py:17
  44.4 234.5 %while.16 = (s32[]{:T(128)}, f32[4,4,16,128]{3,2,1,0:T(8,128)S(1)}, f32[8,4,4,16,128]{4,3,2,1,0:T(8,128)}, f32[4]{0:T(128)S(1)}, f32[18,6,18,130]{3,2,1,0:T(8,12...) while((s32[]{:T(128)}, f32[4,4,16,128]{3,2,1,0:T(8,128)S(1)}, ...), condition=%wide.region_1.2_spmd.clone, body=%wide.region_0.1_spmd.clone.sunk | while | flops 4091605 | bytes 21316484 | solution.py:81
  44.5 1.3 collective-permute-start
  45.8 3.0 collective-permute-start.1
  52.0 4.6 %collective-permute-start.3 = (f32[4,2,16,132]{3,2,1,0:T(8,128)S(1)}, f32[4,2,16,132]{3,2,1,0:T(8,128)S(1)}, u32[]{:S(2)}, u32[]{:S(2)}) collective-permute-start(f32[4,2,16,132]{3,2,1,0:T(8,128)S(1)} %get-tuple-element.311), channel_id=1, source_target_pairs={{0,4},{1,5},{2,6},{3,7},{8,12},{9,13},{10,14},{11,15},{16,20},{17,... | collective-permute-start | bytes 202760 | tf_op jit(solution)/shard_map/while/body/eval_jaxpr/ppermute | solution.py:16
  57.7 1.6 collective-permute-done.3
  61.4 4.5 %collective-permute-start.5 = (f32[4,8,2,132]{3,2,1,0:T(2,128)S(1)}, f32[4,8,2,132]{3,2,1,0:T(2,128)S(1)}, u32[]{:S(2)}, u32[]{:S(2)}) collective-permute-start(f32[4,8,2,132]{3,2,1,0:T(2,128)S(1)} %get-tuple-element.313), channel_id=1, source_target_pairs={{0,1},{1,2},{2,3},{4,5},{5,6},{6,7},{8,9},{9,10},{10,11},{12,13},{... | collective-permute-start | bytes 101384 | tf_op jit(solution)/shard_map/while/body/eval_jaxpr/ppermute | solution.py:16
  66.9 1.4 collective-permute-done.5
  72.2 1.3 collective-permute-start
  73.5 3.0 collective-permute-start.1
  79.7 4.6 %collective-permute-start.3 = (f32[4,2,16,132]{3,2,1,0:T(8,128)S(1)}, f32[4,2,16,132]{3,2,1,0:T(8,128)S(1)}, u32[]{:S(2)}, u32[]{:S(2)}) collective-permute-start(f32[4,2,16,132]{3,2,1,0:T(8,128)S(1)} %get-tuple-element.311), channel_id=1, source_target_pairs={{0,4},{1,5},{2,6},{3,7},{8,12},{9,13},{10,14},{11,15},{16,20},{17,... | collective-permute-start | bytes 202760 | tf_op jit(solution)/shard_map/while/body/eval_jaxpr/ppermute | solution.py:16
  88.8 5.0 %collective-permute-start.5 = (f32[4,8,2,132]{3,2,1,0:T(2,128)S(1)}, f32[4,8,2,132]{3,2,1,0:T(2,128)S(1)}, u32[]{:S(2)}, u32[]{:S(2)}) collective-permute-start(f32[4,8,2,132]{3,2,1,0:T(2,128)S(1)} %get-tuple-element.313), channel_id=1, source_target_pairs={{0,1},{1,2},{2,3},{4,5},{5,6},{6,7},{8,9},{9,10},{10,11},{12,13},{... | collective-permute-start | bytes 101384 | tf_op jit(solution)/shard_map/while/body/eval_jaxpr/ppermute | solution.py:16
  99.6 1.3 collective-permute-start
  100.9 4.9 %collective-permute-start.1 = (f32[4,4,16,2]{3,2,1,0:T(8,128)S(1)}, f32[4,4,16,2]{3,2,1,0:T(8,128)S(1)}, u32[]{:S(2)}, u32[]{:S(2)}) collective-permute-start(f32[4,4,16,2]{3,2,1,0:T(8,128)S(1)} %get-tuple-element.309), channel_id=1, source_target_pairs={{0,8},{8,16},{16,24},{1,9},{9,17},{17,25},{2,10},{10,18},{18,26},{... | collective-permute-start | bytes 6152 | tf_op jit(solution)/shard_map/while/body/eval_jaxpr/ppermute | solution.py:16
  108.9 4.6 %collective-permute-start.3 = (f32[4,2,16,132]{3,2,1,0:T(8,128)S(1)}, f32[4,2,16,132]{3,2,1,0:T(8,128)S(1)}, u32[]{:S(2)}, u32[]{:S(2)}) collective-permute-start(f32[4,2,16,132]{3,2,1,0:T(8,128)S(1)} %get-tuple-element.311), channel_id=1, source_target_pairs={{0,4},{1,5},{2,6},{3,7},{8,12},{9,13},{10,14},{11,15},{16,20},{17,... | collective-permute-start | bytes 202760 | tf_op jit(solution)/shard_map/while/body/eval_jaxpr/ppermute | solution.py:16
  118.0 4.6 %collective-permute-start.5 = (f32[4,8,2,132]{3,2,1,0:T(2,128)S(1)}, f32[4,8,2,132]{3,2,1,0:T(2,128)S(1)}, u32[]{:S(2)}, u32[]{:S(2)}) collective-permute-start(f32[4,8,2,132]{3,2,1,0:T(2,128)S(1)} %get-tuple-element.313), channel_id=1, source_target_pairs={{0,1},{1,2},{2,3},{4,5},{5,6},{6,7},{8,9},{9,10},{10,11},{12,13},{... | collective-permute-start | bytes 101384 | tf_op jit(solution)/shard_map/while/body/eval_jaxpr/ppermute | solution.py:16
  128.4 1.3 collective-permute-start
  129.7 6.2 %collective-permute-start.1 = (f32[4,4,16,2]{3,2,1,0:T(8,128)S(1)}, f32[4,4,16,2]{3,2,1,0:T(8,128)S(1)}, u32[]{:S(2)}, u32[]{:S(2)}) collective-permute-start(f32[4,4,16,2]{3,2,1,0:T(8,128)S(1)} %get-tuple-element.309), channel_id=1, source_target_pairs={{0,8},{8,16},{16,24},{1,9},{9,17},{17,25},{2,10},{10,18},{18,26},{... | collective-permute-start | bytes 6152 | tf_op jit(solution)/shard_map/while/body/eval_jaxpr/ppermute | solution.py:16
  139.0 4.6 %collective-permute-start.3 = (f32[4,2,16,132]{3,2,1,0:T(8,128)S(1)}, f32[4,2,16,132]{3,2,1,0:T(8,128)S(1)}, u32[]{:S(2)}, u32[]{:S(2)}) collective-permute-start(f32[4,2,16,132]{3,2,1,0:T(8,128)S(1)} %get-tuple-element.311), channel_id=1, source_target_pairs={{0,4},{1,5},{2,6},{3,7},{8,12},{9,13},{10,14},{11,15},{16,20},{17,... | collective-permute-start | bytes 202760 | tf_op jit(solution)/shard_map/while/body/eval_jaxpr/ppermute | solution.py:16
  148.1 4.6 %collective-permute-start.5 = (f32[4,8,2,132]{3,2,1,0:T(2,128)S(1)}, f32[4,8,2,132]{3,2,1,0:T(2,128)S(1)}, u32[]{:S(2)}, u32[]{:S(2)}) collective-permute-start(f32[4,8,2,132]{3,2,1,0:T(2,128)S(1)} %get-tuple-element.313), channel_id=1, source_target_pairs={{0,1},{1,2},{2,3},{4,5},{5,6},{6,7},{8,9},{9,10},{10,11},{12,13},{... | collective-permute-start | bytes 101384 | tf_op jit(solution)/shard_map/while/body/eval_jaxpr/ppermute | solution.py:16
  159.8 6.2 %collective-permute-start.1 = (f32[4,4,16,2]{3,2,1,0:T(8,128)S(1)}, f32[4,4,16,2]{3,2,1,0:T(8,128)S(1)}, u32[]{:S(2)}, u32[]{:S(2)}) collective-permute-start(f32[4,4,16,2]{3,2,1,0:T(8,128)S(1)} %get-tuple-element.309), channel_id=1, source_target_pairs={{0,8},{8,16},{16,24},{1,9},{9,17},{17,25},{2,10},{10,18},{18,26},{... | collective-permute-start | bytes 6152 | tf_op jit(solution)/shard_map/while/body/eval_jaxpr/ppermute | solution.py:16
  169.1 4.6 %collective-permute-start.3 = (f32[4,2,16,132]{3,2,1,0:T(8,128)S(1)}, f32[4,2,16,132]{3,2,1,0:T(8,128)S(1)}, u32[]{:S(2)}, u32[]{:S(2)}) collective-permute-start(f32[4,2,16,132]{3,2,1,0:T(8,128)S(1)} %get-tuple-element.311), channel_id=1, source_target_pairs={{0,4},{1,5},{2,6},{3,7},{8,12},{9,13},{10,14},{11,15},{16,20},{17,... | collective-permute-start | bytes 202760 | tf_op jit(solution)/shard_map/while/body/eval_jaxpr/ppermute | solution.py:16
  178.3 4.6 %collective-permute-start.5 = (f32[4,8,2,132]{3,2,1,0:T(2,128)S(1)}, f32[4,8,2,132]{3,2,1,0:T(2,128)S(1)}, u32[]{:S(2)}, u32[]{:S(2)}) collective-permute-start(f32[4,8,2,132]{3,2,1,0:T(2,128)S(1)} %get-tuple-element.313), channel_id=1, source_target_pairs={{0,1},{1,2},{2,3},{4,5},{5,6},{6,7},{8,9},{9,10},{10,11},{12,13},{... | collective-permute-start | bytes 101384 | tf_op jit(solution)/shard_map/while/body/eval_jaxpr/ppermute | solution.py:16
  188.6 1.3 collective-permute-start
  189.9 6.2 %collective-permute-start.1 = (f32[4,4,16,2]{3,2,1,0:T(8,128)S(1)}, f32[4,4,16,2]{3,2,1,0:T(8,128)S(1)}, u32[]{:S(2)}, u32[]{:S(2)}) collective-permute-start(f32[4,4,16,2]{3,2,1,0:T(8,128)S(1)} %get-tuple-element.309), channel_id=1, source_target_pairs={{0,8},{8,16},{16,24},{1,9},{9,17},{17,25},{2,10},{10,18},{18,26},{... | collective-permute-start | bytes 6152 | tf_op jit(solution)/shard_map/while/body/eval_jaxpr/ppermute | solution.py:16
  199.3 4.6 %collective-permute-start.3 = (f32[4,2,16,132]{3,2,1,0:T(8,128)S(1)}, f32[4,2,16,132]{3,2,1,0:T(8,128)S(1)}, u32[]{:S(2)}, u32[]{:S(2)}) collective-permute-start(f32[4,2,16,132]{3,2,1,0:T(8,128)S(1)} %get-tuple-element.311), channel_id=1, source_target_pairs={{0,4},{1,5},{2,6},{3,7},{8,12},{9,13},{10,14},{11,15},{16,20},{17,... | collective-permute-start | bytes 202760 | tf_op jit(solution)/shard_map/while/body/eval_jaxpr/ppermute | solution.py:16
  208.4 4.6 %collective-permute-start.5 = (f32[4,8,2,132]{3,2,1,0:T(2,128)S(1)}, f32[4,8,2,132]{3,2,1,0:T(2,128)S(1)}, u32[]{:S(2)}, u32[]{:S(2)}) collective-permute-start(f32[4,8,2,132]{3,2,1,0:T(2,128)S(1)} %get-tuple-element.313), channel_id=1, source_target_pairs={{0,1},{1,2},{2,3},{4,5},{5,6},{6,7},{8,9},{9,10},{10,11},{12,13},{... | collective-permute-start | bytes 101384 | tf_op jit(solution)/shard_map/while/body/eval_jaxpr/ppermute | solution.py:16
  220.1 6.2 %collective-permute-start.1 = (f32[4,4,16,2]{3,2,1,0:T(8,128)S(1)}, f32[4,4,16,2]{3,2,1,0:T(8,128)S(1)}, u32[]{:S(2)}, u32[]{:S(2)}) collective-permute-start(f32[4,4,16,2]{3,2,1,0:T(8,128)S(1)} %get-tuple-element.309), channel_id=1, source_target_pairs={{0,8},{8,16},{16,24},{1,9},{9,17},{17,25},{2,10},{10,18},{18,26},{... | collective-permute-start | bytes 6152 | tf_op jit(solution)/shard_map/while/body/eval_jaxpr/ppermute | solution.py:16
  229.4 4.6 %collective-permute-start.3 = (f32[4,2,16,132]{3,2,1,0:T(8,128)S(1)}, f32[4,2,16,132]{3,2,1,0:T(8,128)S(1)}, u32[]{:S(2)}, u32[]{:S(2)}) collective-permute-start(f32[4,2,16,132]{3,2,1,0:T(8,128)S(1)} %get-tuple-element.311), channel_id=1, source_target_pairs={{0,4},{1,5},{2,6},{3,7},{8,12},{9,13},{10,14},{11,15},{16,20},{17,... | collective-permute-start | bytes 202760 | tf_op jit(solution)/shard_map/while/body/eval_jaxpr/ppermute | solution.py:16
  238.5 4.6 %collective-permute-start.5 = (f32[4,8,2,132]{3,2,1,0:T(2,128)S(1)}, f32[4,8,2,132]{3,2,1,0:T(2,128)S(1)}, u32[]{:S(2)}, u32[]{:S(2)}) collective-permute-start(f32[4,8,2,132]{3,2,1,0:T(2,128)S(1)} %get-tuple-element.313), channel_id=1, source_target_pairs={{0,1},{1,2},{2,3},{4,5},{5,6},{6,7},{8,9},{9,10},{10,11},{12,13},{... | collective-permute-start | bytes 101384 | tf_op jit(solution)/shard_map/while/body/eval_jaxpr/ppermute | solution.py:16
  250.2 6.2 %collective-permute-start.1 = (f32[4,4,16,2]{3,2,1,0:T(8,128)S(1)}, f32[4,4,16,2]{3,2,1,0:T(8,128)S(1)}, u32[]{:S(2)}, u32[]{:S(2)}) collective-permute-start(f32[4,4,16,2]{3,2,1,0:T(8,128)S(1)} %get-tuple-element.309), channel_id=1, source_target_pairs={{0,8},{8,16},{16,24},{1,9},{9,17},{17,25},{2,10},{10,18},{18,26},{... | collective-permute-start | bytes 6152 | tf_op jit(solution)/shard_map/while/body/eval_jaxpr/ppermute | solution.py:16
  259.5 4.6 %collective-permute-start.3 = (f32[4,2,16,132]{3,2,1,0:T(8,128)S(1)}, f32[4,2,16,132]{3,2,1,0:T(8,128)S(1)}, u32[]{:S(2)}, u32[]{:S(2)}) collective-permute-start(f32[4,2,16,132]{3,2,1,0:T(8,128)S(1)} %get-tuple-element.311), channel_id=1, source_target_pairs={{0,4},{1,5},{2,6},{3,7},{8,12},{9,13},{10,14},{11,15},{16,20},{17,... | collective-permute-start | bytes 202760 | tf_op jit(solution)/shard_map/while/body/eval_jaxpr/ppermute | solution.py:16
  268.7 4.6 %collective-permute-start.5 = (f32[4,8,2,132]{3,2,1,0:T(2,128)S(1)}, f32[4,8,2,132]{3,2,1,0:T(2,128)S(1)}, u32[]{:S(2)}, u32[]{:S(2)}) collective-permute-start(f32[4,8,2,132]{3,2,1,0:T(2,128)S(1)} %get-tuple-element.313), channel_id=1, source_target_pairs={{0,1},{1,2},{2,3},{4,5},{5,6},{6,7},{8,9},{9,10},{10,11},{12,13},{... | collective-permute-start | bytes 101384 | tf_op jit(solution)/shard_map/while/body/eval_jaxpr/ppermute | solution.py:16
  278.9 1.4 copy.28
  280.3 23.5 %all_to_all.15 = f32[8,4,4,16,128]{4,3,2,0,1:T(8,128)S(1)} all-to-all(f32[8,4,4,16,128]{4,3,2,0,1:T(8,128)S(1)} %copy.28), channel_id=1, replica_groups=mesh['grp'=4,'gx'=2,'gy'=4] {'grp'}, dimensions={1} | all-to-all | bytes 2097152 | tf_op jit(solution)/shard_map/all_to_all | solution.py:82
  305.9 8.0 %fusion.32 = f32[8,256]{1,0:T(8,128)S(1)} fusion(bf16[8,32768]{1,0:T(8,128)(2,1)S(1)} %convert_element_type.19, bf16[32768,256]{1,0:T(8,128)(2,1)} %bitcast.35), kind=kOutput, calls=%fused_computation.88 | convolution fusion | flops 134217728 | bytes 17309696 | tf_op jit(solution)/shard_map/dot_general | solution.py:86
  313.9 41.6 %psum.14 = f32[8,256]{1,0:T(8,128)S(1)} all-reduce(f32[8,256]{1,0:T(8,128)S(1)} %fusion.32), channel_id=1, replica_groups=mesh['grp'=4,'gx'=2,'gy'=4] {'grp','gx','gy'}, use_global_device_ids=true, to_apply=%region_2.3 | all-reduce | flops 2048 | bytes 16384 | tf_op jit(solution)/shard_map/psum | solution.py:85
  355.5 17.0 %fusion.15 = f32[8,256]{1,0:T(8,128)S(1)} fusion(bf16[32768,256]{1,0:T(8,128)(2,1)} %bitcast.36, f32[8,32768]{1,0:T(8,128)S(1)} %reshape.65, f32[8,256]{1,0:T(8,128)S(1)} %psum.14), kind=kOutput, calls=%fused_computation.57 | convolution fusion | flops 268961792 | bytes 17842176 | tf_op jit(solution)/shard_map/dot_general | solution.py:97
  372.5 41.6 %psum.15 = f32[8,256]{1,0:T(8,128)S(1)} all-reduce(f32[8,256]{1,0:T(8,128)S(1)} %fusion.15), channel_id=1, replica_groups=mesh['grp'=4,'gx'=2,'gy'=4] {'grp','gx','gy'}, use_global_device_ids=true, to_apply=%region_3.4 | all-reduce | flops 2048 | bytes 16384 | tf_op jit(solution)/shard_map/psum | solution.py:96
  (254 shorter events, 121.4 us)
Async XLA Ops:
  13.5 11.2 %collective-permute-start.8 = (f32[18,1,16,130]{3,0,2,1:T(8,128)S(1)}, f32[18,1,16,130]{3,0,2,1:T(8,128)S(1)}, u32[]{:S(2)}, u32[]{:S(2)}) collective-permute-start(f32[18,1,16,130]{3,0,2,1:T(8,128)S(1)} %get-tuple-element.235), channel_id=1, source_target_pairs={{0,4},{1,5},{2,6},{3,7},{8,12},{9,13},{10,14},{11,15},{16,20},{17,... | collective-permute-start | bytes 449288 | tf_op jit(solution)/shard_map/ppermute | solution.py:16
  17.0 12.5 %collective-permute-start.9 = (f32[18,1,16,130]{3,0,2,1:T(8,128)S(1)}, f32[18,1,16,130]{3,0,2,1:T(8,128)S(1)}, u32[]{:S(2)}, u32[]{:S(2)}) collective-permute-start(f32[18,1,16,130]{3,0,2,1:T(8,128)S(1)} %get-tuple-element.236), channel_id=1, source_target_pairs={{4,0},{5,1},{6,2},{7,3},{12,8},{13,9},{14,10},{15,11},{20,16},{21,... | collective-permute-start | bytes 449288 | tf_op jit(solution)/shard_map/ppermute | solution.py:17
  30.3 7.7 %collective-permute-start.10 = (f32[18,6,1,130]{3,0,2,1:T(8,128)}, f32[18,6,1,130]{3,0,2,1:T(8,128)S(1)}, u32[]{:S(2)}, u32[]{:S(2)}) collective-permute-start(f32[18,6,1,130]{3,0,2,1:T(8,128)} %get-tuple-element.233), channel_id=1, source_target_pairs={{0,1},{1,2},{2,3},{4,5},{5,6},{6,7},{8,9},{9,10},{10,11},{12,13},{... | collective-permute-start | bytes 168488 | tf_op jit(solution)/shard_map/ppermute | solution.py:16
  33.7 8.6 %collective-permute-start.11 = (f32[18,6,1,130]{3,0,2,1:T(8,128)S(1)}, f32[18,6,1,130]{3,0,2,1:T(8,128)S(1)}, u32[]{:S(2)}, u32[]{:S(2)}) collective-permute-start(f32[18,6,1,130]{3,0,2,1:T(8,128)S(1)} %get-tuple-element.234), channel_id=1, source_target_pairs={{1,0},{2,1},{3,2},{5,4},{6,5},{7,6},{9,8},{10,9},{11,10},{13,12},{... | collective-permute-start | bytes 168488 | tf_op jit(solution)/shard_map/ppermute | solution.py:17
  50.7 7.1 %collective-permute-start.2 = (f32[4,2,16,132]{3,2,1,0:T(8,128)}, f32[4,2,16,132]{3,2,1,0:T(8,128)S(1)}, u32[]{:S(2)}, u32[]{:S(2)}) collective-permute-start(f32[4,2,16,132]{3,2,1,0:T(8,128)} %get-tuple-element.310), channel_id=1, source_target_pairs={{4,0},{5,1},{6,2},{7,3},{12,8},{13,9},{14,10},{15,11},{20,16},{21,... | collective-permute-start | bytes 202760 | tf_op jit(solution)/shard_map/while/body/eval_jaxpr/ppermute | solution.py:17
  52.0 7.4 %collective-permute-start.3 = (f32[4,2,16,132]{3,2,1,0:T(8,128)S(1)}, f32[4,2,16,132]{3,2,1,0:T(8,128)S(1)}, u32[]{:S(2)}, u32[]{:S(2)}) collective-permute-start(f32[4,2,16,132]{3,2,1,0:T(8,128)S(1)} %get-tuple-element.311), channel_id=1, source_target_pairs={{0,4},{1,5},{2,6},{3,7},{8,12},{9,13},{10,14},{11,15},{16,20},{17,... | collective-permute-start | bytes 202760 | tf_op jit(solution)/shard_map/while/body/eval_jaxpr/ppermute | solution.py:16
  60.1 6.8 %collective-permute-start.4 = (f32[4,8,2,132]{3,2,1,0:T(2,128)}, f32[4,8,2,132]{3,2,1,0:T(2,128)S(1)}, u32[]{:S(2)}, u32[]{:S(2)}) collective-permute-start(f32[4,8,2,132]{3,2,1,0:T(2,128)} %get-tuple-element.312), channel_id=1, source_target_pairs={{1,0},{2,1},{3,2},{5,4},{6,5},{7,6},{9,8},{10,9},{11,10},{13,12},{... | collective-permute-start | bytes 101384 | tf_op jit(solution)/shard_map/while/body/eval_jaxpr/ppermute | solution.py:17
  61.4 7.0 %collective-permute-start.5 = (f32[4,8,2,132]{3,2,1,0:T(2,128)S(1)}, f32[4,8,2,132]{3,2,1,0:T(2,128)S(1)}, u32[]{:S(2)}, u32[]{:S(2)}) collective-permute-start(f32[4,8,2,132]{3,2,1,0:T(2,128)S(1)} %get-tuple-element.313), channel_id=1, source_target_pairs={{0,1},{1,2},{2,3},{4,5},{5,6},{6,7},{8,9},{9,10},{10,11},{12,13},{... | collective-permute-start | bytes 101384 | tf_op jit(solution)/shard_map/while/body/eval_jaxpr/ppermute | solution.py:16
  78.4 7.1 %collective-permute-start.2 = (f32[4,2,16,132]{3,2,1,0:T(8,128)}, f32[4,2,16,132]{3,2,1,0:T(8,128)S(1)}, u32[]{:S(2)}, u32[]{:S(2)}) collective-permute-start(f32[4,2,16,132]{3,2,1,0:T(8,128)} %get-tuple-element.310), channel_id=1, source_target_pairs={{4,0},{5,1},{6,2},{7,3},{12,8},{13,9},{14,10},{15,11},{20,16},{21,... | collective-permute-start | bytes 202760 | tf_op jit(solution)/shard_map/while/body/eval_jaxpr/ppermute | solution.py:17
  79.7 7.1 %collective-permute-start.3 = (f32[4,2,16,132]{3,2,1,0:T(8,128)S(1)}, f32[4,2,16,132]{3,2,1,0:T(8,128)S(1)}, u32[]{:S(2)}, u32[]{:S(2)}) collective-permute-start(f32[4,2,16,132]{3,2,1,0:T(8,128)S(1)} %get-tuple-element.311), channel_id=1, source_target_pairs={{0,4},{1,5},{2,6},{3,7},{8,12},{9,13},{10,14},{11,15},{16,20},{17,... | collective-permute-start | bytes 202760 | tf_op jit(solution)/shard_map/while/body/eval_jaxpr/ppermute | solution.py:16
  87.5 7.0 %collective-permute-start.4 = (f32[4,8,2,132]{3,2,1,0:T(2,128)}, f32[4,8,2,132]{3,2,1,0:T(2,128)S(1)}, u32[]{:S(2)}, u32[]{:S(2)}) collective-permute-start(f32[4,8,2,132]{3,2,1,0:T(2,128)} %get-tuple-element.312), channel_id=1, source_target_pairs={{1,0},{2,1},{3,2},{5,4},{6,5},{7,6},{9,8},{10,9},{11,10},{13,12},{... | collective-permute-start | bytes 101384 | tf_op jit(solution)/shard_map/while/body/eval_jaxpr/ppermute | solution.py:17
  88.8 6.9 %collective-permute-start.5 = (f32[4,8,2,132]{3,2,1,0:T(2,128)S(1)}, f32[4,8,2,132]{3,2,1,0:T(2,128)S(1)}, u32[]{:S(2)}, u32[]{:S(2)}) collective-permute-start(f32[4,8,2,132]{3,2,1,0:T(2,128)S(1)} %get-tuple-element.313), channel_id=1, source_target_pairs={{0,1},{1,2},{2,3},{4,5},{5,6},{6,7},{8,9},{9,10},{10,11},{12,13},{... | collective-permute-start | bytes 101384 | tf_op jit(solution)/shard_map/while/body/eval_jaxpr/ppermute | solution.py:16
  99.6 6.2 %collective-permute-start = (f32[4,4,16,2]{3,2,1,0:T(8,128)S(1)}, f32[4,4,16,2]{3,2,1,0:T(8,128)S(1)}, u32[]{:S(2)}, u32[]{:S(2)}) collective-permute-start(f32[4,4,16,2]{3,2,1,0:T(8,128)S(1)} %get-tuple-element.308), channel_id=1, source_target_pairs={{8,0},{16,8},{24,16},{9,1},{17,9},{25,17},{10,2},{18,10},{26,18},{... | collective-permute-start | bytes 6152 | tf_op jit(solution)/shard_map/while/body/eval_jaxpr/ppermute | solution.py:17
  100.9 5.9 %collective-permute-start.1 = (f32[4,4,16,2]{3,2,1,0:T(8,128)S(1)}, f32[4,4,16,2]{3,2,1,0:T(8,128)S(1)}, u32[]{:S(2)}, u32[]{:S(2)}) collective-permute-start(f32[4,4,16,2]{3,2,1,0:T(8,128)S(1)} %get-tuple-element.309), channel_id=1, source_target_pairs={{0,8},{8,16},{16,24},{1,9},{9,17},{17,25},{2,10},{10,18},{18,26},{... | collective-permute-start | bytes 6152 | tf_op jit(solution)/shard_map/while/body/eval_jaxpr/ppermute | solution.py:16
  107.6 7.1 %collective-permute-start.2 = (f32[4,2,16,132]{3,2,1,0:T(8,128)}, f32[4,2,16,132]{3,2,1,0:T(8,128)S(1)}, u32[]{:S(2)}, u32[]{:S(2)}) collective-permute-start(f32[4,2,16,132]{3,2,1,0:T(8,128)} %get-tuple-element.310), channel_id=1, source_target_pairs={{4,0},{5,1},{6,2},{7,3},{12,8},{13,9},{14,10},{15,11},{20,16},{21,... | collective-permute-start | bytes 202760 | tf_op jit(solution)/shard_map/while/body/eval_jaxpr/ppermute | solution.py:17
  108.9 7.1 %collective-permute-start.3 = (f32[4,2,16,132]{3,2,1,0:T(8,128)S(1)}, f32[4,2,16,132]{3,2,1,0:T(8,128)S(1)}, u32[]{:S(2)}, u32[]{:S(2)}) collective-permute-start(f32[4,2,16,132]{3,2,1,0:T(8,128)S(1)} %get-tuple-element.311), channel_id=1, source_target_pairs={{0,4},{1,5},{2,6},{3,7},{8,12},{9,13},{10,14},{11,15},{16,20},{17,... | collective-permute-start | bytes 202760 | tf_op jit(solution)/shard_map/while/body/eval_jaxpr/ppermute | solution.py:16
  116.7 6.6 %collective-permute-start.4 = (f32[4,8,2,132]{3,2,1,0:T(2,128)}, f32[4,8,2,132]{3,2,1,0:T(2,128)S(1)}, u32[]{:S(2)}, u32[]{:S(2)}) collective-permute-start(f32[4,8,2,132]{3,2,1,0:T(2,128)} %get-tuple-element.312), channel_id=1, source_target_pairs={{1,0},{2,1},{3,2},{5,4},{6,5},{7,6},{9,8},{10,9},{11,10},{13,12},{... | collective-permute-start | bytes 101384 | tf_op jit(solution)/shard_map/while/body/eval_jaxpr/ppermute | solution.py:17
  118.0 6.5 %collective-permute-start.5 = (f32[4,8,2,132]{3,2,1,0:T(2,128)S(1)}, f32[4,8,2,132]{3,2,1,0:T(2,128)S(1)}, u32[]{:S(2)}, u32[]{:S(2)}) collective-permute-start(f32[4,8,2,132]{3,2,1,0:T(2,128)S(1)} %get-tuple-element.313), channel_id=1, source_target_pairs={{0,1},{1,2},{2,3},{4,5},{5,6},{6,7},{8,9},{9,10},{10,11},{12,13},{... | collective-permute-start | bytes 101384 | tf_op jit(solution)/shard_map/while/body/eval_jaxpr/ppermute | solution.py:16
  128.4 7.6 %collective-permute-start = (f32[4,4,16,2]{3,2,1,0:T(8,128)S(1)}, f32[4,4,16,2]{3,2,1,0:T(8,128)S(1)}, u32[]{:S(2)}, u32[]{:S(2)}) collective-permute-start(f32[4,4,16,2]{3,2,1,0:T(8,128)S(1)} %get-tuple-element.308), channel_id=1, source_target_pairs={{8,0},{16,8},{24,16},{9,1},{17,9},{25,17},{10,2},{18,10},{26,18},{... | collective-permute-start | bytes 6152 | tf_op jit(solution)/shard_map/while/body/eval_jaxpr/ppermute | solution.py:17
  129.7 7.2 %collective-permute-start.1 = (f32[4,4,16,2]{3,2,1,0:T(8,128)S(1)}, f32[4,4,16,2]{3,2,1,0:T(8,128)S(1)}, u32[]{:S(2)}, u32[]{:S(2)}) collective-permute-start(f32[4,4,16,2]{3,2,1,0:T(8,128)S(1)} %get-tuple-element.309), channel_id=1, source_target_pairs={{0,8},{8,16},{16,24},{1,9},{9,17},{17,25},{2,10},{10,18},{18,26},{... | collective-permute-start | bytes 6152 | tf_op jit(solution)/shard_map/while/body/eval_jaxpr/ppermute | solution.py:16
  137.7 7.1 %collective-permute-start.2 = (f32[4,2,16,132]{3,2,1,0:T(8,128)}, f32[4,2,16,132]{3,2,1,0:T(8,128)S(1)}, u32[]{:S(2)}, u32[]{:S(2)}) collective-permute-start(f32[4,2,16,132]{3,2,1,0:T(8,128)} %get-tuple-element.310), channel_id=1, source_target_pairs={{4,0},{5,1},{6,2},{7,3},{12,8},{13,9},{14,10},{15,11},{20,16},{21,... | collective-permute-start | bytes 202760 | tf_op jit(solution)/shard_map/while/body/eval_jaxpr/ppermute | solution.py:17
  139.0 7.1 %collective-permute-start.3 = (f32[4,2,16,132]{3,2,1,0:T(8,128)S(1)}, f32[4,2,16,132]{3,2,1,0:T(8,128)S(1)}, u32[]{:S(2)}, u32[]{:S(2)}) collective-permute-start(f32[4,2,16,132]{3,2,1,0:T(8,128)S(1)} %get-tuple-element.311), channel_id=1, source_target_pairs={{0,4},{1,5},{2,6},{3,7},{8,12},{9,13},{10,14},{11,15},{16,20},{17,... | collective-permute-start | bytes 202760 | tf_op jit(solution)/shard_map/while/body/eval_jaxpr/ppermute | solution.py:16
  146.9 6.6 %collective-permute-start.4 = (f32[4,8,2,132]{3,2,1,0:T(2,128)}, f32[4,8,2,132]{3,2,1,0:T(2,128)S(1)}, u32[]{:S(2)}, u32[]{:S(2)}) collective-permute-start(f32[4,8,2,132]{3,2,1,0:T(2,128)} %get-tuple-element.312), channel_id=1, source_target_pairs={{1,0},{2,1},{3,2},{5,4},{6,5},{7,6},{9,8},{10,9},{11,10},{13,12},{... | collective-permute-start | bytes 101384 | tf_op jit(solution)/shard_map/while/body/eval_jaxpr/ppermute | solution.py:17
  148.1 6.5 %collective-permute-start.5 = (f32[4,8,2,132]{3,2,1,0:T(2,128)S(1)}, f32[4,8,2,132]{3,2,1,0:T(2,128)S(1)}, u32[]{:S(2)}, u32[]{:S(2)}) collective-permute-start(f32[4,8,2,132]{3,2,1,0:T(2,128)S(1)} %get-tuple-element.313), channel_id=1, source_target_pairs={{0,1},{1,2},{2,3},{4,5},{5,6},{6,7},{8,9},{9,10},{10,11},{12,13},{... | collective-permute-start | bytes 101384 | tf_op jit(solution)/shard_map/while/body/eval_jaxpr/ppermute | solution.py:16
  158.5 7.6 %collective-permute-start = (f32[4,4,16,2]{3,2,1,0:T(8,128)S(1)}, f32[4,4,16,2]{3,2,1,0:T(8,128)S(1)}, u32[]{:S(2)}, u32[]{:S(2)}) collective-permute-start(f32[4,4,16,2]{3,2,1,0:T(8,128)S(1)} %get-tuple-element.308), channel_id=1, source_target_pairs={{8,0},{16,8},{24,16},{9,1},{17,9},{25,17},{10,2},{18,10},{26,18},{... | collective-permute-start | bytes 6152 | tf_op jit(solution)/shard_map/while/body/eval_jaxpr/ppermute | solution.py:17
  159.8 7.2 %collective-permute-start.1 = (f32[4,4,16,2]{3,2,1,0:T(8,128)S(1)}, f32[4,4,16,2]{3,2,1,0:T(8,128)S(1)}, u32[]{:S(2)}, u32[]{:S(2)}) collective-permute-start(f32[4,4,16,2]{3,2,1,0:T(8,128)S(1)} %get-tuple-element.309), channel_id=1, source_target_pairs={{0,8},{8,16},{16,24},{1,9},{9,17},{17,25},{2,10},{10,18},{18,26},{... | collective-permute-start | bytes 6152 | tf_op jit(solution)/shard_map/while/body/eval_jaxpr/ppermute | solution.py:16
  167.9 7.1 %collective-permute-start.2 = (f32[4,2,16,132]{3,2,1,0:T(8,128)}, f32[4,2,16,132]{3,2,1,0:T(8,128)S(1)}, u32[]{:S(2)}, u32[]{:S(2)}) collective-permute-start(f32[4,2,16,132]{3,2,1,0:T(8,128)} %get-tuple-element.310), channel_id=1, source_target_pairs={{4,0},{5,1},{6,2},{7,3},{12,8},{13,9},{14,10},{15,11},{20,16},{21,... | collective-permute-start | bytes 202760 | tf_op jit(solution)/shard_map/while/body/eval_jaxpr/ppermute | solution.py:17
  169.1 7.1 %collective-permute-start.3 = (f32[4,2,16,132]{3,2,1,0:T(8,128)S(1)}, f32[4,2,16,132]{3,2,1,0:T(8,128)S(1)}, u32[]{:S(2)}, u32[]{:S(2)}) collective-permute-start(f32[4,2,16,132]{3,2,1,0:T(8,128)S(1)} %get-tuple-element.311), channel_id=1, source_target_pairs={{0,4},{1,5},{2,6},{3,7},{8,12},{9,13},{10,14},{11,15},{16,20},{17,... | collective-permute-start | bytes 202760 | tf_op jit(solution)/shard_map/while/body/eval_jaxpr/ppermute | solution.py:16
  177.0 6.6 %collective-permute-start.4 = (f32[4,8,2,132]{3,2,1,0:T(2,128)}, f32[4,8,2,132]{3,2,1,0:T(2,128)S(1)}, u32[]{:S(2)}, u32[]{:S(2)}) collective-permute-start(f32[4,8,2,132]{3,2,1,0:T(2,128)} %get-tuple-element.312), channel_id=1, source_target_pairs={{1,0},{2,1},{3,2},{5,4},{6,5},{7,6},{9,8},{10,9},{11,10},{13,12},{... | collective-permute-start | bytes 101384 | tf_op jit(solution)/shard_map/while/body/eval_jaxpr/ppermute | solution.py:17
  178.3 6.5 %collective-permute-start.5 = (f32[4,8,2,132]{3,2,1,0:T(2,128)S(1)}, f32[4,8,2,132]{3,2,1,0:T(2,128)S(1)}, u32[]{:S(2)}, u32[]{:S(2)}) collective-permute-start(f32[4,8,2,132]{3,2,1,0:T(2,128)S(1)} %get-tuple-element.313), channel_id=1, source_target_pairs={{0,1},{1,2},{2,3},{4,5},{5,6},{6,7},{8,9},{9,10},{10,11},{12,13},{... | collective-permute-start | bytes 101384 | tf_op jit(solution)/shard_map/while/body/eval_jaxpr/ppermute | solution.py:16
  188.6 7.6 %collective-permute-start = (f32[4,4,16,2]{3,2,1,0:T(8,128)S(1)}, f32[4,4,16,2]{3,2,1,0:T(8,128)S(1)}, u32[]{:S(2)}, u32[]{:S(2)}) collective-permute-start(f32[4,4,16,2]{3,2,1,0:T(8,128)S(1)} %get-tuple-element.308), channel_id=1, source_target_pairs={{8,0},{16,8},{24,16},{9,1},{17,9},{25,17},{10,2},{18,10},{26,18},{... | collective-permute-start | bytes 6152 | tf_op jit(solution)/shard_map/while/body/eval_jaxpr/ppermute | solution.py:17
  189.9 7.2 %collective-permute-start.1 = (f32[4,4,16,2]{3,2,1,0:T(8,128)S(1)}, f32[4,4,16,2]{3,2,1,0:T(8,128)S(1)}, u32[]{:S(2)}, u32[]{:S(2)}) collective-permute-start(f32[4,4,16,2]{3,2,1,0:T(8,128)S(1)} %get-tuple-element.309), channel_id=1, source_target_pairs={{0,8},{8,16},{16,24},{1,9},{9,17},{17,25},{2,10},{10,18},{18,26},{... | collective-permute-start | bytes 6152 | tf_op jit(solution)/shard_map/while/body/eval_jaxpr/ppermute | solution.py:16
  198.0 7.1 %collective-permute-start.2 = (f32[4,2,16,132]{3,2,1,0:T(8,128)}, f32[4,2,16,132]{3,2,1,0:T(8,128)S(1)}, u32[]{:S(2)}, u32[]{:S(2)}) collective-permute-start(f32[4,2,16,132]{3,2,1,0:T(8,128)} %get-tuple-element.310), channel_id=1, source_target_pairs={{4,0},{5,1},{6,2},{7,3},{12,8},{13,9},{14,10},{15,11},{20,16},{21,... | collective-permute-start | bytes 202760 | tf_op jit(solution)/shard_map/while/body/eval_jaxpr/ppermute | solution.py:17
  199.3 7.1 %collective-permute-start.3 = (f32[4,2,16,132]{3,2,1,0:T(8,128)S(1)}, f32[4,2,16,132]{3,2,1,0:T(8,128)S(1)}, u32[]{:S(2)}, u32[]{:S(2)}) collective-permute-start(f32[4,2,16,132]{3,2,1,0:T(8,128)S(1)} %get-tuple-element.311), channel_id=1, source_target_pairs={{0,4},{1,5},{2,6},{3,7},{8,12},{9,13},{10,14},{11,15},{16,20},{17,... | collective-permute-start | bytes 202760 | tf_op jit(solution)/shard_map/while/body/eval_jaxpr/ppermute | solution.py:16
  207.1 6.6 %collective-permute-start.4 = (f32[4,8,2,132]{3,2,1,0:T(2,128)}, f32[4,8,2,132]{3,2,1,0:T(2,128)S(1)}, u32[]{:S(2)}, u32[]{:S(2)}) collective-permute-start(f32[4,8,2,132]{3,2,1,0:T(2,128)} %get-tuple-element.312), channel_id=1, source_target_pairs={{1,0},{2,1},{3,2},{5,4},{6,5},{7,6},{9,8},{10,9},{11,10},{13,12},{... | collective-permute-start | bytes 101384 | tf_op jit(solution)/shard_map/while/body/eval_jaxpr/ppermute | solution.py:17
  208.4 6.5 %collective-permute-start.5 = (f32[4,8,2,132]{3,2,1,0:T(2,128)S(1)}, f32[4,8,2,132]{3,2,1,0:T(2,128)S(1)}, u32[]{:S(2)}, u32[]{:S(2)}) collective-permute-start(f32[4,8,2,132]{3,2,1,0:T(2,128)S(1)} %get-tuple-element.313), channel_id=1, source_target_pairs={{0,1},{1,2},{2,3},{4,5},{5,6},{6,7},{8,9},{9,10},{10,11},{12,13},{... | collective-permute-start | bytes 101384 | tf_op jit(solution)/shard_map/while/body/eval_jaxpr/ppermute | solution.py:16
  218.8 7.6 %collective-permute-start = (f32[4,4,16,2]{3,2,1,0:T(8,128)S(1)}, f32[4,4,16,2]{3,2,1,0:T(8,128)S(1)}, u32[]{:S(2)}, u32[]{:S(2)}) collective-permute-start(f32[4,4,16,2]{3,2,1,0:T(8,128)S(1)} %get-tuple-element.308), channel_id=1, source_target_pairs={{8,0},{16,8},{24,16},{9,1},{17,9},{25,17},{10,2},{18,10},{26,18},{... | collective-permute-start | bytes 6152 | tf_op jit(solution)/shard_map/while/body/eval_jaxpr/ppermute | solution.py:17
  220.1 7.2 %collective-permute-start.1 = (f32[4,4,16,2]{3,2,1,0:T(8,128)S(1)}, f32[4,4,16,2]{3,2,1,0:T(8,128)S(1)}, u32[]{:S(2)}, u32[]{:S(2)}) collective-permute-start(f32[4,4,16,2]{3,2,1,0:T(8,128)S(1)} %get-tuple-element.309), channel_id=1, source_target_pairs={{0,8},{8,16},{16,24},{1,9},{9,17},{17,25},{2,10},{10,18},{18,26},{... | collective-permute-start | bytes 6152 | tf_op jit(solution)/shard_map/while/body/eval_jaxpr/ppermute | solution.py:16
  228.1 7.1 %collective-permute-start.2 = (f32[4,2,16,132]{3,2,1,0:T(8,128)}, f32[4,2,16,132]{3,2,1,0:T(8,128)S(1)}, u32[]{:S(2)}, u32[]{:S(2)}) collective-permute-start(f32[4,2,16,132]{3,2,1,0:T(8,128)} %get-tuple-element.310), channel_id=1, source_target_pairs={{4,0},{5,1},{6,2},{7,3},{12,8},{13,9},{14,10},{15,11},{20,16},{21,... | collective-permute-start | bytes 202760 | tf_op jit(solution)/shard_map/while/body/eval_jaxpr/ppermute | solution.py:17
  229.4 7.1 %collective-permute-start.3 = (f32[4,2,16,132]{3,2,1,0:T(8,128)S(1)}, f32[4,2,16,132]{3,2,1,0:T(8,128)S(1)}, u32[]{:S(2)}, u32[]{:S(2)}) collective-permute-start(f32[4,2,16,132]{3,2,1,0:T(8,128)S(1)} %get-tuple-element.311), channel_id=1, source_target_pairs={{0,4},{1,5},{2,6},{3,7},{8,12},{9,13},{10,14},{11,15},{16,20},{17,... | collective-permute-start | bytes 202760 | tf_op jit(solution)/shard_map/while/body/eval_jaxpr/ppermute | solution.py:16
  237.2 6.6 %collective-permute-start.4 = (f32[4,8,2,132]{3,2,1,0:T(2,128)}, f32[4,8,2,132]{3,2,1,0:T(2,128)S(1)}, u32[]{:S(2)}, u32[]{:S(2)}) collective-permute-start(f32[4,8,2,132]{3,2,1,0:T(2,128)} %get-tuple-element.312), channel_id=1, source_target_pairs={{1,0},{2,1},{3,2},{5,4},{6,5},{7,6},{9,8},{10,9},{11,10},{13,12},{... | collective-permute-start | bytes 101384 | tf_op jit(solution)/shard_map/while/body/eval_jaxpr/ppermute | solution.py:17
  238.5 6.5 %collective-permute-start.5 = (f32[4,8,2,132]{3,2,1,0:T(2,128)S(1)}, f32[4,8,2,132]{3,2,1,0:T(2,128)S(1)}, u32[]{:S(2)}, u32[]{:S(2)}) collective-permute-start(f32[4,8,2,132]{3,2,1,0:T(2,128)S(1)} %get-tuple-element.313), channel_id=1, source_target_pairs={{0,1},{1,2},{2,3},{4,5},{5,6},{6,7},{8,9},{9,10},{10,11},{12,13},{... | collective-permute-start | bytes 101384 | tf_op jit(solution)/shard_map/while/body/eval_jaxpr/ppermute | solution.py:16
  248.9 7.6 %collective-permute-start = (f32[4,4,16,2]{3,2,1,0:T(8,128)S(1)}, f32[4,4,16,2]{3,2,1,0:T(8,128)S(1)}, u32[]{:S(2)}, u32[]{:S(2)}) collective-permute-start(f32[4,4,16,2]{3,2,1,0:T(8,128)S(1)} %get-tuple-element.308), channel_id=1, source_target_pairs={{8,0},{16,8},{24,16},{9,1},{17,9},{25,17},{10,2},{18,10},{26,18},{... | collective-permute-start | bytes 6152 | tf_op jit(solution)/shard_map/while/body/eval_jaxpr/ppermute | solution.py:17
  250.2 7.2 %collective-permute-start.1 = (f32[4,4,16,2]{3,2,1,0:T(8,128)S(1)}, f32[4,4,16,2]{3,2,1,0:T(8,128)S(1)}, u32[]{:S(2)}, u32[]{:S(2)}) collective-permute-start(f32[4,4,16,2]{3,2,1,0:T(8,128)S(1)} %get-tuple-element.309), channel_id=1, source_target_pairs={{0,8},{8,16},{16,24},{1,9},{9,17},{17,25},{2,10},{10,18},{18,26},{... | collective-permute-start | bytes 6152 | tf_op jit(solution)/shard_map/while/body/eval_jaxpr/ppermute | solution.py:16
  258.2 7.1 %collective-permute-start.2 = (f32[4,2,16,132]{3,2,1,0:T(8,128)}, f32[4,2,16,132]{3,2,1,0:T(8,128)S(1)}, u32[]{:S(2)}, u32[]{:S(2)}) collective-permute-start(f32[4,2,16,132]{3,2,1,0:T(8,128)} %get-tuple-element.310), channel_id=1, source_target_pairs={{4,0},{5,1},{6,2},{7,3},{12,8},{13,9},{14,10},{15,11},{20,16},{21,... | collective-permute-start | bytes 202760 | tf_op jit(solution)/shard_map/while/body/eval_jaxpr/ppermute | solution.py:17
  259.5 7.1 %collective-permute-start.3 = (f32[4,2,16,132]{3,2,1,0:T(8,128)S(1)}, f32[4,2,16,132]{3,2,1,0:T(8,128)S(1)}, u32[]{:S(2)}, u32[]{:S(2)}) collective-permute-start(f32[4,2,16,132]{3,2,1,0:T(8,128)S(1)} %get-tuple-element.311), channel_id=1, source_target_pairs={{0,4},{1,5},{2,6},{3,7},{8,12},{9,13},{10,14},{11,15},{16,20},{17,... | collective-permute-start | bytes 202760 | tf_op jit(solution)/shard_map/while/body/eval_jaxpr/ppermute | solution.py:16
  267.4 6.6 %collective-permute-start.4 = (f32[4,8,2,132]{3,2,1,0:T(2,128)}, f32[4,8,2,132]{3,2,1,0:T(2,128)S(1)}, u32[]{:S(2)}, u32[]{:S(2)}) collective-permute-start(f32[4,8,2,132]{3,2,1,0:T(2,128)} %get-tuple-element.312), channel_id=1, source_target_pairs={{1,0},{2,1},{3,2},{5,4},{6,5},{7,6},{9,8},{10,9},{11,10},{13,12},{... | collective-permute-start | bytes 101384 | tf_op jit(solution)/shard_map/while/body/eval_jaxpr/ppermute | solution.py:17
  268.7 6.5 %collective-permute-start.5 = (f32[4,8,2,132]{3,2,1,0:T(2,128)S(1)}, f32[4,8,2,132]{3,2,1,0:T(2,128)S(1)}, u32[]{:S(2)}, u32[]{:S(2)}) collective-permute-start(f32[4,8,2,132]{3,2,1,0:T(2,128)S(1)} %get-tuple-element.313), channel_id=1, source_target_pairs={{0,1},{1,2},{2,3},{4,5},{5,6},{6,7},{8,9},{9,10},{10,11},{12,13},{... | collective-permute-start | bytes 101384 | tf_op jit(solution)/shard_map/while/body/eval_jaxpr/ppermute | solution.py:16
  (35 other events, 96.1 us)
where the time goes:
time: 417 us; the launch traced here: 415 us
  starting transfers between devices  160 us (38%)
  blocking collectives  107 us (26%)
  waiting for transfers between devices  59 us (14%)
  other arithmetic  39 us (9%)
  matrix products  26.3 us (6%)
  local copies, waits for them, and re-layouts  21.7 us (5%)
    ppermute x27, starting transfers between devices, padded_2(): before = lax.ppermute(last, axis, up)  125 us
    psum x1, blocking collectives, body(): lax.psum(jnp.dot(rest.astype(jnp.bfloat16), local, preferred_element_type...  41.6 us
    psum x1, blocking collectives, body(): lax.psum(jnp.dot(flat.astype(jnp.bfloat16), local, preferred_element_type...  41.6 us
    ppermute x27, waiting for transfers between devices, padded_2(): before = lax.ppermute(last, axis, up)  36.5 us
    ppermute x27, starting transfers between devices, padded_2(): after = lax.ppermute(leading, axis, down)  34.7 us
    all_to_all x1, blocking collectives, body(): lax.all_to_all(snaps, 'grp', split_axis=1, concat_axis=4, tiled=True)  23.5 us
    ppermute x27, waiting for transfers between devices, padded_2(): after = lax.ppermute(leading, axis, down)  22.5 us
    dot_general x1, matrix products, body(): jnp.dot(rest.astype(jnp.bfloat16), local, preferred_element_type=jnp.floa...  17 us
  transfers between devices with their start and end apart: 54, of which 38 were waited for; matrix products, arithmetic and copies ran while one was open for 2% of the time, Pallas kernels for 0%

commit v1 on v0

v1 whole, which is shorter than its diff:
```python
import functools

import jax
import jax.numpy as jnp
from jax import lax
from jax.experimental import pallas as pl
from jax.experimental.pallas import tpu as pltpu
from jax.sharding import PartitionSpec as P

STEPS = 16
LANES = 128
GROUPS = LANES // STEPS
VMEM_LIMIT = 60 * 1024 * 1024


def pairs(axis, first):
    count = lax.axis_size(axis)
    lower = range(first, count - 1, 2)
    return [(i, i + 1) for i in lower] + [(i + 1, i) for i in lower]


def exchange(value, axis, flips):
    count = lax.axis_size(axis)
    return lax.ppermute(value, axis, [(i, i ^ flips) for i in range(count)])


def sum_over(value, axis):
    count = lax.axis_size(axis)
    if count == 4:
        near, far, other = (exchange(value, axis, flips) for flips in (1, 2, 3))
        return (value + near) + (far + other)
    flips = 1
    while flips < count:
        value = value + exchange(value, axis, flips)
        flips *= 2
    return value


def sum_all(value):
    for axis in ("grp", "gx", "gy"):
        value = sum_over(value, axis)
    return value


def reaction_table(rates, stoich):
    react_count, spec = stoich.shape
    owner = jnp.arange(react_count) % spec
    pick = (owner[:, None] == jnp.arange(spec)[None, :]).astype(jnp.float32)
    return jnp.einsum(
        "mr,ra,rs->asm", rates, pick, stoich.astype(jnp.float32), precision=lax.Precision.HIGHEST
    )


def whole(count):
    return [pl.BlockSpec(memory_space=pltpu.VMEM)] * count


def scalars(count):
    return [pl.BlockSpec(memory_space=pltpu.SMEM)] * count


def edges_kernel(blocks_x, ids, *refs):
    blocks, (out_a, out_b) = refs[:-2], refs[-2:]
    fields, cells_y, cells_x, cells_z = blocks[0].shape
    per_block = cells_y // GROUPS
    even = ids[0] % 2 == 0
    place = lax.broadcasted_iota(jnp.int32, (blocks_x * cells_x, LANES), 1) // STEPS

    def field_body(field, _):
        for slot in range(len(blocks) // blocks_x):
            mine = blocks[slot * blocks_x : (slot + 1) * blocks_x]
            for part in range(per_block):
                top = bottom = None
                for group in range(GROUPS):
                    row = part * GROUPS + group
                    last = jnp.concatenate(
                        [b[field, row, :, cells_z - LANES :] for b in mine], axis=0
                    )
                    start = jnp.concatenate([b[field, row, :, :LANES] for b in mine], axis=0)
                    high = pltpu.roll(last, (STEPS * (group + 1)) % LANES, 1)
                    low = pltpu.roll(start, STEPS * group, 1) if group else start
                    top = high if top is None else jnp.where(place == group, high, top)
                    bottom = low if bottom is None else jnp.where(place == group, low, bottom)
                out_a[field, slot * per_block + part] = jnp.where(even, top, bottom)
                out_b[field, slot * per_block + part] = jnp.where(even, bottom, top)
        return 0

    lax.fori_loop(0, fields, field_body, 0)


def steps_kernel(blocks_x, ids, plan, diffusion, table, *refs):
    count_blocks = 3 * blocks_x
    blocks = refs[:count_blocks]
    side_a, side_b = refs[count_blocks : count_blocks + 2]
    adjoint = refs[count_blocks + 2]
    kept = refs[count_blocks + 3 : -3]
    state, matrix, speed = refs[-3:]
    spec, rows, all_x, wide = state.shape
    _, cells_y, cells_x, cells_z = blocks[0].shape
    grp, at_x, at_y, count_grp, count_y = (ids[i] for i in range(5))
    snaps = kept[0].shape[2]
    per_block = cells_y // GROUPS
    even_z = grp % 2 == 0
    even_y = at_y % 2 == 0
    starts = (
        cells_y,
        jnp.where(even_y, 2 * cells_y, 0),
        jnp.where(even_y, 0, 2 * cells_y),
    )
    lane = lax.broadcasted_iota(jnp.int32, (all_x, LANES), 1)
    is_right = lane < LANES // 2
    has_right = grp < count_grp - 1
    has_left = grp > 0
    beyond = jnp.where(
        is_right, jnp.where(has_right, 1.0, 0.0), jnp.where(has_left, 1.0, 0.0)
    ).astype(jnp.float32)
    inside = jnp.concatenate(
        [jnp.ones((all_x, LANES), jnp.float32)] * (cells_z // LANES) + [beyond], axis=1
    )
    row_x = lax.broadcasted_iota(jnp.int32, (all_x, wide), 0)
    place_x = (row_x + at_x * cells_x) % all_x
    is_first = place_x == 0
    is_last = place_x == all_x - 1

    for slot in range(3):
        mine = blocks[slot * blocks_x : (slot + 1) * blocks_x]
        for part in range(per_block):

            def load(field, part=part, slot=slot, mine=mine):
                packed_a = side_a[field, slot * per_block + part]
                packed_b = side_b[field, slot * per_block + part]
                right = jnp.where(even_z, packed_a, packed_b)
                left = jnp.where(even_z, packed_b, packed_a)
                out = []
                for group in range(GROUPS):
                    row = part * GROUPS + group
                    own = jnp.concatenate([b[field, row] for b in mine], axis=0)
                    after = pltpu.roll(right, (LANES - STEPS * group) % LANES, 1) if group else right
                    before = pltpu.roll(left, LANES - STEPS * (group + 1), 1) if group < GROUPS - 1 else left
                    out.append(jnp.concatenate([own, jnp.where(is_right, after, before)], axis=1))
                return out

            first_row = starts[slot] + part * GROUPS

            def species_body(s, _, load=load, first_row=first_row):
                for group, tile in enumerate(load(s)):
                    state[s, first_row + group] = tile
                return 0

            lax.fori_loop(0, spec, species_body, 0)
            winds = load(spec)
            kinds = load(spec + 1)
            for group in range(GROUPS):
                speed[first_row + group] = winds[group] * inside
                matrix[0, first_row + group] = kinds[group]

    def coefficients(row, _):
        kind = matrix[0, row].astype(jnp.int32)
        wind = speed[row]
        for a in range(spec):
            stay = inside * (1.0 - 6.0 * diffusion[a]) - wind
            for s in range(spec):
                tab = table[a * spec + s]
                tiles = [
                    jnp.concatenate(
                        [
                            jnp.take_along_axis(tab, kind[x : x + 8, z : z + LANES], axis=0)
                            for z in range(0, wide, LANES)
                        ],
                        axis=1,
                    )
                    for x in range(0, all_x, 8)
                ]
                value = jnp.concatenate(tiles, axis=0) * inside
                matrix[a * spec + s, row] = value + stay if a == s else value
        return 0

    lowest = jnp.where(at_y > 0, 0, cells_y)
    highest = jnp.where(at_y < count_y - 1, rows, rows - cells_y)
    lax.fori_loop(lowest, highest, coefficients, 0)

    def step(index, _):
        low = jnp.maximum(index + 1, lowest)
        high = jnp.minimum(rows - 1 - index, highest)

        def row_body(row, carry):
            before, here = carry
            after = [state[s, row + 1] for s in range(spec)]
            wind = speed[row]
            for a in range(spec):
                ahead = jnp.where(is_last, 0.0, pltpu.roll(here[a], all_x - 1, 0))
                behind = jnp.where(is_first, 0.0, pltpu.roll(here[a], 1, 0))
                beside = (before[a] + after[a]) + (ahead + behind)
                beside = beside + (pltpu.roll(here[a], 1, 1) + pltpu.roll(here[a], wide - 1, 1))
                mix = matrix[a * spec, row] * here[0]
                for s in range(1, spec):
                    mix = mix + matrix[a * spec + s, row] * here[s]
                state[a, row] = mix + wind * ahead + (diffusion[a] * inside) * beside
            return here, after

        def rows_at(row):
            return [state[s, row] for s in range(spec)]

        lax.fori_loop(low, high, row_body, (rows_at(low - 1), rows_at(low)))
        slot = jnp.int32(0)
        hit = jnp.int32(0)
        for j in range(snaps):
            slot = slot + jnp.where(plan[j] < index, 1, 0)
            hit = hit + jnp.where(plan[j] == index, 1, 0)

        @pl.when(hit > 0)
        def _():
            def keep(y, _):
                for flips in range(len(kept)):
                    tile = state[grp ^ flips, cells_y + y, :cells_x, :cells_z]
                    for x in range(cells_x):
                        kept[flips][x, y, pl.ds(slot, 1), :] = tile[x : x + 1]
                return 0

            lax.fori_loop(0, cells_y, keep, 0)

        return 0

    lax.fori_loop(0, STEPS, step, 0)

    def leave(s, _):
        for y in range(cells_y):
            tile = state[s, cells_y + y, :cells_x, :cells_z]
            for x in range(cells_x):
                adjoint[s, x, y : y + 1, :] = tile[x : x + 1]
        return 0

    lax.fori_loop(0, spec, leave, 0)


def product_kernel(_, part, basis, total, out):
    @pl.when(pl.program_id(0) == 0)
    def _():
        out[...] = total[...]

    _, cells_y, snaps, cells_z = part.shape
    values = part[0]
    high = values.astype(jnp.bfloat16)
    low = values - high.astype(jnp.float32)
    left = jnp.concatenate([high.astype(jnp.float32), low], axis=1).astype(jnp.bfloat16)
    acc = out[...]
    for y in range(0, cells_y, 2):
        acc = acc + jnp.dot(
            jnp.concatenate([left[y], left[y + 1]], axis=1),
            basis[0, 0, y : y + 2].reshape(2 * cells_z, basis.shape[-1]),
            preferred_element_type=jnp.float32,
        )
    out[...] = acc


def product(zone, part, basis, total):
    cells_x, cells_y, snaps, cells_z = part.shape
    modes = basis.shape[-1]
    return pl.pallas_call(
        product_kernel,
        out_shape=jax.ShapeDtypeStruct((2 * snaps, modes), jnp.float32),
        grid_spec=pltpu.PrefetchScalarGridSpec(
            num_scalar_prefetch=1,
            grid=(cells_x,),
            in_specs=[
                pl.BlockSpec((1, cells_y, snaps, cells_z), lambda x, z: (x, 0, 0, 0)),
                pl.BlockSpec((1, 1, cells_y, cells_z, modes), lambda x, z: (0, x, 0, z[0], 0)),
                pl.BlockSpec((2 * snaps, modes), lambda x, z: (0, 0)),
            ],
            out_specs=pl.BlockSpec((2 * snaps, modes), lambda x, z: (0, 0)),
        ),
        cost_estimate=pl.CostEstimate(
            flops=4 * snaps * cells_x * cells_y * cells_z * modes,
            bytes_accessed=2 * cells_x * cells_y * cells_z * modes,
            transcendentals=0,
        ),
        name="product",
    )(zone, part, basis, total)


def body(terminal, diffusion, velocity, material, rates, stoich, plan, basis):
    spec, cells_x, cells_y, cells_z = terminal.shape
    snaps, modes = plan.shape[0], basis.shape[-1]
    count_grp, count_x, count_y = (lax.axis_size(axis) for axis in ("grp", "gx", "gy"))
    grp = lax.axis_index("grp")
    ids = jnp.stack(
        [grp, lax.axis_index("gx"), lax.axis_index("gy"), jnp.int32(count_grp), jnp.int32(count_y)]
    ).astype(jnp.int32)
    table = reaction_table(rates, stoich).reshape(spec * spec, rates.shape[0], 1)
    table = jnp.broadcast_to(table, table.shape[:2] + (LANES,))

    own = jnp.concatenate(
        [terminal, velocity[None], material.astype(jnp.float32)[None]], axis=0
    ).transpose(0, 2, 1, 3)
    blocks = [own]
    for shift in range(1, count_x):
        blocks.append(
            lax.ppermute(own, "gx", [(i, (i - shift) % count_x) for i in range(count_x)])
        )
    blocks_a = [lax.ppermute(b, "gy", pairs("gy", 0)) for b in blocks]
    blocks_b = [lax.ppermute(b, "gy", pairs("gy", 1)) for b in blocks]
    blocks = blocks + blocks_a + blocks_b
    fields, all_x = spec + 2, cells_x * count_x
    packed = jax.ShapeDtypeStruct((fields, 3 * cells_y // GROUPS, all_x, LANES), jnp.float32)
    edge_a, edge_b = pl.pallas_call(
        functools.partial(edges_kernel, count_x),
        out_shape=(packed, packed),
        in_specs=scalars(1) + whole(len(blocks)),
        out_specs=tuple(whole(2)),
        compiler_params=pltpu.CompilerParams(vmem_limit_bytes=VMEM_LIMIT),
        name="edges",
    )(ids, *blocks)
    side_a = lax.ppermute(edge_a, "grp", pairs("grp", 0))
    side_b = lax.ppermute(edge_b, "grp", pairs("grp", 1))

    local = basis.reshape(-1, modes)
    gram = lax.dot_general(
        local, local, (((0,), (0,)), ((), ())), preferred_element_type=jnp.float32
    )

    wide = cells_z + LANES
    part = jax.ShapeDtypeStruct((cells_x, cells_y, snaps, cells_z), jnp.float32)
    final, *kept = pl.pallas_call(
        functools.partial(steps_kernel, count_x),
        out_shape=[jax.ShapeDtypeStruct(terminal.shape, jnp.float32)] + [part] * count_grp,
        in_specs=scalars(3) + whole(3 + len(blocks)),
        out_specs=whole(1 + count_grp),
        scratch_shapes=[
            pltpu.VMEM((spec, 3 * cells_y, all_x, wide), jnp.float32),
            pltpu.VMEM((spec * spec, 3 * cells_y, all_x, wide), jnp.float32),
            pltpu.VMEM((3 * cells_y, all_x, wide), jnp.float32),
        ],
        compiler_params=pltpu.CompilerParams(vmem_limit_bytes=VMEM_LIMIT),
        name="steps",
    )(ids, plan, diffusion, table, *blocks, side_a, side_b)

    order = sorted(range(1, count_grp), key=lambda flips: -flips)
    moved = {flips: exchange(kept[flips], "grp", flips) for flips in order}
    moved[0] = kept[0]
    total = jnp.zeros((2 * snaps, modes), jnp.float32)
    for flips in range(count_grp):
        total = product((grp ^ flips).reshape(1).astype(jnp.int32), moved[flips], basis, total)

    first = sum_all(total[:snaps])
    taken = jnp.dot(
        first.astype(jnp.bfloat16).astype(jnp.float32), gram, precision=lax.Precision.HIGHEST
    )
    second = sum_all(total[:snaps] + total[snaps:] - taken)
    return (first + second, final)


def solution(mesh):
    in_specs = (
        P(None, "gx", "gy", "grp"),
        P(),
        P("gx", "gy", "grp"),
        P("gx", "gy", "grp"),
        P(),
        P(),
        P(),
        P("grp", "gx", "gy", None, None),
    )
    out_specs = (P(), P(None, "gx", "gy", "grp"))
    return jax.shard_map(body, mesh=mesh, in_specs=in_specs, out_specs=out_specs, check_vma=False)
```

time: 417 us -> 150 us (0.36)
  starting transfers between devices: 160 us -> 43.6 us
  blocking collectives: 107 us -> 0 us
  Pallas kernels: 0 us -> 60.2 us
  waiting for transfers between devices: 59 us -> 19.7 us
  other arithmetic: 39 us -> 3.5 us
  local copies, waits for them, and re-layouts: 21.7 us -> 7.31 us
  matrix products: 26.3 us -> 14.5 us
    ppermute x54 -> x24, starting transfers between devices: 160 us -> 43.6 us  [the longest x17 33.9 us: exchange(): return lax.ppermute(value, axis, [(i, i ^ flips) for i in range(count)])]
    psum x2 -> x0, blocking collectives: 83.2 us -> none  [the longest x1 41.6 us: body(): lax.psum(jnp.dot(rest.astype(jnp.bfloat16), local, preferred_element_type...]
    pallas_call x0 -> x6, Pallas kernels: none -> 60.2 us  [the longest x1 40.9 us: body(): pl.pallas_call(functools.partial(steps_kernel, count_x), out_shape=[jax.S...]
    ppermute x54 -> x24, waiting for transfers between devices: 59 us -> 19.7 us  [the longest x17 14.3 us: exchange(): return lax.ppermute(value, axis, [(i, i ^ flips) for i in range(count)])]
    all_to_all x1 -> x0, blocking collectives: 23.5 us -> none  [body(): lax.all_to_all(snaps, 'grp', split_axis=1, concat_axis=4, tiled=True)]
    mul x16 -> x0, other arithmetic: 11.8 us -> none  [the longest x8 9.94 us: pair_step(): middle = advance(padded, diffusion, rim[0], rim[2:]) * rim[1][None]]
    dot_general x4 -> x3, matrix products: 26.3 us -> 14.5 us  [the longest x1 14.1 us: body(): lax.dot_general(local, local, (((0,), (0,)), ((), ())), preferred_element...]
    slice x18 -> x0, other arithmetic: 9.97 us -> none  [the longest x10 7.69 us: padded_2(): last = lax.slice_in_dim(value, length - width, length, axis=dim)]
  transfers between devices with their start and end apart: 54 -> 24, of which waited for: 38 -> 11; matrix products, arithmetic and copies ran while one was open for 2% -> 11% of each run, Pallas kernels for 0% -> 8%
where the time goes in v1:
time: 150 us
  Pallas kernels  60.2 us (40%)
  starting transfers between devices  43.6 us (29%)
  waiting for transfers between devices  19.7 us (13%)
  matrix products  14.5 us (10%)
  local copies, waits for them, and re-layouts  7.31 us (5%)
  other arithmetic  3.5 us (2%)
    pallas_call x1, Pallas kernels, body(): pl.pallas_call(functools.partial(steps_kernel, count_x), out_shape=[jax.S...  40.9 us
    ppermute x17, starting transfers between devices, exchange(): return lax.ppermute(value, axis, [(i, i ^ flips) for i in range(count)])  33.9 us
    pallas_call x4, Pallas kernels, product(): pl.pallas_call(product_kernel, out_shape=jax.ShapeDtypeStruct((2 * snaps,...  16.2 us
    ppermute x17, waiting for transfers between devices, exchange(): return lax.ppermute(value, axis, [(i, i ^ flips) for i in range(count)])  14.3 us
    dot_general x1, matrix products, body(): lax.dot_general(local, local, (((0,), (0,)), ((), ())), preferred_element...  14.1 us
    ppermute x2, starting transfers between devices, body(): blocks_a = [lax.ppermute(b, 'gy', pairs('gy', 0)) for b in blocks]  4.67 us
    unnamed x27, local copies, waits for them, and re-layouts  4.39 us
    ppermute x2, waiting for transfers between devices, body(): blocks_a = [lax.ppermute(b, 'gy', pairs('gy', 0)) for b in blocks]  3.34 us
  transfers between devices with their start and end apart: 24, of which 11 were waited for; matrix products, arithmetic and copies ran while one was open for 11% of the time, Pallas kernels for 8%

profile of v1, /device:TPU:0, one launch (start us, length us, event | category | flops | bytes accessed | tf_op | source)
XLA Modules:
  0.0 149.6 jit_solution(7206700435518439283)
XLA Ops:
  0.6 0.8 convert_element_type.14
  1.4 1.0 copy.13
  2.4 0.8 copy_bitcast_fusion
  3.2 3.0 %collective-permute-start = (f32[6,16,4,128]{3,2,1,0:T(4,128)S(1)}, f32[6,16,4,128]{3,2,1,0:T(4,128)S(1)}, u32[]{:S(2)}, u32[]{:S(2)}) collective-permute-start(f32[6,16,4,128]{3,2,1,0:T(4,128)S(1)} %maximum_bitcast_fusion.refs_0_), channel_id=1, source_target_pairs={{0,4},{4,0},{1,5},{5,1},{2,6},{6,2},{3,7},{7,3},{8,12},{12,8},{9,1... | collective-permute-start | bytes 589832 | tf_op jit(solution)/shard_map/ppermute | solution.py:298
  6.2 1.6 %collective-permute-start.1 = (f32[6,16,4,128]{3,2,1,0:T(4,128)S(1)}, f32[6,16,4,128]{3,2,1,0:T(4,128)S(1)}, u32[]{:S(2)}, u32[]{:S(2)}) collective-permute-start(f32[6,16,4,128]{3,2,1,0:T(4,128)S(1)} %maximum_bitcast_fusion.refs_0_), channel_id=1, source_target_pairs={{0,1},{2,3},{1,0},{3,2},{4,5},{6,7},{5,4},{7,6},{8,9},{10,11},{9,8... | collective-permute-start | bytes 589832 | tf_op jit(solution)/shard_map/ppermute | solution.py:300
  7.8 0.7 collective-permute-start.3
  8.5 0.7 convert_element_type.11
  9.2 0.7 pad_add_fusion.ids
  9.8 1.3 collective-permute-done.refs_1_
  11.1 3.1 %collective-permute-start.2 = (f32[6,16,4,128]{3,2,1,0:T(4,128)S(1)}, f32[6,16,4,128]{3,2,1,0:T(4,128)S(1)}, u32[]{:S(2)}, u32[]{:S(2)}) collective-permute-start(f32[6,16,4,128]{3,2,1,0:T(4,128)S(1)} %collective-permute-done.refs_1_), channel_id=1, source_target_pairs={{0,1},{2,3},{1,0},{3,2},{4,5},{6,7},{5,4},{7,6},{8,9},{10,11},{9,8... | collective-permute-start | bytes 589832 | tf_op jit(solution)/shard_map/ppermute | solution.py:300
  14.2 0.7 collective-permute-start.4
  15.0 3.3 %collective-permute-done.2.refs_3_ = f32[6,16,4,128]{3,2,1,0:T(4,128)S(1)} collective-permute-done((f32[6,16,4,128]{3,2,1,0:T(4,128)S(1)}, f32[6,16,4,128]{3,2,1,0:T(4,128)S(1)}, u32[]{:S(2)}, u32[]{:S(2)}) %collective-permute-start.2) | collective-permute-done | bytes 196640 | tf_op jit(solution)/shard_map/ppermute | solution.py:300
  18.3 0.6 copy-done.5
  19.0 0.7 copy-done.6
  19.6 3.0 %edges.1 = (f32[6,6,8,128]{3,2,1,0:T(8,128)}, f32[6,6,8,128]{3,2,1,0:T(8,128)}) custom-call(s32[5]{0:T(128)} %pad_add_fusion.ids, f32[6,16,4,128]{3,2,1,0:T(4,128)} %copy-done.1, f32[6,16,4,128]{3,2,1,0:T(4,128)} %copy-done.2, f32[6,16,4,128]{3,2,1,0:T(4,128)} %copy-done.3, f32[6,16,4,128]{3,2,1,0:T(4,128)} %copy-done.5, f32[6,16,4,128]{3,2,1,0:T(4,128)} %copy-done.4, ...), custom_call_target="tpu_custom_call" | custom-call | tf_op jit(solution)/shard_map/edges/pallas_call | solution.py:305
  22.7 0.7 collective-permute-start.6
  23.5 0.7 collective-permute-done.5.refs_6_
  24.3 0.7 broadcast_in_dim.19.table
  25.0 40.9 %steps.1 = (f32[4,4,16,128]{3,2,1,0:T(8,128)}, f32[4,16,8,128]{3,2,1,0:T(8,128)}, f32[4,16,8,128]{3,2,1,0:T(8,128)}, f32[4,16,8,128]{3,2,1,0:T(8,128)}, f32[4,16,8,128]{3,2,1,0:T(8,128)}) custom-call(s32[5]{0:T(128)} %pad_add_fusion.ids, s32[8]{0:T(128)} %plan.1, f32[4]{0:T(128)} %diffusion.1, f32[16,8,128]{2,1,0:T(8,128)} %broadcast_in_dim.19.table, ...), custom_call_target="tpu_custom_call" | custom-call | tf_op jit(solution)/shard_map/steps/pallas_call | solution.py:323
  65.9 5.5 %collective-permute-start.9 = (f32[4,16,8,128]{3,2,1,0:T(8,128)}, f32[4,16,8,128]{3,2,1,0:T(8,128)S(1)}, u32[]{:S(2)}, u32[]{:S(2)}) collective-permute-start(f32[4,16,8,128]{3,2,1,0:T(8,128)} %get-tuple-element.13), channel_id=1, source_target_pairs={{0,8},{8,0},{16,24},{24,16},{1,9},{9,1},{17,25},{25,17},{2,10},{10... | collective-permute-start | bytes 786440 | tf_op jit(solution)/shard_map/ppermute | solution.py:24
  71.5 1.1 collective-permute-start.8
  73.5 4.0 %product.4.total = f32[16,256]{1,0:T(8,128)} custom-call(s32[1]{0:T(128)} %bitcast.1._, f32[4,16,8,128]{3,2,1,0:T(8,128)} %get-tuple-element.14.part, bf16[1,4,16,512,256]{4,3,2,1,0:T(8,128)(2,1)} %basis.7, f32[16,256]{1,0:T(8,128)} %broadcast_in_dim.22.total), custom_call_target="tpu_custom_call" | custom-call | flops 67108864 | bytes 4194304 | tf_op jit(solution)/shard_map/product/pallas_call | solution.py:259
  77.6 0.7 copy-done.9
  78.3 4.1 %product.5.total = f32[16,256]{1,0:T(8,128)} custom-call(s32[1]{0:T(128)} %bitcast.12._, f32[4,16,8,128]{3,2,1,0:T(8,128)} %copy-done.9, bf16[1,4,16,512,256]{4,3,2,1,0:T(8,128)(2,1)} %basis.7, f32[16,256]{1,0:T(8,128)} %product.4.total), custom_call_target="tpu_custom_call" | custom-call | flops 67108864 | bytes 4194304 | tf_op jit(solution)/shard_map/product/pallas_call | solution.py:259
  82.3 0.7 copy-done.8
  83.0 4.1 %product.6.total = f32[16,256]{1,0:T(8,128)} custom-call(s32[1]{0:T(128)} %bitcast.11._, f32[4,16,8,128]{3,2,1,0:T(8,128)} %copy-done.8, bf16[1,4,16,512,256]{4,3,2,1,0:T(8,128)(2,1)} %basis.7, f32[16,256]{1,0:T(8,128)} %product.5.total), custom_call_target="tpu_custom_call" | custom-call | flops 67108864 | bytes 4194304 | tf_op jit(solution)/shard_map/product/pallas_call | solution.py:259
  87.1 0.7 copy-done.7
  87.8 4.1 %product.7 = f32[16,256]{1,0:T(8,128)} custom-call(s32[1]{0:T(128)} %bitcast._, f32[4,16,8,128]{3,2,1,0:T(8,128)} %copy-done.7, bf16[1,4,16,512,256]{4,3,2,1,0:T(8,128)(2,1)} %basis.7, f32[16,256]{1,0:T(8,128)} %product.6.total), custom_call_target="tpu_custom_call" | custom-call | flops 67108864 | bytes 4194304 | tf_op jit(solution)/shard_map/product/pallas_call | solution.py:259
  91.8 0.8 slice.9
  92.6 0.7 collective-permute-start.10
  93.3 1.1 collective-permute-start.11
  94.7 2.3 %collective-permute-done.11 = f32[8,256]{1,0:T(8,128)S(1)} collective-permute-done((f32[8,256]{1,0:T(8,128)S(1)}, f32[8,256]{1,0:T(8,128)S(1)}, u32[]{:S(2)}, u32[]{:S(2)}) %collective-permute-start.11) | collective-permute-done | bytes 8224 | tf_op jit(solution)/shard_map/ppermute | solution.py:24
  97.5 0.7 add_add_fusion.3
  98.7 3.1 %collective-permute-done.13 = f32[8,256]{1,0:T(8,128)S(1)} collective-permute-done((f32[8,256]{1,0:T(8,128)S(1)}, f32[8,256]{1,0:T(8,128)S(1)}, u32[]{:S(2)}, u32[]{:S(2)}) %collective-permute-start.13) | collective-permute-done | bytes 8224 | tf_op jit(solution)/shard_map/ppermute | solution.py:24
  101.8 13.9 %collective-permute-start.14 = (f32[8,256]{1,0:T(8,128)S(1)}, f32[8,256]{1,0:T(8,128)S(1)}, u32[]{:S(2)}, u32[]{:S(2)}) collective-permute-start(f32[8,256]{1,0:T(8,128)S(1)} %add.62), channel_id=1, source_target_pairs={{0,1},{1,0},{2,3},{3,2},{4,5},{5,4},{6,7},{7,6},{8,9},{9,8},{10,11... | collective-permute-start | bytes 24584 | tf_op jit(solution)/shard_map/ppermute | solution.py:24
  115.8 1.2 collective-permute-start.15
  117.0 1.5 collective-permute-start.16
  118.4 14.1 %fusion.2 = f32[256,256]{1,0:T(8,128)S(1)} fusion(bf16[1,4,16,512,256]{4,3,2,1,0:T(8,128)(2,1)} %basis.7), kind=kOutput, calls=%fused_computation.2 | convolution fusion | flops 4294967296 | bytes 17039360 | tf_op jit(solution)/shard_map/dot_general | solution.py:317
  132.8 1.0 collective-permute-start.18
  133.8 0.9 collective-permute-start.19
  134.7 1.8 %collective-permute-done.18 = f32[8,256]{1,0:T(8,128)S(1)} collective-permute-done((f32[8,256]{1,0:T(8,128)S(1)}, f32[8,256]{1,0:T(8,128)S(1)}, u32[]{:S(2)}, u32[]{:S(2)}) %collective-permute-start.18) | collective-permute-done | bytes 8224 | tf_op jit(solution)/shard_map/ppermute | solution.py:24
  136.9 1.5 collective-permute-start.20
  138.4 2.2 %collective-permute-done.20 = f32[8,256]{1,0:T(8,128)S(1)} collective-permute-done((f32[8,256]{1,0:T(8,128)S(1)}, f32[8,256]{1,0:T(8,128)S(1)}, u32[]{:S(2)}, u32[]{:S(2)}) %collective-permute-start.20) | collective-permute-done | bytes 8224 | tf_op jit(solution)/shard_map/ppermute | solution.py:24
  140.6 0.9 collective-permute-start.21
  141.4 2.1 %collective-permute-start.22 = (f32[8,256]{1,0:T(8,128)S(1)}, f32[8,256]{1,0:T(8,128)S(1)}, u32[]{:S(2)}, u32[]{:S(2)}) collective-permute-start(f32[8,256]{1,0:T(8,128)S(1)} %add.70), channel_id=1, source_target_pairs={{0,2},{1,3},{2,0},{3,1},{4,6},{5,7},{6,4},{7,5},{8,10},{9,11},{10,... | collective-permute-start | bytes 24584 | tf_op jit(solution)/shard_map/ppermute | solution.py:24
  143.5 1.5 collective-permute-start.23
  145.0 1.0 collective-permute-done.22
  146.0 3.0 %collective-permute-done.23 = f32[8,256]{1,0:T(8,128)S(1)} collective-permute-done((f32[8,256]{1,0:T(8,128)S(1)}, f32[8,256]{1,0:T(8,128)S(1)}, u32[]{:S(2)}, u32[]{:S(2)}) %collective-permute-start.23) | collective-permute-done | bytes 8224 | tf_op jit(solution)/shard_map/ppermute | solution.py:24
  (54 shorter events, 3.8 us)
Async XLA Ops:
  0.6 22.7 %copy-start = (f32[8,8]{1,0:T(8,128)S(1)}, f32[8,8]{1,0:T(8,128)}, u32[]{:S(2)}) copy-start(f32[8,8]{1,0:T(8,128)} %param.12) | copy-start | bytes 772
  3.2 15.1 %copy-start.1 = (f32[6,16,4,128]{3,2,1,0:T(4,128)}, f32[6,16,4,128]{3,2,1,0:T(4,128)S(1)}, u32[]{:S(2)}) copy-start(f32[6,16,4,128]{3,2,1,0:T(4,128)S(1)} %maximum_bitcast_fusion.refs_0_) | copy-start | bytes 589828
  3.2 7.9 %collective-permute-start = (f32[6,16,4,128]{3,2,1,0:T(4,128)S(1)}, f32[6,16,4,128]{3,2,1,0:T(4,128)S(1)}, u32[]{:S(2)}, u32[]{:S(2)}) collective-permute-start(f32[6,16,4,128]{3,2,1,0:T(4,128)S(1)} %maximum_bitcast_fusion.refs_0_), channel_id=1, source_target_pairs={{0,4},{4,0},{1,5},{5,1},{2,6},{6,2},{3,7},{7,3},{8,12},{12,8},{9,1... | collective-permute-start | bytes 589832 | tf_op jit(solution)/shard_map/ppermute | solution.py:298
  6.2 8.7 %collective-permute-start.1 = (f32[6,16,4,128]{3,2,1,0:T(4,128)S(1)}, f32[6,16,4,128]{3,2,1,0:T(4,128)S(1)}, u32[]{:S(2)}, u32[]{:S(2)}) collective-permute-start(f32[6,16,4,128]{3,2,1,0:T(4,128)S(1)} %maximum_bitcast_fusion.refs_0_), channel_id=1, source_target_pairs={{0,1},{2,3},{1,0},{3,2},{4,5},{6,7},{5,4},{7,6},{8,9},{10,11},{9,8... | collective-permute-start | bytes 589832 | tf_op jit(solution)/shard_map/ppermute | solution.py:300
  7.8 7.1 %collective-permute-start.3 = (f32[6,16,4,128]{3,2,1,0:T(4,128)S(1)}, f32[6,16,4,128]{3,2,1,0:T(4,128)S(1)}, u32[]{:S(2)}, u32[]{:S(2)}) collective-permute-start(f32[6,16,4,128]{3,2,1,0:T(4,128)S(1)} %maximum_bitcast_fusion.refs_0_), channel_id=1, source_target_pairs={{1,2},{2,1},{5,6},{6,5},{9,10},{10,9},{13,14},{14,13},{17,18},{18,... | collective-permute-start | bytes 589832 | tf_op jit(solution)/shard_map/ppermute | solution.py:301
  11.1 7.2 %copy-start.2 = (f32[6,16,4,128]{3,2,1,0:T(4,128)}, f32[6,16,4,128]{3,2,1,0:T(4,128)S(1)}, u32[]{:S(2)}) copy-start(f32[6,16,4,128]{3,2,1,0:T(4,128)S(1)} %collective-permute-done.refs_1_) | copy-start | bytes 589828
  11.1 7.2 %collective-permute-start.2 = (f32[6,16,4,128]{3,2,1,0:T(4,128)S(1)}, f32[6,16,4,128]{3,2,1,0:T(4,128)S(1)}, u32[]{:S(2)}, u32[]{:S(2)}) collective-permute-start(f32[6,16,4,128]{3,2,1,0:T(4,128)S(1)} %collective-permute-done.refs_1_), channel_id=1, source_target_pairs={{0,1},{2,3},{1,0},{3,2},{4,5},{6,7},{5,4},{7,6},{8,9},{10,11},{9,8... | collective-permute-start | bytes 589832 | tf_op jit(solution)/shard_map/ppermute | solution.py:300
  14.2 4.1 %collective-permute-start.4 = (f32[6,16,4,128]{3,2,1,0:T(4,128)S(1)}, f32[6,16,4,128]{3,2,1,0:T(4,128)S(1)}, u32[]{:S(2)}, u32[]{:S(2)}) collective-permute-start(f32[6,16,4,128]{3,2,1,0:T(4,128)S(1)} %collective-permute-done.refs_1_), channel_id=1, source_target_pairs={{1,2},{2,1},{5,6},{6,5},{9,10},{10,9},{13,14},{14,13},{17,18},{18,... | collective-permute-start | bytes 589832 | tf_op jit(solution)/shard_map/ppermute | solution.py:301
  14.9 3.4 %copy-start.3 = (f32[6,16,4,128]{3,2,1,0:T(4,128)}, f32[6,16,4,128]{3,2,1,0:T(4,128)S(1)}, u32[]{:S(2)}) copy-start(f32[6,16,4,128]{3,2,1,0:T(4,128)S(1)} %collective-permute-done.1.refs_2_) | copy-start | bytes 589828
  14.9 3.4 %copy-start.4 = (f32[6,16,4,128]{3,2,1,0:T(4,128)}, f32[6,16,4,128]{3,2,1,0:T(4,128)S(1)}, u32[]{:S(2)}) copy-start(f32[6,16,4,128]{3,2,1,0:T(4,128)S(1)} %collective-permute-done.3.refs_4_) | copy-start | bytes 589828
  18.3 0.7 copy-start.5
  19.0 0.7 copy-start.6
  22.7 1.6 %collective-permute-start.5 = (f32[6,6,8,128]{3,2,1,0:T(8,128)}, f32[6,6,8,128]{3,2,1,0:T(8,128)S(1)}, u32[]{:S(2)}, u32[]{:S(2)}) collective-permute-start(f32[6,6,8,128]{3,2,1,0:T(8,128)} %get-tuple-element.9), channel_id=1, source_target_pairs={{0,8},{16,24},{8,0},{24,16},{1,9},{17,25},{9,1},{25,17},{2,10},{18... | collective-permute-start | bytes 442376 | tf_op jit(solution)/shard_map/ppermute | solution.py:313
  22.7 1.6 %collective-permute-start.6 = (f32[6,6,8,128]{3,2,1,0:T(8,128)}, f32[6,6,8,128]{3,2,1,0:T(8,128)S(1)}, u32[]{:S(2)}, u32[]{:S(2)}) collective-permute-start(f32[6,6,8,128]{3,2,1,0:T(8,128)} %get-tuple-element.10), channel_id=1, source_target_pairs={{8,16},{16,8},{9,17},{17,9},{10,18},{18,10},{11,19},{19,11},{12,20... | collective-permute-start | bytes 442376 | tf_op jit(solution)/shard_map/ppermute | solution.py:314
  24.3 0.8 copy-start.10
  24.3 0.8 copy-start.11
  65.9 11.6 %collective-permute-start.9 = (f32[4,16,8,128]{3,2,1,0:T(8,128)}, f32[4,16,8,128]{3,2,1,0:T(8,128)S(1)}, u32[]{:S(2)}, u32[]{:S(2)}) collective-permute-start(f32[4,16,8,128]{3,2,1,0:T(8,128)} %get-tuple-element.13), channel_id=1, source_target_pairs={{0,8},{8,0},{16,24},{24,16},{1,9},{9,1},{17,25},{25,17},{2,10},{10... | collective-permute-start | bytes 786440 | tf_op jit(solution)/shard_map/ppermute | solution.py:24
  71.5 10.8 %collective-permute-start.8 = (f32[4,16,8,128]{3,2,1,0:T(8,128)}, f32[4,16,8,128]{3,2,1,0:T(8,128)S(1)}, u32[]{:S(2)}, u32[]{:S(2)}) collective-permute-start(f32[4,16,8,128]{3,2,1,0:T(8,128)} %get-tuple-element.12), channel_id=1, source_target_pairs={{0,16},{8,24},{16,0},{24,8},{1,17},{9,25},{17,1},{25,9},{2,18},{10... | collective-permute-start | bytes 786440 | tf_op jit(solution)/shard_map/ppermute | solution.py:24
  72.6 14.5 %collective-permute-start.7 = (f32[4,16,8,128]{3,2,1,0:T(8,128)}, f32[4,16,8,128]{3,2,1,0:T(8,128)S(1)}, u32[]{:S(2)}, u32[]{:S(2)}) collective-permute-start(f32[4,16,8,128]{3,2,1,0:T(8,128)} %get-tuple-element.11), channel_id=1, source_target_pairs={{0,24},{8,16},{16,8},{24,0},{1,25},{9,17},{17,9},{25,1},{2,26},{10... | collective-permute-start | bytes 786440 | tf_op jit(solution)/shard_map/ppermute | solution.py:24
  77.5 0.7 copy-start.9
  82.3 0.7 copy-start.8
  87.1 0.7 copy-start.7
  91.8 40.8 %copy-start.12 = (f32[16,256]{1,0:T(8,128)S(1)}, f32[16,256]{1,0:T(8,128)}, u32[]{:S(2)}) copy-start(f32[16,256]{1,0:T(8,128)} %product.7) | copy-start | bytes 49156
  92.6 2.1 %collective-permute-start.10 = (f32[8,256]{1,0:T(8,128)S(1)}, f32[8,256]{1,0:T(8,128)S(1)}, u32[]{:S(2)}, u32[]{:S(2)}) collective-permute-start(f32[8,256]{1,0:T(8,128)S(1)} %slice.9), channel_id=1, source_target_pairs={{0,8},{8,0},{16,24},{24,16},{1,9},{9,1},{17,25},{25,17},{2,10},{10... | collective-permute-start | bytes 24584 | tf_op jit(solution)/shard_map/ppermute | solution.py:24
  93.3 3.7 %collective-permute-start.11 = (f32[8,256]{1,0:T(8,128)S(1)}, f32[8,256]{1,0:T(8,128)S(1)}, u32[]{:S(2)}, u32[]{:S(2)}) collective-permute-start(f32[8,256]{1,0:T(8,128)S(1)} %slice.9), channel_id=1, source_target_pairs={{0,16},{8,24},{16,0},{24,8},{1,17},{9,25},{17,1},{25,9},{2,18},{10... | collective-permute-start | bytes 24584 | tf_op jit(solution)/shard_map/ppermute | solution.py:24
  94.4 3.1 %collective-permute-start.12 = (f32[8,256]{1,0:T(8,128)S(1)}, f32[8,256]{1,0:T(8,128)S(1)}, u32[]{:S(2)}, u32[]{:S(2)}) collective-permute-start(f32[8,256]{1,0:T(8,128)S(1)} %slice.9), channel_id=1, source_target_pairs={{0,24},{8,16},{16,8},{24,0},{1,25},{9,17},{17,9},{25,1},{2,26},{10... | collective-permute-start | bytes 24584 | tf_op jit(solution)/shard_map/ppermute | solution.py:24
  98.2 3.7 %collective-permute-start.13 = (f32[8,256]{1,0:T(8,128)S(1)}, f32[8,256]{1,0:T(8,128)S(1)}, u32[]{:S(2)}, u32[]{:S(2)}) collective-permute-start(f32[8,256]{1,0:T(8,128)S(1)} %add_add_fusion.3), channel_id=1, source_target_pairs={{0,4},{4,0},{1,5},{5,1},{2,6},{6,2},{3,7},{7,3},{8,12},{12,8},{9,1... | collective-permute-start | bytes 24584 | tf_op jit(solution)/shard_map/ppermute | solution.py:24
  101.8 30.7 %collective-permute-start.14 = (f32[8,256]{1,0:T(8,128)S(1)}, f32[8,256]{1,0:T(8,128)S(1)}, u32[]{:S(2)}, u32[]{:S(2)}) collective-permute-start(f32[8,256]{1,0:T(8,128)S(1)} %add.62), channel_id=1, source_target_pairs={{0,1},{1,0},{2,3},{3,2},{4,5},{5,4},{6,7},{7,6},{8,9},{9,8},{10,11... | collective-permute-start | bytes 24584 | tf_op jit(solution)/shard_map/ppermute | solution.py:24
  115.8 16.8 %collective-permute-start.15 = (f32[8,256]{1,0:T(8,128)S(1)}, f32[8,256]{1,0:T(8,128)S(1)}, u32[]{:S(2)}, u32[]{:S(2)}) collective-permute-start(f32[8,256]{1,0:T(8,128)S(1)} %add.62), channel_id=1, source_target_pairs={{0,2},{1,3},{2,0},{3,1},{4,6},{5,7},{6,4},{7,5},{8,10},{9,11},{10,... | collective-permute-start | bytes 24584 | tf_op jit(solution)/shard_map/ppermute | solution.py:24
  117.0 15.6 %collective-permute-start.16 = (f32[8,256]{1,0:T(8,128)S(1)}, f32[8,256]{1,0:T(8,128)S(1)}, u32[]{:S(2)}, u32[]{:S(2)}) collective-permute-start(f32[8,256]{1,0:T(8,128)S(1)} %add.62), channel_id=1, source_target_pairs={{0,3},{1,2},{2,1},{3,0},{4,7},{5,6},{6,5},{7,4},{8,11},{9,10},{10,... | collective-permute-start | bytes 24584 | tf_op jit(solution)/shard_map/ppermute | solution.py:24
  132.8 1.9 %collective-permute-start.17 = (f32[8,256]{1,0:T(8,128)S(1)}, f32[8,256]{1,0:T(8,128)S(1)}, u32[]{:S(2)}, u32[]{:S(2)}) collective-permute-start(f32[8,256]{1,0:T(8,128)S(1)} %fusion.5), channel_id=1, source_target_pairs={{0,8},{8,0},{16,24},{24,16},{1,9},{9,1},{17,25},{25,17},{2,10},{10... | collective-permute-start | bytes 24584 | tf_op jit(solution)/shard_map/ppermute | solution.py:24
  132.8 3.7 %collective-permute-start.18 = (f32[8,256]{1,0:T(8,128)S(1)}, f32[8,256]{1,0:T(8,128)S(1)}, u32[]{:S(2)}, u32[]{:S(2)}) collective-permute-start(f32[8,256]{1,0:T(8,128)S(1)} %fusion.5), channel_id=1, source_target_pairs={{0,16},{8,24},{16,0},{24,8},{1,17},{9,25},{17,1},{25,9},{2,18},{10... | collective-permute-start | bytes 24584 | tf_op jit(solution)/shard_map/ppermute | solution.py:24
  133.8 3.1 %collective-permute-start.19 = (f32[8,256]{1,0:T(8,128)S(1)}, f32[8,256]{1,0:T(8,128)S(1)}, u32[]{:S(2)}, u32[]{:S(2)}) collective-permute-start(f32[8,256]{1,0:T(8,128)S(1)} %fusion.5), channel_id=1, source_target_pairs={{0,24},{8,16},{16,8},{24,0},{1,25},{9,17},{17,9},{25,1},{2,26},{10... | collective-permute-start | bytes 24584 | tf_op jit(solution)/shard_map/ppermute | solution.py:24
  136.9 3.7 %collective-permute-start.20 = (f32[8,256]{1,0:T(8,128)S(1)}, f32[8,256]{1,0:T(8,128)S(1)}, u32[]{:S(2)}, u32[]{:S(2)}) collective-permute-start(f32[8,256]{1,0:T(8,128)S(1)} %add_add_fusion.1), channel_id=1, source_target_pairs={{0,4},{4,0},{1,5},{5,1},{2,6},{6,2},{3,7},{7,3},{8,12},{12,8},{9,1... | collective-permute-start | bytes 24584 | tf_op jit(solution)/shard_map/ppermute | solution.py:24
  140.6 4.4 %collective-permute-start.21 = (f32[8,256]{1,0:T(8,128)S(1)}, f32[8,256]{1,0:T(8,128)S(1)}, u32[]{:S(2)}, u32[]{:S(2)}) collective-permute-start(f32[8,256]{1,0:T(8,128)S(1)} %add.70), channel_id=1, source_target_pairs={{0,1},{1,0},{2,3},{3,2},{4,5},{5,4},{6,7},{7,6},{8,9},{9,8},{10,11... | collective-permute-start | bytes 24584 | tf_op jit(solution)/shard_map/ppermute | solution.py:24
  141.4 4.5 %collective-permute-start.22 = (f32[8,256]{1,0:T(8,128)S(1)}, f32[8,256]{1,0:T(8,128)S(1)}, u32[]{:S(2)}, u32[]{:S(2)}) collective-permute-start(f32[8,256]{1,0:T(8,128)S(1)} %add.70), channel_id=1, source_target_pairs={{0,2},{1,3},{2,0},{3,1},{4,6},{5,7},{6,4},{7,5},{8,10},{9,11},{10,... | collective-permute-start | bytes 24584 | tf_op jit(solution)/shard_map/ppermute | solution.py:24
  143.5 5.4 %collective-permute-start.23 = (f32[8,256]{1,0:T(8,128)S(1)}, f32[8,256]{1,0:T(8,128)S(1)}, u32[]{:S(2)}, u32[]{:S(2)}) collective-permute-start(f32[8,256]{1,0:T(8,128)S(1)} %add.70), channel_id=1, source_target_pairs={{0,3},{1,2},{2,1},{3,0},{4,7},{5,6},{6,5},{7,4},{8,11},{9,10},{10,... | collective-permute-start | bytes 24584 | tf_op jit(solution)/shard_map/ppermute | solution.py:24

commit v2 on v1

--- a/solution.py
+++ b/solution.py
@@ -10,6 +10,7 @@
 STEPS = 16
 LANES = 128
 GROUPS = LANES // STEPS
+BLOCK = 8
 VMEM_LIMIT = 60 * 1024 * 1024
 
 
@@ -93,8 +94,8 @@
     blocks = refs[:count_blocks]
     side_a, side_b = refs[count_blocks : count_blocks + 2]
     adjoint = refs[count_blocks + 2]
-    kept = refs[count_blocks + 3 : -3]
-    state, matrix, speed = refs[-3:]
+    kept = refs[count_blocks + 3 : -4]
+    state, other, matrix, speed = refs[-4:]
     spec, rows, all_x, wide = state.shape
     _, cells_y, cells_x, cells_z = blocks[0].shape
     grp, at_x, at_y, count_grp, count_y = (ids[i] for i in range(5))
@@ -103,9 +104,9 @@
     even_z = grp % 2 == 0
     even_y = at_y % 2 == 0
     starts = (
-        cells_y,
-        jnp.where(even_y, 2 * cells_y, 0),
-        jnp.where(even_y, 0, 2 * cells_y),
+        BLOCK + cells_y,
+        BLOCK + jnp.where(even_y, 2 * cells_y, 0),
+        BLOCK + jnp.where(even_y, 0, 2 * cells_y),
     )
     lane = lax.broadcasted_iota(jnp.int32, (all_x, LANES), 1)
     is_right = lane < LANES // 2
@@ -175,33 +176,50 @@
                 matrix[a * spec + s, row] = value + stay if a == s else value
         return 0
 
-    lowest = jnp.where(at_y > 0, 0, cells_y)
-    highest = jnp.where(at_y < count_y - 1, rows, rows - cells_y)
+    zero = jnp.zeros((all_x, wide), jnp.float32)
+
+    def clear(row, _):
+        for s in range(spec):
+            other[s, row] = zero
+        return 0
+
+    lax.fori_loop(0, rows, clear, 0)
+    for row in (*range(BLOCK), *range(rows - BLOCK, rows)):
+        speed[row] = zero
+        for s in range(spec):
+            state[s, row] = zero
+        for k in range(spec * spec):
+            matrix[k, row] = zero
+
+    lowest = jnp.where(at_y > 0, BLOCK, BLOCK + cells_y)
+    highest = jnp.where(at_y < count_y - 1, rows - BLOCK, rows - BLOCK - cells_y)
     lax.fori_loop(lowest, highest, coefficients, 0)
 
-    def step(index, _):
-        low = jnp.maximum(index + 1, lowest)
-        high = jnp.minimum(rows - 1 - index, highest)
-
-        def row_body(row, carry):
-            before, here = carry
-            after = [state[s, row + 1] for s in range(spec)]
-            wind = speed[row]
-            for a in range(spec):
-                ahead = jnp.where(is_last, 0.0, pltpu.roll(here[a], all_x - 1, 0))
-                behind = jnp.where(is_first, 0.0, pltpu.roll(here[a], 1, 0))
-                beside = (before[a] + after[a]) + (ahead + behind)
-                beside = beside + (pltpu.roll(here[a], 1, 1) + pltpu.roll(here[a], wide - 1, 1))
-                mix = matrix[a * spec, row] * here[0]
-                for s in range(1, spec):
-                    mix = mix + matrix[a * spec + s, row] * here[s]
-                state[a, row] = mix + wind * ahead + (diffusion[a] * inside) * beside
-            return here, after
-
-        def rows_at(row):
-            return [state[s, row] for s in range(spec)]
-
-        lax.fori_loop(low, high, row_body, (rows_at(low - 1), rows_at(low)))
+    def step(index, source, target):
+        low = jnp.maximum(BLOCK + index + 1, lowest)
+        high = jnp.minimum(rows - BLOCK - 1 - index, highest)
+        turns = (high - low + BLOCK - 1) // BLOCK
+        start = jnp.where(high == highest, high - turns * BLOCK, low)
+
+        def block_body(turn, _):
+            base = start + turn * BLOCK
+            tiles = [[source[s, base + i] for s in range(spec)] for i in range(-1, BLOCK + 1)]
+            for i in range(BLOCK):
+                row = base + i
+                before, here, after = tiles[i : i + 3]
+                wind = speed[row]
+                for a in range(spec):
+                    ahead = jnp.where(is_last, 0.0, pltpu.roll(here[a], all_x - 1, 0))
+                    behind = jnp.where(is_first, 0.0, pltpu.roll(here[a], 1, 0))
+                    beside = (before[a] + after[a]) + (ahead + behind)
+                    beside = beside + (pltpu.roll(here[a], 1, 1) + pltpu.roll(here[a], wide - 1, 1))
+                    mix = matrix[a * spec, row] * here[0]
+                    for s in range(1, spec):
+                        mix = mix + matrix[a * spec + s, row] * here[s]
+                    target[a, row] = mix + wind * ahead + spread[a] * beside
+            return 0
+
+        lax.fori_loop(0, turns, block_body, 0)
         slot = jnp.int32(0)
         hit = jnp.int32(0)
         for j in range(snaps):
@@ -212,20 +230,25 @@
         def _():
             def keep(y, _):
                 for flips in range(len(kept)):
-                    tile = state[grp ^ flips, cells_y + y, :cells_x, :cells_z]
+                    tile = target[grp ^ flips, BLOCK + cells_y + y, :cells_x, :cells_z]
                     for x in range(cells_x):
                         kept[flips][x, y, pl.ds(slot, 1), :] = tile[x : x + 1]
                 return 0
 
-            lax.fori_loop(0, cells_y, keep, 0)
-
-        return 0
-
-    lax.fori_loop(0, STEPS, step, 0)
+            lax.fori_loop(0, cells_y, keep, 0, unroll=4)
+
+    spread = [inside * diffusion[a] for a in range(spec)]
+
+    def two_steps(pair, _):
+        step(2 * pair, state, other)
+        step(2 * pair + 1, other, state)
+        return 0
+
+    lax.fori_loop(0, STEPS // 2, two_steps, 0)
 
     def leave(s, _):
         for y in range(cells_y):
-            tile = state[s, cells_y + y, :cells_x, :cells_z]
+            tile = state[s, BLOCK + cells_y + y, :cells_x, :cells_z]
             for x in range(cells_x):
                 adjoint[s, x, y : y + 1, :] = tile[x : x + 1]
         return 0
@@ -318,7 +341,8 @@
         local, local, (((0,), (0,)), ((), ())), preferred_element_type=jnp.float32
     )
 
-    wide = cells_z + LANES
+    side_a, side_b, gram = lax.optimization_barrier((side_a, side_b, gram))
+    wide, rows = cells_z + LANES, 3 * cells_y + 2 * BLOCK
     part = jax.ShapeDtypeStruct((cells_x, cells_y, snaps, cells_z), jnp.float32)
     final, *kept = pl.pallas_call(
         functools.partial(steps_kernel, count_x),
@@ -326,9 +350,10 @@
         in_specs=scalars(3) + whole(3 + len(blocks)),
         out_specs=whole(1 + count_grp),
         scratch_shapes=[
-            pltpu.VMEM((spec, 3 * cells_y, all_x, wide), jnp.float32),
-            pltpu.VMEM((spec * spec, 3 * cells_y, all_x, wide), jnp.float32),
-            pltpu.VMEM((3 * cells_y, all_x, wide), jnp.float32),
+            pltpu.VMEM((spec, rows, all_x, wide), jnp.float32),
+            pltpu.VMEM((spec, rows, all_x, wide), jnp.float32),
+            pltpu.VMEM((spec * spec, rows, all_x, wide), jnp.float32),
+            pltpu.VMEM((rows, all_x, wide), jnp.float32),
         ],
         compiler_params=pltpu.CompilerParams(vmem_limit_bytes=VMEM_LIMIT),
         name="steps",

time: 150 us -> 124 us (0.83)
  Pallas kernels: 60.2 us -> 38.6 us
  starting transfers between devices: 43.6 us -> 36.1 us
  waiting for transfers between devices: 19.7 us -> 22.4 us
    pallas_call x1, Pallas kernels: 40.9 us -> 19.3 us  [body(): pl.pallas_call(functools.partial(steps_kernel, count_x), out_shape=[jax.S...]
    ppermute x17, starting transfers between devices: 33.9 us -> 25.1 us  [exchange(): return lax.ppermute(value, axis, [(i, i ^ flips) for i in range(count)])]
    ppermute x17, waiting for transfers between devices: 14.3 us -> 18.3 us  [exchange(): return lax.ppermute(value, axis, [(i, i ^ flips) for i in range(count)])]
  transfers between devices with their start and end apart: 24 -> 24, of which waited for: 11 -> 12; matrix products, arithmetic and copies ran while one was open for 11% -> 13% of each run, Pallas kernels for 8% -> 10%
where the time goes in v2:
time: 124 us; the launch traced here: 123 us
  Pallas kernels  38.6 us (31%)
  starting transfers between devices  36.1 us (29%)
  waiting for transfers between devices  22.4 us (18%)
  matrix products  15.2 us (12%)
  local copies, waits for them, and re-layouts  7.24 us (6%)
  other arithmetic  2.82 us (2%)
    ppermute x17, starting transfers between devices, exchange(): return lax.ppermute(value, axis, [(i, i ^ flips) for i in range(count)])  25.1 us
    pallas_call x1, Pallas kernels, body(): pl.pallas_call(functools.partial(steps_kernel, count_x), out_shape=[jax.S...  19.3 us
    ppermute x17, waiting for transfers between devices, exchange(): return lax.ppermute(value, axis, [(i, i ^ flips) for i in range(count)])  18.3 us
    pallas_call x4, Pallas kernels, product(): pl.pallas_call(product_kernel, out_shape=jax.ShapeDtypeStruct((2 * snaps,...  16.2 us
    dot_general x1, matrix products, body(): lax.dot_general(local, local, (((0,), (0,)), ((), ())), preferred_element...  14.1 us
    ppermute x2, starting transfers between devices, body(): blocks_a = [lax.ppermute(b, 'gy', pairs('gy', 0)) for b in blocks]  5.96 us
    unnamed x27, local copies, waits for them, and re-layouts  4.39 us
    ppermute x2, waiting for transfers between devices, body(): blocks_a = [lax.ppermute(b, 'gy', pairs('gy', 0)) for b in blocks]  3.34 us
  transfers between devices with their start and end apart: 24, of which 12 were waited for; matrix products, arithmetic and copies ran while one was open for 13% of the time, Pallas kernels for 10%

profile of v2, /device:TPU:0, one launch (start us, length us, event | category | flops | bytes accessed | tf_op | source)
XLA Modules:
  0.0 123.2 jit_solution(12755059193965223325)
XLA Ops:
  0.7 0.8 convert_element_type.14
  1.4 1.0 copy.13
  2.4 0.8 copy_bitcast_fusion
  3.2 3.0 %collective-permute-start = (f32[6,16,4,128]{3,2,1,0:T(4,128)S(1)}, f32[6,16,4,128]{3,2,1,0:T(4,128)S(1)}, u32[]{:S(2)}, u32[]{:S(2)}) collective-permute-start(f32[6,16,4,128]{3,2,1,0:T(4,128)S(1)} %maximum_bitcast_fusion.refs_0_), channel_id=1, source_target_pairs={{0,4},{4,0},{1,5},{5,1},{2,6},{6,2},{3,7},{7,3},{8,12},{12,8},{9,1... | collective-permute-start | bytes 589832 | tf_op jit(solution)/shard_map/ppermute | solution.py:321
  6.2 1.6 %collective-permute-start.1 = (f32[6,16,4,128]{3,2,1,0:T(4,128)S(1)}, f32[6,16,4,128]{3,2,1,0:T(4,128)S(1)}, u32[]{:S(2)}, u32[]{:S(2)}) collective-permute-start(f32[6,16,4,128]{3,2,1,0:T(4,128)S(1)} %maximum_bitcast_fusion.refs_0_), channel_id=1, source_target_pairs={{0,1},{2,3},{1,0},{3,2},{4,5},{6,7},{5,4},{7,6},{8,9},{10,11},{9,8... | collective-permute-start | bytes 589832 | tf_op jit(solution)/shard_map/ppermute | solution.py:323
  7.8 0.7 collective-permute-start.3
  8.5 14.1 %fusion.2 = f32[256,256]{1,0:T(8,128)S(1)} fusion(bf16[1,4,16,512,256]{4,3,2,1,0:T(8,128)(2,1)} %basis.7), kind=kOutput, calls=%fused_computation.2 | convolution fusion | flops 4294967296 | bytes 17039360 | tf_op jit(solution)/shard_map/dot_general | solution.py:340
  22.7 0.7 pad_add_fusion.ids
  23.4 4.4 %collective-permute-start.2 = (f32[6,16,4,128]{3,2,1,0:T(4,128)S(1)}, f32[6,16,4,128]{3,2,1,0:T(4,128)S(1)}, u32[]{:S(2)}, u32[]{:S(2)}) collective-permute-start(f32[6,16,4,128]{3,2,1,0:T(4,128)S(1)} %collective-permute-done.refs_1_), channel_id=1, source_target_pairs={{0,1},{2,3},{1,0},{3,2},{4,5},{6,7},{5,4},{7,6},{8,9},{10,11},{9,8... | collective-permute-start | bytes 589832 | tf_op jit(solution)/shard_map/ppermute | solution.py:323
  27.8 0.7 collective-permute-start.4
  28.5 3.3 %collective-permute-done.2.refs_3_ = f32[6,16,4,128]{3,2,1,0:T(4,128)S(1)} collective-permute-done((f32[6,16,4,128]{3,2,1,0:T(4,128)S(1)}, f32[6,16,4,128]{3,2,1,0:T(4,128)S(1)}, u32[]{:S(2)}, u32[]{:S(2)}) %collective-permute-start.2) | collective-permute-done | bytes 196640 | tf_op jit(solution)/shard_map/ppermute | solution.py:323
  31.9 0.6 copy-done.5
  32.5 0.7 copy-done.6
  33.2 3.0 %edges.1 = (f32[6,6,8,128]{3,2,1,0:T(8,128)}, f32[6,6,8,128]{3,2,1,0:T(8,128)}) custom-call(s32[5]{0:T(128)} %pad_add_fusion.ids, f32[6,16,4,128]{3,2,1,0:T(4,128)} %copy-done.1, f32[6,16,4,128]{3,2,1,0:T(4,128)} %copy-done.2, f32[6,16,4,128]{3,2,1,0:T(4,128)} %copy-done.3, f32[6,16,4,128]{3,2,1,0:T(4,128)} %copy-done.5, f32[6,16,4,128]{3,2,1,0:T(4,128)} %copy-done.4, ...), custom_call_target="tpu_custom_call" | custom-call | tf_op jit(solution)/shard_map/edges/pallas_call | solution.py:328
  36.2 0.7 collective-permute-start.6
  37.0 0.7 collective-permute-done.5.refs_6_
  37.8 0.7 broadcast_in_dim.19.table
  38.5 19.3 %steps.1 = (f32[4,4,16,128]{3,2,1,0:T(8,128)}, f32[4,16,8,128]{3,2,1,0:T(8,128)}, f32[4,16,8,128]{3,2,1,0:T(8,128)}, f32[4,16,8,128]{3,2,1,0:T(8,128)}, f32[4,16,8,128]{3,2,1,0:T(8,128)}) custom-call(s32[5]{0:T(128)} %pad_add_fusion.ids, s32[8]{0:T(128)} %plan.1, f32[4]{0:T(128)} %diffusion.1, f32[16,8,128]{2,1,0:T(8,128)} %broadcast_in_dim.19.table, ...), custom_call_target="tpu_custom_call" | custom-call | tf_op jit(solution)/shard_map/steps/pallas_call | solution.py:347
  57.9 5.5 %collective-permute-start.9 = (f32[4,16,8,128]{3,2,1,0:T(8,128)}, f32[4,16,8,128]{3,2,1,0:T(8,128)S(1)}, u32[]{:S(2)}, u32[]{:S(2)}) collective-permute-start(f32[4,16,8,128]{3,2,1,0:T(8,128)} %get-tuple-element.18), channel_id=1, source_target_pairs={{0,8},{8,0},{16,24},{24,16},{1,9},{9,1},{17,25},{25,17},{2,10},{10... | collective-permute-start | bytes 786440 | tf_op jit(solution)/shard_map/ppermute | solution.py:25
  63.4 1.1 collective-permute-start.8
  64.8 0.6 broadcast_in_dim.22.total
  65.4 4.0 %product.4.total = f32[16,256]{1,0:T(8,128)} custom-call(s32[1]{0:T(128)} %bitcast.1._, f32[4,16,8,128]{3,2,1,0:T(8,128)} %get-tuple-element.19.part, bf16[1,4,16,512,256]{4,3,2,1,0:T(8,128)(2,1)} %basis.7, f32[16,256]{1,0:T(8,128)} %broadcast_in_dim.22.total), custom_call_target="tpu_custom_call" | custom-call | flops 67108864 | bytes 4194304 | tf_op jit(solution)/shard_map/product/pallas_call | solution.py:282
  69.5 0.7 copy-done.9
  70.2 4.1 %product.5.total = f32[16,256]{1,0:T(8,128)} custom-call(s32[1]{0:T(128)} %bitcast.15._, f32[4,16,8,128]{3,2,1,0:T(8,128)} %copy-done.9, bf16[1,4,16,512,256]{4,3,2,1,0:T(8,128)(2,1)} %basis.7, f32[16,256]{1,0:T(8,128)} %product.4.total), custom_call_target="tpu_custom_call" | custom-call | flops 67108864 | bytes 4194304 | tf_op jit(solution)/shard_map/product/pallas_call | solution.py:282
  74.3 0.7 copy-done.8
  75.0 4.1 %product.6.total = f32[16,256]{1,0:T(8,128)} custom-call(s32[1]{0:T(128)} %bitcast.14._, f32[4,16,8,128]{3,2,1,0:T(8,128)} %copy-done.8, bf16[1,4,16,512,256]{4,3,2,1,0:T(8,128)(2,1)} %basis.7, f32[16,256]{1,0:T(8,128)} %product.5.total), custom_call_target="tpu_custom_call" | custom-call | flops 67108864 | bytes 4194304 | tf_op jit(solution)/shard_map/product/pallas_call | solution.py:282
  79.0 0.7 copy-done.7
  79.7 4.1 %product.7 = f32[16,256]{1,0:T(8,128)} custom-call(s32[1]{0:T(128)} %bitcast._, f32[4,16,8,128]{3,2,1,0:T(8,128)} %copy-done.7, bf16[1,4,16,512,256]{4,3,2,1,0:T(8,128)(2,1)} %basis.7, f32[16,256]{1,0:T(8,128)} %product.6.total), custom_call_target="tpu_custom_call" | custom-call | flops 67108864 | bytes 4194304 | tf_op jit(solution)/shard_map/product/pallas_call | solution.py:282
  83.8 0.7 slice.9
  84.5 0.7 collective-permute-start.10
  85.2 1.1 collective-permute-start.11
  86.5 2.3 %collective-permute-done.11 = f32[8,256]{1,0:T(8,128)S(1)} collective-permute-done((f32[8,256]{1,0:T(8,128)S(1)}, f32[8,256]{1,0:T(8,128)S(1)}, u32[]{:S(2)}, u32[]{:S(2)}) %collective-permute-start.11) | collective-permute-done | bytes 8224 | tf_op jit(solution)/shard_map/ppermute | solution.py:25
  89.4 0.7 add_add_fusion.3
  90.1 0.5 collective-permute-start.13
  90.6 3.1 %collective-permute-done.13 = f32[8,256]{1,0:T(8,128)S(1)} collective-permute-done((f32[8,256]{1,0:T(8,128)S(1)}, f32[8,256]{1,0:T(8,128)S(1)}, u32[]{:S(2)}, u32[]{:S(2)}) %collective-permute-start.13) | collective-permute-done | bytes 8224 | tf_op jit(solution)/shard_map/ppermute | solution.py:25
  93.7 6.4 %collective-permute-start.14 = (f32[8,256]{1,0:T(8,128)S(1)}, f32[8,256]{1,0:T(8,128)S(1)}, u32[]{:S(2)}, u32[]{:S(2)}) collective-permute-start(f32[8,256]{1,0:T(8,128)S(1)} %add.62), channel_id=1, source_target_pairs={{0,1},{1,0},{2,3},{3,2},{4,5},{5,4},{6,7},{7,6},{8,9},{9,8},{10,11... | collective-permute-start | bytes 24584 | tf_op jit(solution)/shard_map/ppermute | solution.py:25
  100.1 2.4 %collective-permute-start.16 = (f32[8,256]{1,0:T(8,128)S(1)}, f32[8,256]{1,0:T(8,128)S(1)}, u32[]{:S(2)}, u32[]{:S(2)}) collective-permute-start(f32[8,256]{1,0:T(8,128)S(1)} %add.62), channel_id=1, source_target_pairs={{0,3},{1,2},{2,1},{3,0},{4,7},{5,6},{6,5},{7,4},{8,11},{9,10},{10,... | collective-permute-start | bytes 24584 | tf_op jit(solution)/shard_map/ppermute | solution.py:25
  102.5 2.2 %collective-permute-done.15 = f32[8,256]{1,0:T(8,128)S(1)} collective-permute-done((f32[8,256]{1,0:T(8,128)S(1)}, f32[8,256]{1,0:T(8,128)S(1)}, u32[]{:S(2)}, u32[]{:S(2)}) %collective-permute-start.15) | collective-permute-done | bytes 8224 | tf_op jit(solution)/shard_map/ppermute | solution.py:25
  104.7 0.9 collective-permute-done.16
  105.6 0.9 fusion.5
  106.5 1.0 collective-permute-start.18
  107.5 0.9 collective-permute-start.19
  108.4 1.9 %collective-permute-done.18 = f32[8,256]{1,0:T(8,128)S(1)} collective-permute-done((f32[8,256]{1,0:T(8,128)S(1)}, f32[8,256]{1,0:T(8,128)S(1)}, u32[]{:S(2)}, u32[]{:S(2)}) %collective-permute-start.18) | collective-permute-done | bytes 8224 | tf_op jit(solution)/shard_map/ppermute | solution.py:25
  111.1 3.1 %collective-permute-done.20 = f32[8,256]{1,0:T(8,128)S(1)} collective-permute-done((f32[8,256]{1,0:T(8,128)S(1)}, f32[8,256]{1,0:T(8,128)S(1)}, u32[]{:S(2)}, u32[]{:S(2)}) %collective-permute-start.20) | collective-permute-done | bytes 8224 | tf_op jit(solution)/shard_map/ppermute | solution.py:25
  114.2 2.9 %collective-permute-start.22 = (f32[8,256]{1,0:T(8,128)S(1)}, f32[8,256]{1,0:T(8,128)S(1)}, u32[]{:S(2)}, u32[]{:S(2)}) collective-permute-start(f32[8,256]{1,0:T(8,128)S(1)} %add.70), channel_id=1, source_target_pairs={{0,2},{1,3},{2,0},{3,1},{4,6},{5,7},{6,4},{7,5},{8,10},{9,11},{10,... | collective-permute-start | bytes 24584 | tf_op jit(solution)/shard_map/ppermute | solution.py:25
  117.2 1.5 %collective-permute-start.23 = (f32[8,256]{1,0:T(8,128)S(1)}, f32[8,256]{1,0:T(8,128)S(1)}, u32[]{:S(2)}, u32[]{:S(2)}) collective-permute-start(f32[8,256]{1,0:T(8,128)S(1)} %add.70), channel_id=1, source_target_pairs={{0,3},{1,2},{2,1},{3,0},{4,7},{5,6},{6,5},{7,4},{8,11},{9,10},{10,... | collective-permute-start | bytes 24584 | tf_op jit(solution)/shard_map/ppermute | solution.py:25
  118.8 3.8 %collective-permute-done.23 = f32[8,256]{1,0:T(8,128)S(1)} collective-permute-done((f32[8,256]{1,0:T(8,128)S(1)}, f32[8,256]{1,0:T(8,128)S(1)}, u32[]{:S(2)}, u32[]{:S(2)}) %collective-permute-start.23) | collective-permute-done | bytes 8224 | tf_op jit(solution)/shard_map/ppermute | solution.py:25
  122.6 0.6 add_add_fusion
  (54 shorter events, 2.5 us)
Async XLA Ops:
  0.6 36.2 %copy-start = (f32[8,8]{1,0:T(8,128)S(1)}, f32[8,8]{1,0:T(8,128)}, u32[]{:S(2)}) copy-start(f32[8,8]{1,0:T(8,128)} %param.12) | copy-start | bytes 772
  0.6 22.0 %copy-start.12 = (s32[8,4]{0,1:T(4,128)S(1)}, s32[8,4]{0,1:T(4,128)}, u32[]{:S(2)}) copy-start(s32[8,4]{0,1:T(4,128)} %param.13) | copy-start | bytes 388
  3.2 28.6 %copy-start.1 = (f32[6,16,4,128]{3,2,1,0:T(4,128)}, f32[6,16,4,128]{3,2,1,0:T(4,128)S(1)}, u32[]{:S(2)}) copy-start(f32[6,16,4,128]{3,2,1,0:T(4,128)S(1)} %maximum_bitcast_fusion.refs_0_) | copy-start | bytes 589828
  3.2 20.1 %collective-permute-start = (f32[6,16,4,128]{3,2,1,0:T(4,128)S(1)}, f32[6,16,4,128]{3,2,1,0:T(4,128)S(1)}, u32[]{:S(2)}, u32[]{:S(2)}) collective-permute-start(f32[6,16,4,128]{3,2,1,0:T(4,128)S(1)} %maximum_bitcast_fusion.refs_0_), channel_id=1, source_target_pairs={{0,4},{4,0},{1,5},{5,1},{2,6},{6,2},{3,7},{7,3},{8,12},{12,8},{9,1... | collective-permute-start | bytes 589832 | tf_op jit(solution)/shard_map/ppermute | solution.py:321
  6.2 22.2 %collective-permute-start.1 = (f32[6,16,4,128]{3,2,1,0:T(4,128)S(1)}, f32[6,16,4,128]{3,2,1,0:T(4,128)S(1)}, u32[]{:S(2)}, u32[]{:S(2)}) collective-permute-start(f32[6,16,4,128]{3,2,1,0:T(4,128)S(1)} %maximum_bitcast_fusion.refs_0_), channel_id=1, source_target_pairs={{0,1},{2,3},{1,0},{3,2},{4,5},{6,7},{5,4},{7,6},{8,9},{10,11},{9,8... | collective-permute-start | bytes 589832 | tf_op jit(solution)/shard_map/ppermute | solution.py:323
  7.8 20.6 %collective-permute-start.3 = (f32[6,16,4,128]{3,2,1,0:T(4,128)S(1)}, f32[6,16,4,128]{3,2,1,0:T(4,128)S(1)}, u32[]{:S(2)}, u32[]{:S(2)}) collective-permute-start(f32[6,16,4,128]{3,2,1,0:T(4,128)S(1)} %maximum_bitcast_fusion.refs_0_), channel_id=1, source_target_pairs={{1,2},{2,1},{5,6},{6,5},{9,10},{10,9},{13,14},{14,13},{17,18},{18,... | collective-permute-start | bytes 589832 | tf_op jit(solution)/shard_map/ppermute | solution.py:324
  23.4 8.5 %copy-start.2 = (f32[6,16,4,128]{3,2,1,0:T(4,128)}, f32[6,16,4,128]{3,2,1,0:T(4,128)S(1)}, u32[]{:S(2)}) copy-start(f32[6,16,4,128]{3,2,1,0:T(4,128)S(1)} %collective-permute-done.refs_1_) | copy-start | bytes 589828
  23.4 8.4 %collective-permute-start.2 = (f32[6,16,4,128]{3,2,1,0:T(4,128)S(1)}, f32[6,16,4,128]{3,2,1,0:T(4,128)S(1)}, u32[]{:S(2)}, u32[]{:S(2)}) collective-permute-start(f32[6,16,4,128]{3,2,1,0:T(4,128)S(1)} %collective-permute-done.refs_1_), channel_id=1, source_target_pairs={{0,1},{2,3},{1,0},{3,2},{4,5},{6,7},{5,4},{7,6},{8,9},{10,11},{9,8... | collective-permute-start | bytes 589832 | tf_op jit(solution)/shard_map/ppermute | solution.py:323
  27.8 4.1 %collective-permute-start.4 = (f32[6,16,4,128]{3,2,1,0:T(4,128)S(1)}, f32[6,16,4,128]{3,2,1,0:T(4,128)S(1)}, u32[]{:S(2)}, u32[]{:S(2)}) collective-permute-start(f32[6,16,4,128]{3,2,1,0:T(4,128)S(1)} %collective-permute-done.refs_1_), channel_id=1, source_target_pairs={{1,2},{2,1},{5,6},{6,5},{9,10},{10,9},{13,14},{14,13},{17,18},{18,... | collective-permute-start | bytes 589832 | tf_op jit(solution)/shard_map/ppermute | solution.py:324
  28.4 3.4 %copy-start.3 = (f32[6,16,4,128]{3,2,1,0:T(4,128)}, f32[6,16,4,128]{3,2,1,0:T(4,128)S(1)}, u32[]{:S(2)}) copy-start(f32[6,16,4,128]{3,2,1,0:T(4,128)S(1)} %collective-permute-done.1.refs_2_) | copy-start | bytes 589828
  28.5 3.4 %copy-start.4 = (f32[6,16,4,128]{3,2,1,0:T(4,128)}, f32[6,16,4,128]{3,2,1,0:T(4,128)S(1)}, u32[]{:S(2)}) copy-start(f32[6,16,4,128]{3,2,1,0:T(4,128)S(1)} %collective-permute-done.3.refs_4_) | copy-start | bytes 589828
  31.8 0.7 copy-start.5
  32.5 0.7 copy-start.6
  36.2 1.6 %collective-permute-start.5 = (f32[6,6,8,128]{3,2,1,0:T(8,128)}, f32[6,6,8,128]{3,2,1,0:T(8,128)S(1)}, u32[]{:S(2)}, u32[]{:S(2)}) collective-permute-start(f32[6,6,8,128]{3,2,1,0:T(8,128)} %get-tuple-element.12), channel_id=1, source_target_pairs={{0,8},{16,24},{8,0},{24,16},{1,9},{17,25},{9,1},{25,17},{2,10},{18... | collective-permute-start | bytes 442376 | tf_op jit(solution)/shard_map/ppermute | solution.py:336
  36.2 1.6 %collective-permute-start.6 = (f32[6,6,8,128]{3,2,1,0:T(8,128)}, f32[6,6,8,128]{3,2,1,0:T(8,128)S(1)}, u32[]{:S(2)}, u32[]{:S(2)}) collective-permute-start(f32[6,6,8,128]{3,2,1,0:T(8,128)} %get-tuple-element.13), channel_id=1, source_target_pairs={{8,16},{16,8},{9,17},{17,9},{10,18},{18,10},{11,19},{19,11},{12,20... | collective-permute-start | bytes 442376 | tf_op jit(solution)/shard_map/ppermute | solution.py:337
  37.8 0.8 copy-start.10
  37.8 0.8 copy-start.11
  57.9 11.6 %collective-permute-start.9 = (f32[4,16,8,128]{3,2,1,0:T(8,128)}, f32[4,16,8,128]{3,2,1,0:T(8,128)S(1)}, u32[]{:S(2)}, u32[]{:S(2)}) collective-permute-start(f32[4,16,8,128]{3,2,1,0:T(8,128)} %get-tuple-element.18), channel_id=1, source_target_pairs={{0,8},{8,0},{16,24},{24,16},{1,9},{9,1},{17,25},{25,17},{2,10},{10... | collective-permute-start | bytes 786440 | tf_op jit(solution)/shard_map/ppermute | solution.py:25
  63.4 10.8 %collective-permute-start.8 = (f32[4,16,8,128]{3,2,1,0:T(8,128)}, f32[4,16,8,128]{3,2,1,0:T(8,128)S(1)}, u32[]{:S(2)}, u32[]{:S(2)}) collective-permute-start(f32[4,16,8,128]{3,2,1,0:T(8,128)} %get-tuple-element.17), channel_id=1, source_target_pairs={{0,16},{8,24},{16,0},{24,8},{1,17},{9,25},{17,1},{25,9},{2,18},{10... | collective-permute-start | bytes 786440 | tf_op jit(solution)/shard_map/ppermute | solution.py:25
  64.5 14.5 %collective-permute-start.7 = (f32[4,16,8,128]{3,2,1,0:T(8,128)}, f32[4,16,8,128]{3,2,1,0:T(8,128)S(1)}, u32[]{:S(2)}, u32[]{:S(2)}) collective-permute-start(f32[4,16,8,128]{3,2,1,0:T(8,128)} %get-tuple-element.16), channel_id=1, source_target_pairs={{0,24},{8,16},{16,8},{24,0},{1,25},{9,17},{17,9},{25,1},{2,26},{10... | collective-permute-start | bytes 786440 | tf_op jit(solution)/shard_map/ppermute | solution.py:25
  69.5 0.7 copy-start.9
  74.3 0.7 copy-start.8
  79.0 0.7 copy-start.7
  84.5 2.1 %collective-permute-start.10 = (f32[8,256]{1,0:T(8,128)S(1)}, f32[8,256]{1,0:T(8,128)S(1)}, u32[]{:S(2)}, u32[]{:S(2)}) collective-permute-start(f32[8,256]{1,0:T(8,128)S(1)} %slice.9), channel_id=1, source_target_pairs={{0,8},{8,0},{16,24},{24,16},{1,9},{9,1},{17,25},{25,17},{2,10},{10... | collective-permute-start | bytes 24584 | tf_op jit(solution)/shard_map/ppermute | solution.py:25
  85.2 3.7 %collective-permute-start.11 = (f32[8,256]{1,0:T(8,128)S(1)}, f32[8,256]{1,0:T(8,128)S(1)}, u32[]{:S(2)}, u32[]{:S(2)}) collective-permute-start(f32[8,256]{1,0:T(8,128)S(1)} %slice.9), channel_id=1, source_target_pairs={{0,16},{8,24},{16,0},{24,8},{1,17},{9,25},{17,1},{25,9},{2,18},{10... | collective-permute-start | bytes 24584 | tf_op jit(solution)/shard_map/ppermute | solution.py:25
  86.3 3.1 %collective-permute-start.12 = (f32[8,256]{1,0:T(8,128)S(1)}, f32[8,256]{1,0:T(8,128)S(1)}, u32[]{:S(2)}, u32[]{:S(2)}) collective-permute-start(f32[8,256]{1,0:T(8,128)S(1)} %slice.9), channel_id=1, source_target_pairs={{0,24},{8,16},{16,8},{24,0},{1,25},{9,17},{17,9},{25,1},{2,26},{10... | collective-permute-start | bytes 24584 | tf_op jit(solution)/shard_map/ppermute | solution.py:25
  90.1 3.7 %collective-permute-start.13 = (f32[8,256]{1,0:T(8,128)S(1)}, f32[8,256]{1,0:T(8,128)S(1)}, u32[]{:S(2)}, u32[]{:S(2)}) collective-permute-start(f32[8,256]{1,0:T(8,128)S(1)} %add_add_fusion.3), channel_id=1, source_target_pairs={{0,4},{4,0},{1,5},{5,1},{2,6},{6,2},{3,7},{7,3},{8,12},{12,8},{9,1... | collective-permute-start | bytes 24584 | tf_op jit(solution)/shard_map/ppermute | solution.py:25
  93.7 8.8 %collective-permute-start.14 = (f32[8,256]{1,0:T(8,128)S(1)}, f32[8,256]{1,0:T(8,128)S(1)}, u32[]{:S(2)}, u32[]{:S(2)}) collective-permute-start(f32[8,256]{1,0:T(8,128)S(1)} %add.62), channel_id=1, source_target_pairs={{0,1},{1,0},{2,3},{3,2},{4,5},{5,4},{6,7},{7,6},{8,9},{9,8},{10,11... | collective-permute-start | bytes 24584 | tf_op jit(solution)/shard_map/ppermute | solution.py:25
  100.1 4.5 %collective-permute-start.15 = (f32[8,256]{1,0:T(8,128)S(1)}, f32[8,256]{1,0:T(8,128)S(1)}, u32[]{:S(2)}, u32[]{:S(2)}) collective-permute-start(f32[8,256]{1,0:T(8,128)S(1)} %add.62), channel_id=1, source_target_pairs={{0,2},{1,3},{2,0},{3,1},{4,6},{5,7},{6,4},{7,5},{8,10},{9,11},{10,... | collective-permute-start | bytes 24584 | tf_op jit(solution)/shard_map/ppermute | solution.py:25
  100.1 5.4 %collective-permute-start.16 = (f32[8,256]{1,0:T(8,128)S(1)}, f32[8,256]{1,0:T(8,128)S(1)}, u32[]{:S(2)}, u32[]{:S(2)}) collective-permute-start(f32[8,256]{1,0:T(8,128)S(1)} %add.62), channel_id=1, source_target_pairs={{0,3},{1,2},{2,1},{3,0},{4,7},{5,6},{6,5},{7,4},{8,11},{9,10},{10,... | collective-permute-start | bytes 24584 | tf_op jit(solution)/shard_map/ppermute | solution.py:25
  106.5 1.9 %collective-permute-start.17 = (f32[8,256]{1,0:T(8,128)S(1)}, f32[8,256]{1,0:T(8,128)S(1)}, u32[]{:S(2)}, u32[]{:S(2)}) collective-permute-start(f32[8,256]{1,0:T(8,128)S(1)} %fusion.5), channel_id=1, source_target_pairs={{0,8},{8,0},{16,24},{24,16},{1,9},{9,1},{17,25},{25,17},{2,10},{10... | collective-permute-start | bytes 24584 | tf_op jit(solution)/shard_map/ppermute | solution.py:25
  106.5 3.7 %collective-permute-start.18 = (f32[8,256]{1,0:T(8,128)S(1)}, f32[8,256]{1,0:T(8,128)S(1)}, u32[]{:S(2)}, u32[]{:S(2)}) collective-permute-start(f32[8,256]{1,0:T(8,128)S(1)} %fusion.5), channel_id=1, source_target_pairs={{0,16},{8,24},{16,0},{24,8},{1,17},{9,25},{17,1},{25,9},{2,18},{10... | collective-permute-start | bytes 24584 | tf_op jit(solution)/shard_map/ppermute | solution.py:25
  107.5 3.1 %collective-permute-start.19 = (f32[8,256]{1,0:T(8,128)S(1)}, f32[8,256]{1,0:T(8,128)S(1)}, u32[]{:S(2)}, u32[]{:S(2)}) collective-permute-start(f32[8,256]{1,0:T(8,128)S(1)} %fusion.5), channel_id=1, source_target_pairs={{0,24},{8,16},{16,8},{24,0},{1,25},{9,17},{17,9},{25,1},{2,26},{10... | collective-permute-start | bytes 24584 | tf_op jit(solution)/shard_map/ppermute | solution.py:25
  110.6 3.7 %collective-permute-start.20 = (f32[8,256]{1,0:T(8,128)S(1)}, f32[8,256]{1,0:T(8,128)S(1)}, u32[]{:S(2)}, u32[]{:S(2)}) collective-permute-start(f32[8,256]{1,0:T(8,128)S(1)} %add_add_fusion.1), channel_id=1, source_target_pairs={{0,4},{4,0},{1,5},{5,1},{2,6},{6,2},{3,7},{7,3},{8,12},{12,8},{9,1... | collective-permute-start | bytes 24584 | tf_op jit(solution)/shard_map/ppermute | solution.py:25
  114.2 4.4 %collective-permute-start.21 = (f32[8,256]{1,0:T(8,128)S(1)}, f32[8,256]{1,0:T(8,128)S(1)}, u32[]{:S(2)}, u32[]{:S(2)}) collective-permute-start(f32[8,256]{1,0:T(8,128)S(1)} %add.70), channel_id=1, source_target_pairs={{0,1},{1,0},{2,3},{3,2},{4,5},{5,4},{6,7},{7,6},{8,9},{9,8},{10,11... | collective-permute-start | bytes 24584 | tf_op jit(solution)/shard_map/ppermute | solution.py:25
  114.2 4.6 %collective-permute-start.22 = (f32[8,256]{1,0:T(8,128)S(1)}, f32[8,256]{1,0:T(8,128)S(1)}, u32[]{:S(2)}, u32[]{:S(2)}) collective-permute-start(f32[8,256]{1,0:T(8,128)S(1)} %add.70), channel_id=1, source_target_pairs={{0,2},{1,3},{2,0},{3,1},{4,6},{5,7},{6,4},{7,5},{8,10},{9,11},{10,... | collective-permute-start | bytes 24584 | tf_op jit(solution)/shard_map/ppermute | solution.py:25
  117.2 5.4 %collective-permute-start.23 = (f32[8,256]{1,0:T(8,128)S(1)}, f32[8,256]{1,0:T(8,128)S(1)}, u32[]{:S(2)}, u32[]{:S(2)}) collective-permute-start(f32[8,256]{1,0:T(8,128)S(1)} %add.70), channel_id=1, source_target_pairs={{0,3},{1,2},{2,1},{3,0},{4,7},{5,6},{6,5},{7,4},{8,11},{9,10},{10,... | collective-permute-start | bytes 24584 | tf_op jit(solution)/shard_map/ppermute | solution.py:25

commit v3 on v2

--- a/solution.py
+++ b/solution.py
@@ -1,4 +1,5 @@
 import functools
+import math
 
 import jax
 import jax.numpy as jnp
@@ -11,7 +12,7 @@
 LANES = 128
 GROUPS = LANES // STEPS
 BLOCK = 8
-VMEM_LIMIT = 60 * 1024 * 1024
+MIB = 1024 * 1024
 
 
 def pairs(axis, first):
@@ -43,15 +44,6 @@
     return value
 
 
-def reaction_table(rates, stoich):
-    react_count, spec = stoich.shape
-    owner = jnp.arange(react_count) % spec
-    pick = (owner[:, None] == jnp.arange(spec)[None, :]).astype(jnp.float32)
-    return jnp.einsum(
-        "mr,ra,rs->asm", rates, pick, stoich.astype(jnp.float32), precision=lax.Precision.HIGHEST
-    )
-
-
 def whole(count):
     return [pl.BlockSpec(memory_space=pltpu.VMEM)] * count
 
@@ -60,11 +52,42 @@
     return [pl.BlockSpec(memory_space=pltpu.SMEM)] * count
 
 
-def edges_kernel(blocks_x, ids, *refs):
-    blocks, (out_a, out_b) = refs[:-2], refs[-2:]
+def anywhere(count):
+    return [pl.BlockSpec(memory_space=pl.ANY)] * count
+
+
+def vmem(*shapes):
+    return pltpu.CompilerParams(vmem_limit_bytes=4 * sum(map(math.prod, shapes)) + 6 * MIB)
+
+
+def fetch(sources, targets, sems):
+    copies = [
+        pltpu.make_async_copy(source, target, sems.at[i])
+        for i, (source, target) in enumerate(zip(sources, targets))
+    ]
+    for copy in copies:
+        copy.start()
+    return copies
+
+
+def pack_kernel(terminal, velocity, material, out):
+    spec, cells_x, cells_y, cells_z = terminal.shape
+    for x in range(cells_x):
+        for s in range(spec):
+            out[s, :, x, :] = terminal[s, x]
+        out[spec, :, x, :] = velocity[x]
+        out[spec + 1, :, x, :] = material[x].astype(jnp.float32)
+
+
+def edges_kernel(blocks_x, *refs):
+    given, (out_a, out_b, blocks, sems) = refs[:-4], refs[-4:]
+    blocks = [blocks.at[i] for i in range(len(given))]
+    copies = fetch(given, blocks, sems)
     fields, cells_y, cells_x, cells_z = blocks[0].shape
     per_block = cells_y // GROUPS
-    even = ids[0] % 2 == 0
+    even = lax.axis_index("grp") % 2 == 0
+    for copy in copies:
+        copy.wait()
     place = lax.broadcasted_iota(jnp.int32, (blocks_x * cells_x, LANES), 1) // STEPS
 
     def field_body(field, _):
@@ -89,16 +112,19 @@
     lax.fori_loop(0, fields, field_body, 0)
 
 
-def steps_kernel(blocks_x, ids, plan, diffusion, table, *refs):
+def steps_kernel(blocks_x, plan, diffusion, stoich, rates, *refs):
     count_blocks = 3 * blocks_x
-    blocks = refs[:count_blocks]
-    side_a, side_b = refs[count_blocks : count_blocks + 2]
+    given = refs[: count_blocks + 2]
     adjoint = refs[count_blocks + 2]
-    kept = refs[count_blocks + 3 : -4]
-    state, other, matrix, speed = refs[-4:]
+    kept = refs[count_blocks + 3 : -7]
+    state, other, matrix, speed, blocks, sides, sems = refs[-7:]
+    blocks = [blocks.at[i] for i in range(count_blocks)]
+    side_a, side_b = sides.at[0], sides.at[1]
+    copies = fetch(given, blocks + [side_a, side_b], sems)
     spec, rows, all_x, wide = state.shape
     _, cells_y, cells_x, cells_z = blocks[0].shape
-    grp, at_x, at_y, count_grp, count_y = (ids[i] for i in range(5))
+    grp, at_x, at_y = (lax.axis_index(axis) for axis in ("grp", "gx", "gy"))
+    count_grp, count_y = lax.axis_size("grp"), lax.axis_size("gy")
     snaps = kept[0].shape[2]
     per_block = cells_y // GROUPS
     even_z = grp % 2 == 0
@@ -123,6 +149,18 @@
     is_first = place_x == 0
     is_last = place_x == all_x - 1
 
+    columns = [
+        jnp.broadcast_to(rates[:, r : r + 1], (rates.shape[0], LANES)) for r in range(rates.shape[1])
+    ]
+    table = [
+        sum(
+            columns[r] * stoich[r, s].astype(jnp.float32) for r in range(a, rates.shape[1], spec)
+        )
+        for a in range(spec)
+        for s in range(spec)
+    ]
+    for copy in copies:
+        copy.wait()
     for slot in range(3):
         mine = blocks[slot * blocks_x : (slot + 1) * blocks_x]
         for part in range(per_block):
@@ -256,121 +294,171 @@
     lax.fori_loop(0, spec, leave, 0)
 
 
-def product_kernel(_, part, basis, total, out):
-    @pl.when(pl.program_id(0) == 0)
-    def _():
-        out[...] = total[...]
-
-    _, cells_y, snaps, cells_z = part.shape
-    values = part[0]
-    high = values.astype(jnp.bfloat16)
-    low = values - high.astype(jnp.float32)
-    left = jnp.concatenate([high.astype(jnp.float32), low], axis=1).astype(jnp.bfloat16)
-    acc = out[...]
-    for y in range(0, cells_y, 2):
-        acc = acc + jnp.dot(
-            jnp.concatenate([left[y], left[y + 1]], axis=1),
-            basis[0, 0, y : y + 2].reshape(2 * cells_z, basis.shape[-1]),
-            preferred_element_type=jnp.float32,
+def gram_kernel(x, basis, *refs):
+    (out, chunks, sems), total = refs[-3:], refs[:-3]
+    count, rows, cells_z, modes = chunks.shape
+    copies = fetch(
+        [basis.at[0, x, pl.ds(i * rows, rows)] for i in range(count)],
+        [chunks.at[i] for i in range(count)],
+        sems,
+    )
+    acc = total[0][...] if total else None
+    for i, copy in enumerate(copies):
+        copy.wait()
+        chunk = chunks[i].reshape(rows * cells_z, modes)
+        part = lax.dot_general(
+            chunk, chunk, (((0,), (0,)), ((), ())), preferred_element_type=jnp.float32
         )
+        acc = part if acc is None else acc + part
     out[...] = acc
 
 
-def product(zone, part, basis, total):
+def gram_part(x, basis, *total):
+    _, _, cells_y, cells_z, modes = basis.shape
+    chunks = 2
+    size = 2 * cells_y * cells_z * modes
+    return pl.pallas_call(
+        functools.partial(gram_kernel, x),
+        out_shape=jax.ShapeDtypeStruct((modes, modes), jnp.float32),
+        in_specs=anywhere(1) + whole(len(total)),
+        out_specs=whole(1)[0],
+        scratch_shapes=[
+            pltpu.VMEM((chunks, cells_y // chunks, cells_z, modes), jnp.bfloat16),
+            pltpu.SemaphoreType.DMA((chunks,)),
+        ],
+        compiler_params=pltpu.CompilerParams(vmem_limit_bytes=2 * size + 8 * MIB),
+        cost_estimate=pl.CostEstimate(
+            flops=2 * cells_y * cells_z * modes * modes, bytes_accessed=3 * size, transcendentals=0
+        ),
+        name="gram",
+    )(basis, *total)
+
+
+def product_kernel(flips, part, basis, *refs):
+    (out_high, out_low, held, rows, sems), total = refs[-5:], refs[:-5]
+    cells_x, cells_y, snaps, cells_z = held.shape
+    zone = (lax.axis_index("grp") ^ flips) * cells_z
+    copies = fetch(
+        [part] + [basis.at[0, x, :, pl.ds(pl.multiple_of(zone, LANES), cells_z)] for x in range(cells_x)],
+        [held] + [rows.at[x] for x in range(cells_x)],
+        sems,
+    )
+    copies[0].wait()
+    acc = jnp.concatenate([total[0][...], total[1][...]], axis=0) if total else None
+    for x in range(cells_x):
+        values = held[x]
+        high = values.astype(jnp.bfloat16).astype(jnp.float32)
+        left = jnp.concatenate([high, values - high], axis=1).astype(jnp.bfloat16)
+        copies[1 + x].wait()
+        for y in range(0, cells_y, 2):
+            more = jnp.dot(
+                jnp.concatenate([left[y], left[y + 1]], axis=1),
+                rows[x, y : y + 2].reshape(2 * cells_z, basis.shape[-1]),
+                preferred_element_type=jnp.float32,
+            )
+            acc = more if acc is None else acc + more
+    out_high[...] = acc[:snaps]
+    out_low[...] = acc[snaps:]
+
+
+def product(flips, part, basis, *total):
     cells_x, cells_y, snaps, cells_z = part.shape
     modes = basis.shape[-1]
+    size = 2 * cells_x * cells_y * cells_z * modes
+    out = jax.ShapeDtypeStruct((snaps, modes), jnp.float32)
     return pl.pallas_call(
-        product_kernel,
-        out_shape=jax.ShapeDtypeStruct((2 * snaps, modes), jnp.float32),
-        grid_spec=pltpu.PrefetchScalarGridSpec(
-            num_scalar_prefetch=1,
-            grid=(cells_x,),
-            in_specs=[
-                pl.BlockSpec((1, cells_y, snaps, cells_z), lambda x, z: (x, 0, 0, 0)),
-                pl.BlockSpec((1, 1, cells_y, cells_z, modes), lambda x, z: (0, x, 0, z[0], 0)),
-                pl.BlockSpec((2 * snaps, modes), lambda x, z: (0, 0)),
-            ],
-            out_specs=pl.BlockSpec((2 * snaps, modes), lambda x, z: (0, 0)),
-        ),
+        functools.partial(product_kernel, flips),
+        out_shape=(out, out),
+        in_specs=anywhere(2) + whole(len(total)),
+        out_specs=tuple(whole(2)),
+        scratch_shapes=[
+            pltpu.VMEM(part.shape, jnp.float32),
+            pltpu.VMEM((cells_x, cells_y, cells_z, modes), jnp.bfloat16),
+            pltpu.SemaphoreType.DMA((cells_x + 1,)),
+        ],
+        compiler_params=pltpu.CompilerParams(vmem_limit_bytes=size + 8 * MIB),
         cost_estimate=pl.CostEstimate(
-            flops=4 * snaps * cells_x * cells_y * cells_z * modes,
-            bytes_accessed=2 * cells_x * cells_y * cells_z * modes,
-            transcendentals=0,
+            flops=2 * snaps * size, bytes_accessed=2 * size, transcendentals=0
         ),
         name="product",
-    )(zone, part, basis, total)
+    )(part, basis, *total)
 
 
 def body(terminal, diffusion, velocity, material, rates, stoich, plan, basis):
     spec, cells_x, cells_y, cells_z = terminal.shape
     snaps, modes = plan.shape[0], basis.shape[-1]
-    count_grp, count_x, count_y = (lax.axis_size(axis) for axis in ("grp", "gx", "gy"))
-    grp = lax.axis_index("grp")
-    ids = jnp.stack(
-        [grp, lax.axis_index("gx"), lax.axis_index("gy"), jnp.int32(count_grp), jnp.int32(count_y)]
-    ).astype(jnp.int32)
-    table = reaction_table(rates, stoich).reshape(spec * spec, rates.shape[0], 1)
-    table = jnp.broadcast_to(table, table.shape[:2] + (LANES,))
-
-    own = jnp.concatenate(
-        [terminal, velocity[None], material.astype(jnp.float32)[None]], axis=0
-    ).transpose(0, 2, 1, 3)
+    count_grp, count_x = lax.axis_size("grp"), lax.axis_size("gx")
+    fields, all_x = spec + 2, cells_x * count_x
+    wide, rows = cells_z + LANES, 3 * cells_y + 2 * BLOCK
+
+    own = pl.pallas_call(
+        pack_kernel,
+        out_shape=jax.ShapeDtypeStruct((fields, cells_y, cells_x, cells_z), jnp.float32),
+        in_specs=whole(3),
+        out_specs=whole(1)[0],
+        name="pack",
+    )(terminal, velocity, material)
     blocks = [own]
     for shift in range(1, count_x):
         blocks.append(
             lax.ppermute(own, "gx", [(i, (i - shift) % count_x) for i in range(count_x)])
         )
-    blocks_a = [lax.ppermute(b, "gy", pairs("gy", 0)) for b in blocks]
-    blocks_b = [lax.ppermute(b, "gy", pairs("gy", 1)) for b in blocks]
-    blocks = blocks + blocks_a + blocks_b
-    fields, all_x = spec + 2, cells_x * count_x
+    from_a = [lax.ppermute(own, "gy", pairs("gy", 0))]
+    from_b = [lax.ppermute(own, "gy", pairs("gy", 1))]
+    gram = gram_part(0, basis)
+    *blocks, gram = lax.optimization_barrier((*blocks, gram))
+    from_a += [lax.ppermute(b, "gy", pairs("gy", 0)) for b in blocks[1:]]
+    from_b += [lax.ppermute(b, "gy", pairs("gy", 1)) for b in blocks[1:]]
+    gram = gram_part(1, basis, gram)
+    blocks = blocks + from_a + from_b
+    *blocks, gram = lax.optimization_barrier((*blocks, gram))
     packed = jax.ShapeDtypeStruct((fields, 3 * cells_y // GROUPS, all_x, LANES), jnp.float32)
+    held = (len(blocks), fields, cells_y, cells_x, cells_z)
     edge_a, edge_b = pl.pallas_call(
         functools.partial(edges_kernel, count_x),
         out_shape=(packed, packed),
-        in_specs=scalars(1) + whole(len(blocks)),
+        in_specs=anywhere(len(blocks)),
         out_specs=tuple(whole(2)),
-        compiler_params=pltpu.CompilerParams(vmem_limit_bytes=VMEM_LIMIT),
+        scratch_shapes=[pltpu.VMEM(held, jnp.float32), pltpu.SemaphoreType.DMA((len(blocks),))],
+        compiler_params=vmem(held, packed.shape, packed.shape),
         name="edges",
-    )(ids, *blocks)
+    )(*blocks)
     side_a = lax.ppermute(edge_a, "grp", pairs("grp", 0))
     side_b = lax.ppermute(edge_b, "grp", pairs("grp", 1))
-
-    local = basis.reshape(-1, modes)
-    gram = lax.dot_general(
-        local, local, (((0,), (0,)), ((), ())), preferred_element_type=jnp.float32
-    )
-
+    gram = gram_part(2, basis, gram)
     side_a, side_b, gram = lax.optimization_barrier((side_a, side_b, gram))
-    wide, rows = cells_z + LANES, 3 * cells_y + 2 * BLOCK
+
     part = jax.ShapeDtypeStruct((cells_x, cells_y, snaps, cells_z), jnp.float32)
+    room = (rows, all_x, wide)
+    shapes = [(spec, *room), (spec, *room), (spec * spec, *room), room, held, (2, *packed.shape)]
     final, *kept = pl.pallas_call(
         functools.partial(steps_kernel, count_x),
         out_shape=[jax.ShapeDtypeStruct(terminal.shape, jnp.float32)] + [part] * count_grp,
-        in_specs=scalars(3) + whole(3 + len(blocks)),
+        in_specs=scalars(3) + whole(1) + anywhere(len(blocks) + 2),
         out_specs=whole(1 + count_grp),
-        scratch_shapes=[
-            pltpu.VMEM((spec, rows, all_x, wide), jnp.float32),
-            pltpu.VMEM((spec, rows, all_x, wide), jnp.float32),
-            pltpu.VMEM((spec * spec, rows, all_x, wide), jnp.float32),
-            pltpu.VMEM((rows, all_x, wide), jnp.float32),
-        ],
-        compiler_params=pltpu.CompilerParams(vmem_limit_bytes=VMEM_LIMIT),
+        scratch_shapes=[pltpu.VMEM(shape, jnp.float32) for shape in shapes]
+        + [pltpu.SemaphoreType.DMA((len(blocks) + 2,))],
+        compiler_params=vmem(*shapes, terminal.shape, (count_grp, *part.shape)),
         name="steps",
-    )(ids, plan, diffusion, table, *blocks, side_a, side_b)
+    )(plan, diffusion, stoich, rates, *blocks, side_a, side_b)
 
     order = sorted(range(1, count_grp), key=lambda flips: -flips)
     moved = {flips: exchange(kept[flips], "grp", flips) for flips in order}
     moved[0] = kept[0]
-    total = jnp.zeros((2 * snaps, modes), jnp.float32)
+    total = ()
     for flips in range(count_grp):
-        total = product((grp ^ flips).reshape(1).astype(jnp.int32), moved[flips], basis, total)
-
-    first = sum_all(total[:snaps])
+        total = product(flips, moved[flips], basis, *total)
+        if flips == min(1, count_grp - 1):
+            for x in range(3, cells_x):
+                gram = gram_part(x, basis, gram)
+            *total, gram = lax.optimization_barrier((*total, gram))
+    high, low = total
+
+    first = sum_all(high)
     taken = jnp.dot(
         first.astype(jnp.bfloat16).astype(jnp.float32), gram, precision=lax.Precision.HIGHEST
     )
-    second = sum_all(total[:snaps] + total[snaps:] - taken)
+    second = sum_all(high + low - taken)
     return (first + second, final)
 
 

time: 124 us -> 118 us (0.952)
  local copies, waits for them, and re-layouts: 7.24 us -> 24.5 us
  matrix products: 15.2 us -> 0.21 us
  waiting for transfers between devices: 22.4 us -> 17.7 us
  starting transfers between devices: 36.1 us -> 32.5 us
  Pallas kernels: 38.6 us -> 40.9 us
  other arithmetic: 2.82 us -> 0.63 us
    unnamed x27, local copies, waits for them, and re-layouts: 4.39 us -> 24.5 us
    dot_general x2 -> x0, matrix products: 14.3 us -> none  [the longest x1 14.1 us: body(): lax.dot_general(local, local, (((0,), (0,)), ((), ())), preferred_element...]
    ppermute x17, starting transfers between devices: 25.1 us -> 21.1 us  [exchange(): return lax.ppermute(value, axis, [(i, i ^ flips) for i in range(count)])]
    pallas_call x4 -> x9, Pallas kernels: 16.2 us -> 18.6 us  [the longest x4 10.2 us: gram_part(): pl.pallas_call(functools.partial(gram_kernel, x), out_shape=jax.ShapeDtyp...]
    broadcast_in_dim x3 -> x0, local copies, waits for them, and re-layouts: 2.14 us -> none  [the longest x1 0.79 us: body(): material.astype(jnp.float32)[None]]
    ppermute x4, waiting for transfers between devices: 3.34 us -> 1.26 us  [the longest x1 1.25 us: body(): from_a += [lax.ppermute(b, 'gy', pairs('gy', 0)) for b in blocks[1:]]]
    ppermute x17, waiting for transfers between devices: 18.3 us -> 16.4 us  [exchange(): return lax.ppermute(value, axis, [(i, i ^ flips) for i in range(count)])]
  transfers between devices with their start and end apart: 24 -> 24, of which waited for: 12 -> 11; matrix products, arithmetic and copies ran while one was open for 13% -> 0% of each run, Pallas kernels for 10% -> 13%
where the time goes in v3:
time: 118 us; the launch traced here: 117 us
  Pallas kernels  40.9 us (35%)
  starting transfers between devices  32.5 us (28%)
  local copies, waits for them, and re-layouts  24.5 us (21%)
  waiting for transfers between devices  17.7 us (15%)
    unnamed x27, local copies, waits for them, and re-layouts  24.5 us
    ppermute x17, starting transfers between devices, exchange(): return lax.ppermute(value, axis, [(i, i ^ flips) for i in range(count)])  21.1 us
    pallas_call x1, Pallas kernels, body(): pl.pallas_call(functools.partial(steps_kernel, count_x), out_shape=[jax.S...  19.7 us
    ppermute x17, waiting for transfers between devices, exchange(): return lax.ppermute(value, axis, [(i, i ^ flips) for i in range(count)])  16.4 us
    pallas_call x4, Pallas kernels, gram_part(): pl.pallas_call(functools.partial(gram_kernel, x), out_shape=jax.ShapeDtyp...  10.2 us
    pallas_call x4, Pallas kernels, product(): pl.pallas_call(functools.partial(product_kernel, flips), out_shape=(out,...  6.75 us
    ppermute x1, starting transfers between devices, body(): from_a = [lax.ppermute(own, 'gy', pairs('gy', 0))]  4.45 us
    ppermute x1, starting transfers between devices, body(): lax.ppermute(own, 'gx', [(i, (i - shift) % count_x) for i in range(count_...  2.94 us
  transfers between devices with their start and end apart: 24, of which 11 were waited for; matrix products, arithmetic and copies ran while one was open for 0% of the time, Pallas kernels for 13%

profile of v3, /device:TPU:0, one launch (start us, length us, event | category | flops | bytes accessed | tf_op | source)
XLA Modules:
  0.0 117.4 jit_solution(4945141015476828771)
XLA Ops:
  0.6 1.7 %pack.1.refs_0_ = f32[6,16,4,128]{3,2,1,0:T(4,128)} custom-call(f32[4,4,16,128]{3,2,1,0:T(8,128)} %terminal.1, f32[4,16,128]{2,1,0:T(8,128)} %velocity.1, s32[4,16,128]{2,1,0:T(8,128)} %material.1), custom_call_target="tpu_custom_call" | custom-call | tf_op jit(solution)/shard_map/pack/pallas_call | solution.py:394
  2.4 2.9 %collective-permute-start = (f32[6,16,4,128]{3,2,1,0:T(4,128)}, f32[6,16,4,128]{3,2,1,0:T(4,128)S(1)}, u32[]{:S(2)}, u32[]{:S(2)}) collective-permute-start(f32[6,16,4,128]{3,2,1,0:T(4,128)} %pack.1.refs_0_), channel_id=1, source_target_pairs={{0,4},{4,0},{1,5},{5,1},{2,6},{6,2},{3,7},{7,3},{8,12},{12,8},{9,1... | collective-permute-start | bytes 589832 | tf_op jit(solution)/shard_map/ppermute | solution.py:404
  5.3 0.7 collective-permute-start.3
  6.0 4.5 %collective-permute-start.1 = (f32[6,16,4,128]{3,2,1,0:T(4,128)}, f32[6,16,4,128]{3,2,1,0:T(4,128)S(1)}, u32[]{:S(2)}, u32[]{:S(2)}) collective-permute-start(f32[6,16,4,128]{3,2,1,0:T(4,128)} %pack.1.refs_0_), channel_id=1, source_target_pairs={{0,1},{2,3},{1,0},{3,2},{4,5},{6,7},{5,4},{7,6},{8,9},{10,11},{9,8... | collective-permute-start | bytes 589832 | tf_op jit(solution)/shard_map/ppermute | solution.py:406
  10.4 5.8 %copy-done = bf16[1,4,16,512,256]{4,3,2,1,0:T(8,128)(2,1)S(1)} copy-done((bf16[1,4,16,512,256]{4,3,2,1,0:T(8,128)(2,1)S(1)}, bf16[1,4,16,512,256]{4,3,2,1,0:T(8,128)(2,1)}, u32[]{:S(2)}) %copy-start) | copy-done | bytes 16777240
  16.2 1.7 %gram.4.refs_0_ = f32[256,256]{1,0:T(8,128)S(1)} custom-call(bf16[1,4,16,512,256]{4,3,2,1,0:T(8,128)(2,1)S(1)} %copy-done), custom_call_target="tpu_custom_call" | custom-call | flops 1073741824 | bytes 12582912 | tf_op jit(solution)/shard_map/gram/pallas_call | solution.py:320
  18.0 0.7 collective-permute-start.4
  18.7 1.8 %collective-permute-start.2 = (f32[6,16,4,128]{3,2,1,0:T(4,128)S(1)}, f32[6,16,4,128]{3,2,1,0:T(4,128)S(1)}, u32[]{:S(2)}, u32[]{:S(2)}) collective-permute-start(f32[6,16,4,128]{3,2,1,0:T(4,128)S(1)} %collective-permute-done.refs_1_), channel_id=1, source_target_pairs={{0,1},{2,3},{1,0},{3,2},{4,5},{6,7},{5,4},{7,6},{8,9},{10,11},{9,8... | collective-permute-start | bytes 589832 | tf_op jit(solution)/shard_map/ppermute | solution.py:410
  20.4 2.8 %gram.5.refs_0_ = f32[256,256]{1,0:T(8,128)S(1)} custom-call(bf16[1,4,16,512,256]{4,3,2,1,0:T(8,128)(2,1)S(1)} %copy-done, f32[256,256]{1,0:T(8,128)S(1)} %gram.4.refs_0_), custom_call_target="tpu_custom_call" | custom-call | flops 1073741824 | bytes 12582912 | tf_op jit(solution)/shard_map/gram/pallas_call | solution.py:320
  23.3 1.3 %collective-permute-done.2.refs_3_ = f32[6,16,4,128]{3,2,1,0:T(4,128)S(1)} collective-permute-done((f32[6,16,4,128]{3,2,1,0:T(4,128)S(1)}, f32[6,16,4,128]{3,2,1,0:T(4,128)S(1)}, u32[]{:S(2)}, u32[]{:S(2)}) %collective-permute-start.2) | collective-permute-done | bytes 196640 | tf_op jit(solution)/shard_map/ppermute | solution.py:410
  24.5 2.5 %edges.1 = (f32[6,6,8,128]{3,2,1,0:T(8,128)S(1)}, f32[6,6,8,128]{3,2,1,0:T(8,128)S(1)}) custom-call(f32[6,16,4,128]{3,2,1,0:T(4,128)S(1)} %copy-done.4, f32[6,16,4,128]{3,2,1,0:T(4,128)S(1)} %collective-permute-done.refs_1_, f32[6,16,4,128]{3,2,1,0:T(4,128)S(1)} %collective-permute-done.1.refs_2_, f32[6,16,4,128]{3,2,1,0:T(4,128)S(1)} %collective-permute-done.2.refs_3_, ...), custom_call_target="tpu_custom_call" | custom-call | tf_op jit(solution)/shard_map/edges/pallas_call | solution.py:417
  27.1 0.9 collective-permute-start.6
  28.1 5.8 %copy-done.1 = bf16[1,4,16,512,256]{4,3,2,1,0:T(8,128)(2,1)S(1)} copy-done((bf16[1,4,16,512,256]{4,3,2,1,0:T(8,128)(2,1)S(1)}, bf16[1,4,16,512,256]{4,3,2,1,0:T(8,128)(2,1)}, u32[]{:S(2)}) %copy-start.1) | copy-done | bytes 16777240
  33.9 2.8 %gram.6.refs_0_ = f32[256,256]{1,0:T(8,128)S(1)} custom-call(bf16[1,4,16,512,256]{4,3,2,1,0:T(8,128)(2,1)S(1)} %copy-done.1, f32[256,256]{1,0:T(8,128)S(1)} %gram.5.refs_0_), custom_call_target="tpu_custom_call" | custom-call | flops 1073741824 | bytes 12582912 | tf_op jit(solution)/shard_map/gram/pallas_call | solution.py:320
  36.7 19.7 %steps.1 = (f32[4,4,16,128]{3,2,1,0:T(8,128)}, f32[4,16,8,128]{3,2,1,0:T(8,128)S(1)}, f32[4,16,8,128]{3,2,1,0:T(8,128)S(1)}, f32[4,16,8,128]{3,2,1,0:T(8,128)S(1)}, f32[4,16,8,128]{3,2,1,0:T(8,128)S(1)}) custom-call(s32[8]{0:T(128)S(1)} %copy-done.6, f32[4]{0:T(128)S(1)} %copy-done.7, s32[8,4]{1,0:T(8,128)S(1)} %copy.10.stoich, f32[8,8]{1,0:T(8,128)S(1)} %copy-done.5, ...), custom_call_target="tpu_custom_call" | custom-call | tf_op jit(solution)/shard_map/steps/pallas_call | solution.py:434
  56.5 2.9 %collective-permute-start.9 = (f32[4,16,8,128]{3,2,1,0:T(8,128)S(1)}, f32[4,16,8,128]{3,2,1,0:T(8,128)S(1)}, u32[]{:S(2)}, u32[]{:S(2)}) collective-permute-start(f32[4,16,8,128]{3,2,1,0:T(8,128)S(1)} %get-tuple-element.49), channel_id=1, source_target_pairs={{0,8},{8,0},{16,24},{24,16},{1,9},{9,1},{17,25},{25,17},{2,10},{10... | collective-permute-start | bytes 786440 | tf_op jit(solution)/shard_map/ppermute | solution.py:26
  59.4 0.6 collective-permute-start.8
  60.0 0.9 collective-permute-start.7
  60.8 5.8 %copy-done.2 = bf16[1,4,16,512,256]{4,3,2,1,0:T(8,128)(2,1)S(1)} copy-done((bf16[1,4,16,512,256]{4,3,2,1,0:T(8,128)(2,1)S(1)}, bf16[1,4,16,512,256]{4,3,2,1,0:T(8,128)(2,1)}, u32[]{:S(2)}) %copy-start.2) | copy-done | bytes 16777240
  66.6 1.7 %product.4 = (f32[8,256]{1,0:T(8,128)S(1)}, f32[8,256]{1,0:T(8,128)S(1)}) custom-call(f32[4,16,8,128]{3,2,1,0:T(8,128)S(1)} %get-tuple-element.50.part, bf16[1,4,16,512,256]{4,3,2,1,0:T(8,128)(2,1)S(1)} %copy-done.2), custom_call_target="tpu_custom_call" | custom-call | flops 67108864 | bytes 8388608 | tf_op jit(solution)/shard_map/product/pallas_call | solution.py:369
  68.3 6.5 %copy-done.3 = bf16[1,4,16,512,256]{4,3,2,1,0:T(8,128)(2,1)S(1)} copy-done((bf16[1,4,16,512,256]{4,3,2,1,0:T(8,128)(2,1)S(1)}, bf16[1,4,16,512,256]{4,3,2,1,0:T(8,128)(2,1)}, u32[]{:S(2)}) %copy-start.3) | copy-done | bytes 16777240
  74.8 2.8 %gram.7 = f32[256,256]{1,0:T(8,128)S(1)} custom-call(bf16[1,4,16,512,256]{4,3,2,1,0:T(8,128)(2,1)S(1)} %copy-done.3, f32[256,256]{1,0:T(8,128)S(1)} %gram.6.refs_0_), custom_call_target="tpu_custom_call" | custom-call | flops 1073741824 | bytes 12582912 | tf_op jit(solution)/shard_map/gram/pallas_call | solution.py:320
  77.7 0.5 slice-done.3
  78.2 1.7 %product.5 = (f32[8,256]{1,0:T(8,128)S(1)}, f32[8,256]{1,0:T(8,128)S(1)}) custom-call(f32[4,16,8,128]{3,2,1,0:T(8,128)S(1)} %collective-permute-done.9.part, bf16[1,4,16,512,256]{4,3,2,1,0:T(8,128)(2,1)S(1)} %bitcast.2, f32[8,256]{1,0:T(8,128)S(1)} %get-tuple-element.51.refs_0_, f32[8,256]{1,0:T(8,128)S(1)} %get-tuple-element.52.refs_1_), custom_call_target="tpu_custom_call" | custom-call | flops 67108864 | bytes 8388608 | tf_op jit(solution)/shard_map/product/pallas_call | solution.py:369
  79.9 1.7 %product.6 = (f32[8,256]{1,0:T(8,128)S(1)}, f32[8,256]{1,0:T(8,128)S(1)}) custom-call(f32[4,16,8,128]{3,2,1,0:T(8,128)S(1)} %collective-permute-done.8.part, bf16[1,4,16,512,256]{4,3,2,1,0:T(8,128)(2,1)S(1)} %bitcast.2, f32[8,256]{1,0:T(8,128)S(1)} %get-tuple-element.56.refs_0_, f32[8,256]{1,0:T(8,128)S(1)} %get-tuple-element.57.refs_1_), custom_call_target="tpu_custom_call" | custom-call | flops 67108864 | bytes 8388608 | tf_op jit(solution)/shard_map/product/pallas_call | solution.py:369
  81.6 1.7 %product.7 = (f32[8,256]{1,0:T(8,128)S(1)}, f32[8,256]{1,0:T(8,128)S(1)}) custom-call(f32[4,16,8,128]{3,2,1,0:T(8,128)S(1)} %collective-permute-done.7.part, bf16[1,4,16,512,256]{4,3,2,1,0:T(8,128)(2,1)S(1)} %bitcast.2, f32[8,256]{1,0:T(8,128)S(1)} %get-tuple-element.58.refs_0_, f32[8,256]{1,0:T(8,128)S(1)} %get-tuple-element.59.refs_1_), custom_call_target="tpu_custom_call" | custom-call | flops 67108864 | bytes 8388608 | tf_op jit(solution)/shard_map/product/pallas_call | solution.py:369
  83.3 0.9 collective-permute-start.12
  84.3 1.5 %collective-permute-start.11 = (f32[8,256]{1,0:T(8,128)S(1)}, f32[8,256]{1,0:T(8,128)S(1)}, u32[]{:S(2)}, u32[]{:S(2)}) collective-permute-start(f32[8,256]{1,0:T(8,128)S(1)} %get-tuple-element.60), channel_id=1, source_target_pairs={{0,16},{8,24},{16,0},{24,8},{1,17},{9,25},{17,1},{25,9},{2,18},{10... | collective-permute-start | bytes 24584 | tf_op jit(solution)/shard_map/ppermute | solution.py:26
  85.7 0.7 collective-permute-done.12
  86.5 1.5 %collective-permute-done.11 = f32[8,256]{1,0:T(8,128)S(1)} collective-permute-done((f32[8,256]{1,0:T(8,128)S(1)}, f32[8,256]{1,0:T(8,128)S(1)}, u32[]{:S(2)}, u32[]{:S(2)}) %collective-permute-start.11) | collective-permute-done | bytes 8224 | tf_op jit(solution)/shard_map/ppermute | solution.py:26
  87.9 0.6 collective-permute-start.13
  88.5 3.1 %collective-permute-done.13 = f32[8,256]{1,0:T(8,128)S(1)} collective-permute-done((f32[8,256]{1,0:T(8,128)S(1)}, f32[8,256]{1,0:T(8,128)S(1)}, u32[]{:S(2)}, u32[]{:S(2)}) %collective-permute-start.13) | collective-permute-done | bytes 8224 | tf_op jit(solution)/shard_map/ppermute | solution.py:26
  91.7 2.4 %collective-permute-start.16 = (f32[8,256]{1,0:T(8,128)S(1)}, f32[8,256]{1,0:T(8,128)S(1)}, u32[]{:S(2)}, u32[]{:S(2)}) collective-permute-start(f32[8,256]{1,0:T(8,128)S(1)} %add.51), channel_id=1, source_target_pairs={{0,3},{1,2},{2,1},{3,0},{4,7},{5,6},{6,5},{7,4},{8,11},{9,10},{10,... | collective-permute-start | bytes 24584 | tf_op jit(solution)/shard_map/ppermute | solution.py:26
  94.1 4.3 %collective-permute-start.15 = (f32[8,256]{1,0:T(8,128)S(1)}, f32[8,256]{1,0:T(8,128)S(1)}, u32[]{:S(2)}, u32[]{:S(2)}) collective-permute-start(f32[8,256]{1,0:T(8,128)S(1)} %add.51), channel_id=1, source_target_pairs={{0,2},{1,3},{2,0},{3,1},{4,6},{5,7},{6,4},{7,5},{8,10},{9,11},{10,... | collective-permute-start | bytes 24584 | tf_op jit(solution)/shard_map/ppermute | solution.py:26
  98.5 1.6 %collective-permute-done.15 = f32[8,256]{1,0:T(8,128)S(1)} collective-permute-done((f32[8,256]{1,0:T(8,128)S(1)}, f32[8,256]{1,0:T(8,128)S(1)}, u32[]{:S(2)}, u32[]{:S(2)}) %collective-permute-start.15) | collective-permute-done | bytes 8224 | tf_op jit(solution)/shard_map/ppermute | solution.py:26
  100.1 1.9 %collective-permute-done.14 = f32[8,256]{1,0:T(8,128)S(1)} collective-permute-done((f32[8,256]{1,0:T(8,128)S(1)}, f32[8,256]{1,0:T(8,128)S(1)}, u32[]{:S(2)}, u32[]{:S(2)}) %collective-permute-start.14) | collective-permute-done | bytes 8224 | tf_op jit(solution)/shard_map/ppermute | solution.py:26
  102.1 0.2 add_subtract_fusion
  102.3 1.5 %collective-permute-start.18 = (f32[8,256]{1,0:T(8,128)S(1)}, f32[8,256]{1,0:T(8,128)S(1)}, u32[]{:S(2)}, u32[]{:S(2)}) collective-permute-start(f32[8,256]{1,0:T(8,128)S(1)} %add_subtract_fusion), channel_id=1, source_target_pairs={{0,16},{8,24},{16,0},{24,8},{1,17},{9,25},{17,1},{25,9},{2,18},{10... | collective-permute-start | bytes 24584 | tf_op jit(solution)/shard_map/ppermute | solution.py:26
  103.8 0.3 collective-permute-start.17
  104.1 1.3 %collective-permute-done.19 = f32[8,256]{1,0:T(8,128)S(1)} collective-permute-done((f32[8,256]{1,0:T(8,128)S(1)}, f32[8,256]{1,0:T(8,128)S(1)}, u32[]{:S(2)}, u32[]{:S(2)}) %collective-permute-start.19) | collective-permute-done | bytes 8224 | tf_op jit(solution)/shard_map/ppermute | solution.py:26
  105.4 0.6 collective-permute-done.18
  106.0 0.6 collective-permute-start.20
  106.6 3.1 %collective-permute-done.20 = f32[8,256]{1,0:T(8,128)S(1)} collective-permute-done((f32[8,256]{1,0:T(8,128)S(1)}, f32[8,256]{1,0:T(8,128)S(1)}, u32[]{:S(2)}, u32[]{:S(2)}) %collective-permute-start.20) | collective-permute-done | bytes 8224 | tf_op jit(solution)/shard_map/ppermute | solution.py:26
  109.7 2.5 %collective-permute-start.23 = (f32[8,256]{1,0:T(8,128)S(1)}, f32[8,256]{1,0:T(8,128)S(1)}, u32[]{:S(2)}, u32[]{:S(2)}) collective-permute-start(f32[8,256]{1,0:T(8,128)S(1)} %add.59), channel_id=1, source_target_pairs={{0,3},{1,2},{2,1},{3,0},{4,7},{5,6},{6,5},{7,4},{8,11},{9,10},{10,... | collective-permute-start | bytes 24584 | tf_op jit(solution)/shard_map/ppermute | solution.py:26
  112.2 1.9 %collective-permute-start.21 = (f32[8,256]{1,0:T(8,128)S(1)}, f32[8,256]{1,0:T(8,128)S(1)}, u32[]{:S(2)}, u32[]{:S(2)}) collective-permute-start(f32[8,256]{1,0:T(8,128)S(1)} %add.59), channel_id=1, source_target_pairs={{0,1},{1,0},{2,3},{3,2},{4,5},{5,4},{6,7},{7,6},{8,9},{9,8},{10,11... | collective-permute-start | bytes 24584 | tf_op jit(solution)/shard_map/ppermute | solution.py:26
  114.1 1.1 collective-permute-done.23
  115.2 1.6 %collective-permute-done.22 = f32[8,256]{1,0:T(8,128)S(1)} collective-permute-done((f32[8,256]{1,0:T(8,128)S(1)}, f32[8,256]{1,0:T(8,128)S(1)}, u32[]{:S(2)}, u32[]{:S(2)}) %collective-permute-start.22) | collective-permute-done | bytes 8224 | tf_op jit(solution)/shard_map/ppermute | solution.py:26
  116.8 0.6 add_add_fusion
  (46 shorter events, 0.4 us)
Async XLA Ops:
  0.6 27.4 %copy-start.8 = (s32[8,4]{0,1:T(4,128)S(1)}, s32[8,4]{0,1:T(4,128)}, u32[]{:S(2)}) copy-start(s32[8,4]{0,1:T(4,128)} %param.13) | copy-start | bytes 388
  2.4 15.6 %collective-permute-start = (f32[6,16,4,128]{3,2,1,0:T(4,128)}, f32[6,16,4,128]{3,2,1,0:T(4,128)S(1)}, u32[]{:S(2)}, u32[]{:S(2)}) collective-permute-start(f32[6,16,4,128]{3,2,1,0:T(4,128)} %pack.1.refs_0_), channel_id=1, source_target_pairs={{0,4},{4,0},{1,5},{5,1},{2,6},{6,2},{3,7},{7,3},{8,12},{12,8},{9,1... | collective-permute-start | bytes 589832 | tf_op jit(solution)/shard_map/ppermute | solution.py:404
  5.3 17.9 %collective-permute-start.3 = (f32[6,16,4,128]{3,2,1,0:T(4,128)}, f32[6,16,4,128]{3,2,1,0:T(4,128)S(1)}, u32[]{:S(2)}, u32[]{:S(2)}) collective-permute-start(f32[6,16,4,128]{3,2,1,0:T(4,128)} %pack.1.refs_0_), channel_id=1, source_target_pairs={{1,2},{2,1},{5,6},{6,5},{9,10},{10,9},{13,14},{14,13},{17,18},{18,... | collective-permute-start | bytes 589832 | tf_op jit(solution)/shard_map/ppermute | solution.py:407
  6.0 17.3 %collective-permute-start.1 = (f32[6,16,4,128]{3,2,1,0:T(4,128)}, f32[6,16,4,128]{3,2,1,0:T(4,128)S(1)}, u32[]{:S(2)}, u32[]{:S(2)}) collective-permute-start(f32[6,16,4,128]{3,2,1,0:T(4,128)} %pack.1.refs_0_), channel_id=1, source_target_pairs={{0,1},{2,3},{1,0},{3,2},{4,5},{6,7},{5,4},{7,6},{8,9},{10,11},{9,8... | collective-permute-start | bytes 589832 | tf_op jit(solution)/shard_map/ppermute | solution.py:406
  10.4 5.8 %copy-start = (bf16[1,4,16,512,256]{4,3,2,1,0:T(8,128)(2,1)S(1)}, bf16[1,4,16,512,256]{4,3,2,1,0:T(8,128)(2,1)}, u32[]{:S(2)}) copy-start(bf16[1,4,16,512,256]{4,3,2,1,0:T(8,128)(2,1)} %basis.15) | copy-start | bytes 50331652
  16.2 8.3 %copy-start.4 = (f32[6,16,4,128]{3,2,1,0:T(4,128)S(1)}, f32[6,16,4,128]{3,2,1,0:T(4,128)}, u32[]{:S(2)}) copy-start(f32[6,16,4,128]{3,2,1,0:T(4,128)} %pack.1.refs_0_) | copy-start | bytes 589828
  17.9 18.8 %copy-start.5 = (f32[8,8]{1,0:T(8,128)S(1)}, f32[8,8]{1,0:T(8,128)}, u32[]{:S(2)}) copy-start(f32[8,8]{1,0:T(8,128)} %rates.1) | copy-start | bytes 772
  17.9 18.8 %copy-start.6 = (s32[8]{0:T(128)S(1)}, s32[8]{0:T(128)}, u32[]{:S(2)}) copy-start(s32[8]{0:T(128)} %plan.1) | copy-start | bytes 100
  18.0 18.8 %copy-start.7 = (f32[4]{0:T(128)S(1)}, f32[4]{0:T(128)}, u32[]{:S(2)}) copy-start(f32[4]{0:T(128)} %diffusion.1) | copy-start | bytes 52
  18.0 5.3 %collective-permute-start.4 = (f32[6,16,4,128]{3,2,1,0:T(4,128)S(1)}, f32[6,16,4,128]{3,2,1,0:T(4,128)S(1)}, u32[]{:S(2)}, u32[]{:S(2)}) collective-permute-start(f32[6,16,4,128]{3,2,1,0:T(4,128)S(1)} %collective-permute-done.refs_1_), channel_id=1, source_target_pairs={{1,2},{2,1},{5,6},{6,5},{9,10},{10,9},{13,14},{14,13},{17,18},{18,... | collective-permute-start | bytes 589832 | tf_op jit(solution)/shard_map/ppermute | solution.py:411
  18.7 5.9 %collective-permute-start.2 = (f32[6,16,4,128]{3,2,1,0:T(4,128)S(1)}, f32[6,16,4,128]{3,2,1,0:T(4,128)S(1)}, u32[]{:S(2)}, u32[]{:S(2)}) collective-permute-start(f32[6,16,4,128]{3,2,1,0:T(4,128)S(1)} %collective-permute-done.refs_1_), channel_id=1, source_target_pairs={{0,1},{2,3},{1,0},{3,2},{4,5},{6,7},{5,4},{7,6},{8,9},{10,11},{9,8... | collective-permute-start | bytes 589832 | tf_op jit(solution)/shard_map/ppermute | solution.py:410
  27.1 9.6 %collective-permute-start.5 = (f32[6,6,8,128]{3,2,1,0:T(8,128)S(1)}, f32[6,6,8,128]{3,2,1,0:T(8,128)S(1)}, u32[]{:S(2)}, u32[]{:S(2)}) collective-permute-start(f32[6,6,8,128]{3,2,1,0:T(8,128)S(1)} %get-tuple-element.42), channel_id=1, source_target_pairs={{0,8},{16,24},{8,0},{24,16},{1,9},{17,25},{9,1},{25,17},{2,10},{18... | collective-permute-start | bytes 442376 | tf_op jit(solution)/shard_map/ppermute | solution.py:426
  27.1 9.6 %collective-permute-start.6 = (f32[6,6,8,128]{3,2,1,0:T(8,128)S(1)}, f32[6,6,8,128]{3,2,1,0:T(8,128)S(1)}, u32[]{:S(2)}, u32[]{:S(2)}) collective-permute-start(f32[6,6,8,128]{3,2,1,0:T(8,128)S(1)} %get-tuple-element.43), channel_id=1, source_target_pairs={{8,16},{16,8},{9,17},{17,9},{10,18},{18,10},{11,19},{19,11},{12,20... | collective-permute-start | bytes 442376 | tf_op jit(solution)/shard_map/ppermute | solution.py:427
  28.1 5.8 %copy-start.1 = (bf16[1,4,16,512,256]{4,3,2,1,0:T(8,128)(2,1)S(1)}, bf16[1,4,16,512,256]{4,3,2,1,0:T(8,128)(2,1)}, u32[]{:S(2)}) copy-start(bf16[1,4,16,512,256]{4,3,2,1,0:T(8,128)(2,1)} %basis.15) | copy-start | bytes 50331652
  56.5 21.2 %collective-permute-start.9 = (f32[4,16,8,128]{3,2,1,0:T(8,128)S(1)}, f32[4,16,8,128]{3,2,1,0:T(8,128)S(1)}, u32[]{:S(2)}, u32[]{:S(2)}) collective-permute-start(f32[4,16,8,128]{3,2,1,0:T(8,128)S(1)} %get-tuple-element.49), channel_id=1, source_target_pairs={{0,8},{8,0},{16,24},{24,16},{1,9},{9,1},{17,25},{25,17},{2,10},{10... | collective-permute-start | bytes 786440 | tf_op jit(solution)/shard_map/ppermute | solution.py:26
  59.4 20.5 %collective-permute-start.8 = (f32[4,16,8,128]{3,2,1,0:T(8,128)S(1)}, f32[4,16,8,128]{3,2,1,0:T(8,128)S(1)}, u32[]{:S(2)}, u32[]{:S(2)}) collective-permute-start(f32[4,16,8,128]{3,2,1,0:T(8,128)S(1)} %get-tuple-element.48), channel_id=1, source_target_pairs={{0,16},{8,24},{16,0},{24,8},{1,17},{9,25},{17,1},{25,9},{2,18},{10... | collective-permute-start | bytes 786440 | tf_op jit(solution)/shard_map/ppermute | solution.py:26
  60.0 21.6 %collective-permute-start.7 = (f32[4,16,8,128]{3,2,1,0:T(8,128)S(1)}, f32[4,16,8,128]{3,2,1,0:T(8,128)S(1)}, u32[]{:S(2)}, u32[]{:S(2)}) collective-permute-start(f32[4,16,8,128]{3,2,1,0:T(8,128)S(1)} %get-tuple-element.47), channel_id=1, source_target_pairs={{0,24},{8,16},{16,8},{24,0},{1,25},{9,17},{17,9},{25,1},{2,26},{10... | collective-permute-start | bytes 786440 | tf_op jit(solution)/shard_map/ppermute | solution.py:26
  60.8 5.8 %copy-start.2 = (bf16[1,4,16,512,256]{4,3,2,1,0:T(8,128)(2,1)S(1)}, bf16[1,4,16,512,256]{4,3,2,1,0:T(8,128)(2,1)}, u32[]{:S(2)}) copy-start(bf16[1,4,16,512,256]{4,3,2,1,0:T(8,128)(2,1)} %basis.15) | copy-start | bytes 50331652
  66.6 11.0 %slice-start = ((s8[16777216]{0:T(1024)(128)(4,1)}), s8[4194304]{0:T(1024)(128)(4,1)S(1)}, s32[]{:S(2)}) async-start(s8[16777216]{0:T(1024)(128)(4,1)} %bitcast.1), calls=%async_computation | async-start | bytes 8388608
  66.6 11.1 %slice-start.1 = ((s8[16777216]{0:T(1024)(128)(4,1)}), s8[4194304]{0:T(1024)(128)(4,1)S(1)}, s32[]{:S(2)}) async-start(s8[16777216]{0:T(1024)(128)(4,1)} %bitcast.1), calls=%async_computation.1 | async-start | bytes 8388608
  68.3 6.5 %copy-start.3 = (bf16[1,4,16,512,256]{4,3,2,1,0:T(8,128)(2,1)S(1)}, bf16[1,4,16,512,256]{4,3,2,1,0:T(8,128)(2,1)}, u32[]{:S(2)}) copy-start(bf16[1,4,16,512,256]{4,3,2,1,0:T(8,128)(2,1)} %basis.15) | copy-start | bytes 50331652
  74.8 2.9 %slice-start.2 = ((s8[16777216]{0:T(1024)(128)(4,1)}), s8[4194304]{0:T(1024)(128)(4,1)S(1)}, s32[]{:S(2)}) async-start(s8[16777216]{0:T(1024)(128)(4,1)} %bitcast.1), calls=%async_computation.2 | async-start | bytes 8388608
  74.8 3.4 %slice-start.3 = ((s8[16777216]{0:T(1024)(128)(4,1)}), s8[4194304]{0:T(1024)(128)(4,1)S(1)}, s32[]{:S(2)}) async-start(s8[16777216]{0:T(1024)(128)(4,1)} %bitcast.1), calls=%async_computation.3 | async-start | bytes 8388608
  83.3 3.1 %collective-permute-start.12 = (f32[8,256]{1,0:T(8,128)S(1)}, f32[8,256]{1,0:T(8,128)S(1)}, u32[]{:S(2)}, u32[]{:S(2)}) collective-permute-start(f32[8,256]{1,0:T(8,128)S(1)} %get-tuple-element.60), channel_id=1, source_target_pairs={{0,24},{8,16},{16,8},{24,0},{1,25},{9,17},{17,9},{25,1},{2,26},{10... | collective-permute-start | bytes 24584 | tf_op jit(solution)/shard_map/ppermute | solution.py:26
  84.3 3.7 %collective-permute-start.11 = (f32[8,256]{1,0:T(8,128)S(1)}, f32[8,256]{1,0:T(8,128)S(1)}, u32[]{:S(2)}, u32[]{:S(2)}) collective-permute-start(f32[8,256]{1,0:T(8,128)S(1)} %get-tuple-element.60), channel_id=1, source_target_pairs={{0,16},{8,24},{16,0},{24,8},{1,17},{9,25},{17,1},{25,9},{2,18},{10... | collective-permute-start | bytes 24584 | tf_op jit(solution)/shard_map/ppermute | solution.py:26
  85.7 2.2 %collective-permute-start.10 = (f32[8,256]{1,0:T(8,128)S(1)}, f32[8,256]{1,0:T(8,128)S(1)}, u32[]{:S(2)}, u32[]{:S(2)}) collective-permute-start(f32[8,256]{1,0:T(8,128)S(1)} %get-tuple-element.60), channel_id=1, source_target_pairs={{0,8},{8,0},{16,24},{24,16},{1,9},{9,1},{17,25},{25,17},{2,10},{10... | collective-permute-start | bytes 24584 | tf_op jit(solution)/shard_map/ppermute | solution.py:26
  87.9 3.7 %collective-permute-start.13 = (f32[8,256]{1,0:T(8,128)S(1)}, f32[8,256]{1,0:T(8,128)S(1)}, u32[]{:S(2)}, u32[]{:S(2)}) collective-permute-start(f32[8,256]{1,0:T(8,128)S(1)} %add_add_fusion.3), channel_id=1, source_target_pairs={{0,4},{4,0},{1,5},{5,1},{2,6},{6,2},{3,7},{7,3},{8,12},{12,8},{9,1... | collective-permute-start | bytes 24584 | tf_op jit(solution)/shard_map/ppermute | solution.py:26
  91.7 6.9 %collective-permute-start.16 = (f32[8,256]{1,0:T(8,128)S(1)}, f32[8,256]{1,0:T(8,128)S(1)}, u32[]{:S(2)}, u32[]{:S(2)}) collective-permute-start(f32[8,256]{1,0:T(8,128)S(1)} %add.51), channel_id=1, source_target_pairs={{0,3},{1,2},{2,1},{3,0},{4,7},{5,6},{6,5},{7,4},{8,11},{9,10},{10,... | collective-permute-start | bytes 24584 | tf_op jit(solution)/shard_map/ppermute | solution.py:26
  94.1 6.0 %collective-permute-start.15 = (f32[8,256]{1,0:T(8,128)S(1)}, f32[8,256]{1,0:T(8,128)S(1)}, u32[]{:S(2)}, u32[]{:S(2)}) collective-permute-start(f32[8,256]{1,0:T(8,128)S(1)} %add.51), channel_id=1, source_target_pairs={{0,2},{1,3},{2,0},{3,1},{4,6},{5,7},{6,4},{7,5},{8,10},{9,11},{10,... | collective-permute-start | bytes 24584 | tf_op jit(solution)/shard_map/ppermute | solution.py:26
  98.4 3.7 %collective-permute-start.14 = (f32[8,256]{1,0:T(8,128)S(1)}, f32[8,256]{1,0:T(8,128)S(1)}, u32[]{:S(2)}, u32[]{:S(2)}) collective-permute-start(f32[8,256]{1,0:T(8,128)S(1)} %add.51), channel_id=1, source_target_pairs={{0,1},{1,0},{2,3},{3,2},{4,5},{5,4},{6,7},{7,6},{8,9},{9,8},{10,11... | collective-permute-start | bytes 24584 | tf_op jit(solution)/shard_map/ppermute | solution.py:26
  102.3 3.2 %collective-permute-start.19 = (f32[8,256]{1,0:T(8,128)S(1)}, f32[8,256]{1,0:T(8,128)S(1)}, u32[]{:S(2)}, u32[]{:S(2)}) collective-permute-start(f32[8,256]{1,0:T(8,128)S(1)} %add_subtract_fusion), channel_id=1, source_target_pairs={{0,24},{8,16},{16,8},{24,0},{1,25},{9,17},{17,9},{25,1},{2,26},{10... | collective-permute-start | bytes 24584 | tf_op jit(solution)/shard_map/ppermute | solution.py:26
  102.3 3.7 %collective-permute-start.18 = (f32[8,256]{1,0:T(8,128)S(1)}, f32[8,256]{1,0:T(8,128)S(1)}, u32[]{:S(2)}, u32[]{:S(2)}) collective-permute-start(f32[8,256]{1,0:T(8,128)S(1)} %add_subtract_fusion), channel_id=1, source_target_pairs={{0,16},{8,24},{16,0},{24,8},{1,17},{9,25},{17,1},{25,9},{2,18},{10... | collective-permute-start | bytes 24584 | tf_op jit(solution)/shard_map/ppermute | solution.py:26
  103.8 2.2 %collective-permute-start.17 = (f32[8,256]{1,0:T(8,128)S(1)}, f32[8,256]{1,0:T(8,128)S(1)}, u32[]{:S(2)}, u32[]{:S(2)}) collective-permute-start(f32[8,256]{1,0:T(8,128)S(1)} %add_subtract_fusion), channel_id=1, source_target_pairs={{0,8},{8,0},{16,24},{24,16},{1,9},{9,1},{17,25},{25,17},{2,10},{10... | collective-permute-start | bytes 24584 | tf_op jit(solution)/shard_map/ppermute | solution.py:26
  106.0 3.7 %collective-permute-start.20 = (f32[8,256]{1,0:T(8,128)S(1)}, f32[8,256]{1,0:T(8,128)S(1)}, u32[]{:S(2)}, u32[]{:S(2)}) collective-permute-start(f32[8,256]{1,0:T(8,128)S(1)} %add_add_fusion.1), channel_id=1, source_target_pairs={{0,4},{4,0},{1,5},{5,1},{2,6},{6,2},{3,7},{7,3},{8,12},{12,8},{9,1... | collective-permute-start | bytes 24584 | tf_op jit(solution)/shard_map/ppermute | solution.py:26
  109.7 5.4 %collective-permute-start.23 = (f32[8,256]{1,0:T(8,128)S(1)}, f32[8,256]{1,0:T(8,128)S(1)}, u32[]{:S(2)}, u32[]{:S(2)}) collective-permute-start(f32[8,256]{1,0:T(8,128)S(1)} %add.59), channel_id=1, source_target_pairs={{0,3},{1,2},{2,1},{3,0},{4,7},{5,6},{6,5},{7,4},{8,11},{9,10},{10,... | collective-permute-start | bytes 24584 | tf_op jit(solution)/shard_map/ppermute | solution.py:26
  112.2 4.5 %collective-permute-start.22 = (f32[8,256]{1,0:T(8,128)S(1)}, f32[8,256]{1,0:T(8,128)S(1)}, u32[]{:S(2)}, u32[]{:S(2)}) collective-permute-start(f32[8,256]{1,0:T(8,128)S(1)} %add.59), channel_id=1, source_target_pairs={{0,2},{1,3},{2,0},{3,1},{4,6},{5,7},{6,4},{7,5},{8,10},{9,11},{10,... | collective-permute-start | bytes 24584 | tf_op jit(solution)/shard_map/ppermute | solution.py:26
  112.2 4.5 %collective-permute-start.21 = (f32[8,256]{1,0:T(8,128)S(1)}, f32[8,256]{1,0:T(8,128)S(1)}, u32[]{:S(2)}, u32[]{:S(2)}) collective-permute-start(f32[8,256]{1,0:T(8,128)S(1)} %add.59), channel_id=1, source_target_pairs={{0,1},{1,0},{2,3},{3,2},{4,5},{5,4},{6,7},{7,6},{8,9},{9,8},{10,11... | collective-permute-start | bytes 24584 | tf_op jit(solution)/shard_map/ppermute | solution.py:26

commit v4 on v3

--- a/solution.py
+++ b/solution.py
@@ -13,6 +13,7 @@
 GROUPS = LANES // STEPS
 BLOCK = 8
 MIB = 1024 * 1024
+BASIS_VMEM = 50 * MIB
 
 
 def pairs(axis, first):
@@ -294,22 +295,25 @@
     lax.fori_loop(0, spec, leave, 0)
 
 
-def gram_kernel(x, basis, *refs):
-    (out, chunks, sems), total = refs[-3:], refs[:-3]
+def gram_kernel(x, given, basis, *refs):
+    total, (out, chunks, held, sems) = refs[:given], refs[given:]
     count, rows, cells_z, modes = chunks.shape
     copies = fetch(
-        [basis.at[0, x, pl.ds(i * rows, rows)] for i in range(count)],
-        [chunks.at[i] for i in range(count)],
+        [basis.at[0, x, pl.ds(i * rows, rows)] for i in range(count)] + list(total),
+        [chunks.at[i] for i in range(count)] + [held],
         sems,
     )
-    acc = total[0][...] if total else None
-    for i, copy in enumerate(copies):
-        copy.wait()
+    acc = None
+    for i in range(count):
+        copies[i].wait()
         chunk = chunks[i].reshape(rows * cells_z, modes)
         part = lax.dot_general(
             chunk, chunk, (((0,), (0,)), ((), ())), preferred_element_type=jnp.float32
         )
         acc = part if acc is None else acc + part
+    if total:
+        copies[-1].wait()
+        acc = acc + held[...]
     out[...] = acc
 
 
@@ -318,15 +322,16 @@
     chunks = 2
     size = 2 * cells_y * cells_z * modes
     return pl.pallas_call(
-        functools.partial(gram_kernel, x),
+        functools.partial(gram_kernel, x, len(total)),
         out_shape=jax.ShapeDtypeStruct((modes, modes), jnp.float32),
-        in_specs=anywhere(1) + whole(len(total)),
+        in_specs=anywhere(1 + len(total)),
         out_specs=whole(1)[0],
         scratch_shapes=[
             pltpu.VMEM((chunks, cells_y // chunks, cells_z, modes), jnp.bfloat16),
-            pltpu.SemaphoreType.DMA((chunks,)),
+            pltpu.VMEM((modes, modes), jnp.float32),
+            pltpu.SemaphoreType.DMA((chunks + 1,)),
         ],
-        compiler_params=pltpu.CompilerParams(vmem_limit_bytes=2 * size + 8 * MIB),
+        compiler_params=pltpu.CompilerParams(vmem_limit_bytes=BASIS_VMEM),
         cost_estimate=pl.CostEstimate(
             flops=2 * cells_y * cells_z * modes * modes, bytes_accessed=3 * size, transcendentals=0
         ),
@@ -334,34 +339,109 @@
     )(basis, *total)
 
 
-def product_kernel(flips, part, basis, *refs):
-    (out_high, out_low, held, rows, sems), total = refs[-5:], refs[:-5]
+def rows_of(basis, flips, cells_z):
+    zone = (lax.axis_index("grp") ^ flips) * cells_z
+    return [
+        basis.at[0, x, :, pl.ds(pl.multiple_of(zone, LANES), cells_z)]
+        for x in range(basis.shape[1])
+    ]
+
+
+def multiply(held, rows, waits, acc):
     cells_x, cells_y, snaps, cells_z = held.shape
-    zone = (lax.axis_index("grp") ^ flips) * cells_z
-    copies = fetch(
-        [part] + [basis.at[0, x, :, pl.ds(pl.multiple_of(zone, LANES), cells_z)] for x in range(cells_x)],
-        [held] + [rows.at[x] for x in range(cells_x)],
-        sems,
-    )
-    copies[0].wait()
-    acc = jnp.concatenate([total[0][...], total[1][...]], axis=0) if total else None
     for x in range(cells_x):
         values = held[x]
         high = values.astype(jnp.bfloat16).astype(jnp.float32)
         left = jnp.concatenate([high, values - high], axis=1).astype(jnp.bfloat16)
-        copies[1 + x].wait()
+        waits[x].wait()
         for y in range(0, cells_y, 2):
             more = jnp.dot(
                 jnp.concatenate([left[y], left[y + 1]], axis=1),
-                rows[x, y : y + 2].reshape(2 * cells_z, basis.shape[-1]),
+                rows[x, y : y + 2].reshape(2 * cells_z, rows.shape[-1]),
                 preferred_element_type=jnp.float32,
             )
             acc = more if acc is None else acc + more
+    return acc
+
+
+def first_kernel(later, gram_x, part, basis, gram, *refs):
+    out_high, out_low, out_gram, *ahead = refs[: 3 + len(later)]
+    held, rows, chunks, total, sems = refs[3 + len(later) :]
+    cells_x, cells_y, snaps, cells_z = held.shape
+    modes = rows.shape[-1]
+    sources = [part, *rows_of(basis, 0, cells_z)]
+    targets = [held, *(rows.at[x] for x in range(cells_x))]
+    sources += [basis.at[0, x] for x in gram_x] + [gram]
+    targets += [chunks.at[i] for i in range(len(gram_x))] + [total]
+    start_gram = 1 + cells_x
+    for i, flips in enumerate(later):
+        sources += rows_of(basis, flips, cells_z)
+        targets += [ahead[i].at[x] for x in range(cells_x)]
+    copies = fetch(sources, targets, sems)
+    copies[0].wait()
+    acc = multiply(held, rows, copies[1:], None)
     out_high[...] = acc[:snaps]
     out_low[...] = acc[snaps:]
-
-
-def product(flips, part, basis, *total):
+    acc = None
+    for i in range(len(gram_x)):
+        copies[start_gram + i].wait()
+        chunk = chunks[i].reshape(-1, modes)
+        more = lax.dot_general(
+            chunk, chunk, (((0,), (0,)), ((), ())), preferred_element_type=jnp.float32
+        )
+        acc = more if acc is None else acc + more
+    for copy in copies[start_gram + len(gram_x) :]:
+        copy.wait()
+    out_gram[...] = total[...] if acc is None else acc + total[...]
+
+
+def product_kernel(flips, part, basis, high, low, out_high, out_low, held, rows, sums, sems):
+    cells_x, cells_y, snaps, cells_z = held.shape
+    if flips is None:
+        sources = [basis.at[x] for x in range(cells_x)]
+    else:
+        sources = rows_of(basis, flips, cells_z)
+    copies = fetch(
+        [part, *sources, high, low],
+        [held, *(rows.at[x] for x in range(cells_x)), sums.at[0], sums.at[1]],
+        sems,
+    )
+    copies[0].wait()
+    acc = multiply(held, rows, copies[1:], None)
+    copies[-2].wait()
+    copies[-1].wait()
+    out_high[...] = acc[:snaps] + sums[0]
+    out_low[...] = acc[snaps:] + sums[1]
+
+
+def first_product(part, basis, gram, later, gram_x):
+    cells_x, cells_y, snaps, cells_z = part.shape
+    modes = basis.shape[-1]
+    size = 2 * cells_x * cells_y * cells_z * modes
+    out = jax.ShapeDtypeStruct((snaps, modes), jnp.float32)
+    rows = (cells_x, cells_y, cells_z, modes)
+    return pl.pallas_call(
+        functools.partial(first_kernel, later, gram_x),
+        out_shape=[out, out, jax.ShapeDtypeStruct(gram.shape, jnp.float32)]
+        + [jax.ShapeDtypeStruct(rows, jnp.bfloat16)] * len(later),
+        in_specs=anywhere(3),
+        out_specs=whole(3) + anywhere(len(later)),
+        scratch_shapes=[
+            pltpu.VMEM(part.shape, jnp.float32),
+            pltpu.VMEM(rows, jnp.bfloat16),
+            pltpu.VMEM((max(len(gram_x), 1), *basis.shape[2:]), jnp.bfloat16),
+            pltpu.VMEM(gram.shape, jnp.float32),
+            pltpu.SemaphoreType.DMA((2 + cells_x * (1 + len(later)) + len(gram_x),)),
+        ],
+        compiler_params=pltpu.CompilerParams(vmem_limit_bytes=BASIS_VMEM),
+        cost_estimate=pl.CostEstimate(
+            flops=2 * snaps * size, bytes_accessed=4 * size, transcendentals=0
+        ),
+        name="first_product",
+    )(part, basis, gram)
+
+
+def product(flips, part, basis, high, low):
     cells_x, cells_y, snaps, cells_z = part.shape
     modes = basis.shape[-1]
     size = 2 * cells_x * cells_y * cells_z * modes
@@ -369,19 +449,20 @@
     return pl.pallas_call(
         functools.partial(product_kernel, flips),
         out_shape=(out, out),
-        in_specs=anywhere(2) + whole(len(total)),
+        in_specs=anywhere(4),
         out_specs=tuple(whole(2)),
         scratch_shapes=[
             pltpu.VMEM(part.shape, jnp.float32),
             pltpu.VMEM((cells_x, cells_y, cells_z, modes), jnp.bfloat16),
-            pltpu.SemaphoreType.DMA((cells_x + 1,)),
+            pltpu.VMEM((2, snaps, modes), jnp.float32),
+            pltpu.SemaphoreType.DMA((cells_x + 3,)),
         ],
-        compiler_params=pltpu.CompilerParams(vmem_limit_bytes=size + 8 * MIB),
+        compiler_params=pltpu.CompilerParams(vmem_limit_bytes=BASIS_VMEM),
         cost_estimate=pl.CostEstimate(
             flops=2 * snaps * size, bytes_accessed=2 * size, transcendentals=0
         ),
         name="product",
-    )(part, basis, *total)
+    )(part, basis, high, low)
 
 
 def body(terminal, diffusion, velocity, material, rates, stoich, plan, basis):
@@ -389,7 +470,7 @@
     snaps, modes = plan.shape[0], basis.shape[-1]
     count_grp, count_x = lax.axis_size("grp"), lax.axis_size("gx")
     fields, all_x = spec + 2, cells_x * count_x
-    wide, rows = cells_z + LANES, 3 * cells_y + 2 * BLOCK
+    wide, depth = cells_z + LANES, 3 * cells_y + 2 * BLOCK
 
     own = pl.pallas_call(
         pack_kernel,
@@ -429,7 +510,7 @@
     side_a, side_b, gram = lax.optimization_barrier((side_a, side_b, gram))
 
     part = jax.ShapeDtypeStruct((cells_x, cells_y, snaps, cells_z), jnp.float32)
-    room = (rows, all_x, wide)
+    room = (depth, all_x, wide)
     shapes = [(spec, *room), (spec, *room), (spec * spec, *room), room, held, (2, *packed.shape)]
     final, *kept = pl.pallas_call(
         functools.partial(steps_kernel, count_x),
@@ -444,15 +525,14 @@
 
     order = sorted(range(1, count_grp), key=lambda flips: -flips)
     moved = {flips: exchange(kept[flips], "grp", flips) for flips in order}
-    moved[0] = kept[0]
-    total = ()
-    for flips in range(count_grp):
-        total = product(flips, moved[flips], basis, *total)
-        if flips == min(1, count_grp - 1):
-            for x in range(3, cells_x):
-                gram = gram_part(x, basis, gram)
-            *total, gram = lax.optimization_barrier((*total, gram))
-    high, low = total
+    later = tuple(range(2, count_grp))
+    high, low, gram, *ahead = first_product(
+        kept[0], basis, gram, later, tuple(range(3, cells_x))
+    )
+    if count_grp > 1:
+        high, low = product(1, moved[1], basis, high, low)
+    for flips, rows in zip(later, ahead):
+        high, low = product(None, moved[flips], rows, high, low)
 
     first = sum_all(high)
     taken = jnp.dot(

time: 118 us -> 352 us (2.98)
  Pallas kernels: 40.9 us -> 300 us
  local copies, waits for them, and re-layouts: 24.5 us -> 0.1 us
    pallas_call x4, Pallas kernels: 10.2 us -> 268 us  [the longest x1 257 us: first_product(): pl.pallas_call(functools.partial(first_kernel, later, gram_x), out_shape=...]
    unnamed x27 -> x11, local copies, waits for them, and re-layouts: 24.5 us -> 0.1 us
    pallas_call x4 -> x3, Pallas kernels: 6.75 us -> 8.04 us  [product(): pl.pallas_call(functools.partial(product_kernel, flips), out_shape=(out,...]
  transfers between devices with their start and end apart: 24 -> 24, of which waited for: 11 -> 11; matrix products, arithmetic and copies ran while one was open for 0% -> 0% of each run, Pallas kernels for 13% -> 78%
where the time goes in v4:
time: 352 us; the launch traced here: 351 us
  Pallas kernels  300 us (85%)
  starting transfers between devices  32.7 us (9%)
  waiting for transfers between devices  16.9 us (5%)
    pallas_call x1, Pallas kernels, first_product(): pl.pallas_call(functools.partial(first_kernel, later, gram_x), out_shape=...  257 us
    ppermute x17, starting transfers between devices, exchange(): return lax.ppermute(value, axis, [(i, i ^ flips) for i in range(count)])  21.1 us
    pallas_call x1, Pallas kernels, body(): pl.pallas_call(functools.partial(steps_kernel, count_x), out_shape=[jax.S...  19.7 us
    ppermute x17, waiting for transfers between devices, exchange(): return lax.ppermute(value, axis, [(i, i ^ flips) for i in range(count)])  16.4 us
    pallas_call x3, Pallas kernels, gram_part(): pl.pallas_call(functools.partial(gram_kernel, x, len(total)), out_shape=j...  10.7 us
    pallas_call x3, Pallas kernels, product(): pl.pallas_call(functools.partial(product_kernel, flips), out_shape=(out,...  8.04 us
  transfers between devices with their start and end apart: 24, of which 11 were waited for; matrix products, arithmetic and copies ran while one was open for 0% of the time, Pallas kernels for 78%

profile of v4, /device:TPU:0, one launch (start us, length us, event | category | flops | bytes accessed | tf_op | source)
XLA Modules:
  0.0 351.4 jit_solution(16851260363841336566)
XLA Ops:
  0.6 1.7 pack.1.refs_0_
  2.3 2.9 collective-permute-start
  5.3 0.7 collective-permute-start.3
  6.0 4.5 %collective-permute-start.1 = (f32[6,16,4,128]{3,2,1,0:T(4,128)}, f32[6,16,4,128]{3,2,1,0:T(4,128)S(1)}, u32[]{:S(2)}, u32[]{:S(2)}) collective-permute-start(f32[6,16,4,128]{3,2,1,0:T(4,128)} %pack.1.refs_0_), channel_id=1, source_target_pairs={{0,1},{2,3},{1,0},{3,2},{4,5},{6,7},{5,4},{7,6},{8,9},{10,11},{9,8... | collective-permute-start | bytes 589832 | tf_op jit(solution)/shard_map/ppermute | solution.py:487
  10.4 3.5 %gram.3.refs_0_ = f32[256,256]{1,0:T(8,128)S(1)} custom-call(bf16[1,4,16,512,256]{4,3,2,1,0:T(8,128)(2,1)} %basis.9), custom_call_target="tpu_custom_call" | custom-call | flops 1073741824 | bytes 12582912 | tf_op jit(solution)/shard_map/gram/pallas_call | solution.py:324
  14.0 0.0 copy-start.4
  14.0 0.0 collective-permute-done.refs_1_
  14.0 0.8 collective-permute-start.4
  14.8 1.8 collective-permute-start.2
  16.6 3.6 %gram.4.refs_0_ = f32[256,256]{1,0:T(8,128)S(1)} custom-call(bf16[1,4,16,512,256]{4,3,2,1,0:T(8,128)(2,1)} %basis.9, f32[256,256]{1,0:T(8,128)S(1)} %gram.3.refs_0_), custom_call_target="tpu_custom_call" | custom-call | flops 1073741824 | bytes 12582912 | tf_op jit(solution)/shard_map/gram/pallas_call | solution.py:324
  20.2 0.5 collective-permute-done.2.refs_3_
  20.7 2.5 edges.1
  23.2 0.1 collective-permute-start.5
  23.3 0.9 collective-permute-start.6
  24.2 0.1 copy.10.stoich
  24.3 3.6 %gram.5 = f32[256,256]{1,0:T(8,128)S(1)} custom-call(bf16[1,4,16,512,256]{4,3,2,1,0:T(8,128)(2,1)} %basis.9, f32[256,256]{1,0:T(8,128)S(1)} %gram.4.refs_0_), custom_call_target="tpu_custom_call" | custom-call | flops 1073741824 | bytes 12582912 | tf_op jit(solution)/shard_map/gram/pallas_call | solution.py:324
  27.9 19.7 %steps.1 = (f32[4,4,16,128]{3,2,1,0:T(8,128)}, f32[4,16,8,128]{3,2,1,0:T(8,128)S(1)}, f32[4,16,8,128]{3,2,1,0:T(8,128)S(1)}, f32[4,16,8,128]{3,2,1,0:T(8,128)S(1)}, f32[4,16,8,128]{3,2,1,0:T(8,128)S(1)}) custom-call(s32[8]{0:T(128)S(1)} %copy-done.2, f32[4]{0:T(128)S(1)} %copy-done.3, s32[8,4]{1,0:T(8,128)S(1)} %copy.10.stoich, f32[8,8]{1,0:T(8,128)S(1)} %copy-done.1, ...), custom_call_target="tpu_custom_call" | custom-call | tf_op jit(solution)/shard_map/steps/pallas_call | solution.py:515
  47.7 2.9 collective-permute-start.9
  50.6 0.6 collective-permute-start.8
  51.2 0.9 collective-permute-start.7
  52.0 257.2 %first_product.1 = (f32[8,256]{1,0:T(8,128)S(1)}, f32[8,256]{1,0:T(8,128)S(1)}, f32[256,256]{1,0:T(8,128)S(1)}, bf16[4,16,128,256]{3,2,1,0:T(8,128)(2,1)}, bf16[4,16,128,256]{3,2,1,0:T(8,128)(2,1)}) custom-call(f32[4,16,8,128]{3,2,1,0:T(8,128)S(1)} %get-tuple-element.48.part, bf16[1,4,16,512,256]{4,3,2,1,0:T(8,128)(2,1)} %basis.9, f32[256,256]{1,0:T(8,128)S(1)} %gram.5), custom_call_target="tpu_custom_call" | custom-call | flops 67108864 | bytes 16777216 | tf_op jit(solution)/shard_map/first_product/pallas_call | solution.py:423
  309.2 2.7 product.3
  311.9 2.7 product.4
  314.6 2.7 product.5
  317.3 1.0 collective-permute-start.12
  318.3 1.5 collective-permute-start.11
  319.7 0.7 collective-permute-done.12
  320.4 1.5 collective-permute-done.11
  321.9 0.6 collective-permute-start.13
  322.5 3.1 collective-permute-done.13
  325.6 2.4 collective-permute-start.16
  328.1 4.3 %collective-permute-start.15 = (f32[8,256]{1,0:T(8,128)S(1)}, f32[8,256]{1,0:T(8,128)S(1)}, u32[]{:S(2)}, u32[]{:S(2)}) collective-permute-start(f32[8,256]{1,0:T(8,128)S(1)} %add.51), channel_id=1, source_target_pairs={{0,2},{1,3},{2,0},{3,1},{4,6},{5,7},{6,4},{7,5},{8,10},{9,11},{10,... | collective-permute-start | bytes 24584 | tf_op jit(solution)/shard_map/ppermute | solution.py:27
  332.4 0.1 collective-permute-start.14
  332.5 1.6 collective-permute-done.15
  334.1 1.9 collective-permute-done.14
  336.0 0.2 add_subtract_fusion
  336.3 1.5 collective-permute-start.18
  337.8 0.4 collective-permute-start.17
  338.1 1.3 collective-permute-done.19
  339.4 0.5 collective-permute-done.18
  340.0 0.6 collective-permute-start.20
  340.6 3.1 collective-permute-done.20
  343.7 2.5 collective-permute-start.23
  346.2 0.0 collective-permute-start.22
  346.2 1.9 collective-permute-start.21
  348.1 1.1 collective-permute-done.23
  349.2 1.6 collective-permute-done.22
  350.8 0.6 add_add_fusion
  (28 shorter events, 0.1 us)
Async XLA Ops:
  2.3 11.6 %collective-permute-start = (f32[6,16,4,128]{3,2,1,0:T(4,128)}, f32[6,16,4,128]{3,2,1,0:T(4,128)S(1)}, u32[]{:S(2)}, u32[]{:S(2)}) collective-permute-start(f32[6,16,4,128]{3,2,1,0:T(4,128)} %pack.1.refs_0_), channel_id=1, source_target_pairs={{0,4},{4,0},{1,5},{5,1},{2,6},{6,2},{3,7},{7,3},{8,12},{12,8},{9,1... | collective-permute-start | bytes 589832 | tf_op jit(solution)/shard_map/ppermute | solution.py:485
  5.3 14.9 %collective-permute-start.3 = (f32[6,16,4,128]{3,2,1,0:T(4,128)}, f32[6,16,4,128]{3,2,1,0:T(4,128)S(1)}, u32[]{:S(2)}, u32[]{:S(2)}) collective-permute-start(f32[6,16,4,128]{3,2,1,0:T(4,128)} %pack.1.refs_0_), channel_id=1, source_target_pairs={{1,2},{2,1},{5,6},{6,5},{9,10},{10,9},{13,14},{14,13},{17,18},{18,... | collective-permute-start | bytes 589832 | tf_op jit(solution)/shard_map/ppermute | solution.py:488
  6.0 14.2 %collective-permute-start.1 = (f32[6,16,4,128]{3,2,1,0:T(4,128)}, f32[6,16,4,128]{3,2,1,0:T(4,128)S(1)}, u32[]{:S(2)}, u32[]{:S(2)}) collective-permute-start(f32[6,16,4,128]{3,2,1,0:T(4,128)} %pack.1.refs_0_), channel_id=1, source_target_pairs={{0,1},{2,3},{1,0},{3,2},{4,5},{6,7},{5,4},{7,6},{8,9},{10,11},{9,8... | collective-permute-start | bytes 589832 | tf_op jit(solution)/shard_map/ppermute | solution.py:487
  14.0 6.7 %copy-start = (f32[6,16,4,128]{3,2,1,0:T(4,128)S(1)}, f32[6,16,4,128]{3,2,1,0:T(4,128)}, u32[]{:S(2)}) copy-start(f32[6,16,4,128]{3,2,1,0:T(4,128)} %pack.1.refs_0_) | copy-start | bytes 589828
  14.0 10.2 %copy-start.4 = (s32[8,4]{0,1:T(4,128)S(1)}, s32[8,4]{0,1:T(4,128)}, u32[]{:S(2)}) copy-start(s32[8,4]{0,1:T(4,128)} %param.13) | copy-start | bytes 388
  14.0 6.2 %collective-permute-start.4 = (f32[6,16,4,128]{3,2,1,0:T(4,128)S(1)}, f32[6,16,4,128]{3,2,1,0:T(4,128)S(1)}, u32[]{:S(2)}, u32[]{:S(2)}) collective-permute-start(f32[6,16,4,128]{3,2,1,0:T(4,128)S(1)} %collective-permute-done.refs_1_), channel_id=1, source_target_pairs={{1,2},{2,1},{5,6},{6,5},{9,10},{10,9},{13,14},{14,13},{17,18},{18,... | collective-permute-start | bytes 589832 | tf_op jit(solution)/shard_map/ppermute | solution.py:492
  14.8 5.9 %collective-permute-start.2 = (f32[6,16,4,128]{3,2,1,0:T(4,128)S(1)}, f32[6,16,4,128]{3,2,1,0:T(4,128)S(1)}, u32[]{:S(2)}, u32[]{:S(2)}) collective-permute-start(f32[6,16,4,128]{3,2,1,0:T(4,128)S(1)} %collective-permute-done.refs_1_), channel_id=1, source_target_pairs={{0,1},{2,3},{1,0},{3,2},{4,5},{6,7},{5,4},{7,6},{8,9},{10,11},{9,8... | collective-permute-start | bytes 589832 | tf_op jit(solution)/shard_map/ppermute | solution.py:491
  23.2 4.7 %collective-permute-start.5 = (f32[6,6,8,128]{3,2,1,0:T(8,128)S(1)}, f32[6,6,8,128]{3,2,1,0:T(8,128)S(1)}, u32[]{:S(2)}, u32[]{:S(2)}) collective-permute-start(f32[6,6,8,128]{3,2,1,0:T(8,128)S(1)} %get-tuple-element.42), channel_id=1, source_target_pairs={{0,8},{16,24},{8,0},{24,16},{1,9},{17,25},{9,1},{25,17},{2,10},{18... | collective-permute-start | bytes 442376 | tf_op jit(solution)/shard_map/ppermute | solution.py:507
  23.3 4.6 %collective-permute-start.6 = (f32[6,6,8,128]{3,2,1,0:T(8,128)S(1)}, f32[6,6,8,128]{3,2,1,0:T(8,128)S(1)}, u32[]{:S(2)}, u32[]{:S(2)}) collective-permute-start(f32[6,6,8,128]{3,2,1,0:T(8,128)S(1)} %get-tuple-element.43), channel_id=1, source_target_pairs={{8,16},{16,8},{9,17},{17,9},{10,18},{18,10},{11,19},{19,11},{12,20... | collective-permute-start | bytes 442376 | tf_op jit(solution)/shard_map/ppermute | solution.py:508
  24.2 3.6 %copy-start.1 = (f32[8,8]{1,0:T(8,128)S(1)}, f32[8,8]{1,0:T(8,128)}, u32[]{:S(2)}) copy-start(f32[8,8]{1,0:T(8,128)} %rates.1) | copy-start | bytes 772
  24.2 3.7 %copy-start.2 = (s32[8]{0:T(128)S(1)}, s32[8]{0:T(128)}, u32[]{:S(2)}) copy-start(s32[8]{0:T(128)} %plan.1) | copy-start | bytes 100
  24.2 3.7 %copy-start.3 = (f32[4]{0:T(128)S(1)}, f32[4]{0:T(128)}, u32[]{:S(2)}) copy-start(f32[4]{0:T(128)} %diffusion.1) | copy-start | bytes 52
  47.7 261.6 %collective-permute-start.9 = (f32[4,16,8,128]{3,2,1,0:T(8,128)S(1)}, f32[4,16,8,128]{3,2,1,0:T(8,128)S(1)}, u32[]{:S(2)}, u32[]{:S(2)}) collective-permute-start(f32[4,16,8,128]{3,2,1,0:T(8,128)S(1)} %get-tuple-element.53), channel_id=1, source_target_pairs={{0,8},{8,0},{16,24},{24,16},{1,9},{9,1},{17,25},{25,17},{2,10},{10... | collective-permute-start | bytes 786440 | tf_op jit(solution)/shard_map/ppermute | solution.py:27
  50.6 261.3 %collective-permute-start.8 = (f32[4,16,8,128]{3,2,1,0:T(8,128)S(1)}, f32[4,16,8,128]{3,2,1,0:T(8,128)S(1)}, u32[]{:S(2)}, u32[]{:S(2)}) collective-permute-start(f32[4,16,8,128]{3,2,1,0:T(8,128)S(1)} %get-tuple-element.51), channel_id=1, source_target_pairs={{0,16},{8,24},{16,0},{24,8},{1,17},{9,25},{17,1},{25,9},{2,18},{10... | collective-permute-start | bytes 786440 | tf_op jit(solution)/shard_map/ppermute | solution.py:27
  51.2 263.4 %collective-permute-start.7 = (f32[4,16,8,128]{3,2,1,0:T(8,128)S(1)}, f32[4,16,8,128]{3,2,1,0:T(8,128)S(1)}, u32[]{:S(2)}, u32[]{:S(2)}) collective-permute-start(f32[4,16,8,128]{3,2,1,0:T(8,128)S(1)} %get-tuple-element.47), channel_id=1, source_target_pairs={{0,24},{8,16},{16,8},{24,0},{1,25},{9,17},{17,9},{25,1},{2,26},{10... | collective-permute-start | bytes 786440 | tf_op jit(solution)/shard_map/ppermute | solution.py:27
  317.3 3.1 collective-permute-start.12
  318.3 3.7 %collective-permute-start.11 = (f32[8,256]{1,0:T(8,128)S(1)}, f32[8,256]{1,0:T(8,128)S(1)}, u32[]{:S(2)}, u32[]{:S(2)}) collective-permute-start(f32[8,256]{1,0:T(8,128)S(1)} %get-tuple-element.60), channel_id=1, source_target_pairs={{0,16},{8,24},{16,0},{24,8},{1,17},{9,25},{17,1},{25,9},{2,18},{10... | collective-permute-start | bytes 24584 | tf_op jit(solution)/shard_map/ppermute | solution.py:27
  319.7 2.2 collective-permute-start.10
  321.9 3.7 %collective-permute-start.13 = (f32[8,256]{1,0:T(8,128)S(1)}, f32[8,256]{1,0:T(8,128)S(1)}, u32[]{:S(2)}, u32[]{:S(2)}) collective-permute-start(f32[8,256]{1,0:T(8,128)S(1)} %add_add_fusion.3), channel_id=1, source_target_pairs={{0,4},{4,0},{1,5},{5,1},{2,6},{6,2},{3,7},{7,3},{8,12},{12,8},{9,1... | collective-permute-start | bytes 24584 | tf_op jit(solution)/shard_map/ppermute | solution.py:27
  325.6 6.9 %collective-permute-start.16 = (f32[8,256]{1,0:T(8,128)S(1)}, f32[8,256]{1,0:T(8,128)S(1)}, u32[]{:S(2)}, u32[]{:S(2)}) collective-permute-start(f32[8,256]{1,0:T(8,128)S(1)} %add.51), channel_id=1, source_target_pairs={{0,3},{1,2},{2,1},{3,0},{4,7},{5,6},{6,5},{7,4},{8,11},{9,10},{10,... | collective-permute-start | bytes 24584 | tf_op jit(solution)/shard_map/ppermute | solution.py:27
  328.1 6.0 %collective-permute-start.15 = (f32[8,256]{1,0:T(8,128)S(1)}, f32[8,256]{1,0:T(8,128)S(1)}, u32[]{:S(2)}, u32[]{:S(2)}) collective-permute-start(f32[8,256]{1,0:T(8,128)S(1)} %add.51), channel_id=1, source_target_pairs={{0,2},{1,3},{2,0},{3,1},{4,6},{5,7},{6,4},{7,5},{8,10},{9,11},{10,... | collective-permute-start | bytes 24584 | tf_op jit(solution)/shard_map/ppermute | solution.py:27
  332.4 3.7 %collective-permute-start.14 = (f32[8,256]{1,0:T(8,128)S(1)}, f32[8,256]{1,0:T(8,128)S(1)}, u32[]{:S(2)}, u32[]{:S(2)}) collective-permute-start(f32[8,256]{1,0:T(8,128)S(1)} %add.51), channel_id=1, source_target_pairs={{0,1},{1,0},{2,3},{3,2},{4,5},{5,4},{6,7},{7,6},{8,9},{9,8},{10,11... | collective-permute-start | bytes 24584 | tf_op jit(solution)/shard_map/ppermute | solution.py:27
  336.3 3.2 collective-permute-start.19
  336.3 3.7 %collective-permute-start.18 = (f32[8,256]{1,0:T(8,128)S(1)}, f32[8,256]{1,0:T(8,128)S(1)}, u32[]{:S(2)}, u32[]{:S(2)}) collective-permute-start(f32[8,256]{1,0:T(8,128)S(1)} %add_subtract_fusion), channel_id=1, source_target_pairs={{0,16},{8,24},{16,0},{24,8},{1,17},{9,25},{17,1},{25,9},{2,18},{10... | collective-permute-start | bytes 24584 | tf_op jit(solution)/shard_map/ppermute | solution.py:27
  337.8 2.2 collective-permute-start.17
  340.0 3.7 %collective-permute-start.20 = (f32[8,256]{1,0:T(8,128)S(1)}, f32[8,256]{1,0:T(8,128)S(1)}, u32[]{:S(2)}, u32[]{:S(2)}) collective-permute-start(f32[8,256]{1,0:T(8,128)S(1)} %add_add_fusion.1), channel_id=1, source_target_pairs={{0,4},{4,0},{1,5},{5,1},{2,6},{6,2},{3,7},{7,3},{8,12},{12,8},{9,1... | collective-permute-start | bytes 24584 | tf_op jit(solution)/shard_map/ppermute | solution.py:27
  343.7 5.4 %collective-permute-start.23 = (f32[8,256]{1,0:T(8,128)S(1)}, f32[8,256]{1,0:T(8,128)S(1)}, u32[]{:S(2)}, u32[]{:S(2)}) collective-permute-start(f32[8,256]{1,0:T(8,128)S(1)} %add.59), channel_id=1, source_target_pairs={{0,3},{1,2},{2,1},{3,0},{4,7},{5,6},{6,5},{7,4},{8,11},{9,10},{10,... | collective-permute-start | bytes 24584 | tf_op jit(solution)/shard_map/ppermute | solution.py:27
  346.2 4.5 %collective-permute-start.22 = (f32[8,256]{1,0:T(8,128)S(1)}, f32[8,256]{1,0:T(8,128)S(1)}, u32[]{:S(2)}, u32[]{:S(2)}) collective-permute-start(f32[8,256]{1,0:T(8,128)S(1)} %add.59), channel_id=1, source_target_pairs={{0,2},{1,3},{2,0},{3,1},{4,6},{5,7},{6,4},{7,5},{8,10},{9,11},{10,... | collective-permute-start | bytes 24584 | tf_op jit(solution)/shard_map/ppermute | solution.py:27
  346.2 4.5 %collective-permute-start.21 = (f32[8,256]{1,0:T(8,128)S(1)}, f32[8,256]{1,0:T(8,128)S(1)}, u32[]{:S(2)}, u32[]{:S(2)}) collective-permute-start(f32[8,256]{1,0:T(8,128)S(1)} %add.59), channel_id=1, source_target_pairs={{0,1},{1,0},{2,3},{3,2},{4,5},{5,4},{6,7},{7,6},{8,9},{9,8},{10,11... | collective-permute-start | bytes 24584 | tf_op jit(solution)/shard_map/ppermute | solution.py:27

commit v5 on v4

--- a/solution.py
+++ b/solution.py
@@ -364,9 +364,9 @@
     return acc
 
 
-def first_kernel(later, gram_x, part, basis, gram, *refs):
-    out_high, out_low, out_gram, *ahead = refs[: 3 + len(later)]
-    held, rows, chunks, total, sems = refs[3 + len(later) :]
+def first_kernel(
+    gram_x, part, basis, gram, out_high, out_low, out_gram, held, rows, chunks, total, sems
+):
     cells_x, cells_y, snaps, cells_z = held.shape
     modes = rows.shape[-1]
     sources = [part, *rows_of(basis, 0, cells_z)]
@@ -374,9 +374,6 @@
     sources += [basis.at[0, x] for x in gram_x] + [gram]
     targets += [chunks.at[i] for i in range(len(gram_x))] + [total]
     start_gram = 1 + cells_x
-    for i, flips in enumerate(later):
-        sources += rows_of(basis, flips, cells_z)
-        targets += [ahead[i].at[x] for x in range(cells_x)]
     copies = fetch(sources, targets, sems)
     copies[0].wait()
     acc = multiply(held, rows, copies[1:], None)
@@ -395,43 +392,44 @@
     out_gram[...] = total[...] if acc is None else acc + total[...]
 
 
-def product_kernel(flips, part, basis, high, low, out_high, out_low, held, rows, sums, sems):
-    cells_x, cells_y, snaps, cells_z = held.shape
-    if flips is None:
-        sources = [basis.at[x] for x in range(cells_x)]
-    else:
-        sources = rows_of(basis, flips, cells_z)
-    copies = fetch(
-        [part, *sources, high, low],
-        [held, *(rows.at[x] for x in range(cells_x)), sums.at[0], sums.at[1]],
-        sems,
-    )
-    copies[0].wait()
-    acc = multiply(held, rows, copies[1:], None)
+def product_kernel(flips, *refs):
+    count = len(flips)
+    parts, refs = refs[:count], refs[count:]
+    basis, high, low, out_high, out_low, held, rows, sums, sems = refs
+    _, cells_x, cells_y, snaps, cells_z = held.shape
+    sources, targets = [], []
+    for i in range(count):
+        sources += [parts[i], *rows_of(basis, flips[i], cells_z)]
+        targets += [held.at[i], *(rows.at[i, x] for x in range(cells_x))]
+    copies = fetch([*sources, high, low], [*targets, sums.at[0], sums.at[1]], sems)
+    acc = None
+    for i in range(count):
+        start = i * (cells_x + 1)
+        copies[start].wait()
+        acc = multiply(held.at[i], rows.at[i], copies[start + 1 :], acc)
     copies[-2].wait()
     copies[-1].wait()
     out_high[...] = acc[:snaps] + sums[0]
     out_low[...] = acc[snaps:] + sums[1]
 
 
-def first_product(part, basis, gram, later, gram_x):
+def first_product(part, basis, gram, gram_x):
     cells_x, cells_y, snaps, cells_z = part.shape
     modes = basis.shape[-1]
     size = 2 * cells_x * cells_y * cells_z * modes
     out = jax.ShapeDtypeStruct((snaps, modes), jnp.float32)
     rows = (cells_x, cells_y, cells_z, modes)
     return pl.pallas_call(
-        functools.partial(first_kernel, later, gram_x),
-        out_shape=[out, out, jax.ShapeDtypeStruct(gram.shape, jnp.float32)]
-        + [jax.ShapeDtypeStruct(rows, jnp.bfloat16)] * len(later),
+        functools.partial(first_kernel, gram_x),
+        out_shape=[out, out, jax.ShapeDtypeStruct(gram.shape, jnp.float32)],
         in_specs=anywhere(3),
-        out_specs=whole(3) + anywhere(len(later)),
+        out_specs=whole(3),
         scratch_shapes=[
             pltpu.VMEM(part.shape, jnp.float32),
             pltpu.VMEM(rows, jnp.bfloat16),
             pltpu.VMEM((max(len(gram_x), 1), *basis.shape[2:]), jnp.bfloat16),
             pltpu.VMEM(gram.shape, jnp.float32),
-            pltpu.SemaphoreType.DMA((2 + cells_x * (1 + len(later)) + len(gram_x),)),
+            pltpu.SemaphoreType.DMA((2 + cells_x + len(gram_x),)),
         ],
         compiler_params=pltpu.CompilerParams(vmem_limit_bytes=BASIS_VMEM),
         cost_estimate=pl.CostEstimate(
@@ -441,28 +439,28 @@
     )(part, basis, gram)
 
 
-def product(flips, part, basis, high, low):
-    cells_x, cells_y, snaps, cells_z = part.shape
-    modes = basis.shape[-1]
-    size = 2 * cells_x * cells_y * cells_z * modes
+def product(flips, parts, basis, high, low):
+    cells_x, cells_y, snaps, cells_z = parts[0].shape
+    modes, count = basis.shape[-1], len(flips)
+    size = 2 * count * cells_x * cells_y * cells_z * modes
     out = jax.ShapeDtypeStruct((snaps, modes), jnp.float32)
     return pl.pallas_call(
         functools.partial(product_kernel, flips),
         out_shape=(out, out),
-        in_specs=anywhere(4),
+        in_specs=anywhere(3 + count),
         out_specs=tuple(whole(2)),
         scratch_shapes=[
-            pltpu.VMEM(part.shape, jnp.float32),
-            pltpu.VMEM((cells_x, cells_y, cells_z, modes), jnp.bfloat16),
+            pltpu.VMEM((count, *parts[0].shape), jnp.float32),
+            pltpu.VMEM((count, cells_x, cells_y, cells_z, modes), jnp.bfloat16),
             pltpu.VMEM((2, snaps, modes), jnp.float32),
-            pltpu.SemaphoreType.DMA((cells_x + 3,)),
+            pltpu.SemaphoreType.DMA((count * (cells_x + 1) + 2,)),
         ],
         compiler_params=pltpu.CompilerParams(vmem_limit_bytes=BASIS_VMEM),
         cost_estimate=pl.CostEstimate(
             flops=2 * snaps * size, bytes_accessed=2 * size, transcendentals=0
         ),
         name="product",
-    )(part, basis, high, low)
+    )(*parts, basis, high, low)
 
 
 def body(terminal, diffusion, velocity, material, rates, stoich, plan, basis):
@@ -525,14 +523,9 @@
 
     order = sorted(range(1, count_grp), key=lambda flips: -flips)
     moved = {flips: exchange(kept[flips], "grp", flips) for flips in order}
-    later = tuple(range(2, count_grp))
-    high, low, gram, *ahead = first_product(
-        kept[0], basis, gram, later, tuple(range(3, cells_x))
-    )
-    if count_grp > 1:
-        high, low = product(1, moved[1], basis, high, low)
-    for flips, rows in zip(later, ahead):
-        high, low = product(None, moved[flips], rows, high, low)
+    high, low, gram = first_product(kept[0], basis, gram, tuple(range(3, cells_x)))
+    for flips in ((1,), tuple(range(2, count_grp))):
+        high, low = product(flips, [moved[f] for f in flips], basis, high, low)
 
     first = sum_all(high)
     taken = jnp.dot(

time: 352 us -> 102 us (0.29)
  Pallas kernels: 300 us -> 46.9 us
  waiting for transfers between devices: 16.9 us -> 20.5 us
    pallas_call x1, Pallas kernels: 257 us -> 5.61 us  [first_product(): pl.pallas_call(functools.partial(first_kernel, gram_x), out_shape=[out, o...]
    ppermute x17, waiting for transfers between devices: 16.4 us -> 20 us  [exchange(): return lax.ppermute(value, axis, [(i, i ^ flips) for i in range(count)])]
    pallas_call x3 -> x2, Pallas kernels: 8.04 us -> 6.61 us  [product(): pl.pallas_call(functools.partial(product_kernel, flips), out_shape=(out,...]
  transfers between devices with their start and end apart: 24 -> 24, of which waited for: 11 -> 12; matrix products, arithmetic and copies ran while one was open for 0% -> 0% of each run, Pallas kernels for 78% -> 19%
where the time goes in v5:
time: 102 us
  Pallas kernels  46.9 us (46%)
  starting transfers between devices  32.6 us (32%)
  waiting for transfers between devices  20.5 us (20%)
    ppermute x17, starting transfers between devices, exchange(): return lax.ppermute(value, axis, [(i, i ^ flips) for i in range(count)])  21.2 us
    ppermute x17, waiting for transfers between devices, exchange(): return lax.ppermute(value, axis, [(i, i ^ flips) for i in range(count)])  20 us
    pallas_call x1, Pallas kernels, body(): pl.pallas_call(functools.partial(steps_kernel, count_x), out_shape=[jax.S...  19.7 us
    pallas_call x3, Pallas kernels, gram_part(): pl.pallas_call(functools.partial(gram_kernel, x, len(total)), out_shape=j...  10.7 us
    pallas_call x2, Pallas kernels, product(): pl.pallas_call(functools.partial(product_kernel, flips), out_shape=(out,...  6.61 us
    pallas_call x1, Pallas kernels, first_product(): pl.pallas_call(functools.partial(first_kernel, gram_x), out_shape=[out, o...  5.61 us
    ppermute x1, starting transfers between devices, body(): from_a = [lax.ppermute(own, 'gy', pairs('gy', 0))]  4.45 us
    ppermute x1, starting transfers between devices, body(): lax.ppermute(own, 'gx', [(i, (i - shift) % count_x) for i in range(count_...  2.94 us
  transfers between devices with their start and end apart: 24, of which 12 were waited for; matrix products, arithmetic and copies ran while one was open for 0% of the time, Pallas kernels for 19%

profile of v5, /device:TPU:0, one launch (start us, length us, event | category | flops | bytes accessed | tf_op | source)
XLA Modules:
  0.0 101.8 jit_solution(5398110557363150901)
XLA Ops:
  0.6 1.7 %pack.1.refs_0_ = f32[6,16,4,128]{3,2,1,0:T(4,128)} custom-call(f32[4,4,16,128]{3,2,1,0:T(8,128)} %terminal.1, f32[4,16,128]{2,1,0:T(8,128)} %velocity.1, s32[4,16,128]{2,1,0:T(8,128)} %material.1), custom_call_target="tpu_custom_call" | custom-call | tf_op jit(solution)/shard_map/pack/pallas_call | solution.py:473
  2.3 2.9 %collective-permute-start = (f32[6,16,4,128]{3,2,1,0:T(4,128)}, f32[6,16,4,128]{3,2,1,0:T(4,128)S(1)}, u32[]{:S(2)}, u32[]{:S(2)}) collective-permute-start(f32[6,16,4,128]{3,2,1,0:T(4,128)} %pack.1.refs_0_), channel_id=1, source_target_pairs={{0,4},{4,0},{1,5},{5,1},{2,6},{6,2},{3,7},{7,3},{8,12},{12,8},{9,1... | collective-permute-start | bytes 589832 | tf_op jit(solution)/shard_map/ppermute | solution.py:483
  5.3 0.7 collective-permute-start.3
  6.0 4.5 %collective-permute-start.1 = (f32[6,16,4,128]{3,2,1,0:T(4,128)}, f32[6,16,4,128]{3,2,1,0:T(4,128)S(1)}, u32[]{:S(2)}, u32[]{:S(2)}) collective-permute-start(f32[6,16,4,128]{3,2,1,0:T(4,128)} %pack.1.refs_0_), channel_id=1, source_target_pairs={{0,1},{2,3},{1,0},{3,2},{4,5},{6,7},{5,4},{7,6},{8,9},{10,11},{9,8... | collective-permute-start | bytes 589832 | tf_op jit(solution)/shard_map/ppermute | solution.py:485
  10.4 3.5 %gram.3.refs_0_ = f32[256,256]{1,0:T(8,128)S(1)} custom-call(bf16[1,4,16,512,256]{4,3,2,1,0:T(8,128)(2,1)} %refs_2_.1), custom_call_target="tpu_custom_call" | custom-call | flops 1073741824 | bytes 12582912 | tf_op jit(solution)/shard_map/gram/pallas_call | solution.py:324
  14.0 0.0 copy-start.2
  14.0 0.0 copy-start.3
  14.0 0.7 collective-permute-start.4
  14.7 1.8 %collective-permute-start.2 = (f32[6,16,4,128]{3,2,1,0:T(4,128)S(1)}, f32[6,16,4,128]{3,2,1,0:T(4,128)S(1)}, u32[]{:S(2)}, u32[]{:S(2)}) collective-permute-start(f32[6,16,4,128]{3,2,1,0:T(4,128)S(1)} %collective-permute-done.refs_1_), channel_id=1, source_target_pairs={{0,1},{2,3},{1,0},{3,2},{4,5},{6,7},{5,4},{7,6},{8,9},{10,11},{9,8... | collective-permute-start | bytes 589832 | tf_op jit(solution)/shard_map/ppermute | solution.py:489
  16.5 3.6 %gram.4.refs_0_ = f32[256,256]{1,0:T(8,128)S(1)} custom-call(bf16[1,4,16,512,256]{4,3,2,1,0:T(8,128)(2,1)} %refs_2_.1, f32[256,256]{1,0:T(8,128)S(1)} %gram.3.refs_0_), custom_call_target="tpu_custom_call" | custom-call | flops 1073741824 | bytes 12582912 | tf_op jit(solution)/shard_map/gram/pallas_call | solution.py:324
  20.1 0.5 collective-permute-done.2.refs_3_
  20.6 2.5 %edges.1 = (f32[6,6,8,128]{3,2,1,0:T(8,128)S(1)}, f32[6,6,8,128]{3,2,1,0:T(8,128)S(1)}) custom-call(f32[6,16,4,128]{3,2,1,0:T(4,128)S(1)} %copy-done, f32[6,16,4,128]{3,2,1,0:T(4,128)S(1)} %collective-permute-done.refs_1_, f32[6,16,4,128]{3,2,1,0:T(4,128)S(1)} %collective-permute-done.1.refs_2_, f32[6,16,4,128]{3,2,1,0:T(4,128)S(1)} %collective-permute-done.2.refs_3_, ...), custom_call_target="tpu_custom_call" | custom-call | tf_op jit(solution)/shard_map/edges/pallas_call | solution.py:496
  23.1 0.1 collective-permute-start.5
  23.2 0.9 collective-permute-start.6
  24.0 0.1 copy.10.stoich
  24.1 3.6 %gram.5 = f32[256,256]{1,0:T(8,128)S(1)} custom-call(bf16[1,4,16,512,256]{4,3,2,1,0:T(8,128)(2,1)} %refs_2_.1, f32[256,256]{1,0:T(8,128)S(1)} %gram.4.refs_0_), custom_call_target="tpu_custom_call" | custom-call | flops 1073741824 | bytes 12582912 | tf_op jit(solution)/shard_map/gram/pallas_call | solution.py:324
  27.8 19.7 %steps.1 = (f32[4,4,16,128]{3,2,1,0:T(8,128)}, f32[4,16,8,128]{3,2,1,0:T(8,128)S(1)}, f32[4,16,8,128]{3,2,1,0:T(8,128)S(1)}, f32[4,16,8,128]{3,2,1,0:T(8,128)S(1)}, f32[4,16,8,128]{3,2,1,0:T(8,128)S(1)}) custom-call(s32[8]{0:T(128)S(1)} %copy-done.2, f32[4]{0:T(128)S(1)} %copy-done.3, s32[8,4]{1,0:T(8,128)S(1)} %copy.10.stoich, f32[8,8]{1,0:T(8,128)S(1)} %copy-done.1, ...), custom_call_target="tpu_custom_call" | custom-call | tf_op jit(solution)/shard_map/steps/pallas_call | solution.py:513
  47.5 2.9 %collective-permute-start.9 = (f32[4,16,8,128]{3,2,1,0:T(8,128)S(1)}, f32[4,16,8,128]{3,2,1,0:T(8,128)S(1)}, u32[]{:S(2)}, u32[]{:S(2)}) collective-permute-start(f32[4,16,8,128]{3,2,1,0:T(8,128)S(1)} %get-tuple-element.45), channel_id=1, source_target_pairs={{0,8},{8,0},{16,24},{24,16},{1,9},{9,1},{17,25},{25,17},{2,10},{10... | collective-permute-start | bytes 786440 | tf_op jit(solution)/shard_map/ppermute | solution.py:27
  50.4 0.6 collective-permute-start.7
  51.0 0.8 collective-permute-start.8
  51.8 5.6 %first_product.1 = (f32[8,256]{1,0:T(8,128)S(1)}, f32[8,256]{1,0:T(8,128)S(1)}, f32[256,256]{1,0:T(8,128)S(1)}) custom-call(f32[4,16,8,128]{3,2,1,0:T(8,128)S(1)} %get-tuple-element.46.part, bf16[1,4,16,512,256]{4,3,2,1,0:T(8,128)(2,1)} %refs_2_.1, f32[256,256]{1,0:T(8,128)S(1)} %gram.5), custom_call_target="tpu_custom_call" | custom-call | flops 67108864 | bytes 16777216 | tf_op jit(solution)/shard_map/first_product/pallas_call | solution.py:422
  57.5 2.7 %product.2 = (f32[8,256]{1,0:T(8,128)S(1)}, f32[8,256]{1,0:T(8,128)S(1)}) custom-call(f32[4,16,8,128]{3,2,1,0:T(8,128)S(1)} %collective-permute-done.9.refs_0_, bf16[1,4,16,512,256]{4,3,2,1,0:T(8,128)(2,1)} %refs_2_.1, f32[8,256]{1,0:T(8,128)S(1)} %get-tuple-element.48.refs_2_, f32[8,256]{1,0:T(8,128)S(1)} %get-tuple-element.49.refs_3_), custom_call_target="tpu_custom_call" | custom-call | flops 67108864 | bytes 8388608 | tf_op jit(solution)/shard_map/product/pallas_call | solution.py:447
  60.2 3.3 %collective-permute-done.8.refs_1_ = f32[4,16,8,128]{3,2,1,0:T(8,128)S(1)} collective-permute-done((f32[4,16,8,128]{3,2,1,0:T(8,128)S(1)}, f32[4,16,8,128]{3,2,1,0:T(8,128)S(1)}, u32[]{:S(2)}, u32[]{:S(2)}) %collective-permute-start.8) | collective-permute-done | bytes 262176 | tf_op jit(solution)/shard_map/ppermute | solution.py:27
  63.4 3.9 %product.3 = (f32[8,256]{1,0:T(8,128)S(1)}, f32[8,256]{1,0:T(8,128)S(1)}) custom-call(f32[4,16,8,128]{3,2,1,0:T(8,128)S(1)} %collective-permute-done.7.refs_0_, f32[4,16,8,128]{3,2,1,0:T(8,128)S(1)} %collective-permute-done.8.refs_1_, bf16[1,4,16,512,256]{4,3,2,1,0:T(8,128)(2,1)} %refs_2_.1, f32[8,256]{1,0:T(8,128)S(1)} %get-tuple-element.50.refs_3_, ...), custom_call_target="tpu_custom_call" | custom-call | flops 134217728 | bytes 16777216 | tf_op jit(solution)/shard_map/product/pallas_call | solution.py:447
  67.4 1.4 %collective-permute-start.12 = (f32[8,256]{1,0:T(8,128)S(1)}, f32[8,256]{1,0:T(8,128)S(1)}, u32[]{:S(2)}, u32[]{:S(2)}) collective-permute-start(f32[8,256]{1,0:T(8,128)S(1)} %get-tuple-element.52), channel_id=1, source_target_pairs={{0,24},{8,16},{16,8},{24,0},{1,25},{9,17},{17,9},{25,1},{2,26},{10... | collective-permute-start | bytes 24584 | tf_op jit(solution)/shard_map/ppermute | solution.py:27
  68.7 1.0 %collective-permute-start.11 = (f32[8,256]{1,0:T(8,128)S(1)}, f32[8,256]{1,0:T(8,128)S(1)}, u32[]{:S(2)}, u32[]{:S(2)}) collective-permute-start(f32[8,256]{1,0:T(8,128)S(1)} %get-tuple-element.52), channel_id=1, source_target_pairs={{0,16},{8,24},{16,0},{24,8},{1,17},{9,25},{17,1},{25,9},{2,18},{10... | collective-permute-start | bytes 24584 | tf_op jit(solution)/shard_map/ppermute | solution.py:27
  69.8 0.7 collective-permute-done.12
  70.5 1.9 %collective-permute-done.11 = f32[8,256]{1,0:T(8,128)S(1)} collective-permute-done((f32[8,256]{1,0:T(8,128)S(1)}, f32[8,256]{1,0:T(8,128)S(1)}, u32[]{:S(2)}, u32[]{:S(2)}) %collective-permute-start.11) | collective-permute-done | bytes 8224 | tf_op jit(solution)/shard_map/ppermute | solution.py:27
  72.4 0.6 collective-permute-start.13
  73.0 3.1 %collective-permute-done.13 = f32[8,256]{1,0:T(8,128)S(1)} collective-permute-done((f32[8,256]{1,0:T(8,128)S(1)}, f32[8,256]{1,0:T(8,128)S(1)}, u32[]{:S(2)}, u32[]{:S(2)}) %collective-permute-start.13) | collective-permute-done | bytes 8224 | tf_op jit(solution)/shard_map/ppermute | solution.py:27
  76.1 2.4 %collective-permute-start.16 = (f32[8,256]{1,0:T(8,128)S(1)}, f32[8,256]{1,0:T(8,128)S(1)}, u32[]{:S(2)}, u32[]{:S(2)}) collective-permute-start(f32[8,256]{1,0:T(8,128)S(1)} %add.51), channel_id=1, source_target_pairs={{0,3},{1,2},{2,1},{3,0},{4,7},{5,6},{6,5},{7,4},{8,11},{9,10},{10,... | collective-permute-start | bytes 24584 | tf_op jit(solution)/shard_map/ppermute | solution.py:27
  78.6 4.3 %collective-permute-start.15 = (f32[8,256]{1,0:T(8,128)S(1)}, f32[8,256]{1,0:T(8,128)S(1)}, u32[]{:S(2)}, u32[]{:S(2)}) collective-permute-start(f32[8,256]{1,0:T(8,128)S(1)} %add.51), channel_id=1, source_target_pairs={{0,2},{1,3},{2,0},{3,1},{4,6},{5,7},{6,4},{7,5},{8,10},{9,11},{10,... | collective-permute-start | bytes 24584 | tf_op jit(solution)/shard_map/ppermute | solution.py:27
  82.9 0.1 collective-permute-start.14
  83.0 1.6 %collective-permute-done.15 = f32[8,256]{1,0:T(8,128)S(1)} collective-permute-done((f32[8,256]{1,0:T(8,128)S(1)}, f32[8,256]{1,0:T(8,128)S(1)}, u32[]{:S(2)}, u32[]{:S(2)}) %collective-permute-start.15) | collective-permute-done | bytes 8224 | tf_op jit(solution)/shard_map/ppermute | solution.py:27
  84.6 1.9 %collective-permute-done.14 = f32[8,256]{1,0:T(8,128)S(1)} collective-permute-done((f32[8,256]{1,0:T(8,128)S(1)}, f32[8,256]{1,0:T(8,128)S(1)}, u32[]{:S(2)}, u32[]{:S(2)}) %collective-permute-start.14) | collective-permute-done | bytes 8224 | tf_op jit(solution)/shard_map/ppermute | solution.py:27
  86.5 0.2 add_subtract_fusion
  86.7 1.1 %collective-permute-start.18 = (f32[8,256]{1,0:T(8,128)S(1)}, f32[8,256]{1,0:T(8,128)S(1)}, u32[]{:S(2)}, u32[]{:S(2)}) collective-permute-start(f32[8,256]{1,0:T(8,128)S(1)} %add_subtract_fusion), channel_id=1, source_target_pairs={{0,16},{8,24},{16,0},{24,8},{1,17},{9,25},{17,1},{25,9},{2,18},{10... | collective-permute-start | bytes 24584 | tf_op jit(solution)/shard_map/ppermute | solution.py:27
  87.8 0.8 collective-permute-start.17
  88.6 1.2 %collective-permute-done.19 = f32[8,256]{1,0:T(8,128)S(1)} collective-permute-done((f32[8,256]{1,0:T(8,128)S(1)}, f32[8,256]{1,0:T(8,128)S(1)}, u32[]{:S(2)}, u32[]{:S(2)}) %collective-permute-start.19) | collective-permute-done | bytes 8224 | tf_op jit(solution)/shard_map/ppermute | solution.py:27
  89.8 0.6 collective-permute-done.18
  90.5 0.7 collective-permute-start.20
  91.2 3.0 %collective-permute-done.20 = f32[8,256]{1,0:T(8,128)S(1)} collective-permute-done((f32[8,256]{1,0:T(8,128)S(1)}, f32[8,256]{1,0:T(8,128)S(1)}, u32[]{:S(2)}, u32[]{:S(2)}) %collective-permute-start.20) | collective-permute-done | bytes 8224 | tf_op jit(solution)/shard_map/ppermute | solution.py:27
  94.2 2.5 %collective-permute-start.23 = (f32[8,256]{1,0:T(8,128)S(1)}, f32[8,256]{1,0:T(8,128)S(1)}, u32[]{:S(2)}, u32[]{:S(2)}) collective-permute-start(f32[8,256]{1,0:T(8,128)S(1)} %add.59), channel_id=1, source_target_pairs={{0,3},{1,2},{2,1},{3,0},{4,7},{5,6},{6,5},{7,4},{8,11},{9,10},{10,... | collective-permute-start | bytes 24584 | tf_op jit(solution)/shard_map/ppermute | solution.py:27
  96.7 0.0 collective-permute-start.22
  96.7 1.9 %collective-permute-start.21 = (f32[8,256]{1,0:T(8,128)S(1)}, f32[8,256]{1,0:T(8,128)S(1)}, u32[]{:S(2)}, u32[]{:S(2)}) collective-permute-start(f32[8,256]{1,0:T(8,128)S(1)} %add.59), channel_id=1, source_target_pairs={{0,1},{1,0},{2,3},{3,2},{4,5},{5,4},{6,7},{7,6},{8,9},{9,8},{10,11... | collective-permute-start | bytes 24584 | tf_op jit(solution)/shard_map/ppermute | solution.py:27
  98.6 1.1 %collective-permute-done.23 = f32[8,256]{1,0:T(8,128)S(1)} collective-permute-done((f32[8,256]{1,0:T(8,128)S(1)}, f32[8,256]{1,0:T(8,128)S(1)}, u32[]{:S(2)}, u32[]{:S(2)}) %collective-permute-start.23) | collective-permute-done | bytes 8224 | tf_op jit(solution)/shard_map/ppermute | solution.py:27
  99.6 1.6 %collective-permute-done.22 = f32[8,256]{1,0:T(8,128)S(1)} collective-permute-done((f32[8,256]{1,0:T(8,128)S(1)}, f32[8,256]{1,0:T(8,128)S(1)}, u32[]{:S(2)}, u32[]{:S(2)}) %collective-permute-start.22) | collective-permute-done | bytes 8224 | tf_op jit(solution)/shard_map/ppermute | solution.py:27
  101.2 0.6 add_add_fusion
  (27 shorter events, 0.1 us)
Async XLA Ops:
  2.3 18.2 %copy-start = (f32[6,16,4,128]{3,2,1,0:T(4,128)S(1)}, f32[6,16,4,128]{3,2,1,0:T(4,128)}, u32[]{:S(2)}) copy-start(f32[6,16,4,128]{3,2,1,0:T(4,128)} %pack.1.refs_0_) | copy-start | bytes 589828
  2.3 21.7 %copy-start.4 = (s32[8,4]{0,1:T(4,128)S(1)}, s32[8,4]{0,1:T(4,128)}, u32[]{:S(2)}) copy-start(s32[8,4]{0,1:T(4,128)} %param.13) | copy-start | bytes 388
  2.3 11.7 %collective-permute-start = (f32[6,16,4,128]{3,2,1,0:T(4,128)}, f32[6,16,4,128]{3,2,1,0:T(4,128)S(1)}, u32[]{:S(2)}, u32[]{:S(2)}) collective-permute-start(f32[6,16,4,128]{3,2,1,0:T(4,128)} %pack.1.refs_0_), channel_id=1, source_target_pairs={{0,4},{4,0},{1,5},{5,1},{2,6},{6,2},{3,7},{7,3},{8,12},{12,8},{9,1... | collective-permute-start | bytes 589832 | tf_op jit(solution)/shard_map/ppermute | solution.py:483
  5.3 14.7 %collective-permute-start.3 = (f32[6,16,4,128]{3,2,1,0:T(4,128)}, f32[6,16,4,128]{3,2,1,0:T(4,128)S(1)}, u32[]{:S(2)}, u32[]{:S(2)}) collective-permute-start(f32[6,16,4,128]{3,2,1,0:T(4,128)} %pack.1.refs_0_), channel_id=1, source_target_pairs={{1,2},{2,1},{5,6},{6,5},{9,10},{10,9},{13,14},{14,13},{17,18},{18,... | collective-permute-start | bytes 589832 | tf_op jit(solution)/shard_map/ppermute | solution.py:486
  6.0 14.1 %collective-permute-start.1 = (f32[6,16,4,128]{3,2,1,0:T(4,128)}, f32[6,16,4,128]{3,2,1,0:T(4,128)S(1)}, u32[]{:S(2)}, u32[]{:S(2)}) collective-permute-start(f32[6,16,4,128]{3,2,1,0:T(4,128)} %pack.1.refs_0_), channel_id=1, source_target_pairs={{0,1},{2,3},{1,0},{3,2},{4,5},{6,7},{5,4},{7,6},{8,9},{10,11},{9,8... | collective-permute-start | bytes 589832 | tf_op jit(solution)/shard_map/ppermute | solution.py:485
  14.0 13.8 %copy-start.1 = (f32[8,8]{1,0:T(8,128)S(1)}, f32[8,8]{1,0:T(8,128)}, u32[]{:S(2)}) copy-start(f32[8,8]{1,0:T(8,128)} %rates.1) | copy-start | bytes 772
  14.0 13.8 %copy-start.2 = (s32[8]{0:T(128)S(1)}, s32[8]{0:T(128)}, u32[]{:S(2)}) copy-start(s32[8]{0:T(128)} %plan.1) | copy-start | bytes 100
  14.0 13.8 %copy-start.3 = (f32[4]{0:T(128)S(1)}, f32[4]{0:T(128)}, u32[]{:S(2)}) copy-start(f32[4]{0:T(128)} %diffusion.1) | copy-start | bytes 52
  14.0 6.0 %collective-permute-start.4 = (f32[6,16,4,128]{3,2,1,0:T(4,128)S(1)}, f32[6,16,4,128]{3,2,1,0:T(4,128)S(1)}, u32[]{:S(2)}, u32[]{:S(2)}) collective-permute-start(f32[6,16,4,128]{3,2,1,0:T(4,128)S(1)} %collective-permute-done.refs_1_), channel_id=1, source_target_pairs={{1,2},{2,1},{5,6},{6,5},{9,10},{10,9},{13,14},{14,13},{17,18},{18,... | collective-permute-start | bytes 589832 | tf_op jit(solution)/shard_map/ppermute | solution.py:490
  14.7 5.9 %collective-permute-start.2 = (f32[6,16,4,128]{3,2,1,0:T(4,128)S(1)}, f32[6,16,4,128]{3,2,1,0:T(4,128)S(1)}, u32[]{:S(2)}, u32[]{:S(2)}) collective-permute-start(f32[6,16,4,128]{3,2,1,0:T(4,128)S(1)} %collective-permute-done.refs_1_), channel_id=1, source_target_pairs={{0,1},{2,3},{1,0},{3,2},{4,5},{6,7},{5,4},{7,6},{8,9},{10,11},{9,8... | collective-permute-start | bytes 589832 | tf_op jit(solution)/shard_map/ppermute | solution.py:489
  23.1 4.6 %collective-permute-start.5 = (f32[6,6,8,128]{3,2,1,0:T(8,128)S(1)}, f32[6,6,8,128]{3,2,1,0:T(8,128)S(1)}, u32[]{:S(2)}, u32[]{:S(2)}) collective-permute-start(f32[6,6,8,128]{3,2,1,0:T(8,128)S(1)} %get-tuple-element.38), channel_id=1, source_target_pairs={{0,8},{16,24},{8,0},{24,16},{1,9},{17,25},{9,1},{25,17},{2,10},{18... | collective-permute-start | bytes 442376 | tf_op jit(solution)/shard_map/ppermute | solution.py:505
  23.2 4.5 %collective-permute-start.6 = (f32[6,6,8,128]{3,2,1,0:T(8,128)S(1)}, f32[6,6,8,128]{3,2,1,0:T(8,128)S(1)}, u32[]{:S(2)}, u32[]{:S(2)}) collective-permute-start(f32[6,6,8,128]{3,2,1,0:T(8,128)S(1)} %get-tuple-element.39), channel_id=1, source_target_pairs={{8,16},{16,8},{9,17},{17,9},{10,18},{18,10},{11,19},{19,11},{12,20... | collective-permute-start | bytes 442376 | tf_op jit(solution)/shard_map/ppermute | solution.py:506
  47.5 10.0 %collective-permute-start.9 = (f32[4,16,8,128]{3,2,1,0:T(8,128)S(1)}, f32[4,16,8,128]{3,2,1,0:T(8,128)S(1)}, u32[]{:S(2)}, u32[]{:S(2)}) collective-permute-start(f32[4,16,8,128]{3,2,1,0:T(8,128)S(1)} %get-tuple-element.45), channel_id=1, source_target_pairs={{0,8},{8,0},{16,24},{24,16},{1,9},{9,1},{17,25},{25,17},{2,10},{10... | collective-permute-start | bytes 786440 | tf_op jit(solution)/shard_map/ppermute | solution.py:27
  50.4 9.8 %collective-permute-start.7 = (f32[4,16,8,128]{3,2,1,0:T(8,128)S(1)}, f32[4,16,8,128]{3,2,1,0:T(8,128)S(1)}, u32[]{:S(2)}, u32[]{:S(2)}) collective-permute-start(f32[4,16,8,128]{3,2,1,0:T(8,128)S(1)} %get-tuple-element.43), channel_id=1, source_target_pairs={{0,16},{8,24},{16,0},{24,8},{1,17},{9,25},{17,1},{25,9},{2,18},{10... | collective-permute-start | bytes 786440 | tf_op jit(solution)/shard_map/ppermute | solution.py:27
  51.0 12.4 %collective-permute-start.8 = (f32[4,16,8,128]{3,2,1,0:T(8,128)S(1)}, f32[4,16,8,128]{3,2,1,0:T(8,128)S(1)}, u32[]{:S(2)}, u32[]{:S(2)}) collective-permute-start(f32[4,16,8,128]{3,2,1,0:T(8,128)S(1)} %get-tuple-element.44), channel_id=1, source_target_pairs={{0,24},{8,16},{16,8},{24,0},{1,25},{9,17},{17,9},{25,1},{2,26},{10... | collective-permute-start | bytes 786440 | tf_op jit(solution)/shard_map/ppermute | solution.py:27
  67.4 3.1 %collective-permute-start.12 = (f32[8,256]{1,0:T(8,128)S(1)}, f32[8,256]{1,0:T(8,128)S(1)}, u32[]{:S(2)}, u32[]{:S(2)}) collective-permute-start(f32[8,256]{1,0:T(8,128)S(1)} %get-tuple-element.52), channel_id=1, source_target_pairs={{0,24},{8,16},{16,8},{24,0},{1,25},{9,17},{17,9},{25,1},{2,26},{10... | collective-permute-start | bytes 24584 | tf_op jit(solution)/shard_map/ppermute | solution.py:27
  68.7 3.7 %collective-permute-start.11 = (f32[8,256]{1,0:T(8,128)S(1)}, f32[8,256]{1,0:T(8,128)S(1)}, u32[]{:S(2)}, u32[]{:S(2)}) collective-permute-start(f32[8,256]{1,0:T(8,128)S(1)} %get-tuple-element.52), channel_id=1, source_target_pairs={{0,16},{8,24},{16,0},{24,8},{1,17},{9,25},{17,1},{25,9},{2,18},{10... | collective-permute-start | bytes 24584 | tf_op jit(solution)/shard_map/ppermute | solution.py:27
  69.8 2.6 %collective-permute-start.10 = (f32[8,256]{1,0:T(8,128)S(1)}, f32[8,256]{1,0:T(8,128)S(1)}, u32[]{:S(2)}, u32[]{:S(2)}) collective-permute-start(f32[8,256]{1,0:T(8,128)S(1)} %get-tuple-element.52), channel_id=1, source_target_pairs={{0,8},{8,0},{16,24},{24,16},{1,9},{9,1},{17,25},{25,17},{2,10},{10... | collective-permute-start | bytes 24584 | tf_op jit(solution)/shard_map/ppermute | solution.py:27
  72.4 3.7 %collective-permute-start.13 = (f32[8,256]{1,0:T(8,128)S(1)}, f32[8,256]{1,0:T(8,128)S(1)}, u32[]{:S(2)}, u32[]{:S(2)}) collective-permute-start(f32[8,256]{1,0:T(8,128)S(1)} %add_add_fusion.3), channel_id=1, source_target_pairs={{0,4},{4,0},{1,5},{5,1},{2,6},{6,2},{3,7},{7,3},{8,12},{12,8},{9,1... | collective-permute-start | bytes 24584 | tf_op jit(solution)/shard_map/ppermute | solution.py:27
  76.1 6.9 %collective-permute-start.16 = (f32[8,256]{1,0:T(8,128)S(1)}, f32[8,256]{1,0:T(8,128)S(1)}, u32[]{:S(2)}, u32[]{:S(2)}) collective-permute-start(f32[8,256]{1,0:T(8,128)S(1)} %add.51), channel_id=1, source_target_pairs={{0,3},{1,2},{2,1},{3,0},{4,7},{5,6},{6,5},{7,4},{8,11},{9,10},{10,... | collective-permute-start | bytes 24584 | tf_op jit(solution)/shard_map/ppermute | solution.py:27
  78.6 6.0 %collective-permute-start.15 = (f32[8,256]{1,0:T(8,128)S(1)}, f32[8,256]{1,0:T(8,128)S(1)}, u32[]{:S(2)}, u32[]{:S(2)}) collective-permute-start(f32[8,256]{1,0:T(8,128)S(1)} %add.51), channel_id=1, source_target_pairs={{0,2},{1,3},{2,0},{3,1},{4,6},{5,7},{6,4},{7,5},{8,10},{9,11},{10,... | collective-permute-start | bytes 24584 | tf_op jit(solution)/shard_map/ppermute | solution.py:27
  82.9 3.7 %collective-permute-start.14 = (f32[8,256]{1,0:T(8,128)S(1)}, f32[8,256]{1,0:T(8,128)S(1)}, u32[]{:S(2)}, u32[]{:S(2)}) collective-permute-start(f32[8,256]{1,0:T(8,128)S(1)} %add.51), channel_id=1, source_target_pairs={{0,1},{1,0},{2,3},{3,2},{4,5},{5,4},{6,7},{7,6},{8,9},{9,8},{10,11... | collective-permute-start | bytes 24584 | tf_op jit(solution)/shard_map/ppermute | solution.py:27
  86.7 3.1 %collective-permute-start.19 = (f32[8,256]{1,0:T(8,128)S(1)}, f32[8,256]{1,0:T(8,128)S(1)}, u32[]{:S(2)}, u32[]{:S(2)}) collective-permute-start(f32[8,256]{1,0:T(8,128)S(1)} %add_subtract_fusion), channel_id=1, source_target_pairs={{0,24},{8,16},{16,8},{24,0},{1,25},{9,17},{17,9},{25,1},{2,26},{10... | collective-permute-start | bytes 24584 | tf_op jit(solution)/shard_map/ppermute | solution.py:27
  86.7 3.7 %collective-permute-start.18 = (f32[8,256]{1,0:T(8,128)S(1)}, f32[8,256]{1,0:T(8,128)S(1)}, u32[]{:S(2)}, u32[]{:S(2)}) collective-permute-start(f32[8,256]{1,0:T(8,128)S(1)} %add_subtract_fusion), channel_id=1, source_target_pairs={{0,16},{8,24},{16,0},{24,8},{1,17},{9,25},{17,1},{25,9},{2,18},{10... | collective-permute-start | bytes 24584 | tf_op jit(solution)/shard_map/ppermute | solution.py:27
  87.8 2.6 %collective-permute-start.17 = (f32[8,256]{1,0:T(8,128)S(1)}, f32[8,256]{1,0:T(8,128)S(1)}, u32[]{:S(2)}, u32[]{:S(2)}) collective-permute-start(f32[8,256]{1,0:T(8,128)S(1)} %add_subtract_fusion), channel_id=1, source_target_pairs={{0,8},{8,0},{16,24},{24,16},{1,9},{9,1},{17,25},{25,17},{2,10},{10... | collective-permute-start | bytes 24584 | tf_op jit(solution)/shard_map/ppermute | solution.py:27
  90.5 3.7 %collective-permute-start.20 = (f32[8,256]{1,0:T(8,128)S(1)}, f32[8,256]{1,0:T(8,128)S(1)}, u32[]{:S(2)}, u32[]{:S(2)}) collective-permute-start(f32[8,256]{1,0:T(8,128)S(1)} %add_add_fusion.1), channel_id=1, source_target_pairs={{0,4},{4,0},{1,5},{5,1},{2,6},{6,2},{3,7},{7,3},{8,12},{12,8},{9,1... | collective-permute-start | bytes 24584 | tf_op jit(solution)/shard_map/ppermute | solution.py:27
  94.2 5.4 %collective-permute-start.23 = (f32[8,256]{1,0:T(8,128)S(1)}, f32[8,256]{1,0:T(8,128)S(1)}, u32[]{:S(2)}, u32[]{:S(2)}) collective-permute-start(f32[8,256]{1,0:T(8,128)S(1)} %add.59), channel_id=1, source_target_pairs={{0,3},{1,2},{2,1},{3,0},{4,7},{5,6},{6,5},{7,4},{8,11},{9,10},{10,... | collective-permute-start | bytes 24584 | tf_op jit(solution)/shard_map/ppermute | solution.py:27
  96.7 4.5 %collective-permute-start.22 = (f32[8,256]{1,0:T(8,128)S(1)}, f32[8,256]{1,0:T(8,128)S(1)}, u32[]{:S(2)}, u32[]{:S(2)}) collective-permute-start(f32[8,256]{1,0:T(8,128)S(1)} %add.59), channel_id=1, source_target_pairs={{0,2},{1,3},{2,0},{3,1},{4,6},{5,7},{6,4},{7,5},{8,10},{9,11},{10,... | collective-permute-start | bytes 24584 | tf_op jit(solution)/shard_map/ppermute | solution.py:27
  96.7 4.5 %collective-permute-start.21 = (f32[8,256]{1,0:T(8,128)S(1)}, f32[8,256]{1,0:T(8,128)S(1)}, u32[]{:S(2)}, u32[]{:S(2)}) collective-permute-start(f32[8,256]{1,0:T(8,128)S(1)} %add.59), channel_id=1, source_target_pairs={{0,1},{1,0},{2,3},{3,2},{4,5},{5,4},{6,7},{7,6},{8,9},{9,8},{10,11... | collective-permute-start | bytes 24584 | tf_op jit(solution)/shard_map/ppermute | solution.py:27

commit v6 on v5

--- a/solution.py
+++ b/solution.py
@@ -27,22 +27,22 @@
     return lax.ppermute(value, axis, [(i, i ^ flips) for i in range(count)])
 
 
+def copies_over(value, axis):
+    count = lax.axis_size(axis)
+    while count > 4:
+        count //= 2
+        value = value + exchange(value, axis, count)
+    return [value] + [exchange(value, axis, flips) for flips in range(1, count)]
+
+
+def add_up(values):
+    while len(values) > 1:
+        values = [a + b for a, b in zip(values[::2], values[1::2])]
+    return values[0]
+
+
 def sum_over(value, axis):
-    count = lax.axis_size(axis)
-    if count == 4:
-        near, far, other = (exchange(value, axis, flips) for flips in (1, 2, 3))
-        return (value + near) + (far + other)
-    flips = 1
-    while flips < count:
-        value = value + exchange(value, axis, flips)
-        flips *= 2
-    return value
-
-
-def sum_all(value):
-    for axis in ("grp", "gx", "gy"):
-        value = sum_over(value, axis)
-    return value
+    return add_up(copies_over(value, axis))
 
 
 def whole(count):
@@ -295,11 +295,13 @@
     lax.fori_loop(0, spec, leave, 0)
 
 
-def gram_kernel(x, given, basis, *refs):
+def gram_kernel(places, given, basis, *refs):
     total, (out, chunks, held, sems) = refs[:given], refs[given:]
     count, rows, cells_z, modes = chunks.shape
+    halves = count // len(places)
     copies = fetch(
-        [basis.at[0, x, pl.ds(i * rows, rows)] for i in range(count)] + list(total),
+        [basis.at[0, x, pl.ds(i * rows, rows)] for x in places for i in range(halves)]
+        + list(total),
         [chunks.at[i] for i in range(count)] + [held],
         sems,
     )
@@ -317,23 +319,23 @@
     out[...] = acc
 
 
-def gram_part(x, basis, *total):
+def gram_part(places, basis, *total):
     _, _, cells_y, cells_z, modes = basis.shape
-    chunks = 2
-    size = 2 * cells_y * cells_z * modes
+    chunks = 2 * len(places)
+    size = 2 * len(places) * cells_y * cells_z * modes
     return pl.pallas_call(
-        functools.partial(gram_kernel, x, len(total)),
+        functools.partial(gram_kernel, places, len(total)),
         out_shape=jax.ShapeDtypeStruct((modes, modes), jnp.float32),
         in_specs=anywhere(1 + len(total)),
         out_specs=whole(1)[0],
         scratch_shapes=[
-            pltpu.VMEM((chunks, cells_y // chunks, cells_z, modes), jnp.bfloat16),
+            pltpu.VMEM((chunks, cells_y // 2, cells_z, modes), jnp.bfloat16),
             pltpu.VMEM((modes, modes), jnp.float32),
             pltpu.SemaphoreType.DMA((chunks + 1,)),
         ],
         compiler_params=pltpu.CompilerParams(vmem_limit_bytes=BASIS_VMEM),
         cost_estimate=pl.CostEstimate(
-            flops=2 * cells_y * cells_z * modes * modes, bytes_accessed=3 * size, transcendentals=0
+            flops=size * modes, bytes_accessed=3 * size, transcendentals=0
         ),
         name="gram",
     )(basis, *total)
@@ -364,103 +366,48 @@
     return acc
 
 
-def first_kernel(
-    gram_x, part, basis, gram, out_high, out_low, out_gram, held, rows, chunks, total, sems
-):
-    cells_x, cells_y, snaps, cells_z = held.shape
-    modes = rows.shape[-1]
-    sources = [part, *rows_of(basis, 0, cells_z)]
-    targets = [held, *(rows.at[x] for x in range(cells_x))]
-    sources += [basis.at[0, x] for x in gram_x] + [gram]
-    targets += [chunks.at[i] for i in range(len(gram_x))] + [total]
-    start_gram = 1 + cells_x
-    copies = fetch(sources, targets, sems)
-    copies[0].wait()
-    acc = multiply(held, rows, copies[1:], None)
-    out_high[...] = acc[:snaps]
-    out_low[...] = acc[snaps:]
-    acc = None
-    for i in range(len(gram_x)):
-        copies[start_gram + i].wait()
-        chunk = chunks[i].reshape(-1, modes)
-        more = lax.dot_general(
-            chunk, chunk, (((0,), (0,)), ((), ())), preferred_element_type=jnp.float32
-        )
-        acc = more if acc is None else acc + more
-    for copy in copies[start_gram + len(gram_x) :]:
-        copy.wait()
-    out_gram[...] = total[...] if acc is None else acc + total[...]
-
-
-def product_kernel(flips, *refs):
+def product_kernel(flips, given, *refs):
     count = len(flips)
-    parts, refs = refs[:count], refs[count:]
-    basis, high, low, out_high, out_low, held, rows, sums, sems = refs
-    _, cells_x, cells_y, snaps, cells_z = held.shape
+    parts, basis, total = refs[:count], refs[count], refs[count + 1 : count + 1 + given]
+    out, held, rows, sums, sems = refs[count + 1 + given :]
+    cells_x, cells_z = held.shape[1], held.shape[-1]
     sources, targets = [], []
     for i in range(count):
         sources += [parts[i], *rows_of(basis, flips[i], cells_z)]
         targets += [held.at[i], *(rows.at[i, x] for x in range(cells_x))]
-    copies = fetch([*sources, high, low], [*targets, sums.at[0], sums.at[1]], sems)
+    copies = fetch([*sources, *total], [*targets, sums], sems)
     acc = None
     for i in range(count):
         start = i * (cells_x + 1)
         copies[start].wait()
         acc = multiply(held.at[i], rows.at[i], copies[start + 1 :], acc)
-    copies[-2].wait()
-    copies[-1].wait()
-    out_high[...] = acc[:snaps] + sums[0]
-    out_low[...] = acc[snaps:] + sums[1]
-
-
-def first_product(part, basis, gram, gram_x):
-    cells_x, cells_y, snaps, cells_z = part.shape
-    modes = basis.shape[-1]
-    size = 2 * cells_x * cells_y * cells_z * modes
-    out = jax.ShapeDtypeStruct((snaps, modes), jnp.float32)
-    rows = (cells_x, cells_y, cells_z, modes)
-    return pl.pallas_call(
-        functools.partial(first_kernel, gram_x),
-        out_shape=[out, out, jax.ShapeDtypeStruct(gram.shape, jnp.float32)],
-        in_specs=anywhere(3),
-        out_specs=whole(3),
-        scratch_shapes=[
-            pltpu.VMEM(part.shape, jnp.float32),
-            pltpu.VMEM(rows, jnp.bfloat16),
-            pltpu.VMEM((max(len(gram_x), 1), *basis.shape[2:]), jnp.bfloat16),
-            pltpu.VMEM(gram.shape, jnp.float32),
-            pltpu.SemaphoreType.DMA((2 + cells_x + len(gram_x),)),
-        ],
-        compiler_params=pltpu.CompilerParams(vmem_limit_bytes=BASIS_VMEM),
-        cost_estimate=pl.CostEstimate(
-            flops=2 * snaps * size, bytes_accessed=4 * size, transcendentals=0
-        ),
-        name="first_product",
-    )(part, basis, gram)
-
-
-def product(flips, parts, basis, high, low):
+    if total:
+        copies[-1].wait()
+        acc = acc + sums[...]
+    out[...] = acc
+
+
+def product(flips, parts, basis, *total):
     cells_x, cells_y, snaps, cells_z = parts[0].shape
     modes, count = basis.shape[-1], len(flips)
     size = 2 * count * cells_x * cells_y * cells_z * modes
-    out = jax.ShapeDtypeStruct((snaps, modes), jnp.float32)
     return pl.pallas_call(
-        functools.partial(product_kernel, flips),
-        out_shape=(out, out),
-        in_specs=anywhere(3 + count),
-        out_specs=tuple(whole(2)),
+        functools.partial(product_kernel, flips, len(total)),
+        out_shape=jax.ShapeDtypeStruct((2 * snaps, modes), jnp.float32),
+        in_specs=anywhere(1 + count + len(total)),
+        out_specs=whole(1)[0],
         scratch_shapes=[
             pltpu.VMEM((count, *parts[0].shape), jnp.float32),
             pltpu.VMEM((count, cells_x, cells_y, cells_z, modes), jnp.bfloat16),
-            pltpu.VMEM((2, snaps, modes), jnp.float32),
-            pltpu.SemaphoreType.DMA((count * (cells_x + 1) + 2,)),
+            pltpu.VMEM((2 * snaps, modes), jnp.float32),
+            pltpu.SemaphoreType.DMA((count * (cells_x + 1) + 1,)),
         ],
         compiler_params=pltpu.CompilerParams(vmem_limit_bytes=BASIS_VMEM),
         cost_estimate=pl.CostEstimate(
             flops=2 * snaps * size, bytes_accessed=2 * size, transcendentals=0
         ),
         name="product",
-    )(*parts, basis, high, low)
+    )(*parts, basis, *total)
 
 
 def body(terminal, diffusion, velocity, material, rates, stoich, plan, basis):
@@ -484,11 +431,11 @@
         )
     from_a = [lax.ppermute(own, "gy", pairs("gy", 0))]
     from_b = [lax.ppermute(own, "gy", pairs("gy", 1))]
-    gram = gram_part(0, basis)
+    gram = gram_part((0,), basis)
     *blocks, gram = lax.optimization_barrier((*blocks, gram))
     from_a += [lax.ppermute(b, "gy", pairs("gy", 0)) for b in blocks[1:]]
     from_b += [lax.ppermute(b, "gy", pairs("gy", 1)) for b in blocks[1:]]
-    gram = gram_part(1, basis, gram)
+    gram = gram_part(tuple(range(1, cells_x - 1)), basis, gram)
     blocks = blocks + from_a + from_b
     *blocks, gram = lax.optimization_barrier((*blocks, gram))
     packed = jax.ShapeDtypeStruct((fields, 3 * cells_y // GROUPS, all_x, LANES), jnp.float32)
@@ -504,8 +451,9 @@
     )(*blocks)
     side_a = lax.ppermute(edge_a, "grp", pairs("grp", 0))
     side_b = lax.ppermute(edge_b, "grp", pairs("grp", 1))
-    gram = gram_part(2, basis, gram)
+    gram = gram_part((cells_x - 1,), basis, gram)
     side_a, side_b, gram = lax.optimization_barrier((side_a, side_b, gram))
+    grams = copies_over(gram, "grp")
 
     part = jax.ShapeDtypeStruct((cells_x, cells_y, snaps, cells_z), jnp.float32)
     room = (depth, all_x, wide)
@@ -518,20 +466,35 @@
         scratch_shapes=[pltpu.VMEM(shape, jnp.float32) for shape in shapes]
         + [pltpu.SemaphoreType.DMA((len(blocks) + 2,))],
         compiler_params=vmem(*shapes, terminal.shape, (count_grp, *part.shape)),
+        cost_estimate=pl.CostEstimate(
+            flops=0,
+            bytes_accessed=2 * STEPS * spec * (spec + 2) * math.prod(room),
+            transcendentals=0,
+        ),
         name="steps",
     )(plan, diffusion, stoich, rates, *blocks, side_a, side_b)
 
     order = sorted(range(1, count_grp), key=lambda flips: -flips)
     moved = {flips: exchange(kept[flips], "grp", flips) for flips in order}
-    high, low, gram = first_product(kept[0], basis, gram, tuple(range(3, cells_x)))
+    mine, *grams = lax.optimization_barrier((kept[0], *grams))
+    mine, gram = lax.optimization_barrier((mine, add_up(grams)))
+    grams = copies_over(gram, "gy")
+    total = product((0,), [mine], basis)
     for flips in ((1,), tuple(range(2, count_grp))):
-        high, low = product(flips, [moved[f] for f in flips], basis, high, low)
-
-    first = sum_all(high)
+        total = product(flips, [moved[f] for f in flips], basis, total)
+
+    total = sum_over(total, "grp")
+    total, *grams = lax.optimization_barrier((total, *grams))
+    total = copies_over(total, "gy")
+    high = add_up([part[:snaps] for part in total])
+    low = add_up([part[snaps:] for part in total])
+    first = sum_over(high, "gx")
     taken = jnp.dot(
-        first.astype(jnp.bfloat16).astype(jnp.float32), gram, precision=lax.Precision.HIGHEST
+        first.astype(jnp.bfloat16).astype(jnp.float32),
+        add_up(grams),
+        precision=lax.Precision.HIGHEST,
     )
-    second = sum_all(high + low - taken)
+    second = sum_over(high + low - taken, "gx")
     return (first + second, final)
 
 

time: 102 us -> 100 us (0.980)
  waiting for transfers between devices: 20.5 us -> 18.6 us
    ppermute x17, waiting for transfers between devices: 20 us -> 18.6 us  [exchange(): return lax.ppermute(value, axis, [(i, i ^ flips) for i in range(count)])]
  transfers between devices with their start and end apart: 24 -> 24, of which waited for: 12 -> 9; matrix products, arithmetic and copies ran while one was open for 0% -> 0% of each run, Pallas kernels for 19% -> 43%
where the time goes in v6:
time: 100 us; the launch traced here: 99.8 us
  Pallas kernels  47.4 us (47%)
  starting transfers between devices  31.9 us (32%)
  waiting for transfers between devices  18.6 us (19%)
    ppermute x17, starting transfers between devices, exchange(): return lax.ppermute(value, axis, [(i, i ^ flips) for i in range(count)])  20.5 us
    pallas_call x1, Pallas kernels, body(): pl.pallas_call(functools.partial(steps_kernel, count_x), out_shape=[jax.S...  19.7 us
    ppermute x17, waiting for transfers between devices, exchange(): return lax.ppermute(value, axis, [(i, i ^ flips) for i in range(count)])  18.6 us
    pallas_call x3, Pallas kernels, gram_part(): pl.pallas_call(functools.partial(gram_kernel, places, len(total)), out_sh...  14.1 us
    pallas_call x3, Pallas kernels, product(): pl.pallas_call(functools.partial(product_kernel, flips, len(total)), out_...  9.25 us
    ppermute x1, starting transfers between devices, body(): from_a = [lax.ppermute(own, 'gy', pairs('gy', 0))]  4.45 us
    ppermute x1, starting transfers between devices, body(): lax.ppermute(own, 'gx', [(i, (i - shift) % count_x) for i in range(count_...  2.94 us
    pallas_call x1, Pallas kernels, body(): pl.pallas_call(functools.partial(edges_kernel, count_x), out_shape=(packe...  2.56 us
  transfers between devices with their start and end apart: 24, of which 9 were waited for; matrix products, arithmetic and copies ran while one was open for 0% of the time, Pallas kernels for 43%

profile of v6, /device:TPU:0, one launch (start us, length us, event | category | flops | bytes accessed | tf_op | source)
XLA Modules:
  0.0 99.8 jit_solution(12184707047263610018)
XLA Ops:
  0.6 1.7 %pack.1.refs_0_ = f32[6,16,4,128]{3,2,1,0:T(4,128)} custom-call(f32[4,4,16,128]{3,2,1,0:T(8,128)} %terminal.1, f32[4,16,128]{2,1,0:T(8,128)} %velocity.1, s32[4,16,128]{2,1,0:T(8,128)} %material.1), custom_call_target="tpu_custom_call" | custom-call | tf_op jit(solution)/shard_map/pack/pallas_call | solution.py:420
  2.4 2.9 %collective-permute-start = (f32[6,16,4,128]{3,2,1,0:T(4,128)}, f32[6,16,4,128]{3,2,1,0:T(4,128)S(1)}, u32[]{:S(2)}, u32[]{:S(2)}) collective-permute-start(f32[6,16,4,128]{3,2,1,0:T(4,128)} %pack.1.refs_0_), channel_id=1, source_target_pairs={{0,4},{4,0},{1,5},{5,1},{2,6},{6,2},{3,7},{7,3},{8,12},{12,8},{9,1... | collective-permute-start | bytes 589832 | tf_op jit(solution)/shard_map/ppermute | solution.py:430
  5.3 0.7 collective-permute-start.3
  6.0 4.5 %collective-permute-start.1 = (f32[6,16,4,128]{3,2,1,0:T(4,128)}, f32[6,16,4,128]{3,2,1,0:T(4,128)S(1)}, u32[]{:S(2)}, u32[]{:S(2)}) collective-permute-start(f32[6,16,4,128]{3,2,1,0:T(4,128)} %pack.1.refs_0_), channel_id=1, source_target_pairs={{0,1},{2,3},{1,0},{3,2},{4,5},{6,7},{5,4},{7,6},{8,9},{10,11},{9,8... | collective-permute-start | bytes 589832 | tf_op jit(solution)/shard_map/ppermute | solution.py:432
  10.4 3.5 %gram.3.refs_0_ = f32[256,256]{1,0:T(8,128)S(1)} custom-call(bf16[1,4,16,512,256]{4,3,2,1,0:T(8,128)(2,1)} %refs_2_.1), custom_call_target="tpu_custom_call" | custom-call | flops 1073741824 | bytes 12582912 | tf_op jit(solution)/shard_map/gram/pallas_call | solution.py:326
  14.0 0.0 copy-start.4
  14.0 0.0 copy-start.1
  14.0 0.0 copy-start.2
  14.0 0.0 copy-start.3
  14.0 0.7 collective-permute-start.4
  14.7 1.8 %collective-permute-start.2 = (f32[6,16,4,128]{3,2,1,0:T(4,128)S(1)}, f32[6,16,4,128]{3,2,1,0:T(4,128)S(1)}, u32[]{:S(2)}, u32[]{:S(2)}) collective-permute-start(f32[6,16,4,128]{3,2,1,0:T(4,128)S(1)} %collective-permute-done.refs_1_), channel_id=1, source_target_pairs={{0,1},{2,3},{1,0},{3,2},{4,5},{6,7},{5,4},{7,6},{8,9},{10,11},{9,8... | collective-permute-start | bytes 589832 | tf_op jit(solution)/shard_map/ppermute | solution.py:436
  16.5 7.0 %gram.4.refs_0_ = f32[256,256]{1,0:T(8,128)S(1)} custom-call(bf16[1,4,16,512,256]{4,3,2,1,0:T(8,128)(2,1)} %refs_2_.1, f32[256,256]{1,0:T(8,128)S(1)} %gram.3.refs_0_), custom_call_target="tpu_custom_call" | custom-call | flops 2147483648 | bytes 25165824 | tf_op jit(solution)/shard_map/gram/pallas_call | solution.py:326
  23.5 2.6 %edges.1 = (f32[6,6,8,128]{3,2,1,0:T(8,128)S(1)}, f32[6,6,8,128]{3,2,1,0:T(8,128)S(1)}) custom-call(f32[6,16,4,128]{3,2,1,0:T(4,128)S(1)} %copy-done, f32[6,16,4,128]{3,2,1,0:T(4,128)S(1)} %collective-permute-done.refs_1_, f32[6,16,4,128]{3,2,1,0:T(4,128)S(1)} %collective-permute-done.1.refs_2_, f32[6,16,4,128]{3,2,1,0:T(4,128)S(1)} %collective-permute-done.2.refs_3_, ...), custom_call_target="tpu_custom_call" | custom-call | tf_op jit(solution)/shard_map/edges/pallas_call | solution.py:443
  26.1 0.1 collective-permute-start.5
  26.2 0.9 collective-permute-start.6
  27.0 3.6 %gram.5 = f32[256,256]{1,0:T(8,128)S(1)} custom-call(bf16[1,4,16,512,256]{4,3,2,1,0:T(8,128)(2,1)} %refs_2_.1, f32[256,256]{1,0:T(8,128)S(1)} %gram.4.refs_0_), custom_call_target="tpu_custom_call" | custom-call | flops 1073741824 | bytes 12582912 | tf_op jit(solution)/shard_map/gram/pallas_call | solution.py:326
  30.6 1.7 %collective-permute-start.12 = (f32[256,256]{1,0:T(8,128)S(1)}, f32[256,256]{1,0:T(8,128)S(1)}, u32[]{:S(2)}, u32[]{:S(2)}) collective-permute-start(f32[256,256]{1,0:T(8,128)S(1)} %gram.5), channel_id=1, source_target_pairs={{0,24},{8,16},{16,8},{24,0},{1,25},{9,17},{17,9},{25,1},{2,26},{10... | collective-permute-start | bytes 786440 | tf_op jit(solution)/shard_map/ppermute | solution.py:27
  32.3 2.9 %collective-permute-start.11 = (f32[256,256]{1,0:T(8,128)S(1)}, f32[256,256]{1,0:T(8,128)S(1)}, u32[]{:S(2)}, u32[]{:S(2)}) collective-permute-start(f32[256,256]{1,0:T(8,128)S(1)} %gram.5), channel_id=1, source_target_pairs={{0,16},{8,24},{16,0},{24,8},{1,17},{9,25},{17,1},{25,9},{2,18},{10... | collective-permute-start | bytes 786440 | tf_op jit(solution)/shard_map/ppermute | solution.py:27
  35.2 0.1 copy.10.stoich
  35.3 19.7 %steps.1 = (f32[4,4,16,128]{3,2,1,0:T(8,128)}, f32[4,16,8,128]{3,2,1,0:T(8,128)S(1)}, f32[4,16,8,128]{3,2,1,0:T(8,128)S(1)}, f32[4,16,8,128]{3,2,1,0:T(8,128)S(1)}, f32[4,16,8,128]{3,2,1,0:T(8,128)S(1)}) custom-call(s32[8]{0:T(128)S(1)} %copy-done.2, f32[4]{0:T(128)S(1)} %copy-done.3, s32[8,4]{1,0:T(8,128)S(1)} %copy.10.stoich, f32[8,8]{1,0:T(8,128)S(1)} %copy-done.1, ...), custom_call_target="tpu_custom_call" | custom-call | bytes 100663296 | tf_op jit(solution)/shard_map/steps/pallas_call | solution.py:461
  55.0 0.9 collective-permute-start.7
  55.9 1.0 %collective-permute-start.8 = (f32[4,16,8,128]{3,2,1,0:T(8,128)S(1)}, f32[4,16,8,128]{3,2,1,0:T(8,128)S(1)}, u32[]{:S(2)}, u32[]{:S(2)}) collective-permute-start(f32[4,16,8,128]{3,2,1,0:T(8,128)S(1)} %get-tuple-element.49), channel_id=1, source_target_pairs={{0,24},{8,16},{16,8},{24,0},{1,25},{9,17},{17,9},{25,1},{2,26},{10... | collective-permute-start | bytes 786440 | tf_op jit(solution)/shard_map/ppermute | solution.py:27
  56.9 0.3 collective-permute-start.9
  57.2 0.1 add_add_fusion
  57.3 2.5 %collective-permute-start.18 = (f32[256,256]{1,0:T(8,128)S(1)}, f32[256,256]{1,0:T(8,128)S(1)}, u32[]{:S(2)}, u32[]{:S(2)}) collective-permute-start(f32[256,256]{1,0:T(8,128)S(1)} %add_add_fusion), channel_id=1, source_target_pairs={{0,3},{1,2},{2,1},{3,0},{4,7},{5,6},{6,5},{7,4},{8,11},{9,10},{10,... | collective-permute-start | bytes 786440 | tf_op jit(solution)/shard_map/ppermute | solution.py:27
  59.9 2.9 %collective-permute-start.17 = (f32[256,256]{1,0:T(8,128)S(1)}, f32[256,256]{1,0:T(8,128)S(1)}, u32[]{:S(2)}, u32[]{:S(2)}) collective-permute-start(f32[256,256]{1,0:T(8,128)S(1)} %add_add_fusion), channel_id=1, source_target_pairs={{0,2},{1,3},{2,0},{3,1},{4,6},{5,7},{6,4},{7,5},{8,10},{9,11},{10,... | collective-permute-start | bytes 786440 | tf_op jit(solution)/shard_map/ppermute | solution.py:27
  62.8 2.7 %product.3.refs_2_ = f32[16,256]{1,0:T(8,128)S(1)} custom-call(f32[4,16,8,128]{3,2,1,0:T(8,128)S(1)} %get-tuple-element.58.refs_0_, bf16[1,4,16,512,256]{4,3,2,1,0:T(8,128)(2,1)} %refs_2_.1), custom_call_target="tpu_custom_call" | custom-call | flops 67108864 | bytes 8388608 | tf_op jit(solution)/shard_map/product/pallas_call | solution.py:394
  65.4 0.1 collective-permute-start.16
  65.5 2.7 %product.4.refs_3_ = f32[16,256]{1,0:T(8,128)S(1)} custom-call(f32[4,16,8,128]{3,2,1,0:T(8,128)S(1)} %collective-permute-done.9.refs_0_, bf16[1,4,16,512,256]{4,3,2,1,0:T(8,128)(2,1)} %refs_2_.1, f32[16,256]{1,0:T(8,128)S(1)} %product.3.refs_2_), custom_call_target="tpu_custom_call" | custom-call | flops 67108864 | bytes 8388608 | tf_op jit(solution)/shard_map/product/pallas_call | solution.py:394
  68.2 0.8 collective-permute-done.8.refs_1_
  69.0 3.9 %product.5 = f32[16,256]{1,0:T(8,128)S(1)} custom-call(f32[4,16,8,128]{3,2,1,0:T(8,128)S(1)} %collective-permute-done.7.refs_0_, f32[4,16,8,128]{3,2,1,0:T(8,128)S(1)} %collective-permute-done.8.refs_1_, bf16[1,4,16,512,256]{4,3,2,1,0:T(8,128)(2,1)} %refs_2_.1, f32[16,256]{1,0:T(8,128)S(1)} %product.4.refs_3_), custom_call_target="tpu_custom_call" | custom-call | flops 134217728 | bytes 16777216 | tf_op jit(solution)/shard_map/product/pallas_call | solution.py:394
  73.0 0.2 collective-permute-start.15
  73.1 2.0 %collective-permute-start.14 = (f32[16,256]{1,0:T(8,128)S(1)}, f32[16,256]{1,0:T(8,128)S(1)}, u32[]{:S(2)}, u32[]{:S(2)}) collective-permute-start(f32[16,256]{1,0:T(8,128)S(1)} %product.5), channel_id=1, source_target_pairs={{0,16},{8,24},{16,0},{24,8},{1,17},{9,25},{17,1},{25,9},{2,18},{10... | collective-permute-start | bytes 49160 | tf_op jit(solution)/shard_map/ppermute | solution.py:27
  75.2 1.0 %collective-permute-done.15 = f32[16,256]{1,0:T(8,128)S(1)} collective-permute-done((f32[16,256]{1,0:T(8,128)S(1)}, f32[16,256]{1,0:T(8,128)S(1)}, u32[]{:S(2)}, u32[]{:S(2)}) %collective-permute-start.15) | collective-permute-done | bytes 16416 | tf_op jit(solution)/shard_map/ppermute | solution.py:27
  76.2 0.5 collective-permute-start.13
  76.7 0.4 collective-permute-done.14
  77.0 0.5 collective-permute-done.13
  77.5 6.9 %collective-permute-done.17 = f32[256,256]{1,0:T(8,128)S(1)} collective-permute-done((f32[256,256]{1,0:T(8,128)S(1)}, f32[256,256]{1,0:T(8,128)S(1)}, u32[]{:S(2)}, u32[]{:S(2)}) %collective-permute-start.17) | collective-permute-done | bytes 262176 | tf_op jit(solution)/shard_map/ppermute | solution.py:27
  84.5 2.5 %collective-permute-start.21 = (f32[16,256]{1,0:T(8,128)S(1)}, f32[16,256]{1,0:T(8,128)S(1)}, u32[]{:S(2)}, u32[]{:S(2)}) collective-permute-start(f32[16,256]{1,0:T(8,128)S(1)} %add_add_fusion.1), channel_id=1, source_target_pairs={{0,3},{1,2},{2,1},{3,0},{4,7},{5,6},{6,5},{7,4},{8,11},{9,10},{10,... | collective-permute-start | bytes 49160 | tf_op jit(solution)/shard_map/ppermute | solution.py:27
  87.0 1.9 %collective-permute-start.19 = (f32[16,256]{1,0:T(8,128)S(1)}, f32[16,256]{1,0:T(8,128)S(1)}, u32[]{:S(2)}, u32[]{:S(2)}) collective-permute-start(f32[16,256]{1,0:T(8,128)S(1)} %add_add_fusion.1), channel_id=1, source_target_pairs={{0,1},{1,0},{2,3},{3,2},{4,5},{5,4},{6,7},{7,6},{8,9},{9,8},{10,11... | collective-permute-start | bytes 49160 | tf_op jit(solution)/shard_map/ppermute | solution.py:27
  88.9 1.1 %collective-permute-done.21 = f32[16,256]{1,0:T(8,128)S(1)} collective-permute-done((f32[16,256]{1,0:T(8,128)S(1)}, f32[16,256]{1,0:T(8,128)S(1)}, u32[]{:S(2)}, u32[]{:S(2)}) %collective-permute-start.21) | collective-permute-done | bytes 16416 | tf_op jit(solution)/shard_map/ppermute | solution.py:27
  90.0 1.6 %collective-permute-done.20 = f32[16,256]{1,0:T(8,128)S(1)} collective-permute-done((f32[16,256]{1,0:T(8,128)S(1)}, f32[16,256]{1,0:T(8,128)S(1)}, u32[]{:S(2)}, u32[]{:S(2)}) %collective-permute-start.20) | collective-permute-done | bytes 16416 | tf_op jit(solution)/shard_map/ppermute | solution.py:27
  91.6 0.6 collective-permute-start.22
  92.2 3.1 %collective-permute-done.22 = f32[8,256]{1,0:T(8,128)S(1)} collective-permute-done((f32[8,256]{1,0:T(8,128)S(1)}, f32[8,256]{1,0:T(8,128)S(1)}, u32[]{:S(2)}, u32[]{:S(2)}) %collective-permute-start.22) | collective-permute-done | bytes 8224 | tf_op jit(solution)/shard_map/ppermute | solution.py:27
  95.3 0.2 fusion.6
  95.6 0.5 collective-permute-start.23
  96.1 3.1 %collective-permute-done.23 = f32[8,256]{1,0:T(8,128)S(1)} collective-permute-done((f32[8,256]{1,0:T(8,128)S(1)}, f32[8,256]{1,0:T(8,128)S(1)}, u32[]{:S(2)}, u32[]{:S(2)}) %collective-permute-start.23) | collective-permute-done | bytes 8224 | tf_op jit(solution)/shard_map/ppermute | solution.py:27
  99.2 0.6 add_add_fusion.2
  (26 shorter events, 0.1 us)
Async XLA Ops:
  2.4 21.2 %copy-start = (f32[6,16,4,128]{3,2,1,0:T(4,128)S(1)}, f32[6,16,4,128]{3,2,1,0:T(4,128)}, u32[]{:S(2)}) copy-start(f32[6,16,4,128]{3,2,1,0:T(4,128)} %pack.1.refs_0_) | copy-start | bytes 589828
  2.4 11.7 %collective-permute-start = (f32[6,16,4,128]{3,2,1,0:T(4,128)}, f32[6,16,4,128]{3,2,1,0:T(4,128)S(1)}, u32[]{:S(2)}, u32[]{:S(2)}) collective-permute-start(f32[6,16,4,128]{3,2,1,0:T(4,128)} %pack.1.refs_0_), channel_id=1, source_target_pairs={{0,4},{4,0},{1,5},{5,1},{2,6},{6,2},{3,7},{7,3},{8,12},{12,8},{9,1... | collective-permute-start | bytes 589832 | tf_op jit(solution)/shard_map/ppermute | solution.py:430
  5.3 18.2 %collective-permute-start.3 = (f32[6,16,4,128]{3,2,1,0:T(4,128)}, f32[6,16,4,128]{3,2,1,0:T(4,128)S(1)}, u32[]{:S(2)}, u32[]{:S(2)}) collective-permute-start(f32[6,16,4,128]{3,2,1,0:T(4,128)} %pack.1.refs_0_), channel_id=1, source_target_pairs={{1,2},{2,1},{5,6},{6,5},{9,10},{10,9},{13,14},{14,13},{17,18},{18,... | collective-permute-start | bytes 589832 | tf_op jit(solution)/shard_map/ppermute | solution.py:433
  6.0 17.5 %collective-permute-start.1 = (f32[6,16,4,128]{3,2,1,0:T(4,128)}, f32[6,16,4,128]{3,2,1,0:T(4,128)S(1)}, u32[]{:S(2)}, u32[]{:S(2)}) collective-permute-start(f32[6,16,4,128]{3,2,1,0:T(4,128)} %pack.1.refs_0_), channel_id=1, source_target_pairs={{0,1},{2,3},{1,0},{3,2},{4,5},{6,7},{5,4},{7,6},{8,9},{10,11},{9,8... | collective-permute-start | bytes 589832 | tf_op jit(solution)/shard_map/ppermute | solution.py:432
  14.0 21.2 %copy-start.4 = (s32[8,4]{0,1:T(4,128)S(1)}, s32[8,4]{0,1:T(4,128)}, u32[]{:S(2)}) copy-start(s32[8,4]{0,1:T(4,128)} %param.13) | copy-start | bytes 388
  14.0 21.3 %copy-start.1 = (f32[8,8]{1,0:T(8,128)S(1)}, f32[8,8]{1,0:T(8,128)}, u32[]{:S(2)}) copy-start(f32[8,8]{1,0:T(8,128)} %rates.1) | copy-start | bytes 772
  14.0 21.3 %copy-start.2 = (s32[8]{0:T(128)S(1)}, s32[8]{0:T(128)}, u32[]{:S(2)}) copy-start(s32[8]{0:T(128)} %plan.1) | copy-start | bytes 100
  14.0 21.3 %copy-start.3 = (f32[4]{0:T(128)S(1)}, f32[4]{0:T(128)}, u32[]{:S(2)}) copy-start(f32[4]{0:T(128)} %diffusion.1) | copy-start | bytes 52
  14.0 9.5 %collective-permute-start.4 = (f32[6,16,4,128]{3,2,1,0:T(4,128)S(1)}, f32[6,16,4,128]{3,2,1,0:T(4,128)S(1)}, u32[]{:S(2)}, u32[]{:S(2)}) collective-permute-start(f32[6,16,4,128]{3,2,1,0:T(4,128)S(1)} %collective-permute-done.refs_1_), channel_id=1, source_target_pairs={{1,2},{2,1},{5,6},{6,5},{9,10},{10,9},{13,14},{14,13},{17,18},{18,... | collective-permute-start | bytes 589832 | tf_op jit(solution)/shard_map/ppermute | solution.py:437
  14.7 8.8 %collective-permute-start.2 = (f32[6,16,4,128]{3,2,1,0:T(4,128)S(1)}, f32[6,16,4,128]{3,2,1,0:T(4,128)S(1)}, u32[]{:S(2)}, u32[]{:S(2)}) collective-permute-start(f32[6,16,4,128]{3,2,1,0:T(4,128)S(1)} %collective-permute-done.refs_1_), channel_id=1, source_target_pairs={{0,1},{2,3},{1,0},{3,2},{4,5},{6,7},{5,4},{7,6},{8,9},{10,11},{9,8... | collective-permute-start | bytes 589832 | tf_op jit(solution)/shard_map/ppermute | solution.py:436
  26.1 4.5 %collective-permute-start.5 = (f32[6,6,8,128]{3,2,1,0:T(8,128)S(1)}, f32[6,6,8,128]{3,2,1,0:T(8,128)S(1)}, u32[]{:S(2)}, u32[]{:S(2)}) collective-permute-start(f32[6,6,8,128]{3,2,1,0:T(8,128)S(1)} %get-tuple-element.43), channel_id=1, source_target_pairs={{0,8},{16,24},{8,0},{24,16},{1,9},{17,25},{9,1},{25,17},{2,10},{18... | collective-permute-start | bytes 442376 | tf_op jit(solution)/shard_map/ppermute | solution.py:452
  26.2 4.5 %collective-permute-start.6 = (f32[6,6,8,128]{3,2,1,0:T(8,128)S(1)}, f32[6,6,8,128]{3,2,1,0:T(8,128)S(1)}, u32[]{:S(2)}, u32[]{:S(2)}) collective-permute-start(f32[6,6,8,128]{3,2,1,0:T(8,128)S(1)} %get-tuple-element.44), channel_id=1, source_target_pairs={{8,16},{16,8},{9,17},{17,9},{10,18},{18,10},{11,19},{19,11},{12,20... | collective-permute-start | bytes 442376 | tf_op jit(solution)/shard_map/ppermute | solution.py:453
  30.6 26.3 %collective-permute-start.12 = (f32[256,256]{1,0:T(8,128)S(1)}, f32[256,256]{1,0:T(8,128)S(1)}, u32[]{:S(2)}, u32[]{:S(2)}) collective-permute-start(f32[256,256]{1,0:T(8,128)S(1)} %gram.5), channel_id=1, source_target_pairs={{0,24},{8,16},{16,8},{24,0},{1,25},{9,17},{17,9},{25,1},{2,26},{10... | collective-permute-start | bytes 786440 | tf_op jit(solution)/shard_map/ppermute | solution.py:27
  32.3 24.9 %collective-permute-start.11 = (f32[256,256]{1,0:T(8,128)S(1)}, f32[256,256]{1,0:T(8,128)S(1)}, u32[]{:S(2)}, u32[]{:S(2)}) collective-permute-start(f32[256,256]{1,0:T(8,128)S(1)} %gram.5), channel_id=1, source_target_pairs={{0,16},{8,24},{16,0},{24,8},{1,17},{9,25},{17,1},{25,9},{2,18},{10... | collective-permute-start | bytes 786440 | tf_op jit(solution)/shard_map/ppermute | solution.py:27
  35.2 22.0 %collective-permute-start.10 = (f32[256,256]{1,0:T(8,128)S(1)}, f32[256,256]{1,0:T(8,128)S(1)}, u32[]{:S(2)}, u32[]{:S(2)}) collective-permute-start(f32[256,256]{1,0:T(8,128)S(1)} %gram.5), channel_id=1, source_target_pairs={{0,8},{8,0},{16,24},{24,16},{1,9},{9,1},{17,25},{25,17},{2,10},{10... | collective-permute-start | bytes 786440 | tf_op jit(solution)/shard_map/ppermute | solution.py:27
  55.0 13.2 %collective-permute-start.7 = (f32[4,16,8,128]{3,2,1,0:T(8,128)S(1)}, f32[4,16,8,128]{3,2,1,0:T(8,128)S(1)}, u32[]{:S(2)}, u32[]{:S(2)}) collective-permute-start(f32[4,16,8,128]{3,2,1,0:T(8,128)S(1)} %get-tuple-element.48), channel_id=1, source_target_pairs={{0,16},{8,24},{16,0},{24,8},{1,17},{9,25},{17,1},{25,9},{2,18},{10... | collective-permute-start | bytes 786440 | tf_op jit(solution)/shard_map/ppermute | solution.py:27
  55.9 13.1 %collective-permute-start.8 = (f32[4,16,8,128]{3,2,1,0:T(8,128)S(1)}, f32[4,16,8,128]{3,2,1,0:T(8,128)S(1)}, u32[]{:S(2)}, u32[]{:S(2)}) collective-permute-start(f32[4,16,8,128]{3,2,1,0:T(8,128)S(1)} %get-tuple-element.49), channel_id=1, source_target_pairs={{0,24},{8,16},{16,8},{24,0},{1,25},{9,17},{17,9},{25,1},{2,26},{10... | collective-permute-start | bytes 786440 | tf_op jit(solution)/shard_map/ppermute | solution.py:27
  56.9 8.5 %collective-permute-start.9 = (f32[4,16,8,128]{3,2,1,0:T(8,128)S(1)}, f32[4,16,8,128]{3,2,1,0:T(8,128)S(1)}, u32[]{:S(2)}, u32[]{:S(2)}) collective-permute-start(f32[4,16,8,128]{3,2,1,0:T(8,128)S(1)} %get-tuple-element.50), channel_id=1, source_target_pairs={{0,8},{8,0},{16,24},{24,16},{1,9},{9,1},{17,25},{25,17},{2,10},{10... | collective-permute-start | bytes 786440 | tf_op jit(solution)/shard_map/ppermute | solution.py:27
  57.3 20.2 %collective-permute-start.18 = (f32[256,256]{1,0:T(8,128)S(1)}, f32[256,256]{1,0:T(8,128)S(1)}, u32[]{:S(2)}, u32[]{:S(2)}) collective-permute-start(f32[256,256]{1,0:T(8,128)S(1)} %add_add_fusion), channel_id=1, source_target_pairs={{0,3},{1,2},{2,1},{3,0},{4,7},{5,6},{6,5},{7,4},{8,11},{9,10},{10,... | collective-permute-start | bytes 786440 | tf_op jit(solution)/shard_map/ppermute | solution.py:27
  59.9 24.6 %collective-permute-start.17 = (f32[256,256]{1,0:T(8,128)S(1)}, f32[256,256]{1,0:T(8,128)S(1)}, u32[]{:S(2)}, u32[]{:S(2)}) collective-permute-start(f32[256,256]{1,0:T(8,128)S(1)} %add_add_fusion), channel_id=1, source_target_pairs={{0,2},{1,3},{2,0},{3,1},{4,6},{5,7},{6,4},{7,5},{8,10},{9,11},{10,... | collective-permute-start | bytes 786440 | tf_op jit(solution)/shard_map/ppermute | solution.py:27
  65.4 19.0 %collective-permute-start.16 = (f32[256,256]{1,0:T(8,128)S(1)}, f32[256,256]{1,0:T(8,128)S(1)}, u32[]{:S(2)}, u32[]{:S(2)}) collective-permute-start(f32[256,256]{1,0:T(8,128)S(1)} %add_add_fusion), channel_id=1, source_target_pairs={{0,1},{1,0},{2,3},{3,2},{4,5},{5,4},{6,7},{7,6},{8,9},{9,8},{10,11... | collective-permute-start | bytes 786440 | tf_op jit(solution)/shard_map/ppermute | solution.py:27
  73.0 3.2 %collective-permute-start.15 = (f32[16,256]{1,0:T(8,128)S(1)}, f32[16,256]{1,0:T(8,128)S(1)}, u32[]{:S(2)}, u32[]{:S(2)}) collective-permute-start(f32[16,256]{1,0:T(8,128)S(1)} %product.5), channel_id=1, source_target_pairs={{0,24},{8,16},{16,8},{24,0},{1,25},{9,17},{17,9},{25,1},{2,26},{10... | collective-permute-start | bytes 49160 | tf_op jit(solution)/shard_map/ppermute | solution.py:27
  73.1 3.9 %collective-permute-start.14 = (f32[16,256]{1,0:T(8,128)S(1)}, f32[16,256]{1,0:T(8,128)S(1)}, u32[]{:S(2)}, u32[]{:S(2)}) collective-permute-start(f32[16,256]{1,0:T(8,128)S(1)} %product.5), channel_id=1, source_target_pairs={{0,16},{8,24},{16,0},{24,8},{1,17},{9,25},{17,1},{25,9},{2,18},{10... | collective-permute-start | bytes 49160 | tf_op jit(solution)/shard_map/ppermute | solution.py:27
  76.2 1.3 %collective-permute-start.13 = (f32[16,256]{1,0:T(8,128)S(1)}, f32[16,256]{1,0:T(8,128)S(1)}, u32[]{:S(2)}, u32[]{:S(2)}) collective-permute-start(f32[16,256]{1,0:T(8,128)S(1)} %product.5), channel_id=1, source_target_pairs={{0,8},{8,0},{16,24},{24,16},{1,9},{9,1},{17,25},{25,17},{2,10},{10... | collective-permute-start | bytes 49160 | tf_op jit(solution)/shard_map/ppermute | solution.py:27
  84.5 5.5 %collective-permute-start.21 = (f32[16,256]{1,0:T(8,128)S(1)}, f32[16,256]{1,0:T(8,128)S(1)}, u32[]{:S(2)}, u32[]{:S(2)}) collective-permute-start(f32[16,256]{1,0:T(8,128)S(1)} %add_add_fusion.1), channel_id=1, source_target_pairs={{0,3},{1,2},{2,1},{3,0},{4,7},{5,6},{6,5},{7,4},{8,11},{9,10},{10,... | collective-permute-start | bytes 49160 | tf_op jit(solution)/shard_map/ppermute | solution.py:27
  87.0 4.6 %collective-permute-start.20 = (f32[16,256]{1,0:T(8,128)S(1)}, f32[16,256]{1,0:T(8,128)S(1)}, u32[]{:S(2)}, u32[]{:S(2)}) collective-permute-start(f32[16,256]{1,0:T(8,128)S(1)} %add_add_fusion.1), channel_id=1, source_target_pairs={{0,2},{1,3},{2,0},{3,1},{4,6},{5,7},{6,4},{7,5},{8,10},{9,11},{10,... | collective-permute-start | bytes 49160 | tf_op jit(solution)/shard_map/ppermute | solution.py:27
  87.0 4.6 %collective-permute-start.19 = (f32[16,256]{1,0:T(8,128)S(1)}, f32[16,256]{1,0:T(8,128)S(1)}, u32[]{:S(2)}, u32[]{:S(2)}) collective-permute-start(f32[16,256]{1,0:T(8,128)S(1)} %add_add_fusion.1), channel_id=1, source_target_pairs={{0,1},{1,0},{2,3},{3,2},{4,5},{5,4},{6,7},{7,6},{8,9},{9,8},{10,11... | collective-permute-start | bytes 49160 | tf_op jit(solution)/shard_map/ppermute | solution.py:27
  91.6 3.7 %collective-permute-start.22 = (f32[8,256]{1,0:T(8,128)S(1)}, f32[8,256]{1,0:T(8,128)S(1)}, u32[]{:S(2)}, u32[]{:S(2)}) collective-permute-start(f32[8,256]{1,0:T(8,128)S(1)} %fusion.7), channel_id=1, source_target_pairs={{0,4},{4,0},{1,5},{5,1},{2,6},{6,2},{3,7},{7,3},{8,12},{12,8},{9,1... | collective-permute-start | bytes 24584 | tf_op jit(solution)/shard_map/ppermute | solution.py:27
  95.6 3.7 %collective-permute-start.23 = (f32[8,256]{1,0:T(8,128)S(1)}, f32[8,256]{1,0:T(8,128)S(1)}, u32[]{:S(2)}, u32[]{:S(2)}) collective-permute-start(f32[8,256]{1,0:T(8,128)S(1)} %fusion.6), channel_id=1, source_target_pairs={{0,4},{4,0},{1,5},{5,1},{2,6},{6,2},{3,7},{7,3},{8,12},{12,8},{9,1... | collective-permute-start | bytes 24584 | tf_op jit(solution)/shard_map/ppermute | solution.py:27

commit v7 on v6

--- a/solution.py
+++ b/solution.py
@@ -12,6 +12,7 @@
 LANES = 128
 GROUPS = LANES // STEPS
 BLOCK = 8
+ROWS = 4
 MIB = 1024 * 1024
 BASIS_VMEM = 50 * MIB
 
@@ -194,7 +195,12 @@
                 speed[first_row + group] = winds[group] * inside
                 matrix[0, first_row + group] = kinds[group]
 
-    def coefficients(row, _):
+    def coefficients(turn, _):
+        for i in range(ROWS):
+            row_coefficients(lowest + turn * ROWS + i)
+        return 0
+
+    def row_coefficients(row):
         kind = matrix[0, row].astype(jnp.int32)
         wind = speed[row]
         for a in range(spec):
@@ -213,7 +219,6 @@
                 ]
                 value = jnp.concatenate(tiles, axis=0) * inside
                 matrix[a * spec + s, row] = value + stay if a == s else value
-        return 0
 
     zero = jnp.zeros((all_x, wide), jnp.float32)
 
@@ -232,7 +237,7 @@
 
     lowest = jnp.where(at_y > 0, BLOCK, BLOCK + cells_y)
     highest = jnp.where(at_y < count_y - 1, rows - BLOCK, rows - BLOCK - cells_y)
-    lax.fori_loop(lowest, highest, coefficients, 0)
+    lax.fori_loop(0, (highest - lowest) // ROWS, coefficients, 0)
 
     def step(index, source, target):
         low = jnp.maximum(BLOCK + index + 1, lowest)
@@ -478,23 +483,23 @@
     moved = {flips: exchange(kept[flips], "grp", flips) for flips in order}
     mine, *grams = lax.optimization_barrier((kept[0], *grams))
     mine, gram = lax.optimization_barrier((mine, add_up(grams)))
-    grams = copies_over(gram, "gy")
+    grams = copies_over(gram, "gx")
     total = product((0,), [mine], basis)
     for flips in ((1,), tuple(range(2, count_grp))):
         total = product(flips, [moved[f] for f in flips], basis, total)
 
     total = sum_over(total, "grp")
     total, *grams = lax.optimization_barrier((total, *grams))
-    total = copies_over(total, "gy")
+    total = copies_over(total, "gx")
     high = add_up([part[:snaps] for part in total])
     low = add_up([part[snaps:] for part in total])
-    first = sum_over(high, "gx")
+    first = sum_over(high, "gy")
     taken = jnp.dot(
         first.astype(jnp.bfloat16).astype(jnp.float32),
         add_up(grams),
         precision=lax.Precision.HIGHEST,
     )
-    second = sum_over(high + low - taken, "gx")
+    second = sum_over(high + low - taken, "gy")
     return (first + second, final)
 
 

time: 100 us -> 97.4 us (0.974)
  waiting for transfers between devices: 18.6 us -> 16.6 us
    ppermute x17, waiting for transfers between devices: 18.6 us -> 16.6 us  [exchange(): return lax.ppermute(value, axis, [(i, i ^ flips) for i in range(count)])]
  transfers between devices with their start and end apart: 24 -> 24, of which waited for: 9 -> 10; matrix products, arithmetic and copies ran while one was open for 0% -> 0% of each run, Pallas kernels for 43% -> 44%
where the time goes in v7:
time: 97.4 us; the launch traced here: 97.1 us
  Pallas kernels  47.3 us (49%)
  starting transfers between devices  31.3 us (32%)
  waiting for transfers between devices  16.6 us (17%)
    ppermute x17, starting transfers between devices, exchange(): return lax.ppermute(value, axis, [(i, i ^ flips) for i in range(count)])  20.1 us
    pallas_call x1, Pallas kernels, body(): pl.pallas_call(functools.partial(steps_kernel, count_x), out_shape=[jax.S...  19.7 us
    ppermute x17, waiting for transfers between devices, exchange(): return lax.ppermute(value, axis, [(i, i ^ flips) for i in range(count)])  16.6 us
    pallas_call x3, Pallas kernels, gram_part(): pl.pallas_call(functools.partial(gram_kernel, places, len(total)), out_sh...  14.1 us
    pallas_call x3, Pallas kernels, product(): pl.pallas_call(functools.partial(product_kernel, flips, len(total)), out_...  9.25 us
    ppermute x1, starting transfers between devices, body(): from_a = [lax.ppermute(own, 'gy', pairs('gy', 0))]  4.45 us
    ppermute x1, starting transfers between devices, body(): lax.ppermute(own, 'gx', [(i, (i - shift) % count_x) for i in range(count_...  2.94 us
    pallas_call x1, Pallas kernels, body(): pl.pallas_call(functools.partial(edges_kernel, count_x), out_shape=(packe...  2.56 us
  transfers between devices with their start and end apart: 24, of which 10 were waited for; matrix products, arithmetic and copies ran while one was open for 0% of the time, Pallas kernels for 44%

profile of v7, /device:TPU:0, one launch (start us, length us, event | category | flops | bytes accessed | tf_op | source)
XLA Modules:
  0.0 97.1 jit_solution(15531287496078040706)
XLA Ops:
  0.6 1.7 %pack.1.refs_0_ = f32[6,16,4,128]{3,2,1,0:T(4,128)} custom-call(f32[4,4,16,128]{3,2,1,0:T(8,128)} %terminal.1, f32[4,16,128]{2,1,0:T(8,128)} %velocity.1, s32[4,16,128]{2,1,0:T(8,128)} %material.1), custom_call_target="tpu_custom_call" | custom-call | tf_op jit(solution)/shard_map/pack/pallas_call | solution.py:425
  2.4 2.9 %collective-permute-start = (f32[6,16,4,128]{3,2,1,0:T(4,128)}, f32[6,16,4,128]{3,2,1,0:T(4,128)S(1)}, u32[]{:S(2)}, u32[]{:S(2)}) collective-permute-start(f32[6,16,4,128]{3,2,1,0:T(4,128)} %pack.1.refs_0_), channel_id=1, source_target_pairs={{0,4},{4,0},{1,5},{5,1},{2,6},{6,2},{3,7},{7,3},{8,12},{12,8},{9,1... | collective-permute-start | bytes 589832 | tf_op jit(solution)/shard_map/ppermute | solution.py:435
  5.3 0.7 collective-permute-start.3
  6.0 4.5 %collective-permute-start.1 = (f32[6,16,4,128]{3,2,1,0:T(4,128)}, f32[6,16,4,128]{3,2,1,0:T(4,128)S(1)}, u32[]{:S(2)}, u32[]{:S(2)}) collective-permute-start(f32[6,16,4,128]{3,2,1,0:T(4,128)} %pack.1.refs_0_), channel_id=1, source_target_pairs={{0,1},{2,3},{1,0},{3,2},{4,5},{6,7},{5,4},{7,6},{8,9},{10,11},{9,8... | collective-permute-start | bytes 589832 | tf_op jit(solution)/shard_map/ppermute | solution.py:437
  10.4 3.5 %gram.3.refs_0_ = f32[256,256]{1,0:T(8,128)S(1)} custom-call(bf16[1,4,16,512,256]{4,3,2,1,0:T(8,128)(2,1)} %refs_2_.1), custom_call_target="tpu_custom_call" | custom-call | flops 1073741824 | bytes 12582912 | tf_op jit(solution)/shard_map/gram/pallas_call | solution.py:331
  14.0 0.0 copy-start.4
  14.0 0.0 copy-start.2
  14.0 0.0 copy-start.3
  14.0 0.7 collective-permute-start.4
  14.7 1.8 %collective-permute-start.2 = (f32[6,16,4,128]{3,2,1,0:T(4,128)S(1)}, f32[6,16,4,128]{3,2,1,0:T(4,128)S(1)}, u32[]{:S(2)}, u32[]{:S(2)}) collective-permute-start(f32[6,16,4,128]{3,2,1,0:T(4,128)S(1)} %collective-permute-done.refs_1_), channel_id=1, source_target_pairs={{0,1},{2,3},{1,0},{3,2},{4,5},{6,7},{5,4},{7,6},{8,9},{10,11},{9,8... | collective-permute-start | bytes 589832 | tf_op jit(solution)/shard_map/ppermute | solution.py:441
  16.5 7.0 %gram.4.refs_0_ = f32[256,256]{1,0:T(8,128)S(1)} custom-call(bf16[1,4,16,512,256]{4,3,2,1,0:T(8,128)(2,1)} %refs_2_.1, f32[256,256]{1,0:T(8,128)S(1)} %gram.3.refs_0_), custom_call_target="tpu_custom_call" | custom-call | flops 2147483648 | bytes 25165824 | tf_op jit(solution)/shard_map/gram/pallas_call | solution.py:331
  23.5 2.6 %edges.1 = (f32[6,6,8,128]{3,2,1,0:T(8,128)S(1)}, f32[6,6,8,128]{3,2,1,0:T(8,128)S(1)}) custom-call(f32[6,16,4,128]{3,2,1,0:T(4,128)S(1)} %copy-done, f32[6,16,4,128]{3,2,1,0:T(4,128)S(1)} %collective-permute-done.refs_1_, f32[6,16,4,128]{3,2,1,0:T(4,128)S(1)} %collective-permute-done.1.refs_2_, f32[6,16,4,128]{3,2,1,0:T(4,128)S(1)} %collective-permute-done.2.refs_3_, ...), custom_call_target="tpu_custom_call" | custom-call | tf_op jit(solution)/shard_map/edges/pallas_call | solution.py:448
  26.1 0.1 collective-permute-start.5
  26.2 0.7 collective-permute-start.6
  26.9 3.6 %gram.5 = f32[256,256]{1,0:T(8,128)S(1)} custom-call(bf16[1,4,16,512,256]{4,3,2,1,0:T(8,128)(2,1)} %refs_2_.1, f32[256,256]{1,0:T(8,128)S(1)} %gram.4.refs_0_), custom_call_target="tpu_custom_call" | custom-call | flops 1073741824 | bytes 12582912 | tf_op jit(solution)/shard_map/gram/pallas_call | solution.py:331
  30.4 1.7 %collective-permute-start.12 = (f32[256,256]{1,0:T(8,128)S(1)}, f32[256,256]{1,0:T(8,128)S(1)}, u32[]{:S(2)}, u32[]{:S(2)}) collective-permute-start(f32[256,256]{1,0:T(8,128)S(1)} %gram.5), channel_id=1, source_target_pairs={{0,24},{8,16},{16,8},{24,0},{1,25},{9,17},{17,9},{25,1},{2,26},{10... | collective-permute-start | bytes 786440 | tf_op jit(solution)/shard_map/ppermute | solution.py:28
  32.1 2.9 %collective-permute-start.11 = (f32[256,256]{1,0:T(8,128)S(1)}, f32[256,256]{1,0:T(8,128)S(1)}, u32[]{:S(2)}, u32[]{:S(2)}) collective-permute-start(f32[256,256]{1,0:T(8,128)S(1)} %gram.5), channel_id=1, source_target_pairs={{0,16},{8,24},{16,0},{24,8},{1,17},{9,25},{17,1},{25,9},{2,18},{10... | collective-permute-start | bytes 786440 | tf_op jit(solution)/shard_map/ppermute | solution.py:28
  35.0 0.1 copy.10.stoich
  35.1 19.7 %steps.1 = (f32[4,4,16,128]{3,2,1,0:T(8,128)}, f32[4,16,8,128]{3,2,1,0:T(8,128)S(1)}, f32[4,16,8,128]{3,2,1,0:T(8,128)S(1)}, f32[4,16,8,128]{3,2,1,0:T(8,128)S(1)}, f32[4,16,8,128]{3,2,1,0:T(8,128)S(1)}) custom-call(s32[8]{0:T(128)S(1)} %copy-done.2, f32[4]{0:T(128)S(1)} %copy-done.3, s32[8,4]{1,0:T(8,128)S(1)} %copy.10.stoich, f32[8,8]{1,0:T(8,128)S(1)} %copy-done.1, ...), custom_call_target="tpu_custom_call" | custom-call | bytes 100663296 | tf_op jit(solution)/shard_map/steps/pallas_call | solution.py:466
  54.8 1.1 %collective-permute-start.7 = (f32[4,16,8,128]{3,2,1,0:T(8,128)S(1)}, f32[4,16,8,128]{3,2,1,0:T(8,128)S(1)}, u32[]{:S(2)}, u32[]{:S(2)}) collective-permute-start(f32[4,16,8,128]{3,2,1,0:T(8,128)S(1)} %get-tuple-element.46), channel_id=1, source_target_pairs={{0,16},{8,24},{16,0},{24,8},{1,17},{9,25},{17,1},{25,9},{2,18},{10... | collective-permute-start | bytes 786440 | tf_op jit(solution)/shard_map/ppermute | solution.py:28
  55.9 0.9 collective-permute-start.8
  56.7 0.3 collective-permute-start.9
  57.0 0.1 add_add_fusion
  57.1 0.9 collective-permute-start.16
  58.0 2.7 %product.3.refs_2_ = f32[16,256]{1,0:T(8,128)S(1)} custom-call(f32[4,16,8,128]{3,2,1,0:T(8,128)S(1)} %get-tuple-element.56.refs_0_, bf16[1,4,16,512,256]{4,3,2,1,0:T(8,128)(2,1)} %refs_2_.1), custom_call_target="tpu_custom_call" | custom-call | flops 67108864 | bytes 8388608 | tf_op jit(solution)/shard_map/product/pallas_call | solution.py:399
  60.6 2.7 %product.4.refs_3_ = f32[16,256]{1,0:T(8,128)S(1)} custom-call(f32[4,16,8,128]{3,2,1,0:T(8,128)S(1)} %collective-permute-done.9.refs_0_, bf16[1,4,16,512,256]{4,3,2,1,0:T(8,128)(2,1)} %refs_2_.1, f32[16,256]{1,0:T(8,128)S(1)} %product.3.refs_2_), custom_call_target="tpu_custom_call" | custom-call | flops 67108864 | bytes 8388608 | tf_op jit(solution)/shard_map/product/pallas_call | solution.py:399
  63.3 0.7 collective-permute-done.7.refs_0_
  64.0 4.8 %collective-permute-done.8.refs_1_ = f32[4,16,8,128]{3,2,1,0:T(8,128)S(1)} collective-permute-done((f32[4,16,8,128]{3,2,1,0:T(8,128)S(1)}, f32[4,16,8,128]{3,2,1,0:T(8,128)S(1)}, u32[]{:S(2)}, u32[]{:S(2)}) %collective-permute-start.8) | collective-permute-done | bytes 262176 | tf_op jit(solution)/shard_map/ppermute | solution.py:28
  68.8 3.9 %product.5 = f32[16,256]{1,0:T(8,128)S(1)} custom-call(f32[4,16,8,128]{3,2,1,0:T(8,128)S(1)} %collective-permute-done.7.refs_0_, f32[4,16,8,128]{3,2,1,0:T(8,128)S(1)} %collective-permute-done.8.refs_1_, bf16[1,4,16,512,256]{4,3,2,1,0:T(8,128)(2,1)} %refs_2_.1, f32[16,256]{1,0:T(8,128)S(1)} %product.4.refs_3_), custom_call_target="tpu_custom_call" | custom-call | flops 134217728 | bytes 16777216 | tf_op jit(solution)/shard_map/product/pallas_call | solution.py:399
  72.7 0.4 collective-permute-start.15
  73.1 1.5 %collective-permute-start.14 = (f32[16,256]{1,0:T(8,128)S(1)}, f32[16,256]{1,0:T(8,128)S(1)}, u32[]{:S(2)}, u32[]{:S(2)}) collective-permute-start(f32[16,256]{1,0:T(8,128)S(1)} %product.5), channel_id=1, source_target_pairs={{0,16},{8,24},{16,0},{24,8},{1,17},{9,25},{17,1},{25,9},{2,18},{10... | collective-permute-start | bytes 49160 | tf_op jit(solution)/shard_map/ppermute | solution.py:28
  74.6 0.0 collective-permute-start.13
  74.7 1.3 %collective-permute-done.15 = f32[16,256]{1,0:T(8,128)S(1)} collective-permute-done((f32[16,256]{1,0:T(8,128)S(1)}, f32[16,256]{1,0:T(8,128)S(1)}, u32[]{:S(2)}, u32[]{:S(2)}) %collective-permute-start.15) | collective-permute-done | bytes 16416 | tf_op jit(solution)/shard_map/ppermute | solution.py:28
  76.0 0.9 collective-permute-done.14
  76.9 0.9 collective-permute-start.17
  77.7 2.9 %collective-permute-done.17 = f32[16,256]{1,0:T(8,128)S(1)} collective-permute-done((f32[16,256]{1,0:T(8,128)S(1)}, f32[16,256]{1,0:T(8,128)S(1)}, u32[]{:S(2)}, u32[]{:S(2)}) %collective-permute-start.17) | collective-permute-done | bytes 16416 | tf_op jit(solution)/shard_map/ppermute | solution.py:28
  80.7 2.5 %collective-permute-start.20 = (f32[8,256]{1,0:T(8,128)S(1)}, f32[8,256]{1,0:T(8,128)S(1)}, u32[]{:S(2)}, u32[]{:S(2)}) collective-permute-start(f32[8,256]{1,0:T(8,128)S(1)} %slice_add_fusion.1), channel_id=1, source_target_pairs={{0,3},{1,2},{2,1},{3,0},{4,7},{5,6},{6,5},{7,4},{8,11},{9,10},{10,... | collective-permute-start | bytes 24584 | tf_op jit(solution)/shard_map/ppermute | solution.py:28
  83.2 2.8 %collective-permute-start.19 = (f32[8,256]{1,0:T(8,128)S(1)}, f32[8,256]{1,0:T(8,128)S(1)}, u32[]{:S(2)}, u32[]{:S(2)}) collective-permute-start(f32[8,256]{1,0:T(8,128)S(1)} %slice_add_fusion.1), channel_id=1, source_target_pairs={{0,2},{1,3},{2,0},{3,1},{4,6},{5,7},{6,4},{7,5},{8,10},{9,11},{10,... | collective-permute-start | bytes 24584 | tf_op jit(solution)/shard_map/ppermute | solution.py:28
  85.9 0.2 collective-permute-done.20
  86.1 1.6 %collective-permute-done.19 = f32[8,256]{1,0:T(8,128)S(1)} collective-permute-done((f32[8,256]{1,0:T(8,128)S(1)}, f32[8,256]{1,0:T(8,128)S(1)}, u32[]{:S(2)}, u32[]{:S(2)}) %collective-permute-start.19) | collective-permute-done | bytes 8224 | tf_op jit(solution)/shard_map/ppermute | solution.py:28
  87.7 1.9 %collective-permute-done.18 = f32[8,256]{1,0:T(8,128)S(1)} collective-permute-done((f32[8,256]{1,0:T(8,128)S(1)}, f32[8,256]{1,0:T(8,128)S(1)}, u32[]{:S(2)}, u32[]{:S(2)}) %collective-permute-start.18) | collective-permute-done | bytes 8224 | tf_op jit(solution)/shard_map/ppermute | solution.py:28
  89.6 0.2 fusion.3
  89.8 2.2 %collective-permute-start.23 = (f32[8,256]{1,0:T(8,128)S(1)}, f32[8,256]{1,0:T(8,128)S(1)}, u32[]{:S(2)}, u32[]{:S(2)}) collective-permute-start(f32[8,256]{1,0:T(8,128)S(1)} %fusion.3), channel_id=1, source_target_pairs={{0,3},{1,2},{2,1},{3,0},{4,7},{5,6},{6,5},{7,4},{8,11},{9,10},{10,... | collective-permute-start | bytes 24584 | tf_op jit(solution)/shard_map/ppermute | solution.py:28
  92.0 0.0 collective-permute-start.22
  92.0 2.2 %collective-permute-start.21 = (f32[8,256]{1,0:T(8,128)S(1)}, f32[8,256]{1,0:T(8,128)S(1)}, u32[]{:S(2)}, u32[]{:S(2)}) collective-permute-start(f32[8,256]{1,0:T(8,128)S(1)} %fusion.3), channel_id=1, source_target_pairs={{0,1},{1,0},{2,3},{3,2},{4,5},{5,4},{6,7},{7,6},{8,9},{9,8},{10,11... | collective-permute-start | bytes 24584 | tf_op jit(solution)/shard_map/ppermute | solution.py:28
  94.2 1.1 %collective-permute-done.23 = f32[8,256]{1,0:T(8,128)S(1)} collective-permute-done((f32[8,256]{1,0:T(8,128)S(1)}, f32[8,256]{1,0:T(8,128)S(1)}, u32[]{:S(2)}, u32[]{:S(2)}) %collective-permute-start.23) | collective-permute-done | bytes 8224 | tf_op jit(solution)/shard_map/ppermute | solution.py:28
  95.3 1.3 %collective-permute-done.22 = f32[8,256]{1,0:T(8,128)S(1)} collective-permute-done((f32[8,256]{1,0:T(8,128)S(1)}, f32[8,256]{1,0:T(8,128)S(1)}, u32[]{:S(2)}, u32[]{:S(2)}) %collective-permute-start.22) | collective-permute-done | bytes 8224 | tf_op jit(solution)/shard_map/ppermute | solution.py:28
  96.5 0.6 add_add_fusion.2
  (26 shorter events, 0.1 us)
Async XLA Ops:
  2.4 21.2 %copy-start = (f32[6,16,4,128]{3,2,1,0:T(4,128)S(1)}, f32[6,16,4,128]{3,2,1,0:T(4,128)}, u32[]{:S(2)}) copy-start(f32[6,16,4,128]{3,2,1,0:T(4,128)} %pack.1.refs_0_) | copy-start | bytes 589828
  2.4 11.7 %collective-permute-start = (f32[6,16,4,128]{3,2,1,0:T(4,128)}, f32[6,16,4,128]{3,2,1,0:T(4,128)S(1)}, u32[]{:S(2)}, u32[]{:S(2)}) collective-permute-start(f32[6,16,4,128]{3,2,1,0:T(4,128)} %pack.1.refs_0_), channel_id=1, source_target_pairs={{0,4},{4,0},{1,5},{5,1},{2,6},{6,2},{3,7},{7,3},{8,12},{12,8},{9,1... | collective-permute-start | bytes 589832 | tf_op jit(solution)/shard_map/ppermute | solution.py:435
  5.3 18.2 %collective-permute-start.3 = (f32[6,16,4,128]{3,2,1,0:T(4,128)}, f32[6,16,4,128]{3,2,1,0:T(4,128)S(1)}, u32[]{:S(2)}, u32[]{:S(2)}) collective-permute-start(f32[6,16,4,128]{3,2,1,0:T(4,128)} %pack.1.refs_0_), channel_id=1, source_target_pairs={{1,2},{2,1},{5,6},{6,5},{9,10},{10,9},{13,14},{14,13},{17,18},{18,... | collective-permute-start | bytes 589832 | tf_op jit(solution)/shard_map/ppermute | solution.py:438
  6.0 17.5 %collective-permute-start.1 = (f32[6,16,4,128]{3,2,1,0:T(4,128)}, f32[6,16,4,128]{3,2,1,0:T(4,128)S(1)}, u32[]{:S(2)}, u32[]{:S(2)}) collective-permute-start(f32[6,16,4,128]{3,2,1,0:T(4,128)} %pack.1.refs_0_), channel_id=1, source_target_pairs={{0,1},{2,3},{1,0},{3,2},{4,5},{6,7},{5,4},{7,6},{8,9},{10,11},{9,8... | collective-permute-start | bytes 589832 | tf_op jit(solution)/shard_map/ppermute | solution.py:437
  14.0 21.1 %copy-start.4 = (s32[8,4]{0,1:T(4,128)S(1)}, s32[8,4]{0,1:T(4,128)}, u32[]{:S(2)}) copy-start(s32[8,4]{0,1:T(4,128)} %param.13) | copy-start | bytes 388
  14.0 21.1 %copy-start.1 = (f32[8,8]{1,0:T(8,128)S(1)}, f32[8,8]{1,0:T(8,128)}, u32[]{:S(2)}) copy-start(f32[8,8]{1,0:T(8,128)} %rates.1) | copy-start | bytes 772
  14.0 21.1 %copy-start.2 = (s32[8]{0:T(128)S(1)}, s32[8]{0:T(128)}, u32[]{:S(2)}) copy-start(s32[8]{0:T(128)} %plan.1) | copy-start | bytes 100
  14.0 21.1 %copy-start.3 = (f32[4]{0:T(128)S(1)}, f32[4]{0:T(128)}, u32[]{:S(2)}) copy-start(f32[4]{0:T(128)} %diffusion.1) | copy-start | bytes 52
  14.0 9.5 %collective-permute-start.4 = (f32[6,16,4,128]{3,2,1,0:T(4,128)S(1)}, f32[6,16,4,128]{3,2,1,0:T(4,128)S(1)}, u32[]{:S(2)}, u32[]{:S(2)}) collective-permute-start(f32[6,16,4,128]{3,2,1,0:T(4,128)S(1)} %collective-permute-done.refs_1_), channel_id=1, source_target_pairs={{1,2},{2,1},{5,6},{6,5},{9,10},{10,9},{13,14},{14,13},{17,18},{18,... | collective-permute-start | bytes 589832 | tf_op jit(solution)/shard_map/ppermute | solution.py:442
  14.7 8.8 %collective-permute-start.2 = (f32[6,16,4,128]{3,2,1,0:T(4,128)S(1)}, f32[6,16,4,128]{3,2,1,0:T(4,128)S(1)}, u32[]{:S(2)}, u32[]{:S(2)}) collective-permute-start(f32[6,16,4,128]{3,2,1,0:T(4,128)S(1)} %collective-permute-done.refs_1_), channel_id=1, source_target_pairs={{0,1},{2,3},{1,0},{3,2},{4,5},{6,7},{5,4},{7,6},{8,9},{10,11},{9,8... | collective-permute-start | bytes 589832 | tf_op jit(solution)/shard_map/ppermute | solution.py:441
  26.1 4.3 %collective-permute-start.5 = (f32[6,6,8,128]{3,2,1,0:T(8,128)S(1)}, f32[6,6,8,128]{3,2,1,0:T(8,128)S(1)}, u32[]{:S(2)}, u32[]{:S(2)}) collective-permute-start(f32[6,6,8,128]{3,2,1,0:T(8,128)S(1)} %get-tuple-element.41), channel_id=1, source_target_pairs={{0,8},{16,24},{8,0},{24,16},{1,9},{17,25},{9,1},{25,17},{2,10},{18... | collective-permute-start | bytes 442376 | tf_op jit(solution)/shard_map/ppermute | solution.py:457
  26.2 4.3 %collective-permute-start.6 = (f32[6,6,8,128]{3,2,1,0:T(8,128)S(1)}, f32[6,6,8,128]{3,2,1,0:T(8,128)S(1)}, u32[]{:S(2)}, u32[]{:S(2)}) collective-permute-start(f32[6,6,8,128]{3,2,1,0:T(8,128)S(1)} %get-tuple-element.42), channel_id=1, source_target_pairs={{8,16},{16,8},{9,17},{17,9},{10,18},{18,10},{11,19},{19,11},{12,20... | collective-permute-start | bytes 442376 | tf_op jit(solution)/shard_map/ppermute | solution.py:458
  30.4 26.3 %collective-permute-start.12 = (f32[256,256]{1,0:T(8,128)S(1)}, f32[256,256]{1,0:T(8,128)S(1)}, u32[]{:S(2)}, u32[]{:S(2)}) collective-permute-start(f32[256,256]{1,0:T(8,128)S(1)} %gram.5), channel_id=1, source_target_pairs={{0,24},{8,16},{16,8},{24,0},{1,25},{9,17},{17,9},{25,1},{2,26},{10... | collective-permute-start | bytes 786440 | tf_op jit(solution)/shard_map/ppermute | solution.py:28
  32.1 24.9 %collective-permute-start.11 = (f32[256,256]{1,0:T(8,128)S(1)}, f32[256,256]{1,0:T(8,128)S(1)}, u32[]{:S(2)}, u32[]{:S(2)}) collective-permute-start(f32[256,256]{1,0:T(8,128)S(1)} %gram.5), channel_id=1, source_target_pairs={{0,16},{8,24},{16,0},{24,8},{1,17},{9,25},{17,1},{25,9},{2,18},{10... | collective-permute-start | bytes 786440 | tf_op jit(solution)/shard_map/ppermute | solution.py:28
  35.0 22.0 %collective-permute-start.10 = (f32[256,256]{1,0:T(8,128)S(1)}, f32[256,256]{1,0:T(8,128)S(1)}, u32[]{:S(2)}, u32[]{:S(2)}) collective-permute-start(f32[256,256]{1,0:T(8,128)S(1)} %gram.5), channel_id=1, source_target_pairs={{0,8},{8,0},{16,24},{24,16},{1,9},{9,1},{17,25},{25,17},{2,10},{10... | collective-permute-start | bytes 786440 | tf_op jit(solution)/shard_map/ppermute | solution.py:28
  54.8 9.2 %collective-permute-start.7 = (f32[4,16,8,128]{3,2,1,0:T(8,128)S(1)}, f32[4,16,8,128]{3,2,1,0:T(8,128)S(1)}, u32[]{:S(2)}, u32[]{:S(2)}) collective-permute-start(f32[4,16,8,128]{3,2,1,0:T(8,128)S(1)} %get-tuple-element.46), channel_id=1, source_target_pairs={{0,16},{8,24},{16,0},{24,8},{1,17},{9,25},{17,1},{25,9},{2,18},{10... | collective-permute-start | bytes 786440 | tf_op jit(solution)/shard_map/ppermute | solution.py:28
  55.9 13.0 %collective-permute-start.8 = (f32[4,16,8,128]{3,2,1,0:T(8,128)S(1)}, f32[4,16,8,128]{3,2,1,0:T(8,128)S(1)}, u32[]{:S(2)}, u32[]{:S(2)}) collective-permute-start(f32[4,16,8,128]{3,2,1,0:T(8,128)S(1)} %get-tuple-element.47), channel_id=1, source_target_pairs={{0,24},{8,16},{16,8},{24,0},{1,25},{9,17},{17,9},{25,1},{2,26},{10... | collective-permute-start | bytes 786440 | tf_op jit(solution)/shard_map/ppermute | solution.py:28
  56.7 3.9 %collective-permute-start.9 = (f32[4,16,8,128]{3,2,1,0:T(8,128)S(1)}, f32[4,16,8,128]{3,2,1,0:T(8,128)S(1)}, u32[]{:S(2)}, u32[]{:S(2)}) collective-permute-start(f32[4,16,8,128]{3,2,1,0:T(8,128)S(1)} %get-tuple-element.48), channel_id=1, source_target_pairs={{0,8},{8,0},{16,24},{24,16},{1,9},{9,1},{17,25},{25,17},{2,10},{10... | collective-permute-start | bytes 786440 | tf_op jit(solution)/shard_map/ppermute | solution.py:28
  57.1 19.8 %collective-permute-start.16 = (f32[256,256]{1,0:T(8,128)S(1)}, f32[256,256]{1,0:T(8,128)S(1)}, u32[]{:S(2)}, u32[]{:S(2)}) collective-permute-start(f32[256,256]{1,0:T(8,128)S(1)} %add_add_fusion), channel_id=1, source_target_pairs={{0,4},{4,0},{1,5},{5,1},{2,6},{6,2},{3,7},{7,3},{8,12},{12,8},{9,1... | collective-permute-start | bytes 786440 | tf_op jit(solution)/shard_map/ppermute | solution.py:28
  72.7 3.2 %collective-permute-start.15 = (f32[16,256]{1,0:T(8,128)S(1)}, f32[16,256]{1,0:T(8,128)S(1)}, u32[]{:S(2)}, u32[]{:S(2)}) collective-permute-start(f32[16,256]{1,0:T(8,128)S(1)} %product.5), channel_id=1, source_target_pairs={{0,24},{8,16},{16,8},{24,0},{1,25},{9,17},{17,9},{25,1},{2,26},{10... | collective-permute-start | bytes 49160 | tf_op jit(solution)/shard_map/ppermute | solution.py:28
  73.1 3.7 %collective-permute-start.14 = (f32[16,256]{1,0:T(8,128)S(1)}, f32[16,256]{1,0:T(8,128)S(1)}, u32[]{:S(2)}, u32[]{:S(2)}) collective-permute-start(f32[16,256]{1,0:T(8,128)S(1)} %product.5), channel_id=1, source_target_pairs={{0,16},{8,24},{16,0},{24,8},{1,17},{9,25},{17,1},{25,9},{2,18},{10... | collective-permute-start | bytes 49160 | tf_op jit(solution)/shard_map/ppermute | solution.py:28
  74.6 2.2 %collective-permute-start.13 = (f32[16,256]{1,0:T(8,128)S(1)}, f32[16,256]{1,0:T(8,128)S(1)}, u32[]{:S(2)}, u32[]{:S(2)}) collective-permute-start(f32[16,256]{1,0:T(8,128)S(1)} %product.5), channel_id=1, source_target_pairs={{0,8},{8,0},{16,24},{24,16},{1,9},{9,1},{17,25},{25,17},{2,10},{10... | collective-permute-start | bytes 49160 | tf_op jit(solution)/shard_map/ppermute | solution.py:28
  76.9 3.8 %collective-permute-start.17 = (f32[16,256]{1,0:T(8,128)S(1)}, f32[16,256]{1,0:T(8,128)S(1)}, u32[]{:S(2)}, u32[]{:S(2)}) collective-permute-start(f32[16,256]{1,0:T(8,128)S(1)} %add_add_fusion.1), channel_id=1, source_target_pairs={{0,4},{4,0},{1,5},{5,1},{2,6},{6,2},{3,7},{7,3},{8,12},{12,8},{9,1... | collective-permute-start | bytes 49160 | tf_op jit(solution)/shard_map/ppermute | solution.py:28
  80.7 5.4 %collective-permute-start.20 = (f32[8,256]{1,0:T(8,128)S(1)}, f32[8,256]{1,0:T(8,128)S(1)}, u32[]{:S(2)}, u32[]{:S(2)}) collective-permute-start(f32[8,256]{1,0:T(8,128)S(1)} %slice_add_fusion.1), channel_id=1, source_target_pairs={{0,3},{1,2},{2,1},{3,0},{4,7},{5,6},{6,5},{7,4},{8,11},{9,10},{10,... | collective-permute-start | bytes 24584 | tf_op jit(solution)/shard_map/ppermute | solution.py:28
  83.2 4.5 %collective-permute-start.19 = (f32[8,256]{1,0:T(8,128)S(1)}, f32[8,256]{1,0:T(8,128)S(1)}, u32[]{:S(2)}, u32[]{:S(2)}) collective-permute-start(f32[8,256]{1,0:T(8,128)S(1)} %slice_add_fusion.1), channel_id=1, source_target_pairs={{0,2},{1,3},{2,0},{3,1},{4,6},{5,7},{6,4},{7,5},{8,10},{9,11},{10,... | collective-permute-start | bytes 24584 | tf_op jit(solution)/shard_map/ppermute | solution.py:28
  85.9 3.7 %collective-permute-start.18 = (f32[8,256]{1,0:T(8,128)S(1)}, f32[8,256]{1,0:T(8,128)S(1)}, u32[]{:S(2)}, u32[]{:S(2)}) collective-permute-start(f32[8,256]{1,0:T(8,128)S(1)} %slice_add_fusion.1), channel_id=1, source_target_pairs={{0,1},{1,0},{2,3},{3,2},{4,5},{5,4},{6,7},{7,6},{8,9},{9,8},{10,11... | collective-permute-start | bytes 24584 | tf_op jit(solution)/shard_map/ppermute | solution.py:28
  89.8 5.5 %collective-permute-start.23 = (f32[8,256]{1,0:T(8,128)S(1)}, f32[8,256]{1,0:T(8,128)S(1)}, u32[]{:S(2)}, u32[]{:S(2)}) collective-permute-start(f32[8,256]{1,0:T(8,128)S(1)} %fusion.3), channel_id=1, source_target_pairs={{0,3},{1,2},{2,1},{3,0},{4,7},{5,6},{6,5},{7,4},{8,11},{9,10},{10,... | collective-permute-start | bytes 24584 | tf_op jit(solution)/shard_map/ppermute | solution.py:28
  92.0 4.5 %collective-permute-start.22 = (f32[8,256]{1,0:T(8,128)S(1)}, f32[8,256]{1,0:T(8,128)S(1)}, u32[]{:S(2)}, u32[]{:S(2)}) collective-permute-start(f32[8,256]{1,0:T(8,128)S(1)} %fusion.3), channel_id=1, source_target_pairs={{0,2},{1,3},{2,0},{3,1},{4,6},{5,7},{6,4},{7,5},{8,10},{9,11},{10,... | collective-permute-start | bytes 24584 | tf_op jit(solution)/shard_map/ppermute | solution.py:28
  92.0 4.5 %collective-permute-start.21 = (f32[8,256]{1,0:T(8,128)S(1)}, f32[8,256]{1,0:T(8,128)S(1)}, u32[]{:S(2)}, u32[]{:S(2)}) collective-permute-start(f32[8,256]{1,0:T(8,128)S(1)} %fusion.3), channel_id=1, source_target_pairs={{0,1},{1,0},{2,3},{3,2},{4,5},{5,4},{6,7},{7,6},{8,9},{9,8},{10,11... | collective-permute-start | bytes 24584 | tf_op jit(solution)/shard_map/ppermute | solution.py:28

commit v8 on v7

--- a/solution.py
+++ b/solution.py
@@ -14,7 +14,6 @@
 BLOCK = 8
 ROWS = 4
 MIB = 1024 * 1024
-BASIS_VMEM = 50 * MIB
 
 
 def pairs(axis, first):
@@ -188,7 +187,7 @@
                     state[s, first_row + group] = tile
                 return 0
 
-            lax.fori_loop(0, spec, species_body, 0)
+            lax.fori_loop(0, spec, species_body, 0, unroll=True)
             winds = load(spec)
             kinds = load(spec + 1)
             for group in range(GROUPS):
@@ -300,16 +299,17 @@
     lax.fori_loop(0, spec, leave, 0)
 
 
-def gram_kernel(places, given, basis, *refs):
-    total, (out, chunks, held, sems) = refs[:given], refs[given:]
+def gram_kernel(places, later, fetched, given, *refs):
+    tables, refs = refs[: len(places) if fetched else 1], refs[len(places) if fetched else 1 :]
+    total, refs = refs[:given], refs[given:]
+    out, ahead, (chunks, held, sems) = refs[0], refs[1 : 1 + len(later)], refs[1 + len(later) :]
     count, rows, cells_z, modes = chunks.shape
     halves = count // len(places)
-    copies = fetch(
-        [basis.at[0, x, pl.ds(i * rows, rows)] for x in places for i in range(halves)]
-        + list(total),
-        [chunks.at[i] for i in range(count)] + [held],
-        sems,
-    )
+    wholes = list(tables) if fetched else [tables[0].at[0, x] for x in places]
+    sources = [part.at[pl.ds(i * rows, rows)] for part in wholes for i in range(halves)]
+    sources += [*total, *(tables[0].at[0, x] for x in later)]
+    targets = [chunks.at[i] for i in range(count)] + [held][:given] + list(ahead)
+    copies = fetch(sources, targets, sems)
     acc = None
     for i in range(count):
         copies[i].wait()
@@ -318,32 +318,35 @@
             chunk, chunk, (((0,), (0,)), ((), ())), preferred_element_type=jnp.float32
         )
         acc = part if acc is None else acc + part
+    for copy in copies[count:]:
+        copy.wait()
     if total:
-        copies[-1].wait()
         acc = acc + held[...]
     out[...] = acc
 
 
-def gram_part(places, basis, *total):
+def gram_part(places, basis, *total, later=(), parts=()):
     _, _, cells_y, cells_z, modes = basis.shape
-    chunks = 2 * len(places)
+    chunks, given = 2 * len(places), len(total)
     size = 2 * len(places) * cells_y * cells_z * modes
+    tables = parts or (basis,)
     return pl.pallas_call(
-        functools.partial(gram_kernel, places, len(total)),
-        out_shape=jax.ShapeDtypeStruct((modes, modes), jnp.float32),
-        in_specs=anywhere(1 + len(total)),
-        out_specs=whole(1)[0],
+        functools.partial(gram_kernel, places, later, bool(parts), given),
+        out_shape=[jax.ShapeDtypeStruct((modes, modes), jnp.float32)]
+        + [jax.ShapeDtypeStruct((cells_y, cells_z, modes), jnp.bfloat16)] * len(later),
+        in_specs=anywhere(len(tables) + given),
+        out_specs=whole(1) + anywhere(len(later)),
         scratch_shapes=[
             pltpu.VMEM((chunks, cells_y // 2, cells_z, modes), jnp.bfloat16),
             pltpu.VMEM((modes, modes), jnp.float32),
-            pltpu.SemaphoreType.DMA((chunks + 1,)),
+            pltpu.SemaphoreType.DMA((chunks + given + len(later),)),
         ],
-        compiler_params=pltpu.CompilerParams(vmem_limit_bytes=BASIS_VMEM),
+        compiler_params=pltpu.CompilerParams(vmem_limit_bytes=size + 8 * MIB),
         cost_estimate=pl.CostEstimate(
             flops=size * modes, bytes_accessed=3 * size, transcendentals=0
         ),
         name="gram",
-    )(basis, *total)
+    )(*tables, *total)
 
 
 def rows_of(basis, flips, cells_z):
@@ -371,54 +374,72 @@
     return acc
 
 
-def product_kernel(flips, given, *refs):
+def product_kernel(flips, later, fetched, given, *refs):
     count = len(flips)
-    parts, basis, total = refs[:count], refs[count], refs[count + 1 : count + 1 + given]
-    out, held, rows, sums, sems = refs[count + 1 + given :]
+    parts, refs = refs[:count], refs[count:]
+    tables, refs = refs[: count if fetched else 1], refs[count if fetched else 1 :]
+    total, refs = refs[:given], refs[given:]
+    out, ahead, (held, rows, sums, sems) = refs[0], refs[1 : 1 + len(later)], refs[1 + len(later) :]
     cells_x, cells_z = held.shape[1], held.shape[-1]
+    places = range(cells_x)
     sources, targets = [], []
     for i in range(count):
-        sources += [parts[i], *rows_of(basis, flips[i], cells_z)]
-        targets += [held.at[i], *(rows.at[i, x] for x in range(cells_x))]
-    copies = fetch([*sources, *total], [*targets, sums], sems)
+        if fetched:
+            table = [tables[i].at[x] for x in places]
+        else:
+            table = rows_of(tables[0], flips[i], cells_z)
+        sources += [parts[i], *table]
+        targets += [held.at[i], *(rows.at[i, x] for x in places)]
+    sources += total
+    targets += [sums][:given]
+    for i in range(len(later)):
+        sources += rows_of(tables[0], later[i], cells_z)
+        targets += [ahead[i].at[x] for x in places]
+    copies = fetch(sources, targets, sems)
     acc = None
     for i in range(count):
         start = i * (cells_x + 1)
         copies[start].wait()
         acc = multiply(held.at[i], rows.at[i], copies[start + 1 :], acc)
+    for copy in copies[count * (cells_x + 1) :]:
+        copy.wait()
     if total:
-        copies[-1].wait()
         acc = acc + sums[...]
     out[...] = acc
 
 
-def product(flips, parts, basis, *total):
+def product(flips, parts, basis, *total, later=(), rows=()):
     cells_x, cells_y, snaps, cells_z = parts[0].shape
     modes, count = basis.shape[-1], len(flips)
-    size = 2 * count * cells_x * cells_y * cells_z * modes
+    room = (cells_x, cells_y, cells_z, modes)
+    size = 2 * count * math.prod(room)
+    tables = rows or (basis,)
+    given = len(total)
     return pl.pallas_call(
-        functools.partial(product_kernel, flips, len(total)),
-        out_shape=jax.ShapeDtypeStruct((2 * snaps, modes), jnp.float32),
-        in_specs=anywhere(1 + count + len(total)),
-        out_specs=whole(1)[0],
+        functools.partial(product_kernel, flips, later, bool(rows), given),
+        out_shape=[jax.ShapeDtypeStruct((2 * snaps, modes), jnp.float32)]
+        + [jax.ShapeDtypeStruct(room, jnp.bfloat16)] * len(later),
+        in_specs=anywhere(count + len(tables) + given),
+        out_specs=whole(1) + anywhere(len(later)),
         scratch_shapes=[
             pltpu.VMEM((count, *parts[0].shape), jnp.float32),
-            pltpu.VMEM((count, cells_x, cells_y, cells_z, modes), jnp.bfloat16),
+            pltpu.VMEM((count, *room), jnp.bfloat16),
             pltpu.VMEM((2 * snaps, modes), jnp.float32),
-            pltpu.SemaphoreType.DMA((count * (cells_x + 1) + 1,)),
+            pltpu.SemaphoreType.DMA((count * (cells_x + 1) + cells_x * len(later) + given,)),
         ],
-        compiler_params=pltpu.CompilerParams(vmem_limit_bytes=BASIS_VMEM),
+        compiler_params=pltpu.CompilerParams(vmem_limit_bytes=size + 8 * MIB),
         cost_estimate=pl.CostEstimate(
             flops=2 * snaps * size, bytes_accessed=2 * size, transcendentals=0
         ),
         name="product",
-    )(*parts, basis, *total)
+    )(*parts, *tables, *total)
 
 
 def body(terminal, diffusion, velocity, material, rates, stoich, plan, basis):
     spec, cells_x, cells_y, cells_z = terminal.shape
     snaps, modes = plan.shape[0], basis.shape[-1]
     count_grp, count_x = lax.axis_size("grp"), lax.axis_size("gx")
+    basis = pltpu.with_memory_space_constraint(basis, pltpu.HBM)
     fields, all_x = spec + 2, cells_x * count_x
     wide, depth = cells_z + LANES, 3 * cells_y + 2 * BLOCK
 
@@ -436,11 +457,12 @@
         )
     from_a = [lax.ppermute(own, "gy", pairs("gy", 0))]
     from_b = [lax.ppermute(own, "gy", pairs("gy", 1))]
-    gram = gram_part((0,), basis)
+    (gram,) = gram_part((0,), basis)
     *blocks, gram = lax.optimization_barrier((*blocks, gram))
     from_a += [lax.ppermute(b, "gy", pairs("gy", 0)) for b in blocks[1:]]
     from_b += [lax.ppermute(b, "gy", pairs("gy", 1)) for b in blocks[1:]]
-    gram = gram_part(tuple(range(1, cells_x - 1)), basis, gram)
+    later = tuple(range(2, cells_x))
+    gram, *parts = gram_part((1,), basis, gram, later=later)
     blocks = blocks + from_a + from_b
     *blocks, gram = lax.optimization_barrier((*blocks, gram))
     packed = jax.ShapeDtypeStruct((fields, 3 * cells_y // GROUPS, all_x, LANES), jnp.float32)
@@ -456,7 +478,7 @@
     )(*blocks)
     side_a = lax.ppermute(edge_a, "grp", pairs("grp", 0))
     side_b = lax.ppermute(edge_b, "grp", pairs("grp", 1))
-    gram = gram_part((cells_x - 1,), basis, gram)
+    (gram,) = gram_part(later, basis, gram, parts=tuple(parts))
     side_a, side_b, gram = lax.optimization_barrier((side_a, side_b, gram))
     grams = copies_over(gram, "grp")
 
@@ -484,9 +506,10 @@
     mine, *grams = lax.optimization_barrier((kept[0], *grams))
     mine, gram = lax.optimization_barrier((mine, add_up(grams)))
     grams = copies_over(gram, "gx")
-    total = product((0,), [mine], basis)
-    for flips in ((1,), tuple(range(2, count_grp))):
-        total = product(flips, [moved[f] for f in flips], basis, total)
+    later = tuple(range(2, count_grp))
+    total, *rows = product((0,), [mine], basis, later=later)
+    (total,) = product((1,), [moved[1]], basis, total)
+    (total,) = product(later, [moved[f] for f in later], basis, total, rows=tuple(rows))
 
     total = sum_over(total, "grp")
     total, *grams = lax.optimization_barrier((total, *grams))

time: 97.4 us -> 95.2 us (0.977)
  waiting for transfers between devices: 16.6 us -> 14.7 us
  Pallas kernels: 47.3 us -> 46.3 us
    pallas_call x1, Pallas kernels: 19.7 us -> 17.7 us  [body(): pl.pallas_call(functools.partial(steps_kernel, count_x), out_shape=[jax.S...]
    ppermute x17, waiting for transfers between devices: 16.6 us -> 14.7 us  [exchange(): return lax.ppermute(value, axis, [(i, i ^ flips) for i in range(count)])]
  transfers between devices with their start and end apart: 24 -> 24, of which waited for: 10 -> 8; matrix products, arithmetic and copies ran while one was open for 0% -> 0% of each run, Pallas kernels for 44% -> 44%
where the time goes in v8:
time: 95.2 us; the launch traced here: 95 us
  Pallas kernels  46.3 us (49%)
  starting transfers between devices  32.1 us (34%)
  waiting for transfers between devices  14.7 us (15%)
    ppermute x17, starting transfers between devices, exchange(): return lax.ppermute(value, axis, [(i, i ^ flips) for i in range(count)])  20.7 us
    pallas_call x1, Pallas kernels, body(): pl.pallas_call(functools.partial(steps_kernel, count_x), out_shape=[jax.S...  17.7 us
    ppermute x17, waiting for transfers between devices, exchange(): return lax.ppermute(value, axis, [(i, i ^ flips) for i in range(count)])  14.7 us
    pallas_call x3, Pallas kernels, gram_part(): pl.pallas_call(functools.partial(gram_kernel, places, later, bool(parts),...  13.7 us
    pallas_call x3, Pallas kernels, product(): pl.pallas_call(functools.partial(product_kernel, flips, later, bool(rows)...  10.6 us
    ppermute x1, starting transfers between devices, body(): from_a = [lax.ppermute(own, 'gy', pairs('gy', 0))]  4.45 us
    ppermute x1, starting transfers between devices, body(): lax.ppermute(own, 'gx', [(i, (i - shift) % count_x) for i in range(count_...  2.94 us
    pallas_call x1, Pallas kernels, body(): pl.pallas_call(functools.partial(edges_kernel, count_x), out_shape=(packe...  2.56 us
  transfers between devices with their start and end apart: 24, of which 8 were waited for; matrix products, arithmetic and copies ran while one was open for 0% of the time, Pallas kernels for 44%

profile of v8, /device:TPU:0, one launch (start us, length us, event | category | flops | bytes accessed | tf_op | source)
XLA Modules:
  0.0 95.0 jit_solution(14355021553559028566)
XLA Ops:
  0.6 1.7 %pack.1.refs_0_ = f32[6,16,4,128]{3,2,1,0:T(4,128)} custom-call(f32[4,4,16,128]{3,2,1,0:T(8,128)} %terminal.1, f32[4,16,128]{2,1,0:T(8,128)} %velocity.1, s32[4,16,128]{2,1,0:T(8,128)} %material.1), custom_call_target="tpu_custom_call" | custom-call | tf_op jit(solution)/shard_map/pack/pallas_call | solution.py:446
  2.3 2.9 %collective-permute-start = (f32[6,16,4,128]{3,2,1,0:T(4,128)}, f32[6,16,4,128]{3,2,1,0:T(4,128)S(1)}, u32[]{:S(2)}, u32[]{:S(2)}) collective-permute-start(f32[6,16,4,128]{3,2,1,0:T(4,128)} %pack.1.refs_0_), channel_id=1, source_target_pairs={{0,4},{4,0},{1,5},{5,1},{2,6},{6,2},{3,7},{7,3},{8,12},{12,8},{9,1... | collective-permute-start | bytes 589832 | tf_op jit(solution)/shard_map/ppermute | solution.py:456
  5.3 0.7 collective-permute-start.3
  6.0 4.5 %collective-permute-start.1 = (f32[6,16,4,128]{3,2,1,0:T(4,128)}, f32[6,16,4,128]{3,2,1,0:T(4,128)S(1)}, u32[]{:S(2)}, u32[]{:S(2)}) collective-permute-start(f32[6,16,4,128]{3,2,1,0:T(4,128)} %pack.1.refs_0_), channel_id=1, source_target_pairs={{0,1},{2,3},{1,0},{3,2},{4,5},{6,7},{5,4},{7,6},{8,9},{10,11},{9,8... | collective-permute-start | bytes 589832 | tf_op jit(solution)/shard_map/ppermute | solution.py:458
  10.4 3.5 %gram.3.refs_1_ = f32[256,256]{1,0:T(8,128)S(1)} custom-call(bf16[1,4,16,512,256]{4,3,2,1,0:T(8,128)(2,1)} %refs_1_.3), custom_call_target="tpu_custom_call" | custom-call | flops 1073741824 | bytes 12582912 | tf_op jit(solution)/shard_map/gram/pallas_call | solution.py:333
  14.0 0.8 collective-permute-start.4
  14.8 1.8 %collective-permute-start.2 = (f32[6,16,4,128]{3,2,1,0:T(4,128)S(1)}, f32[6,16,4,128]{3,2,1,0:T(4,128)S(1)}, u32[]{:S(2)}, u32[]{:S(2)}) collective-permute-start(f32[6,16,4,128]{3,2,1,0:T(4,128)S(1)} %collective-permute-done.refs_1_), channel_id=1, source_target_pairs={{0,1},{2,3},{1,0},{3,2},{4,5},{6,7},{5,4},{7,6},{8,9},{10,11},{9,8... | collective-permute-start | bytes 589832 | tf_op jit(solution)/shard_map/ppermute | solution.py:462
  16.6 4.7 %gram.4 = (f32[256,256]{1,0:T(8,128)S(1)}, bf16[16,512,256]{2,1,0:T(8,128)(2,1)S(1)}, bf16[16,512,256]{2,1,0:T(8,128)(2,1)S(1)}) custom-call(bf16[1,4,16,512,256]{4,3,2,1,0:T(8,128)(2,1)} %refs_1_.3, f32[256,256]{1,0:T(8,128)S(1)} %gram.3.refs_1_), custom_call_target="tpu_custom_call" | custom-call | flops 1073741824 | bytes 12582912 | tf_op jit(solution)/shard_map/gram/pallas_call | solution.py:333
  21.3 2.6 %edges.1 = (f32[6,6,8,128]{3,2,1,0:T(8,128)S(1)}, f32[6,6,8,128]{3,2,1,0:T(8,128)S(1)}) custom-call(f32[6,16,4,128]{3,2,1,0:T(4,128)S(1)} %copy-done, f32[6,16,4,128]{3,2,1,0:T(4,128)S(1)} %collective-permute-done.refs_1_, f32[6,16,4,128]{3,2,1,0:T(4,128)S(1)} %collective-permute-done.1.refs_2_, f32[6,16,4,128]{3,2,1,0:T(4,128)S(1)} %collective-permute-done.2.refs_3_, ...), custom_call_target="tpu_custom_call" | custom-call | tf_op jit(solution)/shard_map/edges/pallas_call | solution.py:470
  23.9 0.1 collective-permute-start.5
  24.0 0.7 collective-permute-start.6
  24.7 0.0 copy-start.4
  24.7 0.0 copy-start.1
  24.7 0.0 copy-start.2
  24.7 0.0 copy-start.3
  24.7 5.5 %gram.5 = f32[256,256]{1,0:T(8,128)S(1)} custom-call(bf16[16,512,256]{2,1,0:T(8,128)(2,1)S(1)} %get-tuple-element.50.refs_0_, bf16[16,512,256]{2,1,0:T(8,128)(2,1)S(1)} %get-tuple-element.51.refs_1_, f32[256,256]{1,0:T(8,128)S(1)} %get-tuple-element.52.refs_2_), custom_call_target="tpu_custom_call" | custom-call | flops 2147483648 | bytes 25165824 | tf_op jit(solution)/shard_map/gram/pallas_call | solution.py:333
  30.2 1.7 %collective-permute-start.11 = (f32[256,256]{1,0:T(8,128)S(1)}, f32[256,256]{1,0:T(8,128)S(1)}, u32[]{:S(2)}, u32[]{:S(2)}) collective-permute-start(f32[256,256]{1,0:T(8,128)S(1)} %gram.5), channel_id=1, source_target_pairs={{0,24},{8,16},{16,8},{24,0},{1,25},{9,17},{17,9},{25,1},{2,26},{10... | collective-permute-start | bytes 786440 | tf_op jit(solution)/shard_map/ppermute | solution.py:27
  31.9 2.9 %collective-permute-start.10 = (f32[256,256]{1,0:T(8,128)S(1)}, f32[256,256]{1,0:T(8,128)S(1)}, u32[]{:S(2)}, u32[]{:S(2)}) collective-permute-start(f32[256,256]{1,0:T(8,128)S(1)} %gram.5), channel_id=1, source_target_pairs={{0,16},{8,24},{16,0},{24,8},{1,17},{9,25},{17,1},{25,9},{2,18},{10... | collective-permute-start | bytes 786440 | tf_op jit(solution)/shard_map/ppermute | solution.py:27
  34.8 0.1 copy.10.stoich
  34.9 17.7 %steps.1 = (f32[4,4,16,128]{3,2,1,0:T(8,128)}, f32[4,16,8,128]{3,2,1,0:T(8,128)S(1)}, f32[4,16,8,128]{3,2,1,0:T(8,128)S(1)}, f32[4,16,8,128]{3,2,1,0:T(8,128)S(1)}, f32[4,16,8,128]{3,2,1,0:T(8,128)S(1)}) custom-call(s32[8]{0:T(128)S(1)} %copy-done.2, f32[4]{0:T(128)S(1)} %copy-done.3, s32[8,4]{1,0:T(8,128)S(1)} %copy.10.stoich, f32[8,8]{1,0:T(8,128)S(1)} %copy-done.1, ...), custom_call_target="tpu_custom_call" | custom-call | bytes 100663296 | tf_op jit(solution)/shard_map/steps/pallas_call | solution.py:488
  52.6 0.8 collective-permute-start.7
  53.4 1.2 %collective-permute-start.8 = (f32[4,16,8,128]{3,2,1,0:T(8,128)S(1)}, f32[4,16,8,128]{3,2,1,0:T(8,128)S(1)}, u32[]{:S(2)}, u32[]{:S(2)}) collective-permute-start(f32[4,16,8,128]{3,2,1,0:T(8,128)S(1)} %get-tuple-element.56), channel_id=1, source_target_pairs={{0,24},{8,16},{16,8},{24,0},{1,25},{9,17},{17,9},{25,1},{2,26},{10... | collective-permute-start | bytes 786440 | tf_op jit(solution)/shard_map/ppermute | solution.py:27
  54.6 0.3 collective-permute-start.12
  54.9 0.1 add_add_fusion
  54.9 0.8 collective-permute-start.16
  55.7 4.7 %product.3 = (f32[16,256]{1,0:T(8,128)S(1)}, bf16[4,16,128,256]{3,2,1,0:T(8,128)(2,1)S(1)}, bf16[4,16,128,256]{3,2,1,0:T(8,128)(2,1)S(1)}) custom-call(f32[4,16,8,128]{3,2,1,0:T(8,128)S(1)} %get-tuple-element.64.refs_0_, bf16[1,4,16,512,256]{4,3,2,1,0:T(8,128)(2,1)} %refs_1_.3), custom_call_target="tpu_custom_call" | custom-call | flops 67108864 | bytes 8388608 | tf_op jit(solution)/shard_map/product/pallas_call | solution.py:418
  60.4 2.7 %product.4.refs_4_ = f32[16,256]{1,0:T(8,128)S(1)} custom-call(f32[4,16,8,128]{3,2,1,0:T(8,128)S(1)} %collective-permute-done.12.refs_0_, bf16[1,4,16,512,256]{4,3,2,1,0:T(8,128)(2,1)} %refs_1_.3, f32[16,256]{1,0:T(8,128)S(1)} %get-tuple-element.68.refs_2_), custom_call_target="tpu_custom_call" | custom-call | flops 67108864 | bytes 8388608 | tf_op jit(solution)/shard_map/product/pallas_call | solution.py:418
  63.1 3.5 %collective-permute-done.8.refs_1_ = f32[4,16,8,128]{3,2,1,0:T(8,128)S(1)} collective-permute-done((f32[4,16,8,128]{3,2,1,0:T(8,128)S(1)}, f32[4,16,8,128]{3,2,1,0:T(8,128)S(1)}, u32[]{:S(2)}, u32[]{:S(2)}) %collective-permute-start.8) | collective-permute-done | bytes 262176 | tf_op jit(solution)/shard_map/ppermute | solution.py:27
  66.6 3.2 %product.5 = f32[16,256]{1,0:T(8,128)S(1)} custom-call(f32[4,16,8,128]{3,2,1,0:T(8,128)S(1)} %collective-permute-done.7.refs_0_, f32[4,16,8,128]{3,2,1,0:T(8,128)S(1)} %collective-permute-done.8.refs_1_, bf16[4,16,128,256]{3,2,1,0:T(8,128)(2,1)S(1)} %get-tuple-element.65.refs_2_, bf16[4,16,128,256]{3,2,1,0:T(8,128)(2,1)S(1)} %get-tuple-element.66.refs_3_, ...), custom_call_target="tpu_custom_call" | custom-call | flops 134217728 | bytes 16777216 | tf_op jit(solution)/shard_map/product/pallas_call | solution.py:418
  69.8 0.2 collective-permute-start.15
  70.0 1.7 %collective-permute-start.14 = (f32[16,256]{1,0:T(8,128)S(1)}, f32[16,256]{1,0:T(8,128)S(1)}, u32[]{:S(2)}, u32[]{:S(2)}) collective-permute-start(f32[16,256]{1,0:T(8,128)S(1)} %product.5), channel_id=1, source_target_pairs={{0,16},{8,24},{16,0},{24,8},{1,17},{9,25},{17,1},{25,9},{2,18},{10... | collective-permute-start | bytes 49160 | tf_op jit(solution)/shard_map/ppermute | solution.py:27
  71.7 0.0 collective-permute-start.13
  71.7 1.3 %collective-permute-done.15 = f32[16,256]{1,0:T(8,128)S(1)} collective-permute-done((f32[16,256]{1,0:T(8,128)S(1)}, f32[16,256]{1,0:T(8,128)S(1)}, u32[]{:S(2)}, u32[]{:S(2)}) %collective-permute-start.15) | collective-permute-done | bytes 16416 | tf_op jit(solution)/shard_map/ppermute | solution.py:27
  73.0 0.7 collective-permute-done.14
  73.7 0.8 collective-permute-start.17
  74.5 3.0 %collective-permute-done.17 = f32[16,256]{1,0:T(8,128)S(1)} collective-permute-done((f32[16,256]{1,0:T(8,128)S(1)}, f32[16,256]{1,0:T(8,128)S(1)}, u32[]{:S(2)}, u32[]{:S(2)}) %collective-permute-start.17) | collective-permute-done | bytes 16416 | tf_op jit(solution)/shard_map/ppermute | solution.py:27
  77.6 2.5 %collective-permute-start.20 = (f32[8,256]{1,0:T(8,128)S(1)}, f32[8,256]{1,0:T(8,128)S(1)}, u32[]{:S(2)}, u32[]{:S(2)}) collective-permute-start(f32[8,256]{1,0:T(8,128)S(1)} %slice_add_fusion.1), channel_id=1, source_target_pairs={{0,3},{1,2},{2,1},{3,0},{4,7},{5,6},{6,5},{7,4},{8,11},{9,10},{10,... | collective-permute-start | bytes 24584 | tf_op jit(solution)/shard_map/ppermute | solution.py:27
  80.0 3.5 %collective-permute-start.19 = (f32[8,256]{1,0:T(8,128)S(1)}, f32[8,256]{1,0:T(8,128)S(1)}, u32[]{:S(2)}, u32[]{:S(2)}) collective-permute-start(f32[8,256]{1,0:T(8,128)S(1)} %slice_add_fusion.1), channel_id=1, source_target_pairs={{0,2},{1,3},{2,0},{3,1},{4,6},{5,7},{6,4},{7,5},{8,10},{9,11},{10,... | collective-permute-start | bytes 24584 | tf_op jit(solution)/shard_map/ppermute | solution.py:27
  83.5 0.1 collective-permute-start.18
  83.6 1.6 %collective-permute-done.19 = f32[8,256]{1,0:T(8,128)S(1)} collective-permute-done((f32[8,256]{1,0:T(8,128)S(1)}, f32[8,256]{1,0:T(8,128)S(1)}, u32[]{:S(2)}, u32[]{:S(2)}) %collective-permute-start.19) | collective-permute-done | bytes 8224 | tf_op jit(solution)/shard_map/ppermute | solution.py:27
  85.2 1.9 %collective-permute-done.18 = f32[8,256]{1,0:T(8,128)S(1)} collective-permute-done((f32[8,256]{1,0:T(8,128)S(1)}, f32[8,256]{1,0:T(8,128)S(1)}, u32[]{:S(2)}, u32[]{:S(2)}) %collective-permute-start.18) | collective-permute-done | bytes 8224 | tf_op jit(solution)/shard_map/ppermute | solution.py:27
  87.1 0.2 fusion.3
  87.4 2.5 %collective-permute-start.23 = (f32[8,256]{1,0:T(8,128)S(1)}, f32[8,256]{1,0:T(8,128)S(1)}, u32[]{:S(2)}, u32[]{:S(2)}) collective-permute-start(f32[8,256]{1,0:T(8,128)S(1)} %fusion.3), channel_id=1, source_target_pairs={{0,3},{1,2},{2,1},{3,0},{4,7},{5,6},{6,5},{7,4},{8,11},{9,10},{10,... | collective-permute-start | bytes 24584 | tf_op jit(solution)/shard_map/ppermute | solution.py:27
  89.8 0.0 collective-permute-start.22
  89.9 1.9 %collective-permute-start.21 = (f32[8,256]{1,0:T(8,128)S(1)}, f32[8,256]{1,0:T(8,128)S(1)}, u32[]{:S(2)}, u32[]{:S(2)}) collective-permute-start(f32[8,256]{1,0:T(8,128)S(1)} %fusion.3), channel_id=1, source_target_pairs={{0,1},{1,0},{2,3},{3,2},{4,5},{5,4},{6,7},{7,6},{8,9},{9,8},{10,11... | collective-permute-start | bytes 24584 | tf_op jit(solution)/shard_map/ppermute | solution.py:27
  91.8 1.1 %collective-permute-done.23 = f32[8,256]{1,0:T(8,128)S(1)} collective-permute-done((f32[8,256]{1,0:T(8,128)S(1)}, f32[8,256]{1,0:T(8,128)S(1)}, u32[]{:S(2)}, u32[]{:S(2)}) %collective-permute-start.23) | collective-permute-done | bytes 8224 | tf_op jit(solution)/shard_map/ppermute | solution.py:27
  92.8 1.6 %collective-permute-done.22 = f32[8,256]{1,0:T(8,128)S(1)} collective-permute-done((f32[8,256]{1,0:T(8,128)S(1)}, f32[8,256]{1,0:T(8,128)S(1)}, u32[]{:S(2)}, u32[]{:S(2)}) %collective-permute-start.22) | collective-permute-done | bytes 8224 | tf_op jit(solution)/shard_map/ppermute | solution.py:27
  94.4 0.6 add_add_fusion.2
  (26 shorter events, 0.1 us)
Async XLA Ops:
  2.3 11.6 %collective-permute-start = (f32[6,16,4,128]{3,2,1,0:T(4,128)}, f32[6,16,4,128]{3,2,1,0:T(4,128)S(1)}, u32[]{:S(2)}, u32[]{:S(2)}) collective-permute-start(f32[6,16,4,128]{3,2,1,0:T(4,128)} %pack.1.refs_0_), channel_id=1, source_target_pairs={{0,4},{4,0},{1,5},{5,1},{2,6},{6,2},{3,7},{7,3},{8,12},{12,8},{9,1... | collective-permute-start | bytes 589832 | tf_op jit(solution)/shard_map/ppermute | solution.py:456
  5.3 16.0 %collective-permute-start.3 = (f32[6,16,4,128]{3,2,1,0:T(4,128)}, f32[6,16,4,128]{3,2,1,0:T(4,128)S(1)}, u32[]{:S(2)}, u32[]{:S(2)}) collective-permute-start(f32[6,16,4,128]{3,2,1,0:T(4,128)} %pack.1.refs_0_), channel_id=1, source_target_pairs={{1,2},{2,1},{5,6},{6,5},{9,10},{10,9},{13,14},{14,13},{17,18},{18,... | collective-permute-start | bytes 589832 | tf_op jit(solution)/shard_map/ppermute | solution.py:459
  6.0 15.3 %collective-permute-start.1 = (f32[6,16,4,128]{3,2,1,0:T(4,128)}, f32[6,16,4,128]{3,2,1,0:T(4,128)S(1)}, u32[]{:S(2)}, u32[]{:S(2)}) collective-permute-start(f32[6,16,4,128]{3,2,1,0:T(4,128)} %pack.1.refs_0_), channel_id=1, source_target_pairs={{0,1},{2,3},{1,0},{3,2},{4,5},{6,7},{5,4},{7,6},{8,9},{10,11},{9,8... | collective-permute-start | bytes 589832 | tf_op jit(solution)/shard_map/ppermute | solution.py:458
  14.0 7.4 %copy-start = (f32[6,16,4,128]{3,2,1,0:T(4,128)S(1)}, f32[6,16,4,128]{3,2,1,0:T(4,128)}, u32[]{:S(2)}) copy-start(f32[6,16,4,128]{3,2,1,0:T(4,128)} %pack.1.refs_0_) | copy-start | bytes 589828
  14.0 7.3 %collective-permute-start.4 = (f32[6,16,4,128]{3,2,1,0:T(4,128)S(1)}, f32[6,16,4,128]{3,2,1,0:T(4,128)S(1)}, u32[]{:S(2)}, u32[]{:S(2)}) collective-permute-start(f32[6,16,4,128]{3,2,1,0:T(4,128)S(1)} %collective-permute-done.refs_1_), channel_id=1, source_target_pairs={{1,2},{2,1},{5,6},{6,5},{9,10},{10,9},{13,14},{14,13},{17,18},{18,... | collective-permute-start | bytes 589832 | tf_op jit(solution)/shard_map/ppermute | solution.py:463
  14.8 6.5 %collective-permute-start.2 = (f32[6,16,4,128]{3,2,1,0:T(4,128)S(1)}, f32[6,16,4,128]{3,2,1,0:T(4,128)S(1)}, u32[]{:S(2)}, u32[]{:S(2)}) collective-permute-start(f32[6,16,4,128]{3,2,1,0:T(4,128)S(1)} %collective-permute-done.refs_1_), channel_id=1, source_target_pairs={{0,1},{2,3},{1,0},{3,2},{4,5},{6,7},{5,4},{7,6},{8,9},{10,11},{9,8... | collective-permute-start | bytes 589832 | tf_op jit(solution)/shard_map/ppermute | solution.py:462
  23.9 6.3 %collective-permute-start.5 = (f32[6,6,8,128]{3,2,1,0:T(8,128)S(1)}, f32[6,6,8,128]{3,2,1,0:T(8,128)S(1)}, u32[]{:S(2)}, u32[]{:S(2)}) collective-permute-start(f32[6,6,8,128]{3,2,1,0:T(8,128)S(1)} %get-tuple-element.48), channel_id=1, source_target_pairs={{0,8},{16,24},{8,0},{24,16},{1,9},{17,25},{9,1},{25,17},{2,10},{18... | collective-permute-start | bytes 442376 | tf_op jit(solution)/shard_map/ppermute | solution.py:479
  24.0 6.2 %collective-permute-start.6 = (f32[6,6,8,128]{3,2,1,0:T(8,128)S(1)}, f32[6,6,8,128]{3,2,1,0:T(8,128)S(1)}, u32[]{:S(2)}, u32[]{:S(2)}) collective-permute-start(f32[6,6,8,128]{3,2,1,0:T(8,128)S(1)} %get-tuple-element.49), channel_id=1, source_target_pairs={{8,16},{16,8},{9,17},{17,9},{10,18},{18,10},{11,19},{19,11},{12,20... | collective-permute-start | bytes 442376 | tf_op jit(solution)/shard_map/ppermute | solution.py:480
  24.7 10.1 %copy-start.4 = (s32[8,4]{0,1:T(4,128)S(1)}, s32[8,4]{0,1:T(4,128)}, u32[]{:S(2)}) copy-start(s32[8,4]{0,1:T(4,128)} %param.13) | copy-start | bytes 388
  24.7 10.2 %copy-start.1 = (f32[8,8]{1,0:T(8,128)S(1)}, f32[8,8]{1,0:T(8,128)}, u32[]{:S(2)}) copy-start(f32[8,8]{1,0:T(8,128)} %rates.1) | copy-start | bytes 772
  24.7 10.2 %copy-start.2 = (s32[8]{0:T(128)S(1)}, s32[8]{0:T(128)}, u32[]{:S(2)}) copy-start(s32[8]{0:T(128)} %plan.1) | copy-start | bytes 100
  24.7 10.2 %copy-start.3 = (f32[4]{0:T(128)S(1)}, f32[4]{0:T(128)}, u32[]{:S(2)}) copy-start(f32[4]{0:T(128)} %diffusion.1) | copy-start | bytes 52
  30.2 24.3 %collective-permute-start.11 = (f32[256,256]{1,0:T(8,128)S(1)}, f32[256,256]{1,0:T(8,128)S(1)}, u32[]{:S(2)}, u32[]{:S(2)}) collective-permute-start(f32[256,256]{1,0:T(8,128)S(1)} %gram.5), channel_id=1, source_target_pairs={{0,24},{8,16},{16,8},{24,0},{1,25},{9,17},{17,9},{25,1},{2,26},{10... | collective-permute-start | bytes 786440 | tf_op jit(solution)/shard_map/ppermute | solution.py:27
  31.9 23.0 %collective-permute-start.10 = (f32[256,256]{1,0:T(8,128)S(1)}, f32[256,256]{1,0:T(8,128)S(1)}, u32[]{:S(2)}, u32[]{:S(2)}) collective-permute-start(f32[256,256]{1,0:T(8,128)S(1)} %gram.5), channel_id=1, source_target_pairs={{0,16},{8,24},{16,0},{24,8},{1,17},{9,25},{17,1},{25,9},{2,18},{10... | collective-permute-start | bytes 786440 | tf_op jit(solution)/shard_map/ppermute | solution.py:27
  34.8 20.1 %collective-permute-start.9 = (f32[256,256]{1,0:T(8,128)S(1)}, f32[256,256]{1,0:T(8,128)S(1)}, u32[]{:S(2)}, u32[]{:S(2)}) collective-permute-start(f32[256,256]{1,0:T(8,128)S(1)} %gram.5), channel_id=1, source_target_pairs={{0,8},{8,0},{16,24},{24,16},{1,9},{9,1},{17,25},{25,17},{2,10},{10... | collective-permute-start | bytes 786440 | tf_op jit(solution)/shard_map/ppermute | solution.py:27
  52.6 10.5 %collective-permute-start.7 = (f32[4,16,8,128]{3,2,1,0:T(8,128)S(1)}, f32[4,16,8,128]{3,2,1,0:T(8,128)S(1)}, u32[]{:S(2)}, u32[]{:S(2)}) collective-permute-start(f32[4,16,8,128]{3,2,1,0:T(8,128)S(1)} %get-tuple-element.55), channel_id=1, source_target_pairs={{0,16},{8,24},{16,0},{24,8},{1,17},{9,25},{17,1},{25,9},{2,18},{10... | collective-permute-start | bytes 786440 | tf_op jit(solution)/shard_map/ppermute | solution.py:27
  53.4 13.2 %collective-permute-start.8 = (f32[4,16,8,128]{3,2,1,0:T(8,128)S(1)}, f32[4,16,8,128]{3,2,1,0:T(8,128)S(1)}, u32[]{:S(2)}, u32[]{:S(2)}) collective-permute-start(f32[4,16,8,128]{3,2,1,0:T(8,128)S(1)} %get-tuple-element.56), channel_id=1, source_target_pairs={{0,24},{8,16},{16,8},{24,0},{1,25},{9,17},{17,9},{25,1},{2,26},{10... | collective-permute-start | bytes 786440 | tf_op jit(solution)/shard_map/ppermute | solution.py:27
  54.6 5.9 %collective-permute-start.12 = (f32[4,16,8,128]{3,2,1,0:T(8,128)S(1)}, f32[4,16,8,128]{3,2,1,0:T(8,128)S(1)}, u32[]{:S(2)}, u32[]{:S(2)}) collective-permute-start(f32[4,16,8,128]{3,2,1,0:T(8,128)S(1)} %get-tuple-element.67), channel_id=1, source_target_pairs={{0,8},{8,0},{16,24},{24,16},{1,9},{9,1},{17,25},{25,17},{2,10},{10... | collective-permute-start | bytes 786440 | tf_op jit(solution)/shard_map/ppermute | solution.py:27
  54.9 18.8 %collective-permute-start.16 = (f32[256,256]{1,0:T(8,128)S(1)}, f32[256,256]{1,0:T(8,128)S(1)}, u32[]{:S(2)}, u32[]{:S(2)}) collective-permute-start(f32[256,256]{1,0:T(8,128)S(1)} %add_add_fusion), channel_id=1, source_target_pairs={{0,4},{4,0},{1,5},{5,1},{2,6},{6,2},{3,7},{7,3},{8,12},{12,8},{9,1... | collective-permute-start | bytes 786440 | tf_op jit(solution)/shard_map/ppermute | solution.py:27
  69.8 3.2 %collective-permute-start.15 = (f32[16,256]{1,0:T(8,128)S(1)}, f32[16,256]{1,0:T(8,128)S(1)}, u32[]{:S(2)}, u32[]{:S(2)}) collective-permute-start(f32[16,256]{1,0:T(8,128)S(1)} %product.5), channel_id=1, source_target_pairs={{0,24},{8,16},{16,8},{24,0},{1,25},{9,17},{17,9},{25,1},{2,26},{10... | collective-permute-start | bytes 49160 | tf_op jit(solution)/shard_map/ppermute | solution.py:27
  70.0 3.7 %collective-permute-start.14 = (f32[16,256]{1,0:T(8,128)S(1)}, f32[16,256]{1,0:T(8,128)S(1)}, u32[]{:S(2)}, u32[]{:S(2)}) collective-permute-start(f32[16,256]{1,0:T(8,128)S(1)} %product.5), channel_id=1, source_target_pairs={{0,16},{8,24},{16,0},{24,8},{1,17},{9,25},{17,1},{25,9},{2,18},{10... | collective-permute-start | bytes 49160 | tf_op jit(solution)/shard_map/ppermute | solution.py:27
  71.7 2.0 %collective-permute-start.13 = (f32[16,256]{1,0:T(8,128)S(1)}, f32[16,256]{1,0:T(8,128)S(1)}, u32[]{:S(2)}, u32[]{:S(2)}) collective-permute-start(f32[16,256]{1,0:T(8,128)S(1)} %product.5), channel_id=1, source_target_pairs={{0,8},{8,0},{16,24},{24,16},{1,9},{9,1},{17,25},{25,17},{2,10},{10... | collective-permute-start | bytes 49160 | tf_op jit(solution)/shard_map/ppermute | solution.py:27
  73.7 3.8 %collective-permute-start.17 = (f32[16,256]{1,0:T(8,128)S(1)}, f32[16,256]{1,0:T(8,128)S(1)}, u32[]{:S(2)}, u32[]{:S(2)}) collective-permute-start(f32[16,256]{1,0:T(8,128)S(1)} %add_add_fusion.1), channel_id=1, source_target_pairs={{0,4},{4,0},{1,5},{5,1},{2,6},{6,2},{3,7},{7,3},{8,12},{12,8},{9,1... | collective-permute-start | bytes 49160 | tf_op jit(solution)/shard_map/ppermute | solution.py:27
  77.6 6.1 %collective-permute-start.20 = (f32[8,256]{1,0:T(8,128)S(1)}, f32[8,256]{1,0:T(8,128)S(1)}, u32[]{:S(2)}, u32[]{:S(2)}) collective-permute-start(f32[8,256]{1,0:T(8,128)S(1)} %slice_add_fusion.1), channel_id=1, source_target_pairs={{0,3},{1,2},{2,1},{3,0},{4,7},{5,6},{6,5},{7,4},{8,11},{9,10},{10,... | collective-permute-start | bytes 24584 | tf_op jit(solution)/shard_map/ppermute | solution.py:27
  80.0 5.2 %collective-permute-start.19 = (f32[8,256]{1,0:T(8,128)S(1)}, f32[8,256]{1,0:T(8,128)S(1)}, u32[]{:S(2)}, u32[]{:S(2)}) collective-permute-start(f32[8,256]{1,0:T(8,128)S(1)} %slice_add_fusion.1), channel_id=1, source_target_pairs={{0,2},{1,3},{2,0},{3,1},{4,6},{5,7},{6,4},{7,5},{8,10},{9,11},{10,... | collective-permute-start | bytes 24584 | tf_op jit(solution)/shard_map/ppermute | solution.py:27
  83.5 3.7 %collective-permute-start.18 = (f32[8,256]{1,0:T(8,128)S(1)}, f32[8,256]{1,0:T(8,128)S(1)}, u32[]{:S(2)}, u32[]{:S(2)}) collective-permute-start(f32[8,256]{1,0:T(8,128)S(1)} %slice_add_fusion.1), channel_id=1, source_target_pairs={{0,1},{1,0},{2,3},{3,2},{4,5},{5,4},{6,7},{7,6},{8,9},{9,8},{10,11... | collective-permute-start | bytes 24584 | tf_op jit(solution)/shard_map/ppermute | solution.py:27
  87.4 5.5 %collective-permute-start.23 = (f32[8,256]{1,0:T(8,128)S(1)}, f32[8,256]{1,0:T(8,128)S(1)}, u32[]{:S(2)}, u32[]{:S(2)}) collective-permute-start(f32[8,256]{1,0:T(8,128)S(1)} %fusion.3), channel_id=1, source_target_pairs={{0,3},{1,2},{2,1},{3,0},{4,7},{5,6},{6,5},{7,4},{8,11},{9,10},{10,... | collective-permute-start | bytes 24584 | tf_op jit(solution)/shard_map/ppermute | solution.py:27
  89.8 4.5 %collective-permute-start.22 = (f32[8,256]{1,0:T(8,128)S(1)}, f32[8,256]{1,0:T(8,128)S(1)}, u32[]{:S(2)}, u32[]{:S(2)}) collective-permute-start(f32[8,256]{1,0:T(8,128)S(1)} %fusion.3), channel_id=1, source_target_pairs={{0,2},{1,3},{2,0},{3,1},{4,6},{5,7},{6,4},{7,5},{8,10},{9,11},{10,... | collective-permute-start | bytes 24584 | tf_op jit(solution)/shard_map/ppermute | solution.py:27
  89.9 4.5 %collective-permute-start.21 = (f32[8,256]{1,0:T(8,128)S(1)}, f32[8,256]{1,0:T(8,128)S(1)}, u32[]{:S(2)}, u32[]{:S(2)}) collective-permute-start(f32[8,256]{1,0:T(8,128)S(1)} %fusion.3), channel_id=1, source_target_pairs={{0,1},{1,0},{2,3},{3,2},{4,5},{5,4},{6,7},{7,6},{8,9},{9,8},{10,11... | collective-permute-start | bytes 24584 | tf_op jit(solution)/shard_map/ppermute | solution.py:27

commit v9 on v8

--- a/solution.py
+++ b/solution.py
@@ -98,13 +98,16 @@
                 top = bottom = None
                 for group in range(GROUPS):
                     row = part * GROUPS + group
-                    last = jnp.concatenate(
-                        [b[field, row, :, cells_z - LANES :] for b in mine], axis=0
-                    )
-                    start = jnp.concatenate([b[field, row, :, :LANES] for b in mine], axis=0)
-                    high = pltpu.roll(last, (STEPS * (group + 1)) % LANES, 1)
-                    low = pltpu.roll(start, STEPS * group, 1) if group else start
-                    top = high if top is None else jnp.where(place == group, high, top)
+                    low = jnp.concatenate([b[field, row, :, :LANES] for b in mine], axis=0)
+                    low = pltpu.roll(low, STEPS * group, 1) if group else low
+                    high = low
+                    if cells_z > LANES:
+                        high = jnp.concatenate(
+                            [b[field, row, :, cells_z - LANES :] for b in mine], axis=0
+                        )
+                        high = pltpu.roll(high, STEPS * group, 1) if group else high
+                    is_high = place == (group - 1) % GROUPS
+                    top = high if top is None else jnp.where(is_high, high, top)
                     bottom = low if bottom is None else jnp.where(place == group, low, bottom)
                 out_a[field, slot * per_block + part] = jnp.where(even, top, bottom)
                 out_b[field, slot * per_block + part] = jnp.where(even, bottom, top)
@@ -136,6 +139,7 @@
         BLOCK + jnp.where(even_y, 0, 2 * cells_y),
     )
     lane = lax.broadcasted_iota(jnp.int32, (all_x, LANES), 1)
+    place = lane // STEPS
     is_right = lane < LANES // 2
     has_right = grp < count_grp - 1
     has_left = grp > 0
@@ -175,9 +179,10 @@
                 for group in range(GROUPS):
                     row = part * GROUPS + group
                     own = jnp.concatenate([b[field, row] for b in mine], axis=0)
-                    after = pltpu.roll(right, (LANES - STEPS * group) % LANES, 1) if group else right
-                    before = pltpu.roll(left, LANES - STEPS * (group + 1), 1) if group < GROUPS - 1 else left
-                    out.append(jnp.concatenate([own, jnp.where(is_right, after, before)], axis=1))
+                    beyond = jnp.where(place == group, right, left)
+                    if group:
+                        beyond = pltpu.roll(beyond, LANES - STEPS * group, 1)
+                    out.append(jnp.concatenate([own, beyond], axis=1))
                 return out
 
             first_row = starts[slot] + part * GROUPS
@@ -311,9 +316,11 @@
     targets = [chunks.at[i] for i in range(count)] + [held][:given] + list(ahead)
     copies = fetch(sources, targets, sems)
     acc = None
-    for i in range(count):
-        copies[i].wait()
-        chunk = chunks[i].reshape(rows * cells_z, modes)
+    together = count if fetched else 1
+    for i in range(0, count, together):
+        for copy in copies[i : i + together]:
+            copy.wait()
+        chunk = chunks[i : i + together].reshape(together * rows * cells_z, modes)
         part = lax.dot_general(
             chunk, chunk, (((0,), (0,)), ((), ())), preferred_element_type=jnp.float32
         )
@@ -327,7 +334,8 @@
 
 def gram_part(places, basis, *total, later=(), parts=()):
     _, _, cells_y, cells_z, modes = basis.shape
-    chunks, given = 2 * len(places), len(total)
+    halves, given = 1 if parts else 2, len(total)
+    chunks = halves * len(places)
     size = 2 * len(places) * cells_y * cells_z * modes
     tables = parts or (basis,)
     return pl.pallas_call(
@@ -337,11 +345,11 @@
         in_specs=anywhere(len(tables) + given),
         out_specs=whole(1) + anywhere(len(later)),
         scratch_shapes=[
-            pltpu.VMEM((chunks, cells_y // 2, cells_z, modes), jnp.bfloat16),
+            pltpu.VMEM((chunks, cells_y // halves, cells_z, modes), jnp.bfloat16),
             pltpu.VMEM((modes, modes), jnp.float32),
             pltpu.SemaphoreType.DMA((chunks + given + len(later),)),
         ],
-        compiler_params=pltpu.CompilerParams(vmem_limit_bytes=size + 8 * MIB),
+        compiler_params=pltpu.CompilerParams(vmem_limit_bytes=3 * size + 8 * MIB),
         cost_estimate=pl.CostEstimate(
             flops=size * modes, bytes_accessed=3 * size, transcendentals=0
         ),

time: 95.2 us -> 93 us (0.977)
  Pallas kernels: 46.3 us -> 43.8 us
    pallas_call x3, Pallas kernels: 13.7 us -> 11.8 us  [gram_part(): pl.pallas_call(functools.partial(gram_kernel, places, later, bool(parts),...]
  transfers between devices with their start and end apart: 24 -> 24, of which waited for: 8 -> 8; matrix products, arithmetic and copies ran while one was open for 0% -> 0% of each run, Pallas kernels for 44% -> 43%
where the time goes in v9:
time: 93 us; the launch traced here: 92.8 us
  Pallas kernels  43.8 us (47%)
  starting transfers between devices  32.1 us (35%)
  waiting for transfers between devices  14.9 us (16%)
    ppermute x17, starting transfers between devices, exchange(): return lax.ppermute(value, axis, [(i, i ^ flips) for i in range(count)])  20.7 us
    pallas_call x1, Pallas kernels, body(): pl.pallas_call(functools.partial(steps_kernel, count_x), out_shape=[jax.S...  17.5 us
    ppermute x17, waiting for transfers between devices, exchange(): return lax.ppermute(value, axis, [(i, i ^ flips) for i in range(count)])  14.9 us
    pallas_call x3, Pallas kernels, gram_part(): pl.pallas_call(functools.partial(gram_kernel, places, later, bool(parts),...  11.8 us
    pallas_call x3, Pallas kernels, product(): pl.pallas_call(functools.partial(product_kernel, flips, later, bool(rows)...  10.6 us
    ppermute x1, starting transfers between devices, body(): from_a = [lax.ppermute(own, 'gy', pairs('gy', 0))]  4.45 us
    ppermute x1, starting transfers between devices, body(): lax.ppermute(own, 'gx', [(i, (i - shift) % count_x) for i in range(count_...  2.94 us
    pallas_call x1, Pallas kernels, body(): pl.pallas_call(functools.partial(edges_kernel, count_x), out_shape=(packe...  2.29 us
  transfers between devices with their start and end apart: 24, of which 8 were waited for; matrix products, arithmetic and copies ran while one was open for 0% of the time, Pallas kernels for 43%

profile of v9, /device:TPU:0, one launch (start us, length us, event | category | flops | bytes accessed | tf_op | source)
XLA Modules:
  0.0 92.8 jit_solution(4747842818470695924)
XLA Ops:
  0.6 1.7 %pack.1.refs_0_ = f32[6,16,4,128]{3,2,1,0:T(4,128)} custom-call(f32[4,4,16,128]{3,2,1,0:T(8,128)} %terminal.1, f32[4,16,128]{2,1,0:T(8,128)} %velocity.1, s32[4,16,128]{2,1,0:T(8,128)} %material.1), custom_call_target="tpu_custom_call" | custom-call | tf_op jit(solution)/shard_map/pack/pallas_call | solution.py:454
  2.3 2.9 %collective-permute-start = (f32[6,16,4,128]{3,2,1,0:T(4,128)}, f32[6,16,4,128]{3,2,1,0:T(4,128)S(1)}, u32[]{:S(2)}, u32[]{:S(2)}) collective-permute-start(f32[6,16,4,128]{3,2,1,0:T(4,128)} %pack.1.refs_0_), channel_id=1, source_target_pairs={{0,4},{4,0},{1,5},{5,1},{2,6},{6,2},{3,7},{7,3},{8,12},{12,8},{9,1... | collective-permute-start | bytes 589832 | tf_op jit(solution)/shard_map/ppermute | solution.py:464
  5.3 0.7 collective-permute-start.3
  6.0 4.5 %collective-permute-start.1 = (f32[6,16,4,128]{3,2,1,0:T(4,128)}, f32[6,16,4,128]{3,2,1,0:T(4,128)S(1)}, u32[]{:S(2)}, u32[]{:S(2)}) collective-permute-start(f32[6,16,4,128]{3,2,1,0:T(4,128)} %pack.1.refs_0_), channel_id=1, source_target_pairs={{0,1},{2,3},{1,0},{3,2},{4,5},{6,7},{5,4},{7,6},{8,9},{10,11},{9,8... | collective-permute-start | bytes 589832 | tf_op jit(solution)/shard_map/ppermute | solution.py:466
  10.4 3.5 %gram.3.refs_1_ = f32[256,256]{1,0:T(8,128)S(1)} custom-call(bf16[1,4,16,512,256]{4,3,2,1,0:T(8,128)(2,1)} %refs_1_.3), custom_call_target="tpu_custom_call" | custom-call | flops 1073741824 | bytes 12582912 | tf_op jit(solution)/shard_map/gram/pallas_call | solution.py:341
  14.0 0.8 collective-permute-start.4
  14.8 1.8 %collective-permute-start.2 = (f32[6,16,4,128]{3,2,1,0:T(4,128)S(1)}, f32[6,16,4,128]{3,2,1,0:T(4,128)S(1)}, u32[]{:S(2)}, u32[]{:S(2)}) collective-permute-start(f32[6,16,4,128]{3,2,1,0:T(4,128)S(1)} %collective-permute-done.refs_1_), channel_id=1, source_target_pairs={{0,1},{2,3},{1,0},{3,2},{4,5},{6,7},{5,4},{7,6},{8,9},{10,11},{9,8... | collective-permute-start | bytes 589832 | tf_op jit(solution)/shard_map/ppermute | solution.py:470
  16.6 4.7 %gram.4 = (f32[256,256]{1,0:T(8,128)S(1)}, bf16[16,512,256]{2,1,0:T(8,128)(2,1)S(1)}, bf16[16,512,256]{2,1,0:T(8,128)(2,1)S(1)}) custom-call(bf16[1,4,16,512,256]{4,3,2,1,0:T(8,128)(2,1)} %refs_1_.3, f32[256,256]{1,0:T(8,128)S(1)} %gram.3.refs_1_), custom_call_target="tpu_custom_call" | custom-call | flops 1073741824 | bytes 12582912 | tf_op jit(solution)/shard_map/gram/pallas_call | solution.py:341
  21.3 2.3 %edges.1 = (f32[6,6,8,128]{3,2,1,0:T(8,128)S(1)}, f32[6,6,8,128]{3,2,1,0:T(8,128)S(1)}) custom-call(f32[6,16,4,128]{3,2,1,0:T(4,128)S(1)} %copy-done, f32[6,16,4,128]{3,2,1,0:T(4,128)S(1)} %collective-permute-done.refs_1_, f32[6,16,4,128]{3,2,1,0:T(4,128)S(1)} %collective-permute-done.1.refs_2_, f32[6,16,4,128]{3,2,1,0:T(4,128)S(1)} %collective-permute-done.2.refs_3_, ...), custom_call_target="tpu_custom_call" | custom-call | tf_op jit(solution)/shard_map/edges/pallas_call | solution.py:478
  23.6 0.1 collective-permute-start.5
  23.7 0.7 collective-permute-start.6
  24.4 0.0 copy-start.4
  24.4 0.0 copy-start.1
  24.4 0.0 copy-start.2
  24.4 0.0 copy-start.3
  24.4 3.5 %gram.5 = f32[256,256]{1,0:T(8,128)S(1)} custom-call(bf16[16,512,256]{2,1,0:T(8,128)(2,1)S(1)} %get-tuple-element.50.refs_0_, bf16[16,512,256]{2,1,0:T(8,128)(2,1)S(1)} %get-tuple-element.51.refs_1_, f32[256,256]{1,0:T(8,128)S(1)} %get-tuple-element.52.refs_2_), custom_call_target="tpu_custom_call" | custom-call | flops 2147483648 | bytes 25165824 | tf_op jit(solution)/shard_map/gram/pallas_call | solution.py:341
  28.0 1.7 %collective-permute-start.11 = (f32[256,256]{1,0:T(8,128)S(1)}, f32[256,256]{1,0:T(8,128)S(1)}, u32[]{:S(2)}, u32[]{:S(2)}) collective-permute-start(f32[256,256]{1,0:T(8,128)S(1)} %gram.5), channel_id=1, source_target_pairs={{0,24},{8,16},{16,8},{24,0},{1,25},{9,17},{17,9},{25,1},{2,26},{10... | collective-permute-start | bytes 786440 | tf_op jit(solution)/shard_map/ppermute | solution.py:27
  29.6 2.9 %collective-permute-start.10 = (f32[256,256]{1,0:T(8,128)S(1)}, f32[256,256]{1,0:T(8,128)S(1)}, u32[]{:S(2)}, u32[]{:S(2)}) collective-permute-start(f32[256,256]{1,0:T(8,128)S(1)} %gram.5), channel_id=1, source_target_pairs={{0,16},{8,24},{16,0},{24,8},{1,17},{9,25},{17,1},{25,9},{2,18},{10... | collective-permute-start | bytes 786440 | tf_op jit(solution)/shard_map/ppermute | solution.py:27
  32.5 0.1 copy.10.stoich
  32.6 17.5 %steps.1 = (f32[4,4,16,128]{3,2,1,0:T(8,128)}, f32[4,16,8,128]{3,2,1,0:T(8,128)S(1)}, f32[4,16,8,128]{3,2,1,0:T(8,128)S(1)}, f32[4,16,8,128]{3,2,1,0:T(8,128)S(1)}, f32[4,16,8,128]{3,2,1,0:T(8,128)S(1)}) custom-call(s32[8]{0:T(128)S(1)} %copy-done.2, f32[4]{0:T(128)S(1)} %copy-done.3, s32[8,4]{1,0:T(8,128)S(1)} %copy.10.stoich, f32[8,8]{1,0:T(8,128)S(1)} %copy-done.1, ...), custom_call_target="tpu_custom_call" | custom-call | bytes 100663296 | tf_op jit(solution)/shard_map/steps/pallas_call | solution.py:496
  50.1 1.1 %collective-permute-start.7 = (f32[4,16,8,128]{3,2,1,0:T(8,128)S(1)}, f32[4,16,8,128]{3,2,1,0:T(8,128)S(1)}, u32[]{:S(2)}, u32[]{:S(2)}) collective-permute-start(f32[4,16,8,128]{3,2,1,0:T(8,128)S(1)} %get-tuple-element.55), channel_id=1, source_target_pairs={{0,16},{8,24},{16,0},{24,8},{1,17},{9,25},{17,1},{25,9},{2,18},{10... | collective-permute-start | bytes 786440 | tf_op jit(solution)/shard_map/ppermute | solution.py:27
  51.2 0.8 collective-permute-start.8
  52.1 0.3 collective-permute-start.12
  52.4 0.1 add_add_fusion
  52.4 0.8 collective-permute-start.16
  53.2 4.7 %product.3 = (f32[16,256]{1,0:T(8,128)S(1)}, bf16[4,16,128,256]{3,2,1,0:T(8,128)(2,1)S(1)}, bf16[4,16,128,256]{3,2,1,0:T(8,128)(2,1)S(1)}) custom-call(f32[4,16,8,128]{3,2,1,0:T(8,128)S(1)} %get-tuple-element.64.refs_0_, bf16[1,4,16,512,256]{4,3,2,1,0:T(8,128)(2,1)} %refs_1_.3), custom_call_target="tpu_custom_call" | custom-call | flops 67108864 | bytes 8388608 | tf_op jit(solution)/shard_map/product/pallas_call | solution.py:426
  58.0 2.7 %product.4.refs_4_ = f32[16,256]{1,0:T(8,128)S(1)} custom-call(f32[4,16,8,128]{3,2,1,0:T(8,128)S(1)} %collective-permute-done.12.refs_0_, bf16[1,4,16,512,256]{4,3,2,1,0:T(8,128)(2,1)} %refs_1_.3, f32[16,256]{1,0:T(8,128)S(1)} %get-tuple-element.68.refs_2_), custom_call_target="tpu_custom_call" | custom-call | flops 67108864 | bytes 8388608 | tf_op jit(solution)/shard_map/product/pallas_call | solution.py:426
  60.7 3.5 %collective-permute-done.8.refs_1_ = f32[4,16,8,128]{3,2,1,0:T(8,128)S(1)} collective-permute-done((f32[4,16,8,128]{3,2,1,0:T(8,128)S(1)}, f32[4,16,8,128]{3,2,1,0:T(8,128)S(1)}, u32[]{:S(2)}, u32[]{:S(2)}) %collective-permute-start.8) | collective-permute-done | bytes 262176 | tf_op jit(solution)/shard_map/ppermute | solution.py:27
  64.2 3.2 %product.5 = f32[16,256]{1,0:T(8,128)S(1)} custom-call(f32[4,16,8,128]{3,2,1,0:T(8,128)S(1)} %collective-permute-done.7.refs_0_, f32[4,16,8,128]{3,2,1,0:T(8,128)S(1)} %collective-permute-done.8.refs_1_, bf16[4,16,128,256]{3,2,1,0:T(8,128)(2,1)S(1)} %get-tuple-element.65.refs_2_, bf16[4,16,128,256]{3,2,1,0:T(8,128)(2,1)S(1)} %get-tuple-element.66.refs_3_, ...), custom_call_target="tpu_custom_call" | custom-call | flops 134217728 | bytes 16777216 | tf_op jit(solution)/shard_map/product/pallas_call | solution.py:426
  67.3 0.4 collective-permute-start.15
  67.7 1.5 %collective-permute-start.14 = (f32[16,256]{1,0:T(8,128)S(1)}, f32[16,256]{1,0:T(8,128)S(1)}, u32[]{:S(2)}, u32[]{:S(2)}) collective-permute-start(f32[16,256]{1,0:T(8,128)S(1)} %product.5), channel_id=1, source_target_pairs={{0,16},{8,24},{16,0},{24,8},{1,17},{9,25},{17,1},{25,9},{2,18},{10... | collective-permute-start | bytes 49160 | tf_op jit(solution)/shard_map/ppermute | solution.py:27
  69.2 0.0 collective-permute-start.13
  69.3 1.3 %collective-permute-done.15 = f32[16,256]{1,0:T(8,128)S(1)} collective-permute-done((f32[16,256]{1,0:T(8,128)S(1)}, f32[16,256]{1,0:T(8,128)S(1)}, u32[]{:S(2)}, u32[]{:S(2)}) %collective-permute-start.15) | collective-permute-done | bytes 16416 | tf_op jit(solution)/shard_map/ppermute | solution.py:27
  70.6 0.9 collective-permute-done.14
  71.5 0.8 collective-permute-start.17
  72.3 3.0 %collective-permute-done.17 = f32[16,256]{1,0:T(8,128)S(1)} collective-permute-done((f32[16,256]{1,0:T(8,128)S(1)}, f32[16,256]{1,0:T(8,128)S(1)}, u32[]{:S(2)}, u32[]{:S(2)}) %collective-permute-start.17) | collective-permute-done | bytes 16416 | tf_op jit(solution)/shard_map/ppermute | solution.py:27
  75.3 2.5 %collective-permute-start.20 = (f32[8,256]{1,0:T(8,128)S(1)}, f32[8,256]{1,0:T(8,128)S(1)}, u32[]{:S(2)}, u32[]{:S(2)}) collective-permute-start(f32[8,256]{1,0:T(8,128)S(1)} %slice_add_fusion.1), channel_id=1, source_target_pairs={{0,3},{1,2},{2,1},{3,0},{4,7},{5,6},{6,5},{7,4},{8,11},{9,10},{10,... | collective-permute-start | bytes 24584 | tf_op jit(solution)/shard_map/ppermute | solution.py:27
  77.8 3.5 %collective-permute-start.19 = (f32[8,256]{1,0:T(8,128)S(1)}, f32[8,256]{1,0:T(8,128)S(1)}, u32[]{:S(2)}, u32[]{:S(2)}) collective-permute-start(f32[8,256]{1,0:T(8,128)S(1)} %slice_add_fusion.1), channel_id=1, source_target_pairs={{0,2},{1,3},{2,0},{3,1},{4,6},{5,7},{6,4},{7,5},{8,10},{9,11},{10,... | collective-permute-start | bytes 24584 | tf_op jit(solution)/shard_map/ppermute | solution.py:27
  81.3 0.1 collective-permute-start.18
  81.4 1.6 %collective-permute-done.19 = f32[8,256]{1,0:T(8,128)S(1)} collective-permute-done((f32[8,256]{1,0:T(8,128)S(1)}, f32[8,256]{1,0:T(8,128)S(1)}, u32[]{:S(2)}, u32[]{:S(2)}) %collective-permute-start.19) | collective-permute-done | bytes 8224 | tf_op jit(solution)/shard_map/ppermute | solution.py:27
  83.0 1.9 %collective-permute-done.18 = f32[8,256]{1,0:T(8,128)S(1)} collective-permute-done((f32[8,256]{1,0:T(8,128)S(1)}, f32[8,256]{1,0:T(8,128)S(1)}, u32[]{:S(2)}, u32[]{:S(2)}) %collective-permute-start.18) | collective-permute-done | bytes 8224 | tf_op jit(solution)/shard_map/ppermute | solution.py:27
  84.9 0.2 fusion.3
  85.1 2.5 %collective-permute-start.23 = (f32[8,256]{1,0:T(8,128)S(1)}, f32[8,256]{1,0:T(8,128)S(1)}, u32[]{:S(2)}, u32[]{:S(2)}) collective-permute-start(f32[8,256]{1,0:T(8,128)S(1)} %fusion.3), channel_id=1, source_target_pairs={{0,3},{1,2},{2,1},{3,0},{4,7},{5,6},{6,5},{7,4},{8,11},{9,10},{10,... | collective-permute-start | bytes 24584 | tf_op jit(solution)/shard_map/ppermute | solution.py:27
  87.6 0.0 collective-permute-start.22
  87.6 1.9 %collective-permute-start.21 = (f32[8,256]{1,0:T(8,128)S(1)}, f32[8,256]{1,0:T(8,128)S(1)}, u32[]{:S(2)}, u32[]{:S(2)}) collective-permute-start(f32[8,256]{1,0:T(8,128)S(1)} %fusion.3), channel_id=1, source_target_pairs={{0,1},{1,0},{2,3},{3,2},{4,5},{5,4},{6,7},{7,6},{8,9},{9,8},{10,11... | collective-permute-start | bytes 24584 | tf_op jit(solution)/shard_map/ppermute | solution.py:27
  89.5 1.1 %collective-permute-done.23 = f32[8,256]{1,0:T(8,128)S(1)} collective-permute-done((f32[8,256]{1,0:T(8,128)S(1)}, f32[8,256]{1,0:T(8,128)S(1)}, u32[]{:S(2)}, u32[]{:S(2)}) %collective-permute-start.23) | collective-permute-done | bytes 8224 | tf_op jit(solution)/shard_map/ppermute | solution.py:27
  90.6 1.6 %collective-permute-done.22 = f32[8,256]{1,0:T(8,128)S(1)} collective-permute-done((f32[8,256]{1,0:T(8,128)S(1)}, f32[8,256]{1,0:T(8,128)S(1)}, u32[]{:S(2)}, u32[]{:S(2)}) %collective-permute-start.22) | collective-permute-done | bytes 8224 | tf_op jit(solution)/shard_map/ppermute | solution.py:27
  92.2 0.6 add_add_fusion.2
  (26 shorter events, 0.1 us)
Async XLA Ops:
  2.3 11.6 %collective-permute-start = (f32[6,16,4,128]{3,2,1,0:T(4,128)}, f32[6,16,4,128]{3,2,1,0:T(4,128)S(1)}, u32[]{:S(2)}, u32[]{:S(2)}) collective-permute-start(f32[6,16,4,128]{3,2,1,0:T(4,128)} %pack.1.refs_0_), channel_id=1, source_target_pairs={{0,4},{4,0},{1,5},{5,1},{2,6},{6,2},{3,7},{7,3},{8,12},{12,8},{9,1... | collective-permute-start | bytes 589832 | tf_op jit(solution)/shard_map/ppermute | solution.py:464
  5.3 16.0 %collective-permute-start.3 = (f32[6,16,4,128]{3,2,1,0:T(4,128)}, f32[6,16,4,128]{3,2,1,0:T(4,128)S(1)}, u32[]{:S(2)}, u32[]{:S(2)}) collective-permute-start(f32[6,16,4,128]{3,2,1,0:T(4,128)} %pack.1.refs_0_), channel_id=1, source_target_pairs={{1,2},{2,1},{5,6},{6,5},{9,10},{10,9},{13,14},{14,13},{17,18},{18,... | collective-permute-start | bytes 589832 | tf_op jit(solution)/shard_map/ppermute | solution.py:467
  6.0 15.3 %collective-permute-start.1 = (f32[6,16,4,128]{3,2,1,0:T(4,128)}, f32[6,16,4,128]{3,2,1,0:T(4,128)S(1)}, u32[]{:S(2)}, u32[]{:S(2)}) collective-permute-start(f32[6,16,4,128]{3,2,1,0:T(4,128)} %pack.1.refs_0_), channel_id=1, source_target_pairs={{0,1},{2,3},{1,0},{3,2},{4,5},{6,7},{5,4},{7,6},{8,9},{10,11},{9,8... | collective-permute-start | bytes 589832 | tf_op jit(solution)/shard_map/ppermute | solution.py:466
  14.0 7.4 %copy-start = (f32[6,16,4,128]{3,2,1,0:T(4,128)S(1)}, f32[6,16,4,128]{3,2,1,0:T(4,128)}, u32[]{:S(2)}) copy-start(f32[6,16,4,128]{3,2,1,0:T(4,128)} %pack.1.refs_0_) | copy-start | bytes 589828
  14.0 7.3 %collective-permute-start.4 = (f32[6,16,4,128]{3,2,1,0:T(4,128)S(1)}, f32[6,16,4,128]{3,2,1,0:T(4,128)S(1)}, u32[]{:S(2)}, u32[]{:S(2)}) collective-permute-start(f32[6,16,4,128]{3,2,1,0:T(4,128)S(1)} %collective-permute-done.refs_1_), channel_id=1, source_target_pairs={{1,2},{2,1},{5,6},{6,5},{9,10},{10,9},{13,14},{14,13},{17,18},{18,... | collective-permute-start | bytes 589832 | tf_op jit(solution)/shard_map/ppermute | solution.py:471
  14.8 6.5 %collective-permute-start.2 = (f32[6,16,4,128]{3,2,1,0:T(4,128)S(1)}, f32[6,16,4,128]{3,2,1,0:T(4,128)S(1)}, u32[]{:S(2)}, u32[]{:S(2)}) collective-permute-start(f32[6,16,4,128]{3,2,1,0:T(4,128)S(1)} %collective-permute-done.refs_1_), channel_id=1, source_target_pairs={{0,1},{2,3},{1,0},{3,2},{4,5},{6,7},{5,4},{7,6},{8,9},{10,11},{9,8... | collective-permute-start | bytes 589832 | tf_op jit(solution)/shard_map/ppermute | solution.py:470
  23.6 4.3 %collective-permute-start.5 = (f32[6,6,8,128]{3,2,1,0:T(8,128)S(1)}, f32[6,6,8,128]{3,2,1,0:T(8,128)S(1)}, u32[]{:S(2)}, u32[]{:S(2)}) collective-permute-start(f32[6,6,8,128]{3,2,1,0:T(8,128)S(1)} %get-tuple-element.48), channel_id=1, source_target_pairs={{0,8},{16,24},{8,0},{24,16},{1,9},{17,25},{9,1},{25,17},{2,10},{18... | collective-permute-start | bytes 442376 | tf_op jit(solution)/shard_map/ppermute | solution.py:487
  23.7 4.3 %collective-permute-start.6 = (f32[6,6,8,128]{3,2,1,0:T(8,128)S(1)}, f32[6,6,8,128]{3,2,1,0:T(8,128)S(1)}, u32[]{:S(2)}, u32[]{:S(2)}) collective-permute-start(f32[6,6,8,128]{3,2,1,0:T(8,128)S(1)} %get-tuple-element.49), channel_id=1, source_target_pairs={{8,16},{16,8},{9,17},{17,9},{10,18},{18,10},{11,19},{19,11},{12,20... | collective-permute-start | bytes 442376 | tf_op jit(solution)/shard_map/ppermute | solution.py:488
  24.4 8.2 %copy-start.4 = (s32[8,4]{0,1:T(4,128)S(1)}, s32[8,4]{0,1:T(4,128)}, u32[]{:S(2)}) copy-start(s32[8,4]{0,1:T(4,128)} %param.13) | copy-start | bytes 388
  24.4 8.2 %copy-start.1 = (f32[8,8]{1,0:T(8,128)S(1)}, f32[8,8]{1,0:T(8,128)}, u32[]{:S(2)}) copy-start(f32[8,8]{1,0:T(8,128)} %rates.1) | copy-start | bytes 772
  24.4 8.2 %copy-start.2 = (s32[8]{0:T(128)S(1)}, s32[8]{0:T(128)}, u32[]{:S(2)}) copy-start(s32[8]{0:T(128)} %plan.1) | copy-start | bytes 100
  24.4 8.2 %copy-start.3 = (f32[4]{0:T(128)S(1)}, f32[4]{0:T(128)}, u32[]{:S(2)}) copy-start(f32[4]{0:T(128)} %diffusion.1) | copy-start | bytes 52
  28.0 24.1 %collective-permute-start.11 = (f32[256,256]{1,0:T(8,128)S(1)}, f32[256,256]{1,0:T(8,128)S(1)}, u32[]{:S(2)}, u32[]{:S(2)}) collective-permute-start(f32[256,256]{1,0:T(8,128)S(1)} %gram.5), channel_id=1, source_target_pairs={{0,24},{8,16},{16,8},{24,0},{1,25},{9,17},{17,9},{25,1},{2,26},{10... | collective-permute-start | bytes 786440 | tf_op jit(solution)/shard_map/ppermute | solution.py:27
  29.6 22.7 %collective-permute-start.10 = (f32[256,256]{1,0:T(8,128)S(1)}, f32[256,256]{1,0:T(8,128)S(1)}, u32[]{:S(2)}, u32[]{:S(2)}) collective-permute-start(f32[256,256]{1,0:T(8,128)S(1)} %gram.5), channel_id=1, source_target_pairs={{0,16},{8,24},{16,0},{24,8},{1,17},{9,25},{17,1},{25,9},{2,18},{10... | collective-permute-start | bytes 786440 | tf_op jit(solution)/shard_map/ppermute | solution.py:27
  32.5 19.8 %collective-permute-start.9 = (f32[256,256]{1,0:T(8,128)S(1)}, f32[256,256]{1,0:T(8,128)S(1)}, u32[]{:S(2)}, u32[]{:S(2)}) collective-permute-start(f32[256,256]{1,0:T(8,128)S(1)} %gram.5), channel_id=1, source_target_pairs={{0,8},{8,0},{16,24},{24,16},{1,9},{9,1},{17,25},{25,17},{2,10},{10... | collective-permute-start | bytes 786440 | tf_op jit(solution)/shard_map/ppermute | solution.py:27
  50.1 10.5 %collective-permute-start.7 = (f32[4,16,8,128]{3,2,1,0:T(8,128)S(1)}, f32[4,16,8,128]{3,2,1,0:T(8,128)S(1)}, u32[]{:S(2)}, u32[]{:S(2)}) collective-permute-start(f32[4,16,8,128]{3,2,1,0:T(8,128)S(1)} %get-tuple-element.55), channel_id=1, source_target_pairs={{0,16},{8,24},{16,0},{24,8},{1,17},{9,25},{17,1},{25,9},{2,18},{10... | collective-permute-start | bytes 786440 | tf_op jit(solution)/shard_map/ppermute | solution.py:27
  51.2 12.9 %collective-permute-start.8 = (f32[4,16,8,128]{3,2,1,0:T(8,128)S(1)}, f32[4,16,8,128]{3,2,1,0:T(8,128)S(1)}, u32[]{:S(2)}, u32[]{:S(2)}) collective-permute-start(f32[4,16,8,128]{3,2,1,0:T(8,128)S(1)} %get-tuple-element.56), channel_id=1, source_target_pairs={{0,24},{8,16},{16,8},{24,0},{1,25},{9,17},{17,9},{25,1},{2,26},{10... | collective-permute-start | bytes 786440 | tf_op jit(solution)/shard_map/ppermute | solution.py:27
  52.1 5.9 %collective-permute-start.12 = (f32[4,16,8,128]{3,2,1,0:T(8,128)S(1)}, f32[4,16,8,128]{3,2,1,0:T(8,128)S(1)}, u32[]{:S(2)}, u32[]{:S(2)}) collective-permute-start(f32[4,16,8,128]{3,2,1,0:T(8,128)S(1)} %get-tuple-element.67), channel_id=1, source_target_pairs={{0,8},{8,0},{16,24},{24,16},{1,9},{9,1},{17,25},{25,17},{2,10},{10... | collective-permute-start | bytes 786440 | tf_op jit(solution)/shard_map/ppermute | solution.py:27
  52.4 19.0 %collective-permute-start.16 = (f32[256,256]{1,0:T(8,128)S(1)}, f32[256,256]{1,0:T(8,128)S(1)}, u32[]{:S(2)}, u32[]{:S(2)}) collective-permute-start(f32[256,256]{1,0:T(8,128)S(1)} %add_add_fusion), channel_id=1, source_target_pairs={{0,4},{4,0},{1,5},{5,1},{2,6},{6,2},{3,7},{7,3},{8,12},{12,8},{9,1... | collective-permute-start | bytes 786440 | tf_op jit(solution)/shard_map/ppermute | solution.py:27
  67.3 3.2 %collective-permute-start.15 = (f32[16,256]{1,0:T(8,128)S(1)}, f32[16,256]{1,0:T(8,128)S(1)}, u32[]{:S(2)}, u32[]{:S(2)}) collective-permute-start(f32[16,256]{1,0:T(8,128)S(1)} %product.5), channel_id=1, source_target_pairs={{0,24},{8,16},{16,8},{24,0},{1,25},{9,17},{17,9},{25,1},{2,26},{10... | collective-permute-start | bytes 49160 | tf_op jit(solution)/shard_map/ppermute | solution.py:27
  67.7 3.7 %collective-permute-start.14 = (f32[16,256]{1,0:T(8,128)S(1)}, f32[16,256]{1,0:T(8,128)S(1)}, u32[]{:S(2)}, u32[]{:S(2)}) collective-permute-start(f32[16,256]{1,0:T(8,128)S(1)} %product.5), channel_id=1, source_target_pairs={{0,16},{8,24},{16,0},{24,8},{1,17},{9,25},{17,1},{25,9},{2,18},{10... | collective-permute-start | bytes 49160 | tf_op jit(solution)/shard_map/ppermute | solution.py:27
  69.2 2.2 %collective-permute-start.13 = (f32[16,256]{1,0:T(8,128)S(1)}, f32[16,256]{1,0:T(8,128)S(1)}, u32[]{:S(2)}, u32[]{:S(2)}) collective-permute-start(f32[16,256]{1,0:T(8,128)S(1)} %product.5), channel_id=1, source_target_pairs={{0,8},{8,0},{16,24},{24,16},{1,9},{9,1},{17,25},{25,17},{2,10},{10... | collective-permute-start | bytes 49160 | tf_op jit(solution)/shard_map/ppermute | solution.py:27
  71.5 3.8 %collective-permute-start.17 = (f32[16,256]{1,0:T(8,128)S(1)}, f32[16,256]{1,0:T(8,128)S(1)}, u32[]{:S(2)}, u32[]{:S(2)}) collective-permute-start(f32[16,256]{1,0:T(8,128)S(1)} %add_add_fusion.1), channel_id=1, source_target_pairs={{0,4},{4,0},{1,5},{5,1},{2,6},{6,2},{3,7},{7,3},{8,12},{12,8},{9,1... | collective-permute-start | bytes 49160 | tf_op jit(solution)/shard_map/ppermute | solution.py:27
  75.3 6.1 %collective-permute-start.20 = (f32[8,256]{1,0:T(8,128)S(1)}, f32[8,256]{1,0:T(8,128)S(1)}, u32[]{:S(2)}, u32[]{:S(2)}) collective-permute-start(f32[8,256]{1,0:T(8,128)S(1)} %slice_add_fusion.1), channel_id=1, source_target_pairs={{0,3},{1,2},{2,1},{3,0},{4,7},{5,6},{6,5},{7,4},{8,11},{9,10},{10,... | collective-permute-start | bytes 24584 | tf_op jit(solution)/shard_map/ppermute | solution.py:27
  77.8 5.2 %collective-permute-start.19 = (f32[8,256]{1,0:T(8,128)S(1)}, f32[8,256]{1,0:T(8,128)S(1)}, u32[]{:S(2)}, u32[]{:S(2)}) collective-permute-start(f32[8,256]{1,0:T(8,128)S(1)} %slice_add_fusion.1), channel_id=1, source_target_pairs={{0,2},{1,3},{2,0},{3,1},{4,6},{5,7},{6,4},{7,5},{8,10},{9,11},{10,... | collective-permute-start | bytes 24584 | tf_op jit(solution)/shard_map/ppermute | solution.py:27
  81.3 3.7 %collective-permute-start.18 = (f32[8,256]{1,0:T(8,128)S(1)}, f32[8,256]{1,0:T(8,128)S(1)}, u32[]{:S(2)}, u32[]{:S(2)}) collective-permute-start(f32[8,256]{1,0:T(8,128)S(1)} %slice_add_fusion.1), channel_id=1, source_target_pairs={{0,1},{1,0},{2,3},{3,2},{4,5},{5,4},{6,7},{7,6},{8,9},{9,8},{10,11... | collective-permute-start | bytes 24584 | tf_op jit(solution)/shard_map/ppermute | solution.py:27
  85.1 5.5 %collective-permute-start.23 = (f32[8,256]{1,0:T(8,128)S(1)}, f32[8,256]{1,0:T(8,128)S(1)}, u32[]{:S(2)}, u32[]{:S(2)}) collective-permute-start(f32[8,256]{1,0:T(8,128)S(1)} %fusion.3), channel_id=1, source_target_pairs={{0,3},{1,2},{2,1},{3,0},{4,7},{5,6},{6,5},{7,4},{8,11},{9,10},{10,... | collective-permute-start | bytes 24584 | tf_op jit(solution)/shard_map/ppermute | solution.py:27
  87.6 4.5 %collective-permute-start.22 = (f32[8,256]{1,0:T(8,128)S(1)}, f32[8,256]{1,0:T(8,128)S(1)}, u32[]{:S(2)}, u32[]{:S(2)}) collective-permute-start(f32[8,256]{1,0:T(8,128)S(1)} %fusion.3), channel_id=1, source_target_pairs={{0,2},{1,3},{2,0},{3,1},{4,6},{5,7},{6,4},{7,5},{8,10},{9,11},{10,... | collective-permute-start | bytes 24584 | tf_op jit(solution)/shard_map/ppermute | solution.py:27
  87.6 4.5 %collective-permute-start.21 = (f32[8,256]{1,0:T(8,128)S(1)}, f32[8,256]{1,0:T(8,128)S(1)}, u32[]{:S(2)}, u32[]{:S(2)}) collective-permute-start(f32[8,256]{1,0:T(8,128)S(1)} %fusion.3), channel_id=1, source_target_pairs={{0,1},{1,0},{2,3},{3,2},{4,5},{5,4},{6,7},{7,6},{8,9},{9,8},{10,11... | collective-permute-start | bytes 24584 | tf_op jit(solution)/shard_map/ppermute | solution.py:27

commit v10 on v9

--- a/solution.py
+++ b/solution.py
@@ -509,15 +509,17 @@
         name="steps",
     )(plan, diffusion, stoich, rates, *blocks, side_a, side_b)
 
-    order = sorted(range(1, count_grp), key=lambda flips: -flips)
-    moved = {flips: exchange(kept[flips], "grp", flips) for flips in order}
+    last = count_grp - 1
+    moved = {flips: exchange(kept[flips], "grp", flips) for flips in range(1, last)}
     mine, *grams = lax.optimization_barrier((kept[0], *grams))
-    mine, gram = lax.optimization_barrier((mine, add_up(grams)))
+    mine, final_part, gram = lax.optimization_barrier((mine, kept[last], add_up(grams)))
+    moved[last] = exchange(final_part, "grp", last)
     grams = copies_over(gram, "gx")
     later = tuple(range(2, count_grp))
     total, *rows = product((0,), [mine], basis, later=later)
     (total,) = product((1,), [moved[1]], basis, total)
-    (total,) = product(later, [moved[f] for f in later], basis, total, rows=tuple(rows))
+    for flips, table in zip(later, rows):
+        (total,) = product((flips,), [moved[flips]], basis, total, rows=(table,))
 
     total = sum_over(total, "grp")
     total, *grams = lax.optimization_barrier((total, *grams))

time: 93 us -> 91.5 us (0.984)
  waiting for transfers between devices: 14.9 us -> 13.2 us
    ppermute x17, waiting for transfers between devices: 14.9 us -> 13.2 us  [exchange(): return lax.ppermute(value, axis, [(i, i ^ flips) for i in range(count)])]
    pallas_call x3 -> x4, Pallas kernels: 10.6 us -> 10.8 us  [product(): pl.pallas_call(functools.partial(product_kernel, flips, later, bool(rows)...]
  transfers between devices with their start and end apart: 24 -> 24, of which waited for: 8 -> 8; matrix products, arithmetic and copies ran while one was open for 0% -> 0% of each run, Pallas kernels for 43% -> 44%
where the time goes in v10:
time: 91.5 us; the launch traced here: 91.3 us
  Pallas kernels  44.1 us (48%)
  starting transfers between devices  32.1 us (35%)
  waiting for transfers between devices  13.2 us (14%)
    ppermute x17, starting transfers between devices, exchange(): return lax.ppermute(value, axis, [(i, i ^ flips) for i in range(count)])  20.7 us
    pallas_call x1, Pallas kernels, body(): pl.pallas_call(functools.partial(steps_kernel, count_x), out_shape=[jax.S...  17.5 us
    ppermute x17, waiting for transfers between devices, exchange(): return lax.ppermute(value, axis, [(i, i ^ flips) for i in range(count)])  13.2 us
    pallas_call x3, Pallas kernels, gram_part(): pl.pallas_call(functools.partial(gram_kernel, places, later, bool(parts),...  11.8 us
    pallas_call x4, Pallas kernels, product(): pl.pallas_call(functools.partial(product_kernel, flips, later, bool(rows)...  10.8 us
    ppermute x1, starting transfers between devices, body(): from_a = [lax.ppermute(own, 'gy', pairs('gy', 0))]  4.45 us
    ppermute x1, starting transfers between devices, body(): lax.ppermute(own, 'gx', [(i, (i - shift) % count_x) for i in range(count_...  2.94 us
    pallas_call x1, Pallas kernels, body(): pl.pallas_call(functools.partial(edges_kernel, count_x), out_shape=(packe...  2.29 us
  transfers between devices with their start and end apart: 24, of which 8 were waited for; matrix products, arithmetic and copies ran while one was open for 0% of the time, Pallas kernels for 44%

profile of v10, /device:TPU:0, one launch (start us, length us, event | category | flops | bytes accessed | tf_op | source)
XLA Modules:
  0.0 91.3 jit_solution(6694468663942770206)
XLA Ops:
  0.6 1.7 %pack.1.refs_0_ = f32[6,16,4,128]{3,2,1,0:T(4,128)} custom-call(f32[4,4,16,128]{3,2,1,0:T(8,128)} %terminal.1, f32[4,16,128]{2,1,0:T(8,128)} %velocity.1, s32[4,16,128]{2,1,0:T(8,128)} %material.1), custom_call_target="tpu_custom_call" | custom-call | tf_op jit(solution)/shard_map/pack/pallas_call | solution.py:454
  2.3 2.9 %collective-permute-start = (f32[6,16,4,128]{3,2,1,0:T(4,128)}, f32[6,16,4,128]{3,2,1,0:T(4,128)S(1)}, u32[]{:S(2)}, u32[]{:S(2)}) collective-permute-start(f32[6,16,4,128]{3,2,1,0:T(4,128)} %pack.1.refs_0_), channel_id=1, source_target_pairs={{0,4},{4,0},{1,5},{5,1},{2,6},{6,2},{3,7},{7,3},{8,12},{12,8},{9,1... | collective-permute-start | bytes 589832 | tf_op jit(solution)/shard_map/ppermute | solution.py:464
  5.3 0.7 collective-permute-start.3
  6.0 4.5 %collective-permute-start.1 = (f32[6,16,4,128]{3,2,1,0:T(4,128)}, f32[6,16,4,128]{3,2,1,0:T(4,128)S(1)}, u32[]{:S(2)}, u32[]{:S(2)}) collective-permute-start(f32[6,16,4,128]{3,2,1,0:T(4,128)} %pack.1.refs_0_), channel_id=1, source_target_pairs={{0,1},{2,3},{1,0},{3,2},{4,5},{6,7},{5,4},{7,6},{8,9},{10,11},{9,8... | collective-permute-start | bytes 589832 | tf_op jit(solution)/shard_map/ppermute | solution.py:466
  10.4 3.5 %gram.3.refs_1_ = f32[256,256]{1,0:T(8,128)S(1)} custom-call(bf16[1,4,16,512,256]{4,3,2,1,0:T(8,128)(2,1)} %refs_1_.3), custom_call_target="tpu_custom_call" | custom-call | flops 1073741824 | bytes 12582912 | tf_op jit(solution)/shard_map/gram/pallas_call | solution.py:341
  14.0 0.8 collective-permute-start.4
  14.8 1.8 %collective-permute-start.2 = (f32[6,16,4,128]{3,2,1,0:T(4,128)S(1)}, f32[6,16,4,128]{3,2,1,0:T(4,128)S(1)}, u32[]{:S(2)}, u32[]{:S(2)}) collective-permute-start(f32[6,16,4,128]{3,2,1,0:T(4,128)S(1)} %collective-permute-done.refs_1_), channel_id=1, source_target_pairs={{0,1},{2,3},{1,0},{3,2},{4,5},{6,7},{5,4},{7,6},{8,9},{10,11},{9,8... | collective-permute-start | bytes 589832 | tf_op jit(solution)/shard_map/ppermute | solution.py:470
  16.6 4.7 %gram.4 = (f32[256,256]{1,0:T(8,128)S(1)}, bf16[16,512,256]{2,1,0:T(8,128)(2,1)S(1)}, bf16[16,512,256]{2,1,0:T(8,128)(2,1)S(1)}) custom-call(bf16[1,4,16,512,256]{4,3,2,1,0:T(8,128)(2,1)} %refs_1_.3, f32[256,256]{1,0:T(8,128)S(1)} %gram.3.refs_1_), custom_call_target="tpu_custom_call" | custom-call | flops 1073741824 | bytes 12582912 | tf_op jit(solution)/shard_map/gram/pallas_call | solution.py:341
  21.3 2.3 %edges.1 = (f32[6,6,8,128]{3,2,1,0:T(8,128)S(1)}, f32[6,6,8,128]{3,2,1,0:T(8,128)S(1)}) custom-call(f32[6,16,4,128]{3,2,1,0:T(4,128)S(1)} %copy-done, f32[6,16,4,128]{3,2,1,0:T(4,128)S(1)} %collective-permute-done.refs_1_, f32[6,16,4,128]{3,2,1,0:T(4,128)S(1)} %collective-permute-done.1.refs_2_, f32[6,16,4,128]{3,2,1,0:T(4,128)S(1)} %collective-permute-done.2.refs_3_, ...), custom_call_target="tpu_custom_call" | custom-call | tf_op jit(solution)/shard_map/edges/pallas_call | solution.py:478
  23.6 0.1 collective-permute-start.5
  23.7 0.7 collective-permute-start.6
  24.4 0.0 copy-start.4
  24.4 0.0 copy-start.1
  24.4 0.0 copy-start.2
  24.4 0.0 copy-start.3
  24.4 3.5 %gram.5 = f32[256,256]{1,0:T(8,128)S(1)} custom-call(bf16[16,512,256]{2,1,0:T(8,128)(2,1)S(1)} %get-tuple-element.51.refs_0_, bf16[16,512,256]{2,1,0:T(8,128)(2,1)S(1)} %get-tuple-element.52.refs_1_, f32[256,256]{1,0:T(8,128)S(1)} %get-tuple-element.53.refs_2_), custom_call_target="tpu_custom_call" | custom-call | flops 2147483648 | bytes 25165824 | tf_op jit(solution)/shard_map/gram/pallas_call | solution.py:341
  28.0 1.7 %collective-permute-start.9 = (f32[256,256]{1,0:T(8,128)S(1)}, f32[256,256]{1,0:T(8,128)S(1)}, u32[]{:S(2)}, u32[]{:S(2)}) collective-permute-start(f32[256,256]{1,0:T(8,128)S(1)} %gram.5), channel_id=1, source_target_pairs={{0,24},{8,16},{16,8},{24,0},{1,25},{9,17},{17,9},{25,1},{2,26},{10... | collective-permute-start | bytes 786440 | tf_op jit(solution)/shard_map/ppermute | solution.py:27
  29.6 2.9 %collective-permute-start.8 = (f32[256,256]{1,0:T(8,128)S(1)}, f32[256,256]{1,0:T(8,128)S(1)}, u32[]{:S(2)}, u32[]{:S(2)}) collective-permute-start(f32[256,256]{1,0:T(8,128)S(1)} %gram.5), channel_id=1, source_target_pairs={{0,16},{8,24},{16,0},{24,8},{1,17},{9,25},{17,1},{25,9},{2,18},{10... | collective-permute-start | bytes 786440 | tf_op jit(solution)/shard_map/ppermute | solution.py:27
  32.5 0.1 copy.10.stoich
  32.6 17.5 %steps.1 = (f32[4,4,16,128]{3,2,1,0:T(8,128)}, f32[4,16,8,128]{3,2,1,0:T(8,128)S(1)}, f32[4,16,8,128]{3,2,1,0:T(8,128)S(1)}, f32[4,16,8,128]{3,2,1,0:T(8,128)S(1)}, f32[4,16,8,128]{3,2,1,0:T(8,128)S(1)}) custom-call(s32[8]{0:T(128)S(1)} %copy-done.2, f32[4]{0:T(128)S(1)} %copy-done.3, s32[8,4]{1,0:T(8,128)S(1)} %copy.10.stoich, f32[8,8]{1,0:T(8,128)S(1)} %copy-done.1, ...), custom_call_target="tpu_custom_call" | custom-call | bytes 100663296 | tf_op jit(solution)/shard_map/steps/pallas_call | solution.py:496
  50.1 1.1 %collective-permute-start.11 = (f32[4,16,8,128]{3,2,1,0:T(8,128)S(1)}, f32[4,16,8,128]{3,2,1,0:T(8,128)S(1)}, u32[]{:S(2)}, u32[]{:S(2)}) collective-permute-start(f32[4,16,8,128]{3,2,1,0:T(8,128)S(1)} %get-tuple-element.67), channel_id=1, source_target_pairs={{0,16},{8,24},{16,0},{24,8},{1,17},{9,25},{17,1},{25,9},{2,18},{10... | collective-permute-start | bytes 786440 | tf_op jit(solution)/shard_map/ppermute | solution.py:27
  51.2 0.1 add_add_fusion
  51.3 1.2 %collective-permute-start.10 = (f32[4,16,8,128]{3,2,1,0:T(8,128)S(1)}, f32[4,16,8,128]{3,2,1,0:T(8,128)S(1)}, u32[]{:S(2)}, u32[]{:S(2)}) collective-permute-start(f32[4,16,8,128]{3,2,1,0:T(8,128)S(1)} %get-tuple-element.64), channel_id=1, source_target_pairs={{0,24},{8,16},{16,8},{24,0},{1,25},{9,17},{17,9},{25,1},{2,26},{10... | collective-permute-start | bytes 786440 | tf_op jit(solution)/shard_map/ppermute | solution.py:27
  52.5 0.7 collective-permute-start.16
  53.2 4.7 %product.4 = (f32[16,256]{1,0:T(8,128)S(1)}, bf16[4,16,128,256]{3,2,1,0:T(8,128)(2,1)S(1)}, bf16[4,16,128,256]{3,2,1,0:T(8,128)(2,1)S(1)}) custom-call(f32[4,16,8,128]{3,2,1,0:T(8,128)S(1)} %get-tuple-element.65.refs_0_, bf16[1,4,16,512,256]{4,3,2,1,0:T(8,128)(2,1)} %refs_1_.3), custom_call_target="tpu_custom_call" | custom-call | flops 67108864 | bytes 8388608 | tf_op jit(solution)/shard_map/product/pallas_call | solution.py:426
  58.0 2.7 %product.5.refs_2_ = f32[16,256]{1,0:T(8,128)S(1)} custom-call(f32[4,16,8,128]{3,2,1,0:T(8,128)S(1)} %collective-permute-done.12.refs_0_, bf16[1,4,16,512,256]{4,3,2,1,0:T(8,128)(2,1)} %refs_1_.3, f32[16,256]{1,0:T(8,128)S(1)} %get-tuple-element.70.refs_2_), custom_call_target="tpu_custom_call" | custom-call | flops 67108864 | bytes 8388608 | tf_op jit(solution)/shard_map/product/pallas_call | solution.py:426
  60.7 1.7 %product.6.refs_2_ = f32[16,256]{1,0:T(8,128)S(1)} custom-call(f32[4,16,8,128]{3,2,1,0:T(8,128)S(1)} %collective-permute-done.11.refs_0_, bf16[4,16,128,256]{3,2,1,0:T(8,128)(2,1)S(1)} %get-tuple-element.68.refs_1_, f32[16,256]{1,0:T(8,128)S(1)} %product.5.refs_2_), custom_call_target="tpu_custom_call" | custom-call | flops 67108864 | bytes 8388608 | tf_op jit(solution)/shard_map/product/pallas_call | solution.py:426
  62.4 1.8 %collective-permute-done.10.refs_0_ = f32[4,16,8,128]{3,2,1,0:T(8,128)S(1)} collective-permute-done((f32[4,16,8,128]{3,2,1,0:T(8,128)S(1)}, f32[4,16,8,128]{3,2,1,0:T(8,128)S(1)}, u32[]{:S(2)}, u32[]{:S(2)}) %collective-permute-start.10) | collective-permute-done | bytes 262176 | tf_op jit(solution)/shard_map/ppermute | solution.py:27
  64.2 1.7 %product.7 = f32[16,256]{1,0:T(8,128)S(1)} custom-call(f32[4,16,8,128]{3,2,1,0:T(8,128)S(1)} %collective-permute-done.10.refs_0_, bf16[4,16,128,256]{3,2,1,0:T(8,128)(2,1)S(1)} %get-tuple-element.66.refs_1_, f32[16,256]{1,0:T(8,128)S(1)} %product.6.refs_2_), custom_call_target="tpu_custom_call" | custom-call | flops 67108864 | bytes 8388608 | tf_op jit(solution)/shard_map/product/pallas_call | solution.py:426
  65.9 0.4 collective-permute-start.15
  66.3 1.5 %collective-permute-start.14 = (f32[16,256]{1,0:T(8,128)S(1)}, f32[16,256]{1,0:T(8,128)S(1)}, u32[]{:S(2)}, u32[]{:S(2)}) collective-permute-start(f32[16,256]{1,0:T(8,128)S(1)} %product.7), channel_id=1, source_target_pairs={{0,16},{8,24},{16,0},{24,8},{1,17},{9,25},{17,1},{25,9},{2,18},{10... | collective-permute-start | bytes 49160 | tf_op jit(solution)/shard_map/ppermute | solution.py:27
  67.8 0.0 collective-permute-start.13
  67.8 1.3 %collective-permute-done.15 = f32[16,256]{1,0:T(8,128)S(1)} collective-permute-done((f32[16,256]{1,0:T(8,128)S(1)}, f32[16,256]{1,0:T(8,128)S(1)}, u32[]{:S(2)}, u32[]{:S(2)}) %collective-permute-start.15) | collective-permute-done | bytes 16416 | tf_op jit(solution)/shard_map/ppermute | solution.py:27
  69.1 0.9 collective-permute-done.14
  70.0 0.8 collective-permute-start.17
  70.8 3.0 %collective-permute-done.17 = f32[16,256]{1,0:T(8,128)S(1)} collective-permute-done((f32[16,256]{1,0:T(8,128)S(1)}, f32[16,256]{1,0:T(8,128)S(1)}, u32[]{:S(2)}, u32[]{:S(2)}) %collective-permute-start.17) | collective-permute-done | bytes 16416 | tf_op jit(solution)/shard_map/ppermute | solution.py:27
  73.8 2.5 %collective-permute-start.20 = (f32[8,256]{1,0:T(8,128)S(1)}, f32[8,256]{1,0:T(8,128)S(1)}, u32[]{:S(2)}, u32[]{:S(2)}) collective-permute-start(f32[8,256]{1,0:T(8,128)S(1)} %slice_add_fusion.1), channel_id=1, source_target_pairs={{0,3},{1,2},{2,1},{3,0},{4,7},{5,6},{6,5},{7,4},{8,11},{9,10},{10,... | collective-permute-start | bytes 24584 | tf_op jit(solution)/shard_map/ppermute | solution.py:27
  76.3 3.5 %collective-permute-start.19 = (f32[8,256]{1,0:T(8,128)S(1)}, f32[8,256]{1,0:T(8,128)S(1)}, u32[]{:S(2)}, u32[]{:S(2)}) collective-permute-start(f32[8,256]{1,0:T(8,128)S(1)} %slice_add_fusion.1), channel_id=1, source_target_pairs={{0,2},{1,3},{2,0},{3,1},{4,6},{5,7},{6,4},{7,5},{8,10},{9,11},{10,... | collective-permute-start | bytes 24584 | tf_op jit(solution)/shard_map/ppermute | solution.py:27
  79.8 0.1 collective-permute-start.18
  79.9 1.6 %collective-permute-done.19 = f32[8,256]{1,0:T(8,128)S(1)} collective-permute-done((f32[8,256]{1,0:T(8,128)S(1)}, f32[8,256]{1,0:T(8,128)S(1)}, u32[]{:S(2)}, u32[]{:S(2)}) %collective-permute-start.19) | collective-permute-done | bytes 8224 | tf_op jit(solution)/shard_map/ppermute | solution.py:27
  81.5 1.9 %collective-permute-done.18 = f32[8,256]{1,0:T(8,128)S(1)} collective-permute-done((f32[8,256]{1,0:T(8,128)S(1)}, f32[8,256]{1,0:T(8,128)S(1)}, u32[]{:S(2)}, u32[]{:S(2)}) %collective-permute-start.18) | collective-permute-done | bytes 8224 | tf_op jit(solution)/shard_map/ppermute | solution.py:27
  83.5 0.2 fusion.3
  83.7 2.5 %collective-permute-start.23 = (f32[8,256]{1,0:T(8,128)S(1)}, f32[8,256]{1,0:T(8,128)S(1)}, u32[]{:S(2)}, u32[]{:S(2)}) collective-permute-start(f32[8,256]{1,0:T(8,128)S(1)} %fusion.3), channel_id=1, source_target_pairs={{0,3},{1,2},{2,1},{3,0},{4,7},{5,6},{6,5},{7,4},{8,11},{9,10},{10,... | collective-permute-start | bytes 24584 | tf_op jit(solution)/shard_map/ppermute | solution.py:27
  86.2 0.0 collective-permute-start.22
  86.2 1.9 %collective-permute-start.21 = (f32[8,256]{1,0:T(8,128)S(1)}, f32[8,256]{1,0:T(8,128)S(1)}, u32[]{:S(2)}, u32[]{:S(2)}) collective-permute-start(f32[8,256]{1,0:T(8,128)S(1)} %fusion.3), channel_id=1, source_target_pairs={{0,1},{1,0},{2,3},{3,2},{4,5},{5,4},{6,7},{7,6},{8,9},{9,8},{10,11... | collective-permute-start | bytes 24584 | tf_op jit(solution)/shard_map/ppermute | solution.py:27
  88.1 1.1 %collective-permute-done.23 = f32[8,256]{1,0:T(8,128)S(1)} collective-permute-done((f32[8,256]{1,0:T(8,128)S(1)}, f32[8,256]{1,0:T(8,128)S(1)}, u32[]{:S(2)}, u32[]{:S(2)}) %collective-permute-start.23) | collective-permute-done | bytes 8224 | tf_op jit(solution)/shard_map/ppermute | solution.py:27
  89.1 1.6 %collective-permute-done.22 = f32[8,256]{1,0:T(8,128)S(1)} collective-permute-done((f32[8,256]{1,0:T(8,128)S(1)}, f32[8,256]{1,0:T(8,128)S(1)}, u32[]{:S(2)}, u32[]{:S(2)}) %collective-permute-start.22) | collective-permute-done | bytes 8224 | tf_op jit(solution)/shard_map/ppermute | solution.py:27
  90.7 0.6 add_add_fusion.2
  (27 shorter events, 0.1 us)
Async XLA Ops:
  2.3 11.6 %collective-permute-start = (f32[6,16,4,128]{3,2,1,0:T(4,128)}, f32[6,16,4,128]{3,2,1,0:T(4,128)S(1)}, u32[]{:S(2)}, u32[]{:S(2)}) collective-permute-start(f32[6,16,4,128]{3,2,1,0:T(4,128)} %pack.1.refs_0_), channel_id=1, source_target_pairs={{0,4},{4,0},{1,5},{5,1},{2,6},{6,2},{3,7},{7,3},{8,12},{12,8},{9,1... | collective-permute-start | bytes 589832 | tf_op jit(solution)/shard_map/ppermute | solution.py:464
  5.3 16.0 %collective-permute-start.3 = (f32[6,16,4,128]{3,2,1,0:T(4,128)}, f32[6,16,4,128]{3,2,1,0:T(4,128)S(1)}, u32[]{:S(2)}, u32[]{:S(2)}) collective-permute-start(f32[6,16,4,128]{3,2,1,0:T(4,128)} %pack.1.refs_0_), channel_id=1, source_target_pairs={{1,2},{2,1},{5,6},{6,5},{9,10},{10,9},{13,14},{14,13},{17,18},{18,... | collective-permute-start | bytes 589832 | tf_op jit(solution)/shard_map/ppermute | solution.py:467
  6.0 15.3 %collective-permute-start.1 = (f32[6,16,4,128]{3,2,1,0:T(4,128)}, f32[6,16,4,128]{3,2,1,0:T(4,128)S(1)}, u32[]{:S(2)}, u32[]{:S(2)}) collective-permute-start(f32[6,16,4,128]{3,2,1,0:T(4,128)} %pack.1.refs_0_), channel_id=1, source_target_pairs={{0,1},{2,3},{1,0},{3,2},{4,5},{6,7},{5,4},{7,6},{8,9},{10,11},{9,8... | collective-permute-start | bytes 589832 | tf_op jit(solution)/shard_map/ppermute | solution.py:466
  14.0 7.4 %copy-start = (f32[6,16,4,128]{3,2,1,0:T(4,128)S(1)}, f32[6,16,4,128]{3,2,1,0:T(4,128)}, u32[]{:S(2)}) copy-start(f32[6,16,4,128]{3,2,1,0:T(4,128)} %pack.1.refs_0_) | copy-start | bytes 589828
  14.0 7.3 %collective-permute-start.4 = (f32[6,16,4,128]{3,2,1,0:T(4,128)S(1)}, f32[6,16,4,128]{3,2,1,0:T(4,128)S(1)}, u32[]{:S(2)}, u32[]{:S(2)}) collective-permute-start(f32[6,16,4,128]{3,2,1,0:T(4,128)S(1)} %collective-permute-done.refs_1_), channel_id=1, source_target_pairs={{1,2},{2,1},{5,6},{6,5},{9,10},{10,9},{13,14},{14,13},{17,18},{18,... | collective-permute-start | bytes 589832 | tf_op jit(solution)/shard_map/ppermute | solution.py:471
  14.8 6.5 %collective-permute-start.2 = (f32[6,16,4,128]{3,2,1,0:T(4,128)S(1)}, f32[6,16,4,128]{3,2,1,0:T(4,128)S(1)}, u32[]{:S(2)}, u32[]{:S(2)}) collective-permute-start(f32[6,16,4,128]{3,2,1,0:T(4,128)S(1)} %collective-permute-done.refs_1_), channel_id=1, source_target_pairs={{0,1},{2,3},{1,0},{3,2},{4,5},{6,7},{5,4},{7,6},{8,9},{10,11},{9,8... | collective-permute-start | bytes 589832 | tf_op jit(solution)/shard_map/ppermute | solution.py:470
  23.6 4.3 %collective-permute-start.5 = (f32[6,6,8,128]{3,2,1,0:T(8,128)S(1)}, f32[6,6,8,128]{3,2,1,0:T(8,128)S(1)}, u32[]{:S(2)}, u32[]{:S(2)}) collective-permute-start(f32[6,6,8,128]{3,2,1,0:T(8,128)S(1)} %get-tuple-element.49), channel_id=1, source_target_pairs={{0,8},{16,24},{8,0},{24,16},{1,9},{17,25},{9,1},{25,17},{2,10},{18... | collective-permute-start | bytes 442376 | tf_op jit(solution)/shard_map/ppermute | solution.py:487
  23.7 4.3 %collective-permute-start.6 = (f32[6,6,8,128]{3,2,1,0:T(8,128)S(1)}, f32[6,6,8,128]{3,2,1,0:T(8,128)S(1)}, u32[]{:S(2)}, u32[]{:S(2)}) collective-permute-start(f32[6,6,8,128]{3,2,1,0:T(8,128)S(1)} %get-tuple-element.50), channel_id=1, source_target_pairs={{8,16},{16,8},{9,17},{17,9},{10,18},{18,10},{11,19},{19,11},{12,20... | collective-permute-start | bytes 442376 | tf_op jit(solution)/shard_map/ppermute | solution.py:488
  24.4 8.2 %copy-start.4 = (s32[8,4]{0,1:T(4,128)S(1)}, s32[8,4]{0,1:T(4,128)}, u32[]{:S(2)}) copy-start(s32[8,4]{0,1:T(4,128)} %param.13) | copy-start | bytes 388
  24.4 8.2 %copy-start.1 = (f32[8,8]{1,0:T(8,128)S(1)}, f32[8,8]{1,0:T(8,128)}, u32[]{:S(2)}) copy-start(f32[8,8]{1,0:T(8,128)} %rates.1) | copy-start | bytes 772
  24.4 8.2 %copy-start.2 = (s32[8]{0:T(128)S(1)}, s32[8]{0:T(128)}, u32[]{:S(2)}) copy-start(s32[8]{0:T(128)} %plan.1) | copy-start | bytes 100
  24.4 8.2 %copy-start.3 = (f32[4]{0:T(128)S(1)}, f32[4]{0:T(128)}, u32[]{:S(2)}) copy-start(f32[4]{0:T(128)} %diffusion.1) | copy-start | bytes 52
  28.0 23.3 %collective-permute-start.9 = (f32[256,256]{1,0:T(8,128)S(1)}, f32[256,256]{1,0:T(8,128)S(1)}, u32[]{:S(2)}, u32[]{:S(2)}) collective-permute-start(f32[256,256]{1,0:T(8,128)S(1)} %gram.5), channel_id=1, source_target_pairs={{0,24},{8,16},{16,8},{24,0},{1,25},{9,17},{17,9},{25,1},{2,26},{10... | collective-permute-start | bytes 786440 | tf_op jit(solution)/shard_map/ppermute | solution.py:27
  29.6 21.6 %collective-permute-start.8 = (f32[256,256]{1,0:T(8,128)S(1)}, f32[256,256]{1,0:T(8,128)S(1)}, u32[]{:S(2)}, u32[]{:S(2)}) collective-permute-start(f32[256,256]{1,0:T(8,128)S(1)} %gram.5), channel_id=1, source_target_pairs={{0,16},{8,24},{16,0},{24,8},{1,17},{9,25},{17,1},{25,9},{2,18},{10... | collective-permute-start | bytes 786440 | tf_op jit(solution)/shard_map/ppermute | solution.py:27
  32.5 18.7 %collective-permute-start.7 = (f32[256,256]{1,0:T(8,128)S(1)}, f32[256,256]{1,0:T(8,128)S(1)}, u32[]{:S(2)}, u32[]{:S(2)}) collective-permute-start(f32[256,256]{1,0:T(8,128)S(1)} %gram.5), channel_id=1, source_target_pairs={{0,8},{8,0},{16,24},{24,16},{1,9},{9,1},{17,25},{25,17},{2,10},{10... | collective-permute-start | bytes 786440 | tf_op jit(solution)/shard_map/ppermute | solution.py:27
  50.1 10.5 %collective-permute-start.11 = (f32[4,16,8,128]{3,2,1,0:T(8,128)S(1)}, f32[4,16,8,128]{3,2,1,0:T(8,128)S(1)}, u32[]{:S(2)}, u32[]{:S(2)}) collective-permute-start(f32[4,16,8,128]{3,2,1,0:T(8,128)S(1)} %get-tuple-element.67), channel_id=1, source_target_pairs={{0,16},{8,24},{16,0},{24,8},{1,17},{9,25},{17,1},{25,9},{2,18},{10... | collective-permute-start | bytes 786440 | tf_op jit(solution)/shard_map/ppermute | solution.py:27
  51.2 6.7 %collective-permute-start.12 = (f32[4,16,8,128]{3,2,1,0:T(8,128)S(1)}, f32[4,16,8,128]{3,2,1,0:T(8,128)S(1)}, u32[]{:S(2)}, u32[]{:S(2)}) collective-permute-start(f32[4,16,8,128]{3,2,1,0:T(8,128)S(1)} %get-tuple-element.69), channel_id=1, source_target_pairs={{0,8},{8,0},{16,24},{24,16},{1,9},{9,1},{17,25},{25,17},{2,10},{10... | collective-permute-start | bytes 786440 | tf_op jit(solution)/shard_map/ppermute | solution.py:27
  51.3 12.8 %collective-permute-start.10 = (f32[4,16,8,128]{3,2,1,0:T(8,128)S(1)}, f32[4,16,8,128]{3,2,1,0:T(8,128)S(1)}, u32[]{:S(2)}, u32[]{:S(2)}) collective-permute-start(f32[4,16,8,128]{3,2,1,0:T(8,128)S(1)} %get-tuple-element.64), channel_id=1, source_target_pairs={{0,24},{8,16},{16,8},{24,0},{1,25},{9,17},{17,9},{25,1},{2,26},{10... | collective-permute-start | bytes 786440 | tf_op jit(solution)/shard_map/ppermute | solution.py:27
  52.5 17.5 %collective-permute-start.16 = (f32[256,256]{1,0:T(8,128)S(1)}, f32[256,256]{1,0:T(8,128)S(1)}, u32[]{:S(2)}, u32[]{:S(2)}) collective-permute-start(f32[256,256]{1,0:T(8,128)S(1)} %add_add_fusion), channel_id=1, source_target_pairs={{0,4},{4,0},{1,5},{5,1},{2,6},{6,2},{3,7},{7,3},{8,12},{12,8},{9,1... | collective-permute-start | bytes 786440 | tf_op jit(solution)/shard_map/ppermute | solution.py:27
  65.9 3.2 %collective-permute-start.15 = (f32[16,256]{1,0:T(8,128)S(1)}, f32[16,256]{1,0:T(8,128)S(1)}, u32[]{:S(2)}, u32[]{:S(2)}) collective-permute-start(f32[16,256]{1,0:T(8,128)S(1)} %product.7), channel_id=1, source_target_pairs={{0,24},{8,16},{16,8},{24,0},{1,25},{9,17},{17,9},{25,1},{2,26},{10... | collective-permute-start | bytes 49160 | tf_op jit(solution)/shard_map/ppermute | solution.py:27
  66.3 3.7 %collective-permute-start.14 = (f32[16,256]{1,0:T(8,128)S(1)}, f32[16,256]{1,0:T(8,128)S(1)}, u32[]{:S(2)}, u32[]{:S(2)}) collective-permute-start(f32[16,256]{1,0:T(8,128)S(1)} %product.7), channel_id=1, source_target_pairs={{0,16},{8,24},{16,0},{24,8},{1,17},{9,25},{17,1},{25,9},{2,18},{10... | collective-permute-start | bytes 49160 | tf_op jit(solution)/shard_map/ppermute | solution.py:27
  67.8 2.2 %collective-permute-start.13 = (f32[16,256]{1,0:T(8,128)S(1)}, f32[16,256]{1,0:T(8,128)S(1)}, u32[]{:S(2)}, u32[]{:S(2)}) collective-permute-start(f32[16,256]{1,0:T(8,128)S(1)} %product.7), channel_id=1, source_target_pairs={{0,8},{8,0},{16,24},{24,16},{1,9},{9,1},{17,25},{25,17},{2,10},{10... | collective-permute-start | bytes 49160 | tf_op jit(solution)/shard_map/ppermute | solution.py:27
  70.0 3.8 %collective-permute-start.17 = (f32[16,256]{1,0:T(8,128)S(1)}, f32[16,256]{1,0:T(8,128)S(1)}, u32[]{:S(2)}, u32[]{:S(2)}) collective-permute-start(f32[16,256]{1,0:T(8,128)S(1)} %add_add_fusion.1), channel_id=1, source_target_pairs={{0,4},{4,0},{1,5},{5,1},{2,6},{6,2},{3,7},{7,3},{8,12},{12,8},{9,1... | collective-permute-start | bytes 49160 | tf_op jit(solution)/shard_map/ppermute | solution.py:27
  73.8 6.1 %collective-permute-start.20 = (f32[8,256]{1,0:T(8,128)S(1)}, f32[8,256]{1,0:T(8,128)S(1)}, u32[]{:S(2)}, u32[]{:S(2)}) collective-permute-start(f32[8,256]{1,0:T(8,128)S(1)} %slice_add_fusion.1), channel_id=1, source_target_pairs={{0,3},{1,2},{2,1},{3,0},{4,7},{5,6},{6,5},{7,4},{8,11},{9,10},{10,... | collective-permute-start | bytes 24584 | tf_op jit(solution)/shard_map/ppermute | solution.py:27
  76.3 5.2 %collective-permute-start.19 = (f32[8,256]{1,0:T(8,128)S(1)}, f32[8,256]{1,0:T(8,128)S(1)}, u32[]{:S(2)}, u32[]{:S(2)}) collective-permute-start(f32[8,256]{1,0:T(8,128)S(1)} %slice_add_fusion.1), channel_id=1, source_target_pairs={{0,2},{1,3},{2,0},{3,1},{4,6},{5,7},{6,4},{7,5},{8,10},{9,11},{10,... | collective-permute-start | bytes 24584 | tf_op jit(solution)/shard_map/ppermute | solution.py:27
  79.8 3.7 %collective-permute-start.18 = (f32[8,256]{1,0:T(8,128)S(1)}, f32[8,256]{1,0:T(8,128)S(1)}, u32[]{:S(2)}, u32[]{:S(2)}) collective-permute-start(f32[8,256]{1,0:T(8,128)S(1)} %slice_add_fusion.1), channel_id=1, source_target_pairs={{0,1},{1,0},{2,3},{3,2},{4,5},{5,4},{6,7},{7,6},{8,9},{9,8},{10,11... | collective-permute-start | bytes 24584 | tf_op jit(solution)/shard_map/ppermute | solution.py:27
  83.7 5.5 %collective-permute-start.23 = (f32[8,256]{1,0:T(8,128)S(1)}, f32[8,256]{1,0:T(8,128)S(1)}, u32[]{:S(2)}, u32[]{:S(2)}) collective-permute-start(f32[8,256]{1,0:T(8,128)S(1)} %fusion.3), channel_id=1, source_target_pairs={{0,3},{1,2},{2,1},{3,0},{4,7},{5,6},{6,5},{7,4},{8,11},{9,10},{10,... | collective-permute-start | bytes 24584 | tf_op jit(solution)/shard_map/ppermute | solution.py:27
  86.2 4.5 %collective-permute-start.22 = (f32[8,256]{1,0:T(8,128)S(1)}, f32[8,256]{1,0:T(8,128)S(1)}, u32[]{:S(2)}, u32[]{:S(2)}) collective-permute-start(f32[8,256]{1,0:T(8,128)S(1)} %fusion.3), channel_id=1, source_target_pairs={{0,2},{1,3},{2,0},{3,1},{4,6},{5,7},{6,4},{7,5},{8,10},{9,11},{10,... | collective-permute-start | bytes 24584 | tf_op jit(solution)/shard_map/ppermute | solution.py:27
  86.2 4.5 %collective-permute-start.21 = (f32[8,256]{1,0:T(8,128)S(1)}, f32[8,256]{1,0:T(8,128)S(1)}, u32[]{:S(2)}, u32[]{:S(2)}) collective-permute-start(f32[8,256]{1,0:T(8,128)S(1)} %fusion.3), channel_id=1, source_target_pairs={{0,1},{1,0},{2,3},{3,2},{4,5},{5,4},{6,7},{7,6},{8,9},{9,8},{10,11... | collective-permute-start | bytes 24584 | tf_op jit(solution)/shard_map/ppermute | solution.py:27

commit v11 on v10

--- a/solution.py
+++ b/solution.py
@@ -371,7 +371,8 @@
         values = held[x]
         high = values.astype(jnp.bfloat16).astype(jnp.float32)
         left = jnp.concatenate([high, values - high], axis=1).astype(jnp.bfloat16)
-        waits[x].wait()
+        if waits:
+            waits[x].wait()
         for y in range(0, cells_y, 2):
             more = jnp.dot(
                 jnp.concatenate([left[y], left[y + 1]], axis=1),
@@ -403,6 +404,12 @@
     for i in range(len(later)):
         sources += rows_of(tables[0], later[i], cells_z)
         targets += [ahead[i].at[x] for x in places]
+    if fetched:
+        acc = None
+        for i in range(count):
+            acc = multiply(parts[i], tables[i], None, acc)
+        out[...] = acc + total[0][...] if total else acc
+        return
     copies = fetch(sources, targets, sems)
     acc = None
     for i in range(count):
@@ -423,11 +430,18 @@
     size = 2 * count * math.prod(room)
     tables = rows or (basis,)
     given = len(total)
+    place = anywhere
+    if rows:
+        place = whole
+        parts, tables, total = (
+            [pltpu.with_memory_space_constraint(a, pltpu.VMEM) for a in arrays]
+            for arrays in (parts, tables, total)
+        )
     return pl.pallas_call(
         functools.partial(product_kernel, flips, later, bool(rows), given),
         out_shape=[jax.ShapeDtypeStruct((2 * snaps, modes), jnp.float32)]
         + [jax.ShapeDtypeStruct(room, jnp.bfloat16)] * len(later),
-        in_specs=anywhere(count + len(tables) + given),
+        in_specs=place(count + len(tables) + given),
         out_specs=whole(1) + anywhere(len(later)),
         scratch_shapes=[
             pltpu.VMEM((count, *parts[0].shape), jnp.float32),

time: 91.5 us -> 90.5 us (0.989)
  Pallas kernels: 44.1 us -> 42.1 us
  waiting for transfers between devices: 13.2 us -> 14.2 us
    pallas_call x4, Pallas kernels: 10.8 us -> 8.83 us  [product(): pl.pallas_call(functools.partial(product_kernel, flips, later, bool(rows)...]
    ppermute x17, waiting for transfers between devices: 13.2 us -> 14.2 us  [exchange(): return lax.ppermute(value, axis, [(i, i ^ flips) for i in range(count)])]
  transfers between devices with their start and end apart: 24 -> 24, of which waited for: 8 -> 8; matrix products, arithmetic and copies ran while one was open for 0% -> 0% of each run, Pallas kernels for 44% -> 42%
where the time goes in v11:
time: 90.5 us; the launch traced here: 90.3 us
  Pallas kernels  42.1 us (47%)
  starting transfers between devices  32.1 us (35%)
  waiting for transfers between devices  14.2 us (16%)
    ppermute x17, starting transfers between devices, exchange(): return lax.ppermute(value, axis, [(i, i ^ flips) for i in range(count)])  20.7 us
    pallas_call x1, Pallas kernels, body(): pl.pallas_call(functools.partial(steps_kernel, count_x), out_shape=[jax.S...  17.5 us
    ppermute x17, waiting for transfers between devices, exchange(): return lax.ppermute(value, axis, [(i, i ^ flips) for i in range(count)])  14.2 us
    pallas_call x3, Pallas kernels, gram_part(): pl.pallas_call(functools.partial(gram_kernel, places, later, bool(parts),...  11.8 us
    pallas_call x4, Pallas kernels, product(): pl.pallas_call(functools.partial(product_kernel, flips, later, bool(rows)...  8.83 us
    ppermute x1, starting transfers between devices, body(): from_a = [lax.ppermute(own, 'gy', pairs('gy', 0))]  4.45 us
    ppermute x1, starting transfers between devices, body(): lax.ppermute(own, 'gx', [(i, (i - shift) % count_x) for i in range(count_...  2.94 us
    pallas_call x1, Pallas kernels, body(): pl.pallas_call(functools.partial(edges_kernel, count_x), out_shape=(packe...  2.29 us
  transfers between devices with their start and end apart: 24, of which 8 were waited for; matrix products, arithmetic and copies ran while one was open for 0% of the time, Pallas kernels for 42%

profile of v11, /device:TPU:0, one launch (start us, length us, event | category | flops | bytes accessed | tf_op | source)
XLA Modules:
  0.0 90.3 jit_solution(11822087488421880649)
XLA Ops:
  0.6 1.7 %pack.1.refs_0_ = f32[6,16,4,128]{3,2,1,0:T(4,128)} custom-call(f32[4,4,16,128]{3,2,1,0:T(8,128)} %terminal.1, f32[4,16,128]{2,1,0:T(8,128)} %velocity.1, s32[4,16,128]{2,1,0:T(8,128)} %material.1), custom_call_target="tpu_custom_call" | custom-call | tf_op jit(solution)/shard_map/pack/pallas_call | solution.py:468
  2.3 2.9 %collective-permute-start = (f32[6,16,4,128]{3,2,1,0:T(4,128)}, f32[6,16,4,128]{3,2,1,0:T(4,128)S(1)}, u32[]{:S(2)}, u32[]{:S(2)}) collective-permute-start(f32[6,16,4,128]{3,2,1,0:T(4,128)} %pack.1.refs_0_), channel_id=1, source_target_pairs={{0,4},{4,0},{1,5},{5,1},{2,6},{6,2},{3,7},{7,3},{8,12},{12,8},{9,1... | collective-permute-start | bytes 589832 | tf_op jit(solution)/shard_map/ppermute | solution.py:478
  5.3 0.7 collective-permute-start.3
  6.0 4.5 %collective-permute-start.1 = (f32[6,16,4,128]{3,2,1,0:T(4,128)}, f32[6,16,4,128]{3,2,1,0:T(4,128)S(1)}, u32[]{:S(2)}, u32[]{:S(2)}) collective-permute-start(f32[6,16,4,128]{3,2,1,0:T(4,128)} %pack.1.refs_0_), channel_id=1, source_target_pairs={{0,1},{2,3},{1,0},{3,2},{4,5},{6,7},{5,4},{7,6},{8,9},{10,11},{9,8... | collective-permute-start | bytes 589832 | tf_op jit(solution)/shard_map/ppermute | solution.py:480
  10.4 3.5 %gram.3.refs_1_ = f32[256,256]{1,0:T(8,128)S(1)} custom-call(bf16[1,4,16,512,256]{4,3,2,1,0:T(8,128)(2,1)} %refs_1_.3), custom_call_target="tpu_custom_call" | custom-call | flops 1073741824 | bytes 12582912 | tf_op jit(solution)/shard_map/gram/pallas_call | solution.py:341
  14.0 0.8 collective-permute-start.4
  14.8 1.8 %collective-permute-start.2 = (f32[6,16,4,128]{3,2,1,0:T(4,128)S(1)}, f32[6,16,4,128]{3,2,1,0:T(4,128)S(1)}, u32[]{:S(2)}, u32[]{:S(2)}) collective-permute-start(f32[6,16,4,128]{3,2,1,0:T(4,128)S(1)} %collective-permute-done.refs_1_), channel_id=1, source_target_pairs={{0,1},{2,3},{1,0},{3,2},{4,5},{6,7},{5,4},{7,6},{8,9},{10,11},{9,8... | collective-permute-start | bytes 589832 | tf_op jit(solution)/shard_map/ppermute | solution.py:484
  16.6 4.7 %gram.4 = (f32[256,256]{1,0:T(8,128)S(1)}, bf16[16,512,256]{2,1,0:T(8,128)(2,1)S(1)}, bf16[16,512,256]{2,1,0:T(8,128)(2,1)S(1)}) custom-call(bf16[1,4,16,512,256]{4,3,2,1,0:T(8,128)(2,1)} %refs_1_.3, f32[256,256]{1,0:T(8,128)S(1)} %gram.3.refs_1_), custom_call_target="tpu_custom_call" | custom-call | flops 1073741824 | bytes 12582912 | tf_op jit(solution)/shard_map/gram/pallas_call | solution.py:341
  21.3 2.3 %edges.1 = (f32[6,6,8,128]{3,2,1,0:T(8,128)S(1)}, f32[6,6,8,128]{3,2,1,0:T(8,128)S(1)}) custom-call(f32[6,16,4,128]{3,2,1,0:T(4,128)S(1)} %copy-done, f32[6,16,4,128]{3,2,1,0:T(4,128)S(1)} %collective-permute-done.refs_1_, f32[6,16,4,128]{3,2,1,0:T(4,128)S(1)} %collective-permute-done.1.refs_2_, f32[6,16,4,128]{3,2,1,0:T(4,128)S(1)} %collective-permute-done.2.refs_3_, ...), custom_call_target="tpu_custom_call" | custom-call | tf_op jit(solution)/shard_map/edges/pallas_call | solution.py:492
  23.6 0.1 collective-permute-start.5
  23.7 0.7 collective-permute-start.6
  24.4 0.0 copy-start.4
  24.4 0.0 copy-start.1
  24.4 0.0 copy-start.2
  24.4 0.0 copy-start.3
  24.4 3.5 %gram.5 = f32[256,256]{1,0:T(8,128)S(1)} custom-call(bf16[16,512,256]{2,1,0:T(8,128)(2,1)S(1)} %get-tuple-element.51.refs_0_, bf16[16,512,256]{2,1,0:T(8,128)(2,1)S(1)} %get-tuple-element.52.refs_1_, f32[256,256]{1,0:T(8,128)S(1)} %get-tuple-element.53.refs_2_), custom_call_target="tpu_custom_call" | custom-call | flops 2147483648 | bytes 25165824 | tf_op jit(solution)/shard_map/gram/pallas_call | solution.py:341
  28.0 1.7 %collective-permute-start.9 = (f32[256,256]{1,0:T(8,128)S(1)}, f32[256,256]{1,0:T(8,128)S(1)}, u32[]{:S(2)}, u32[]{:S(2)}) collective-permute-start(f32[256,256]{1,0:T(8,128)S(1)} %gram.5), channel_id=1, source_target_pairs={{0,24},{8,16},{16,8},{24,0},{1,25},{9,17},{17,9},{25,1},{2,26},{10... | collective-permute-start | bytes 786440 | tf_op jit(solution)/shard_map/ppermute | solution.py:27
  29.6 2.9 %collective-permute-start.8 = (f32[256,256]{1,0:T(8,128)S(1)}, f32[256,256]{1,0:T(8,128)S(1)}, u32[]{:S(2)}, u32[]{:S(2)}) collective-permute-start(f32[256,256]{1,0:T(8,128)S(1)} %gram.5), channel_id=1, source_target_pairs={{0,16},{8,24},{16,0},{24,8},{1,17},{9,25},{17,1},{25,9},{2,18},{10... | collective-permute-start | bytes 786440 | tf_op jit(solution)/shard_map/ppermute | solution.py:27
  32.5 0.1 copy.10.stoich
  32.6 17.5 %steps.1 = (f32[4,4,16,128]{3,2,1,0:T(8,128)}, f32[4,16,8,128]{3,2,1,0:T(8,128)S(1)}, f32[4,16,8,128]{3,2,1,0:T(8,128)S(1)}, f32[4,16,8,128]{3,2,1,0:T(8,128)S(1)}, f32[4,16,8,128]{3,2,1,0:T(8,128)S(1)}) custom-call(s32[8]{0:T(128)S(1)} %copy-done.2, f32[4]{0:T(128)S(1)} %copy-done.3, s32[8,4]{1,0:T(8,128)S(1)} %copy.10.stoich, f32[8,8]{1,0:T(8,128)S(1)} %copy-done.1, ...), custom_call_target="tpu_custom_call" | custom-call | bytes 100663296 | tf_op jit(solution)/shard_map/steps/pallas_call | solution.py:510
  50.1 1.1 %collective-permute-start.11 = (f32[4,16,8,128]{3,2,1,0:T(8,128)S(1)}, f32[4,16,8,128]{3,2,1,0:T(8,128)S(1)}, u32[]{:S(2)}, u32[]{:S(2)}) collective-permute-start(f32[4,16,8,128]{3,2,1,0:T(8,128)S(1)} %get-tuple-element.67), channel_id=1, source_target_pairs={{0,16},{8,24},{16,0},{24,8},{1,17},{9,25},{17,1},{25,9},{2,18},{10... | collective-permute-start | bytes 786440 | tf_op jit(solution)/shard_map/ppermute | solution.py:27
  51.2 0.1 add_add_fusion
  51.3 1.2 %collective-permute-start.10 = (f32[4,16,8,128]{3,2,1,0:T(8,128)S(1)}, f32[4,16,8,128]{3,2,1,0:T(8,128)S(1)}, u32[]{:S(2)}, u32[]{:S(2)}) collective-permute-start(f32[4,16,8,128]{3,2,1,0:T(8,128)S(1)} %get-tuple-element.64), channel_id=1, source_target_pairs={{0,24},{8,16},{16,8},{24,0},{1,25},{9,17},{17,9},{25,1},{2,26},{10... | collective-permute-start | bytes 786440 | tf_op jit(solution)/shard_map/ppermute | solution.py:27
  52.5 0.7 collective-permute-start.16
  53.2 4.7 %product.4 = (f32[16,256]{1,0:T(8,128)S(1)}, bf16[4,16,128,256]{3,2,1,0:T(8,128)(2,1)S(1)}, bf16[4,16,128,256]{3,2,1,0:T(8,128)(2,1)S(1)}) custom-call(f32[4,16,8,128]{3,2,1,0:T(8,128)S(1)} %get-tuple-element.65.refs_0_, bf16[1,4,16,512,256]{4,3,2,1,0:T(8,128)(2,1)} %refs_1_.3), custom_call_target="tpu_custom_call" | custom-call | flops 67108864 | bytes 8388608 | tf_op jit(solution)/shard_map/product/pallas_call | solution.py:440
  58.0 2.7 %product.5.refs_2_ = f32[16,256]{1,0:T(8,128)S(1)} custom-call(f32[4,16,8,128]{3,2,1,0:T(8,128)S(1)} %collective-permute-done.12.refs_0_, bf16[1,4,16,512,256]{4,3,2,1,0:T(8,128)(2,1)} %refs_1_.3, f32[16,256]{1,0:T(8,128)S(1)} %get-tuple-element.70.refs_2_), custom_call_target="tpu_custom_call" | custom-call | flops 67108864 | bytes 8388608 | tf_op jit(solution)/shard_map/product/pallas_call | solution.py:440
  60.7 0.7 product.6.refs_2_
  61.4 2.8 %collective-permute-done.10.refs_0_ = f32[4,16,8,128]{3,2,1,0:T(8,128)S(1)} collective-permute-done((f32[4,16,8,128]{3,2,1,0:T(8,128)S(1)}, f32[4,16,8,128]{3,2,1,0:T(8,128)S(1)}, u32[]{:S(2)}, u32[]{:S(2)}) %collective-permute-start.10) | collective-permute-done | bytes 262176 | tf_op jit(solution)/shard_map/ppermute | solution.py:27
  64.2 0.7 product.7
  64.9 0.4 collective-permute-start.15
  65.3 1.5 %collective-permute-start.14 = (f32[16,256]{1,0:T(8,128)S(1)}, f32[16,256]{1,0:T(8,128)S(1)}, u32[]{:S(2)}, u32[]{:S(2)}) collective-permute-start(f32[16,256]{1,0:T(8,128)S(1)} %product.7), channel_id=1, source_target_pairs={{0,16},{8,24},{16,0},{24,8},{1,17},{9,25},{17,1},{25,9},{2,18},{10... | collective-permute-start | bytes 49160 | tf_op jit(solution)/shard_map/ppermute | solution.py:27
  66.8 0.0 collective-permute-start.13
  66.8 1.3 %collective-permute-done.15 = f32[16,256]{1,0:T(8,128)S(1)} collective-permute-done((f32[16,256]{1,0:T(8,128)S(1)}, f32[16,256]{1,0:T(8,128)S(1)}, u32[]{:S(2)}, u32[]{:S(2)}) %collective-permute-start.15) | collective-permute-done | bytes 16416 | tf_op jit(solution)/shard_map/ppermute | solution.py:27
  68.1 0.9 collective-permute-done.14
  69.0 0.8 collective-permute-start.17
  69.8 3.0 %collective-permute-done.17 = f32[16,256]{1,0:T(8,128)S(1)} collective-permute-done((f32[16,256]{1,0:T(8,128)S(1)}, f32[16,256]{1,0:T(8,128)S(1)}, u32[]{:S(2)}, u32[]{:S(2)}) %collective-permute-start.17) | collective-permute-done | bytes 16416 | tf_op jit(solution)/shard_map/ppermute | solution.py:27
  72.8 2.5 %collective-permute-start.20 = (f32[8,256]{1,0:T(8,128)S(1)}, f32[8,256]{1,0:T(8,128)S(1)}, u32[]{:S(2)}, u32[]{:S(2)}) collective-permute-start(f32[8,256]{1,0:T(8,128)S(1)} %slice_add_fusion.1), channel_id=1, source_target_pairs={{0,3},{1,2},{2,1},{3,0},{4,7},{5,6},{6,5},{7,4},{8,11},{9,10},{10,... | collective-permute-start | bytes 24584 | tf_op jit(solution)/shard_map/ppermute | solution.py:27
  75.3 3.5 %collective-permute-start.19 = (f32[8,256]{1,0:T(8,128)S(1)}, f32[8,256]{1,0:T(8,128)S(1)}, u32[]{:S(2)}, u32[]{:S(2)}) collective-permute-start(f32[8,256]{1,0:T(8,128)S(1)} %slice_add_fusion.1), channel_id=1, source_target_pairs={{0,2},{1,3},{2,0},{3,1},{4,6},{5,7},{6,4},{7,5},{8,10},{9,11},{10,... | collective-permute-start | bytes 24584 | tf_op jit(solution)/shard_map/ppermute | solution.py:27
  78.8 0.1 collective-permute-start.18
  78.9 1.6 %collective-permute-done.19 = f32[8,256]{1,0:T(8,128)S(1)} collective-permute-done((f32[8,256]{1,0:T(8,128)S(1)}, f32[8,256]{1,0:T(8,128)S(1)}, u32[]{:S(2)}, u32[]{:S(2)}) %collective-permute-start.19) | collective-permute-done | bytes 8224 | tf_op jit(solution)/shard_map/ppermute | solution.py:27
  80.5 1.9 %collective-permute-done.18 = f32[8,256]{1,0:T(8,128)S(1)} collective-permute-done((f32[8,256]{1,0:T(8,128)S(1)}, f32[8,256]{1,0:T(8,128)S(1)}, u32[]{:S(2)}, u32[]{:S(2)}) %collective-permute-start.18) | collective-permute-done | bytes 8224 | tf_op jit(solution)/shard_map/ppermute | solution.py:27
  82.5 0.2 fusion.3
  82.7 2.5 %collective-permute-start.23 = (f32[8,256]{1,0:T(8,128)S(1)}, f32[8,256]{1,0:T(8,128)S(1)}, u32[]{:S(2)}, u32[]{:S(2)}) collective-permute-start(f32[8,256]{1,0:T(8,128)S(1)} %fusion.3), channel_id=1, source_target_pairs={{0,3},{1,2},{2,1},{3,0},{4,7},{5,6},{6,5},{7,4},{8,11},{9,10},{10,... | collective-permute-start | bytes 24584 | tf_op jit(solution)/shard_map/ppermute | solution.py:27
  85.2 0.0 collective-permute-start.22
  85.2 1.9 %collective-permute-start.21 = (f32[8,256]{1,0:T(8,128)S(1)}, f32[8,256]{1,0:T(8,128)S(1)}, u32[]{:S(2)}, u32[]{:S(2)}) collective-permute-start(f32[8,256]{1,0:T(8,128)S(1)} %fusion.3), channel_id=1, source_target_pairs={{0,1},{1,0},{2,3},{3,2},{4,5},{5,4},{6,7},{7,6},{8,9},{9,8},{10,11... | collective-permute-start | bytes 24584 | tf_op jit(solution)/shard_map/ppermute | solution.py:27
  87.1 1.1 %collective-permute-done.23 = f32[8,256]{1,0:T(8,128)S(1)} collective-permute-done((f32[8,256]{1,0:T(8,128)S(1)}, f32[8,256]{1,0:T(8,128)S(1)}, u32[]{:S(2)}, u32[]{:S(2)}) %collective-permute-start.23) | collective-permute-done | bytes 8224 | tf_op jit(solution)/shard_map/ppermute | solution.py:27
  88.1 1.6 %collective-permute-done.22 = f32[8,256]{1,0:T(8,128)S(1)} collective-permute-done((f32[8,256]{1,0:T(8,128)S(1)}, f32[8,256]{1,0:T(8,128)S(1)}, u32[]{:S(2)}, u32[]{:S(2)}) %collective-permute-start.22) | collective-permute-done | bytes 8224 | tf_op jit(solution)/shard_map/ppermute | solution.py:27
  89.7 0.6 add_add_fusion.2
  (27 shorter events, 0.1 us)
Async XLA Ops:
  2.3 11.6 %collective-permute-start = (f32[6,16,4,128]{3,2,1,0:T(4,128)}, f32[6,16,4,128]{3,2,1,0:T(4,128)S(1)}, u32[]{:S(2)}, u32[]{:S(2)}) collective-permute-start(f32[6,16,4,128]{3,2,1,0:T(4,128)} %pack.1.refs_0_), channel_id=1, source_target_pairs={{0,4},{4,0},{1,5},{5,1},{2,6},{6,2},{3,7},{7,3},{8,12},{12,8},{9,1... | collective-permute-start | bytes 589832 | tf_op jit(solution)/shard_map/ppermute | solution.py:478
  5.3 16.0 %collective-permute-start.3 = (f32[6,16,4,128]{3,2,1,0:T(4,128)}, f32[6,16,4,128]{3,2,1,0:T(4,128)S(1)}, u32[]{:S(2)}, u32[]{:S(2)}) collective-permute-start(f32[6,16,4,128]{3,2,1,0:T(4,128)} %pack.1.refs_0_), channel_id=1, source_target_pairs={{1,2},{2,1},{5,6},{6,5},{9,10},{10,9},{13,14},{14,13},{17,18},{18,... | collective-permute-start | bytes 589832 | tf_op jit(solution)/shard_map/ppermute | solution.py:481
  6.0 15.3 %collective-permute-start.1 = (f32[6,16,4,128]{3,2,1,0:T(4,128)}, f32[6,16,4,128]{3,2,1,0:T(4,128)S(1)}, u32[]{:S(2)}, u32[]{:S(2)}) collective-permute-start(f32[6,16,4,128]{3,2,1,0:T(4,128)} %pack.1.refs_0_), channel_id=1, source_target_pairs={{0,1},{2,3},{1,0},{3,2},{4,5},{6,7},{5,4},{7,6},{8,9},{10,11},{9,8... | collective-permute-start | bytes 589832 | tf_op jit(solution)/shard_map/ppermute | solution.py:480
  14.0 7.4 %copy-start = (f32[6,16,4,128]{3,2,1,0:T(4,128)S(1)}, f32[6,16,4,128]{3,2,1,0:T(4,128)}, u32[]{:S(2)}) copy-start(f32[6,16,4,128]{3,2,1,0:T(4,128)} %pack.1.refs_0_) | copy-start | bytes 589828
  14.0 7.3 %collective-permute-start.4 = (f32[6,16,4,128]{3,2,1,0:T(4,128)S(1)}, f32[6,16,4,128]{3,2,1,0:T(4,128)S(1)}, u32[]{:S(2)}, u32[]{:S(2)}) collective-permute-start(f32[6,16,4,128]{3,2,1,0:T(4,128)S(1)} %collective-permute-done.refs_1_), channel_id=1, source_target_pairs={{1,2},{2,1},{5,6},{6,5},{9,10},{10,9},{13,14},{14,13},{17,18},{18,... | collective-permute-start | bytes 589832 | tf_op jit(solution)/shard_map/ppermute | solution.py:485
  14.8 6.5 %collective-permute-start.2 = (f32[6,16,4,128]{3,2,1,0:T(4,128)S(1)}, f32[6,16,4,128]{3,2,1,0:T(4,128)S(1)}, u32[]{:S(2)}, u32[]{:S(2)}) collective-permute-start(f32[6,16,4,128]{3,2,1,0:T(4,128)S(1)} %collective-permute-done.refs_1_), channel_id=1, source_target_pairs={{0,1},{2,3},{1,0},{3,2},{4,5},{6,7},{5,4},{7,6},{8,9},{10,11},{9,8... | collective-permute-start | bytes 589832 | tf_op jit(solution)/shard_map/ppermute | solution.py:484
  23.6 4.3 %collective-permute-start.5 = (f32[6,6,8,128]{3,2,1,0:T(8,128)S(1)}, f32[6,6,8,128]{3,2,1,0:T(8,128)S(1)}, u32[]{:S(2)}, u32[]{:S(2)}) collective-permute-start(f32[6,6,8,128]{3,2,1,0:T(8,128)S(1)} %get-tuple-element.49), channel_id=1, source_target_pairs={{0,8},{16,24},{8,0},{24,16},{1,9},{17,25},{9,1},{25,17},{2,10},{18... | collective-permute-start | bytes 442376 | tf_op jit(solution)/shard_map/ppermute | solution.py:501
  23.7 4.3 %collective-permute-start.6 = (f32[6,6,8,128]{3,2,1,0:T(8,128)S(1)}, f32[6,6,8,128]{3,2,1,0:T(8,128)S(1)}, u32[]{:S(2)}, u32[]{:S(2)}) collective-permute-start(f32[6,6,8,128]{3,2,1,0:T(8,128)S(1)} %get-tuple-element.50), channel_id=1, source_target_pairs={{8,16},{16,8},{9,17},{17,9},{10,18},{18,10},{11,19},{19,11},{12,20... | collective-permute-start | bytes 442376 | tf_op jit(solution)/shard_map/ppermute | solution.py:502
  24.4 8.2 %copy-start.4 = (s32[8,4]{0,1:T(4,128)S(1)}, s32[8,4]{0,1:T(4,128)}, u32[]{:S(2)}) copy-start(s32[8,4]{0,1:T(4,128)} %param.13) | copy-start | bytes 388
  24.4 8.2 %copy-start.1 = (f32[8,8]{1,0:T(8,128)S(1)}, f32[8,8]{1,0:T(8,128)}, u32[]{:S(2)}) copy-start(f32[8,8]{1,0:T(8,128)} %rates.1) | copy-start | bytes 772
  24.4 8.2 %copy-start.2 = (s32[8]{0:T(128)S(1)}, s32[8]{0:T(128)}, u32[]{:S(2)}) copy-start(s32[8]{0:T(128)} %plan.1) | copy-start | bytes 100
  24.4 8.2 %copy-start.3 = (f32[4]{0:T(128)S(1)}, f32[4]{0:T(128)}, u32[]{:S(2)}) copy-start(f32[4]{0:T(128)} %diffusion.1) | copy-start | bytes 52
  28.0 23.3 %collective-permute-start.9 = (f32[256,256]{1,0:T(8,128)S(1)}, f32[256,256]{1,0:T(8,128)S(1)}, u32[]{:S(2)}, u32[]{:S(2)}) collective-permute-start(f32[256,256]{1,0:T(8,128)S(1)} %gram.5), channel_id=1, source_target_pairs={{0,24},{8,16},{16,8},{24,0},{1,25},{9,17},{17,9},{25,1},{2,26},{10... | collective-permute-start | bytes 786440 | tf_op jit(solution)/shard_map/ppermute | solution.py:27
  29.6 21.6 %collective-permute-start.8 = (f32[256,256]{1,0:T(8,128)S(1)}, f32[256,256]{1,0:T(8,128)S(1)}, u32[]{:S(2)}, u32[]{:S(2)}) collective-permute-start(f32[256,256]{1,0:T(8,128)S(1)} %gram.5), channel_id=1, source_target_pairs={{0,16},{8,24},{16,0},{24,8},{1,17},{9,25},{17,1},{25,9},{2,18},{10... | collective-permute-start | bytes 786440 | tf_op jit(solution)/shard_map/ppermute | solution.py:27
  32.5 18.7 %collective-permute-start.7 = (f32[256,256]{1,0:T(8,128)S(1)}, f32[256,256]{1,0:T(8,128)S(1)}, u32[]{:S(2)}, u32[]{:S(2)}) collective-permute-start(f32[256,256]{1,0:T(8,128)S(1)} %gram.5), channel_id=1, source_target_pairs={{0,8},{8,0},{16,24},{24,16},{1,9},{9,1},{17,25},{25,17},{2,10},{10... | collective-permute-start | bytes 786440 | tf_op jit(solution)/shard_map/ppermute | solution.py:27
  50.1 10.5 %collective-permute-start.11 = (f32[4,16,8,128]{3,2,1,0:T(8,128)S(1)}, f32[4,16,8,128]{3,2,1,0:T(8,128)S(1)}, u32[]{:S(2)}, u32[]{:S(2)}) collective-permute-start(f32[4,16,8,128]{3,2,1,0:T(8,128)S(1)} %get-tuple-element.67), channel_id=1, source_target_pairs={{0,16},{8,24},{16,0},{24,8},{1,17},{9,25},{17,1},{25,9},{2,18},{10... | collective-permute-start | bytes 786440 | tf_op jit(solution)/shard_map/ppermute | solution.py:27
  51.2 6.7 %collective-permute-start.12 = (f32[4,16,8,128]{3,2,1,0:T(8,128)S(1)}, f32[4,16,8,128]{3,2,1,0:T(8,128)S(1)}, u32[]{:S(2)}, u32[]{:S(2)}) collective-permute-start(f32[4,16,8,128]{3,2,1,0:T(8,128)S(1)} %get-tuple-element.69), channel_id=1, source_target_pairs={{0,8},{8,0},{16,24},{24,16},{1,9},{9,1},{17,25},{25,17},{2,10},{10... | collective-permute-start | bytes 786440 | tf_op jit(solution)/shard_map/ppermute | solution.py:27
  51.3 12.8 %collective-permute-start.10 = (f32[4,16,8,128]{3,2,1,0:T(8,128)S(1)}, f32[4,16,8,128]{3,2,1,0:T(8,128)S(1)}, u32[]{:S(2)}, u32[]{:S(2)}) collective-permute-start(f32[4,16,8,128]{3,2,1,0:T(8,128)S(1)} %get-tuple-element.64), channel_id=1, source_target_pairs={{0,24},{8,16},{16,8},{24,0},{1,25},{9,17},{17,9},{25,1},{2,26},{10... | collective-permute-start | bytes 786440 | tf_op jit(solution)/shard_map/ppermute | solution.py:27
  52.5 16.5 %collective-permute-start.16 = (f32[256,256]{1,0:T(8,128)S(1)}, f32[256,256]{1,0:T(8,128)S(1)}, u32[]{:S(2)}, u32[]{:S(2)}) collective-permute-start(f32[256,256]{1,0:T(8,128)S(1)} %add_add_fusion), channel_id=1, source_target_pairs={{0,4},{4,0},{1,5},{5,1},{2,6},{6,2},{3,7},{7,3},{8,12},{12,8},{9,1... | collective-permute-start | bytes 786440 | tf_op jit(solution)/shard_map/ppermute | solution.py:27
  64.9 3.2 %collective-permute-start.15 = (f32[16,256]{1,0:T(8,128)S(1)}, f32[16,256]{1,0:T(8,128)S(1)}, u32[]{:S(2)}, u32[]{:S(2)}) collective-permute-start(f32[16,256]{1,0:T(8,128)S(1)} %product.7), channel_id=1, source_target_pairs={{0,24},{8,16},{16,8},{24,0},{1,25},{9,17},{17,9},{25,1},{2,26},{10... | collective-permute-start | bytes 49160 | tf_op jit(solution)/shard_map/ppermute | solution.py:27
  65.3 3.7 %collective-permute-start.14 = (f32[16,256]{1,0:T(8,128)S(1)}, f32[16,256]{1,0:T(8,128)S(1)}, u32[]{:S(2)}, u32[]{:S(2)}) collective-permute-start(f32[16,256]{1,0:T(8,128)S(1)} %product.7), channel_id=1, source_target_pairs={{0,16},{8,24},{16,0},{24,8},{1,17},{9,25},{17,1},{25,9},{2,18},{10... | collective-permute-start | bytes 49160 | tf_op jit(solution)/shard_map/ppermute | solution.py:27
  66.8 2.2 %collective-permute-start.13 = (f32[16,256]{1,0:T(8,128)S(1)}, f32[16,256]{1,0:T(8,128)S(1)}, u32[]{:S(2)}, u32[]{:S(2)}) collective-permute-start(f32[16,256]{1,0:T(8,128)S(1)} %product.7), channel_id=1, source_target_pairs={{0,8},{8,0},{16,24},{24,16},{1,9},{9,1},{17,25},{25,17},{2,10},{10... | collective-permute-start | bytes 49160 | tf_op jit(solution)/shard_map/ppermute | solution.py:27
  69.0 3.8 %collective-permute-start.17 = (f32[16,256]{1,0:T(8,128)S(1)}, f32[16,256]{1,0:T(8,128)S(1)}, u32[]{:S(2)}, u32[]{:S(2)}) collective-permute-start(f32[16,256]{1,0:T(8,128)S(1)} %add_add_fusion.1), channel_id=1, source_target_pairs={{0,4},{4,0},{1,5},{5,1},{2,6},{6,2},{3,7},{7,3},{8,12},{12,8},{9,1... | collective-permute-start | bytes 49160 | tf_op jit(solution)/shard_map/ppermute | solution.py:27
  72.8 6.1 %collective-permute-start.20 = (f32[8,256]{1,0:T(8,128)S(1)}, f32[8,256]{1,0:T(8,128)S(1)}, u32[]{:S(2)}, u32[]{:S(2)}) collective-permute-start(f32[8,256]{1,0:T(8,128)S(1)} %slice_add_fusion.1), channel_id=1, source_target_pairs={{0,3},{1,2},{2,1},{3,0},{4,7},{5,6},{6,5},{7,4},{8,11},{9,10},{10,... | collective-permute-start | bytes 24584 | tf_op jit(solution)/shard_map/ppermute | solution.py:27
  75.3 5.2 %collective-permute-start.19 = (f32[8,256]{1,0:T(8,128)S(1)}, f32[8,256]{1,0:T(8,128)S(1)}, u32[]{:S(2)}, u32[]{:S(2)}) collective-permute-start(f32[8,256]{1,0:T(8,128)S(1)} %slice_add_fusion.1), channel_id=1, source_target_pairs={{0,2},{1,3},{2,0},{3,1},{4,6},{5,7},{6,4},{7,5},{8,10},{9,11},{10,... | collective-permute-start | bytes 24584 | tf_op jit(solution)/shard_map/ppermute | solution.py:27
  78.8 3.7 %collective-permute-start.18 = (f32[8,256]{1,0:T(8,128)S(1)}, f32[8,256]{1,0:T(8,128)S(1)}, u32[]{:S(2)}, u32[]{:S(2)}) collective-permute-start(f32[8,256]{1,0:T(8,128)S(1)} %slice_add_fusion.1), channel_id=1, source_target_pairs={{0,1},{1,0},{2,3},{3,2},{4,5},{5,4},{6,7},{7,6},{8,9},{9,8},{10,11... | collective-permute-start | bytes 24584 | tf_op jit(solution)/shard_map/ppermute | solution.py:27
  82.7 5.5 %collective-permute-start.23 = (f32[8,256]{1,0:T(8,128)S(1)}, f32[8,256]{1,0:T(8,128)S(1)}, u32[]{:S(2)}, u32[]{:S(2)}) collective-permute-start(f32[8,256]{1,0:T(8,128)S(1)} %fusion.3), channel_id=1, source_target_pairs={{0,3},{1,2},{2,1},{3,0},{4,7},{5,6},{6,5},{7,4},{8,11},{9,10},{10,... | collective-permute-start | bytes 24584 | tf_op jit(solution)/shard_map/ppermute | solution.py:27
  85.2 4.5 %collective-permute-start.22 = (f32[8,256]{1,0:T(8,128)S(1)}, f32[8,256]{1,0:T(8,128)S(1)}, u32[]{:S(2)}, u32[]{:S(2)}) collective-permute-start(f32[8,256]{1,0:T(8,128)S(1)} %fusion.3), channel_id=1, source_target_pairs={{0,2},{1,3},{2,0},{3,1},{4,6},{5,7},{6,4},{7,5},{8,10},{9,11},{10,... | collective-permute-start | bytes 24584 | tf_op jit(solution)/shard_map/ppermute | solution.py:27
  85.2 4.5 %collective-permute-start.21 = (f32[8,256]{1,0:T(8,128)S(1)}, f32[8,256]{1,0:T(8,128)S(1)}, u32[]{:S(2)}, u32[]{:S(2)}) collective-permute-start(f32[8,256]{1,0:T(8,128)S(1)} %fusion.3), channel_id=1, source_target_pairs={{0,1},{1,0},{2,3},{3,2},{4,5},{5,4},{6,7},{7,6},{8,9},{9,8},{10,11... | collective-permute-start | bytes 24584 | tf_op jit(solution)/shard_map/ppermute | solution.py:27

commit v12 on v11

--- a/solution.py
+++ b/solution.py
@@ -55,6 +55,10 @@
 
 def anywhere(count):
     return [pl.BlockSpec(memory_space=pl.ANY)] * count
+
+
+def in_vmem(arrays):
+    return [pltpu.with_memory_space_constraint(a, pltpu.VMEM) for a in arrays]
 
 
 def vmem(*shapes):
@@ -81,14 +85,10 @@
 
 
 def edges_kernel(blocks_x, *refs):
-    given, (out_a, out_b, blocks, sems) = refs[:-4], refs[-4:]
-    blocks = [blocks.at[i] for i in range(len(given))]
-    copies = fetch(given, blocks, sems)
+    blocks, (out_a, out_b) = refs[:-2], refs[-2:]
     fields, cells_y, cells_x, cells_z = blocks[0].shape
     per_block = cells_y // GROUPS
     even = lax.axis_index("grp") % 2 == 0
-    for copy in copies:
-        copy.wait()
     place = lax.broadcasted_iota(jnp.int32, (blocks_x * cells_x, LANES), 1) // STEPS
 
     def field_body(field, _):
@@ -118,13 +118,11 @@
 
 def steps_kernel(blocks_x, plan, diffusion, stoich, rates, *refs):
     count_blocks = 3 * blocks_x
-    given = refs[: count_blocks + 2]
+    blocks = refs[:count_blocks]
+    side_a, side_b = refs[count_blocks : count_blocks + 2]
     adjoint = refs[count_blocks + 2]
-    kept = refs[count_blocks + 3 : -7]
-    state, other, matrix, speed, blocks, sides, sems = refs[-7:]
-    blocks = [blocks.at[i] for i in range(count_blocks)]
-    side_a, side_b = sides.at[0], sides.at[1]
-    copies = fetch(given, blocks + [side_a, side_b], sems)
+    kept = refs[count_blocks + 3 : -4]
+    state, other, matrix, speed = refs[-4:]
     spec, rows, all_x, wide = state.shape
     _, cells_y, cells_x, cells_z = blocks[0].shape
     grp, at_x, at_y = (lax.axis_index(axis) for axis in ("grp", "gx", "gy"))
@@ -164,8 +162,6 @@
         for a in range(spec)
         for s in range(spec)
     ]
-    for copy in copies:
-        copy.wait()
     for slot in range(3):
         mine = blocks[slot * blocks_x : (slot + 1) * blocks_x]
         for part in range(per_block):
@@ -488,16 +484,14 @@
     blocks = blocks + from_a + from_b
     *blocks, gram = lax.optimization_barrier((*blocks, gram))
     packed = jax.ShapeDtypeStruct((fields, 3 * cells_y // GROUPS, all_x, LANES), jnp.float32)
-    held = (len(blocks), fields, cells_y, cells_x, cells_z)
     edge_a, edge_b = pl.pallas_call(
         functools.partial(edges_kernel, count_x),
         out_shape=(packed, packed),
-        in_specs=anywhere(len(blocks)),
+        in_specs=whole(len(blocks)),
         out_specs=tuple(whole(2)),
-        scratch_shapes=[pltpu.VMEM(held, jnp.float32), pltpu.SemaphoreType.DMA((len(blocks),))],
-        compiler_params=vmem(held, packed.shape, packed.shape),
+        compiler_params=vmem(packed.shape, packed.shape),
         name="edges",
-    )(*blocks)
+    )(*in_vmem(blocks))
     side_a = lax.ppermute(edge_a, "grp", pairs("grp", 0))
     side_b = lax.ppermute(edge_b, "grp", pairs("grp", 1))
     (gram,) = gram_part(later, basis, gram, parts=tuple(parts))
@@ -506,14 +500,13 @@
 
     part = jax.ShapeDtypeStruct((cells_x, cells_y, snaps, cells_z), jnp.float32)
     room = (depth, all_x, wide)
-    shapes = [(spec, *room), (spec, *room), (spec * spec, *room), room, held, (2, *packed.shape)]
+    shapes = [(spec, *room), (spec, *room), (spec * spec, *room), room]
     final, *kept = pl.pallas_call(
         functools.partial(steps_kernel, count_x),
         out_shape=[jax.ShapeDtypeStruct(terminal.shape, jnp.float32)] + [part] * count_grp,
-        in_specs=scalars(3) + whole(1) + anywhere(len(blocks) + 2),
+        in_specs=scalars(3) + whole(3 + len(blocks)),
         out_specs=whole(1 + count_grp),
-        scratch_shapes=[pltpu.VMEM(shape, jnp.float32) for shape in shapes]
-        + [pltpu.SemaphoreType.DMA((len(blocks) + 2,))],
+        scratch_shapes=[pltpu.VMEM(shape, jnp.float32) for shape in shapes],
         compiler_params=vmem(*shapes, terminal.shape, (count_grp, *part.shape)),
         cost_estimate=pl.CostEstimate(
             flops=0,
@@ -521,7 +514,7 @@
             transcendentals=0,
         ),
         name="steps",
-    )(plan, diffusion, stoich, rates, *blocks, side_a, side_b)
+    )(plan, diffusion, stoich, rates, *in_vmem((*blocks, side_a, side_b)))
 
     last = count_grp - 1
     moved = {flips: exchange(kept[flips], "grp", flips) for flips in range(1, last)}

time: 90.5 us -> 86.7 us (0.958)
  Pallas kernels: 42.1 us -> 38.3 us
    pallas_call x1, Pallas kernels: 17.5 us -> 15.3 us  [body(): pl.pallas_call(functools.partial(steps_kernel, count_x), out_shape=[jax.S...]
    pallas_call x1, Pallas kernels: 2.29 us -> 0.7 us  [body(): pl.pallas_call(functools.partial(edges_kernel, count_x), out_shape=(packe...]
where the time goes in v12:
time: 86.7 us; the launch traced here: 86.5 us
  Pallas kernels  38.3 us (44%)
  starting transfers between devices  32.1 us (37%)
  waiting for transfers between devices  14.2 us (16%)
  between operations  0.89 us (1%)
    ppermute x17, starting transfers between devices, exchange(): return lax.ppermute(value, axis, [(i, i ^ flips) for i in range(count)])  20.7 us
    pallas_call x1, Pallas kernels, body(): pl.pallas_call(functools.partial(steps_kernel, count_x), out_shape=[jax.S...  15.3 us
    ppermute x17, waiting for transfers between devices, exchange(): return lax.ppermute(value, axis, [(i, i ^ flips) for i in range(count)])  14.2 us
    pallas_call x3, Pallas kernels, gram_part(): pl.pallas_call(functools.partial(gram_kernel, places, later, bool(parts),...  11.8 us
    pallas_call x4, Pallas kernels, product(): pl.pallas_call(functools.partial(product_kernel, flips, later, bool(rows)...  8.83 us
    ppermute x1, starting transfers between devices, body(): from_a = [lax.ppermute(own, 'gy', pairs('gy', 0))]  4.45 us
    ppermute x1, starting transfers between devices, body(): lax.ppermute(own, 'gx', [(i, (i - shift) % count_x) for i in range(count_...  2.94 us
    ppermute x1, starting transfers between devices, body(): from_a += [lax.ppermute(b, 'gy', pairs('gy', 0)) for b in blocks[1:]]  1.77 us
  transfers between devices with their start and end apart: 24, of which 8 were waited for; matrix products, arithmetic and copies ran while one was open for 0% of the time, Pallas kernels for 42%

profile of v12, /device:TPU:0, one launch (start us, length us, event | category | flops | bytes accessed | tf_op | source)
XLA Modules:
  0.0 86.5 jit_solution(16262376891741729481)
XLA Ops:
  0.6 1.7 %pack.1.refs_0_ = f32[6,16,4,128]{3,2,1,0:T(4,128)} custom-call(f32[4,4,16,128]{3,2,1,0:T(8,128)} %terminal.1, f32[4,16,128]{2,1,0:T(8,128)} %velocity.1, s32[4,16,128]{2,1,0:T(8,128)} %material.1), custom_call_target="tpu_custom_call" | custom-call | tf_op jit(solution)/shard_map/pack/pallas_call | solution.py:464
  2.3 2.9 %collective-permute-start = (f32[6,16,4,128]{3,2,1,0:T(4,128)}, f32[6,16,4,128]{3,2,1,0:T(4,128)S(1)}, u32[]{:S(2)}, u32[]{:S(2)}) collective-permute-start(f32[6,16,4,128]{3,2,1,0:T(4,128)} %pack.1.refs_0_), channel_id=1, source_target_pairs={{0,4},{4,0},{1,5},{5,1},{2,6},{6,2},{3,7},{7,3},{8,12},{12,8},{9,1... | collective-permute-start | bytes 589832 | tf_op jit(solution)/shard_map/ppermute | solution.py:474
  5.3 0.7 collective-permute-start.3
  6.0 4.5 %collective-permute-start.1 = (f32[6,16,4,128]{3,2,1,0:T(4,128)}, f32[6,16,4,128]{3,2,1,0:T(4,128)S(1)}, u32[]{:S(2)}, u32[]{:S(2)}) collective-permute-start(f32[6,16,4,128]{3,2,1,0:T(4,128)} %pack.1.refs_0_), channel_id=1, source_target_pairs={{0,1},{2,3},{1,0},{3,2},{4,5},{6,7},{5,4},{7,6},{8,9},{10,11},{9,8... | collective-permute-start | bytes 589832 | tf_op jit(solution)/shard_map/ppermute | solution.py:476
  10.4 3.5 %gram.3.refs_1_ = f32[256,256]{1,0:T(8,128)S(1)} custom-call(bf16[1,4,16,512,256]{4,3,2,1,0:T(8,128)(2,1)} %refs_1_.3), custom_call_target="tpu_custom_call" | custom-call | flops 1073741824 | bytes 12582912 | tf_op jit(solution)/shard_map/gram/pallas_call | solution.py:337
  14.0 0.8 collective-permute-start.4
  14.8 1.8 %collective-permute-start.2 = (f32[6,16,4,128]{3,2,1,0:T(4,128)S(1)}, f32[6,16,4,128]{3,2,1,0:T(4,128)S(1)}, u32[]{:S(2)}, u32[]{:S(2)}) collective-permute-start(f32[6,16,4,128]{3,2,1,0:T(4,128)S(1)} %collective-permute-done.refs_1_), channel_id=1, source_target_pairs={{0,1},{2,3},{1,0},{3,2},{4,5},{6,7},{5,4},{7,6},{8,9},{10,11},{9,8... | collective-permute-start | bytes 589832 | tf_op jit(solution)/shard_map/ppermute | solution.py:480
  16.6 4.7 %gram.4 = (f32[256,256]{1,0:T(8,128)S(1)}, bf16[16,512,256]{2,1,0:T(8,128)(2,1)S(1)}, bf16[16,512,256]{2,1,0:T(8,128)(2,1)S(1)}) custom-call(bf16[1,4,16,512,256]{4,3,2,1,0:T(8,128)(2,1)} %refs_1_.3, f32[256,256]{1,0:T(8,128)S(1)} %gram.3.refs_1_), custom_call_target="tpu_custom_call" | custom-call | flops 1073741824 | bytes 12582912 | tf_op jit(solution)/shard_map/gram/pallas_call | solution.py:337
  21.3 0.7 edges.1
  22.0 0.1 collective-permute-start.5
  22.1 0.7 collective-permute-start.6
  22.8 0.0 copy-start.4
  22.8 0.0 copy-start.1
  22.8 0.0 copy-start.2
  22.8 0.0 copy-start.3
  22.8 3.5 %gram.5 = f32[256,256]{1,0:T(8,128)S(1)} custom-call(bf16[16,512,256]{2,1,0:T(8,128)(2,1)S(1)} %get-tuple-element.51.refs_0_, bf16[16,512,256]{2,1,0:T(8,128)(2,1)S(1)} %get-tuple-element.52.refs_1_, f32[256,256]{1,0:T(8,128)S(1)} %get-tuple-element.53.refs_2_), custom_call_target="tpu_custom_call" | custom-call | flops 2147483648 | bytes 25165824 | tf_op jit(solution)/shard_map/gram/pallas_call | solution.py:337
  26.4 1.7 %collective-permute-start.9 = (f32[256,256]{1,0:T(8,128)S(1)}, f32[256,256]{1,0:T(8,128)S(1)}, u32[]{:S(2)}, u32[]{:S(2)}) collective-permute-start(f32[256,256]{1,0:T(8,128)S(1)} %gram.5), channel_id=1, source_target_pairs={{0,24},{8,16},{16,8},{24,0},{1,25},{9,17},{17,9},{25,1},{2,26},{10... | collective-permute-start | bytes 786440 | tf_op jit(solution)/shard_map/ppermute | solution.py:27
  28.1 2.9 %collective-permute-start.8 = (f32[256,256]{1,0:T(8,128)S(1)}, f32[256,256]{1,0:T(8,128)S(1)}, u32[]{:S(2)}, u32[]{:S(2)}) collective-permute-start(f32[256,256]{1,0:T(8,128)S(1)} %gram.5), channel_id=1, source_target_pairs={{0,16},{8,24},{16,0},{24,8},{1,17},{9,25},{17,1},{25,9},{2,18},{10... | collective-permute-start | bytes 786440 | tf_op jit(solution)/shard_map/ppermute | solution.py:27
  31.0 0.1 copy.10.stoich
  31.0 15.3 %steps.1 = (f32[4,4,16,128]{3,2,1,0:T(8,128)}, f32[4,16,8,128]{3,2,1,0:T(8,128)S(1)}, f32[4,16,8,128]{3,2,1,0:T(8,128)S(1)}, f32[4,16,8,128]{3,2,1,0:T(8,128)S(1)}, f32[4,16,8,128]{3,2,1,0:T(8,128)S(1)}) custom-call(s32[8]{0:T(128)S(1)} %copy-done.2, f32[4]{0:T(128)S(1)} %copy-done.3, s32[8,4]{1,0:T(8,128)S(1)} %copy.10.stoich, f32[8,8]{1,0:T(8,128)S(1)} %copy-done.1, ...), custom_call_target="tpu_custom_call" | custom-call | bytes 100663296 | tf_op jit(solution)/shard_map/steps/pallas_call | solution.py:504
  46.4 1.0 %collective-permute-start.11 = (f32[4,16,8,128]{3,2,1,0:T(8,128)S(1)}, f32[4,16,8,128]{3,2,1,0:T(8,128)S(1)}, u32[]{:S(2)}, u32[]{:S(2)}) collective-permute-start(f32[4,16,8,128]{3,2,1,0:T(8,128)S(1)} %get-tuple-element.67), channel_id=1, source_target_pairs={{0,16},{8,24},{16,0},{24,8},{1,17},{9,25},{17,1},{25,9},{2,18},{10... | collective-permute-start | bytes 786440 | tf_op jit(solution)/shard_map/ppermute | solution.py:27
  47.4 0.1 add_add_fusion
  47.5 1.2 %collective-permute-start.10 = (f32[4,16,8,128]{3,2,1,0:T(8,128)S(1)}, f32[4,16,8,128]{3,2,1,0:T(8,128)S(1)}, u32[]{:S(2)}, u32[]{:S(2)}) collective-permute-start(f32[4,16,8,128]{3,2,1,0:T(8,128)S(1)} %get-tuple-element.64), channel_id=1, source_target_pairs={{0,24},{8,16},{16,8},{24,0},{1,25},{9,17},{17,9},{25,1},{2,26},{10... | collective-permute-start | bytes 786440 | tf_op jit(solution)/shard_map/ppermute | solution.py:27
  48.7 0.7 collective-permute-start.16
  49.4 4.7 %product.4 = (f32[16,256]{1,0:T(8,128)S(1)}, bf16[4,16,128,256]{3,2,1,0:T(8,128)(2,1)S(1)}, bf16[4,16,128,256]{3,2,1,0:T(8,128)(2,1)S(1)}) custom-call(f32[4,16,8,128]{3,2,1,0:T(8,128)S(1)} %get-tuple-element.65.refs_0_, bf16[1,4,16,512,256]{4,3,2,1,0:T(8,128)(2,1)} %refs_1_.3), custom_call_target="tpu_custom_call" | custom-call | flops 67108864 | bytes 8388608 | tf_op jit(solution)/shard_map/product/pallas_call | solution.py:436
  54.1 2.7 %product.5.refs_2_ = f32[16,256]{1,0:T(8,128)S(1)} custom-call(f32[4,16,8,128]{3,2,1,0:T(8,128)S(1)} %collective-permute-done.12.refs_0_, bf16[1,4,16,512,256]{4,3,2,1,0:T(8,128)(2,1)} %refs_1_.3, f32[16,256]{1,0:T(8,128)S(1)} %get-tuple-element.70.refs_2_), custom_call_target="tpu_custom_call" | custom-call | flops 67108864 | bytes 8388608 | tf_op jit(solution)/shard_map/product/pallas_call | solution.py:436
  56.8 0.7 product.6.refs_2_
  57.5 2.8 %collective-permute-done.10.refs_0_ = f32[4,16,8,128]{3,2,1,0:T(8,128)S(1)} collective-permute-done((f32[4,16,8,128]{3,2,1,0:T(8,128)S(1)}, f32[4,16,8,128]{3,2,1,0:T(8,128)S(1)}, u32[]{:S(2)}, u32[]{:S(2)}) %collective-permute-start.10) | collective-permute-done | bytes 262176 | tf_op jit(solution)/shard_map/ppermute | solution.py:27
  60.3 0.7 product.7
  61.0 0.4 collective-permute-start.15
  61.4 1.5 %collective-permute-start.14 = (f32[16,256]{1,0:T(8,128)S(1)}, f32[16,256]{1,0:T(8,128)S(1)}, u32[]{:S(2)}, u32[]{:S(2)}) collective-permute-start(f32[16,256]{1,0:T(8,128)S(1)} %product.7), channel_id=1, source_target_pairs={{0,16},{8,24},{16,0},{24,8},{1,17},{9,25},{17,1},{25,9},{2,18},{10... | collective-permute-start | bytes 49160 | tf_op jit(solution)/shard_map/ppermute | solution.py:27
  62.9 0.0 collective-permute-start.13
  63.0 1.3 %collective-permute-done.15 = f32[16,256]{1,0:T(8,128)S(1)} collective-permute-done((f32[16,256]{1,0:T(8,128)S(1)}, f32[16,256]{1,0:T(8,128)S(1)}, u32[]{:S(2)}, u32[]{:S(2)}) %collective-permute-start.15) | collective-permute-done | bytes 16416 | tf_op jit(solution)/shard_map/ppermute | solution.py:27
  64.3 0.9 %collective-permute-done.14 = f32[16,256]{1,0:T(8,128)S(1)} collective-permute-done((f32[16,256]{1,0:T(8,128)S(1)}, f32[16,256]{1,0:T(8,128)S(1)}, u32[]{:S(2)}, u32[]{:S(2)}) %collective-permute-start.14) | collective-permute-done | bytes 16416 | tf_op jit(solution)/shard_map/ppermute | solution.py:27
  65.2 0.8 collective-permute-start.17
  66.0 3.0 %collective-permute-done.17 = f32[16,256]{1,0:T(8,128)S(1)} collective-permute-done((f32[16,256]{1,0:T(8,128)S(1)}, f32[16,256]{1,0:T(8,128)S(1)}, u32[]{:S(2)}, u32[]{:S(2)}) %collective-permute-start.17) | collective-permute-done | bytes 16416 | tf_op jit(solution)/shard_map/ppermute | solution.py:27
  69.0 2.5 %collective-permute-start.20 = (f32[8,256]{1,0:T(8,128)S(1)}, f32[8,256]{1,0:T(8,128)S(1)}, u32[]{:S(2)}, u32[]{:S(2)}) collective-permute-start(f32[8,256]{1,0:T(8,128)S(1)} %slice_add_fusion.1), channel_id=1, source_target_pairs={{0,3},{1,2},{2,1},{3,0},{4,7},{5,6},{6,5},{7,4},{8,11},{9,10},{10,... | collective-permute-start | bytes 24584 | tf_op jit(solution)/shard_map/ppermute | solution.py:27
  71.5 3.5 %collective-permute-start.19 = (f32[8,256]{1,0:T(8,128)S(1)}, f32[8,256]{1,0:T(8,128)S(1)}, u32[]{:S(2)}, u32[]{:S(2)}) collective-permute-start(f32[8,256]{1,0:T(8,128)S(1)} %slice_add_fusion.1), channel_id=1, source_target_pairs={{0,2},{1,3},{2,0},{3,1},{4,6},{5,7},{6,4},{7,5},{8,10},{9,11},{10,... | collective-permute-start | bytes 24584 | tf_op jit(solution)/shard_map/ppermute | solution.py:27
  75.0 0.1 collective-permute-start.18
  75.1 1.6 %collective-permute-done.19 = f32[8,256]{1,0:T(8,128)S(1)} collective-permute-done((f32[8,256]{1,0:T(8,128)S(1)}, f32[8,256]{1,0:T(8,128)S(1)}, u32[]{:S(2)}, u32[]{:S(2)}) %collective-permute-start.19) | collective-permute-done | bytes 8224 | tf_op jit(solution)/shard_map/ppermute | solution.py:27
  76.7 1.9 %collective-permute-done.18 = f32[8,256]{1,0:T(8,128)S(1)} collective-permute-done((f32[8,256]{1,0:T(8,128)S(1)}, f32[8,256]{1,0:T(8,128)S(1)}, u32[]{:S(2)}, u32[]{:S(2)}) %collective-permute-start.18) | collective-permute-done | bytes 8224 | tf_op jit(solution)/shard_map/ppermute | solution.py:27
  78.6 0.2 fusion.3
  78.9 2.5 %collective-permute-start.23 = (f32[8,256]{1,0:T(8,128)S(1)}, f32[8,256]{1,0:T(8,128)S(1)}, u32[]{:S(2)}, u32[]{:S(2)}) collective-permute-start(f32[8,256]{1,0:T(8,128)S(1)} %fusion.3), channel_id=1, source_target_pairs={{0,3},{1,2},{2,1},{3,0},{4,7},{5,6},{6,5},{7,4},{8,11},{9,10},{10,... | collective-permute-start | bytes 24584 | tf_op jit(solution)/shard_map/ppermute | solution.py:27
  81.3 0.0 collective-permute-start.22
  81.4 1.9 %collective-permute-start.21 = (f32[8,256]{1,0:T(8,128)S(1)}, f32[8,256]{1,0:T(8,128)S(1)}, u32[]{:S(2)}, u32[]{:S(2)}) collective-permute-start(f32[8,256]{1,0:T(8,128)S(1)} %fusion.3), channel_id=1, source_target_pairs={{0,1},{1,0},{2,3},{3,2},{4,5},{5,4},{6,7},{7,6},{8,9},{9,8},{10,11... | collective-permute-start | bytes 24584 | tf_op jit(solution)/shard_map/ppermute | solution.py:27
  83.3 1.1 %collective-permute-done.23 = f32[8,256]{1,0:T(8,128)S(1)} collective-permute-done((f32[8,256]{1,0:T(8,128)S(1)}, f32[8,256]{1,0:T(8,128)S(1)}, u32[]{:S(2)}, u32[]{:S(2)}) %collective-permute-start.23) | collective-permute-done | bytes 8224 | tf_op jit(solution)/shard_map/ppermute | solution.py:27
  84.3 1.6 %collective-permute-done.22 = f32[8,256]{1,0:T(8,128)S(1)} collective-permute-done((f32[8,256]{1,0:T(8,128)S(1)}, f32[8,256]{1,0:T(8,128)S(1)}, u32[]{:S(2)}, u32[]{:S(2)}) %collective-permute-start.22) | collective-permute-done | bytes 8224 | tf_op jit(solution)/shard_map/ppermute | solution.py:27
  85.9 0.6 add_add_fusion.2
  (27 shorter events, 0.1 us)
Async XLA Ops:
  2.3 11.6 %collective-permute-start = (f32[6,16,4,128]{3,2,1,0:T(4,128)}, f32[6,16,4,128]{3,2,1,0:T(4,128)S(1)}, u32[]{:S(2)}, u32[]{:S(2)}) collective-permute-start(f32[6,16,4,128]{3,2,1,0:T(4,128)} %pack.1.refs_0_), channel_id=1, source_target_pairs={{0,4},{4,0},{1,5},{5,1},{2,6},{6,2},{3,7},{7,3},{8,12},{12,8},{9,1... | collective-permute-start | bytes 589832 | tf_op jit(solution)/shard_map/ppermute | solution.py:474
  5.3 16.0 %collective-permute-start.3 = (f32[6,16,4,128]{3,2,1,0:T(4,128)}, f32[6,16,4,128]{3,2,1,0:T(4,128)S(1)}, u32[]{:S(2)}, u32[]{:S(2)}) collective-permute-start(f32[6,16,4,128]{3,2,1,0:T(4,128)} %pack.1.refs_0_), channel_id=1, source_target_pairs={{1,2},{2,1},{5,6},{6,5},{9,10},{10,9},{13,14},{14,13},{17,18},{18,... | collective-permute-start | bytes 589832 | tf_op jit(solution)/shard_map/ppermute | solution.py:477
  6.0 15.3 %collective-permute-start.1 = (f32[6,16,4,128]{3,2,1,0:T(4,128)}, f32[6,16,4,128]{3,2,1,0:T(4,128)S(1)}, u32[]{:S(2)}, u32[]{:S(2)}) collective-permute-start(f32[6,16,4,128]{3,2,1,0:T(4,128)} %pack.1.refs_0_), channel_id=1, source_target_pairs={{0,1},{2,3},{1,0},{3,2},{4,5},{6,7},{5,4},{7,6},{8,9},{10,11},{9,8... | collective-permute-start | bytes 589832 | tf_op jit(solution)/shard_map/ppermute | solution.py:476
  13.9 7.4 %copy-start = (f32[6,16,4,128]{3,2,1,0:T(4,128)S(1)}, f32[6,16,4,128]{3,2,1,0:T(4,128)}, u32[]{:S(2)}) copy-start(f32[6,16,4,128]{3,2,1,0:T(4,128)} %pack.1.refs_0_) | copy-start | bytes 589828
  14.0 7.3 %collective-permute-start.4 = (f32[6,16,4,128]{3,2,1,0:T(4,128)S(1)}, f32[6,16,4,128]{3,2,1,0:T(4,128)S(1)}, u32[]{:S(2)}, u32[]{:S(2)}) collective-permute-start(f32[6,16,4,128]{3,2,1,0:T(4,128)S(1)} %collective-permute-done.refs_1_), channel_id=1, source_target_pairs={{1,2},{2,1},{5,6},{6,5},{9,10},{10,9},{13,14},{14,13},{17,18},{18,... | collective-permute-start | bytes 589832 | tf_op jit(solution)/shard_map/ppermute | solution.py:481
  14.8 6.5 %collective-permute-start.2 = (f32[6,16,4,128]{3,2,1,0:T(4,128)S(1)}, f32[6,16,4,128]{3,2,1,0:T(4,128)S(1)}, u32[]{:S(2)}, u32[]{:S(2)}) collective-permute-start(f32[6,16,4,128]{3,2,1,0:T(4,128)S(1)} %collective-permute-done.refs_1_), channel_id=1, source_target_pairs={{0,1},{2,3},{1,0},{3,2},{4,5},{6,7},{5,4},{7,6},{8,9},{10,11},{9,8... | collective-permute-start | bytes 589832 | tf_op jit(solution)/shard_map/ppermute | solution.py:480
  22.0 4.3 %collective-permute-start.5 = (f32[6,6,8,128]{3,2,1,0:T(8,128)S(1)}, f32[6,6,8,128]{3,2,1,0:T(8,128)S(1)}, u32[]{:S(2)}, u32[]{:S(2)}) collective-permute-start(f32[6,6,8,128]{3,2,1,0:T(8,128)S(1)} %get-tuple-element.49), channel_id=1, source_target_pairs={{0,8},{16,24},{8,0},{24,16},{1,9},{17,25},{9,1},{25,17},{2,10},{18... | collective-permute-start | bytes 442376 | tf_op jit(solution)/shard_map/ppermute | solution.py:495
  22.1 4.3 %collective-permute-start.6 = (f32[6,6,8,128]{3,2,1,0:T(8,128)S(1)}, f32[6,6,8,128]{3,2,1,0:T(8,128)S(1)}, u32[]{:S(2)}, u32[]{:S(2)}) collective-permute-start(f32[6,6,8,128]{3,2,1,0:T(8,128)S(1)} %get-tuple-element.50), channel_id=1, source_target_pairs={{8,16},{16,8},{9,17},{17,9},{10,18},{18,10},{11,19},{19,11},{12,20... | collective-permute-start | bytes 442376 | tf_op jit(solution)/shard_map/ppermute | solution.py:496
  22.8 8.2 %copy-start.4 = (s32[8,4]{0,1:T(4,128)S(1)}, s32[8,4]{0,1:T(4,128)}, u32[]{:S(2)}) copy-start(s32[8,4]{0,1:T(4,128)} %param.13) | copy-start | bytes 388
  22.8 8.2 %copy-start.1 = (f32[8,8]{1,0:T(8,128)S(1)}, f32[8,8]{1,0:T(8,128)}, u32[]{:S(2)}) copy-start(f32[8,8]{1,0:T(8,128)} %rates.1) | copy-start | bytes 772
  22.8 8.2 %copy-start.2 = (s32[8]{0:T(128)S(1)}, s32[8]{0:T(128)}, u32[]{:S(2)}) copy-start(s32[8]{0:T(128)} %plan.1) | copy-start | bytes 100
  22.8 8.2 %copy-start.3 = (f32[4]{0:T(128)S(1)}, f32[4]{0:T(128)}, u32[]{:S(2)}) copy-start(f32[4]{0:T(128)} %diffusion.1) | copy-start | bytes 52
  26.4 21.0 %collective-permute-start.9 = (f32[256,256]{1,0:T(8,128)S(1)}, f32[256,256]{1,0:T(8,128)S(1)}, u32[]{:S(2)}, u32[]{:S(2)}) collective-permute-start(f32[256,256]{1,0:T(8,128)S(1)} %gram.5), channel_id=1, source_target_pairs={{0,24},{8,16},{16,8},{24,0},{1,25},{9,17},{17,9},{25,1},{2,26},{10... | collective-permute-start | bytes 786440 | tf_op jit(solution)/shard_map/ppermute | solution.py:27
  28.1 19.3 %collective-permute-start.8 = (f32[256,256]{1,0:T(8,128)S(1)}, f32[256,256]{1,0:T(8,128)S(1)}, u32[]{:S(2)}, u32[]{:S(2)}) collective-permute-start(f32[256,256]{1,0:T(8,128)S(1)} %gram.5), channel_id=1, source_target_pairs={{0,16},{8,24},{16,0},{24,8},{1,17},{9,25},{17,1},{25,9},{2,18},{10... | collective-permute-start | bytes 786440 | tf_op jit(solution)/shard_map/ppermute | solution.py:27
  30.9 16.4 %collective-permute-start.7 = (f32[256,256]{1,0:T(8,128)S(1)}, f32[256,256]{1,0:T(8,128)S(1)}, u32[]{:S(2)}, u32[]{:S(2)}) collective-permute-start(f32[256,256]{1,0:T(8,128)S(1)} %gram.5), channel_id=1, source_target_pairs={{0,8},{8,0},{16,24},{24,16},{1,9},{9,1},{17,25},{25,17},{2,10},{10... | collective-permute-start | bytes 786440 | tf_op jit(solution)/shard_map/ppermute | solution.py:27
  46.4 10.4 %collective-permute-start.11 = (f32[4,16,8,128]{3,2,1,0:T(8,128)S(1)}, f32[4,16,8,128]{3,2,1,0:T(8,128)S(1)}, u32[]{:S(2)}, u32[]{:S(2)}) collective-permute-start(f32[4,16,8,128]{3,2,1,0:T(8,128)S(1)} %get-tuple-element.67), channel_id=1, source_target_pairs={{0,16},{8,24},{16,0},{24,8},{1,17},{9,25},{17,1},{25,9},{2,18},{10... | collective-permute-start | bytes 786440 | tf_op jit(solution)/shard_map/ppermute | solution.py:27
  47.4 6.7 %collective-permute-start.12 = (f32[4,16,8,128]{3,2,1,0:T(8,128)S(1)}, f32[4,16,8,128]{3,2,1,0:T(8,128)S(1)}, u32[]{:S(2)}, u32[]{:S(2)}) collective-permute-start(f32[4,16,8,128]{3,2,1,0:T(8,128)S(1)} %get-tuple-element.69), channel_id=1, source_target_pairs={{0,8},{8,0},{16,24},{24,16},{1,9},{9,1},{17,25},{25,17},{2,10},{10... | collective-permute-start | bytes 786440 | tf_op jit(solution)/shard_map/ppermute | solution.py:27
  47.5 12.8 %collective-permute-start.10 = (f32[4,16,8,128]{3,2,1,0:T(8,128)S(1)}, f32[4,16,8,128]{3,2,1,0:T(8,128)S(1)}, u32[]{:S(2)}, u32[]{:S(2)}) collective-permute-start(f32[4,16,8,128]{3,2,1,0:T(8,128)S(1)} %get-tuple-element.64), channel_id=1, source_target_pairs={{0,24},{8,16},{16,8},{24,0},{1,25},{9,17},{17,9},{25,1},{2,26},{10... | collective-permute-start | bytes 786440 | tf_op jit(solution)/shard_map/ppermute | solution.py:27
  48.7 16.5 %collective-permute-start.16 = (f32[256,256]{1,0:T(8,128)S(1)}, f32[256,256]{1,0:T(8,128)S(1)}, u32[]{:S(2)}, u32[]{:S(2)}) collective-permute-start(f32[256,256]{1,0:T(8,128)S(1)} %add_add_fusion), channel_id=1, source_target_pairs={{0,4},{4,0},{1,5},{5,1},{2,6},{6,2},{3,7},{7,3},{8,12},{12,8},{9,1... | collective-permute-start | bytes 786440 | tf_op jit(solution)/shard_map/ppermute | solution.py:27
  61.0 3.2 %collective-permute-start.15 = (f32[16,256]{1,0:T(8,128)S(1)}, f32[16,256]{1,0:T(8,128)S(1)}, u32[]{:S(2)}, u32[]{:S(2)}) collective-permute-start(f32[16,256]{1,0:T(8,128)S(1)} %product.7), channel_id=1, source_target_pairs={{0,24},{8,16},{16,8},{24,0},{1,25},{9,17},{17,9},{25,1},{2,26},{10... | collective-permute-start | bytes 49160 | tf_op jit(solution)/shard_map/ppermute | solution.py:27
  61.4 3.7 %collective-permute-start.14 = (f32[16,256]{1,0:T(8,128)S(1)}, f32[16,256]{1,0:T(8,128)S(1)}, u32[]{:S(2)}, u32[]{:S(2)}) collective-permute-start(f32[16,256]{1,0:T(8,128)S(1)} %product.7), channel_id=1, source_target_pairs={{0,16},{8,24},{16,0},{24,8},{1,17},{9,25},{17,1},{25,9},{2,18},{10... | collective-permute-start | bytes 49160 | tf_op jit(solution)/shard_map/ppermute | solution.py:27
  62.9 2.2 %collective-permute-start.13 = (f32[16,256]{1,0:T(8,128)S(1)}, f32[16,256]{1,0:T(8,128)S(1)}, u32[]{:S(2)}, u32[]{:S(2)}) collective-permute-start(f32[16,256]{1,0:T(8,128)S(1)} %product.7), channel_id=1, source_target_pairs={{0,8},{8,0},{16,24},{24,16},{1,9},{9,1},{17,25},{25,17},{2,10},{10... | collective-permute-start | bytes 49160 | tf_op jit(solution)/shard_map/ppermute | solution.py:27
  65.2 3.8 %collective-permute-start.17 = (f32[16,256]{1,0:T(8,128)S(1)}, f32[16,256]{1,0:T(8,128)S(1)}, u32[]{:S(2)}, u32[]{:S(2)}) collective-permute-start(f32[16,256]{1,0:T(8,128)S(1)} %add_add_fusion.1), channel_id=1, source_target_pairs={{0,4},{4,0},{1,5},{5,1},{2,6},{6,2},{3,7},{7,3},{8,12},{12,8},{9,1... | collective-permute-start | bytes 49160 | tf_op jit(solution)/shard_map/ppermute | solution.py:27
  69.0 6.1 %collective-permute-start.20 = (f32[8,256]{1,0:T(8,128)S(1)}, f32[8,256]{1,0:T(8,128)S(1)}, u32[]{:S(2)}, u32[]{:S(2)}) collective-permute-start(f32[8,256]{1,0:T(8,128)S(1)} %slice_add_fusion.1), channel_id=1, source_target_pairs={{0,3},{1,2},{2,1},{3,0},{4,7},{5,6},{6,5},{7,4},{8,11},{9,10},{10,... | collective-permute-start | bytes 24584 | tf_op jit(solution)/shard_map/ppermute | solution.py:27
  71.5 5.2 %collective-permute-start.19 = (f32[8,256]{1,0:T(8,128)S(1)}, f32[8,256]{1,0:T(8,128)S(1)}, u32[]{:S(2)}, u32[]{:S(2)}) collective-permute-start(f32[8,256]{1,0:T(8,128)S(1)} %slice_add_fusion.1), channel_id=1, source_target_pairs={{0,2},{1,3},{2,0},{3,1},{4,6},{5,7},{6,4},{7,5},{8,10},{9,11},{10,... | collective-permute-start | bytes 24584 | tf_op jit(solution)/shard_map/ppermute | solution.py:27
  75.0 3.7 %collective-permute-start.18 = (f32[8,256]{1,0:T(8,128)S(1)}, f32[8,256]{1,0:T(8,128)S(1)}, u32[]{:S(2)}, u32[]{:S(2)}) collective-permute-start(f32[8,256]{1,0:T(8,128)S(1)} %slice_add_fusion.1), channel_id=1, source_target_pairs={{0,1},{1,0},{2,3},{3,2},{4,5},{5,4},{6,7},{7,6},{8,9},{9,8},{10,11... | collective-permute-start | bytes 24584 | tf_op jit(solution)/shard_map/ppermute | solution.py:27
  78.9 5.5 %collective-permute-start.23 = (f32[8,256]{1,0:T(8,128)S(1)}, f32[8,256]{1,0:T(8,128)S(1)}, u32[]{:S(2)}, u32[]{:S(2)}) collective-permute-start(f32[8,256]{1,0:T(8,128)S(1)} %fusion.3), channel_id=1, source_target_pairs={{0,3},{1,2},{2,1},{3,0},{4,7},{5,6},{6,5},{7,4},{8,11},{9,10},{10,... | collective-permute-start | bytes 24584 | tf_op jit(solution)/shard_map/ppermute | solution.py:27
  81.3 4.5 %collective-permute-start.22 = (f32[8,256]{1,0:T(8,128)S(1)}, f32[8,256]{1,0:T(8,128)S(1)}, u32[]{:S(2)}, u32[]{:S(2)}) collective-permute-start(f32[8,256]{1,0:T(8,128)S(1)} %fusion.3), channel_id=1, source_target_pairs={{0,2},{1,3},{2,0},{3,1},{4,6},{5,7},{6,4},{7,5},{8,10},{9,11},{10,... | collective-permute-start | bytes 24584 | tf_op jit(solution)/shard_map/ppermute | solution.py:27
  81.4 4.5 %collective-permute-start.21 = (f32[8,256]{1,0:T(8,128)S(1)}, f32[8,256]{1,0:T(8,128)S(1)}, u32[]{:S(2)}, u32[]{:S(2)}) collective-permute-start(f32[8,256]{1,0:T(8,128)S(1)} %fusion.3), channel_id=1, source_target_pairs={{0,1},{1,0},{2,3},{3,2},{4,5},{5,4},{6,7},{7,6},{8,9},{9,8},{10,11... | collective-permute-start | bytes 24584 | tf_op jit(solution)/shard_map/ppermute | solution.py:27
